TPU v7x, 128 devices: a whole 4x4x4 slice. The times are simulated.
128 devices in a mesh: row: 8 (over y, x_hi), col: 16 (over z, x_lo, core).
Axes of the slice: x: 4 (x_hi: 2, x_lo: 2; x = x_hi * 2 + x_lo), y: 4, z: 4, core: 2. Of those that a mesh axis runs over, the one named last changes fastest.
Arguments:
- ancestor_inverse: float32 [24576, 24576], P('row', 'col'), may hold values from -0.0546875 to 0.0546875
- lower_panel: float32 [2, 24576, 256], P(None, ('row', 'col')), may hold values from -6 to 6
- diag_factor: float32 [2, 256, 256], replicated, may hold values from -0.09375 to 0.09375
- diag_block: float32 [2, 256, 256], replicated, may hold values from -24 to 24
- pattern: int32 [2, 384], replicated, may hold values 0 or 1
Outputs:
- panel_inverse: float32 [2, 24576, 256], P(None, ('row', 'col'))
- diag_inverse: float32 [2, 256, 256], replicated
All inputs are finite; a program needn't handle non-finite values.
Results may differ from a plain program's by a relative error of at most 0.000071.
Values sent between devices are 32-bit elements; how exact they have to be, the bound alone decides.
No kernel may reach another device: no remote copies, remote signals or barrier semaphores. Data moves between devices by JAX's collectives and lax.ppermute only.
A program may use at most 128 MiB of HBM per device.

v0:
```python
import jax
import jax.numpy as jnp
from jax import lax
from jax.sharding import PartitionSpec as P

BS = 64
NS = 2


HIGHEST_PREC = lax.Precision.HIGHEST


def from_root(block, axis, owner):
    block = jnp.where(lax.axis_index(axis) == owner, block, jnp.zeros_like(block))
    return lax.psum(block, axis)


def mask_rows(pattern_part, row_start, length):
    blocks = lax.dynamic_slice_in_dim(pattern_part, row_start // BS, length // BS, 1)
    return jnp.repeat(blocks, BS, axis=1).astype(jnp.float32)


def local(ancestor_inverse, lower_panel, diag_factor, diag_block, pattern):
    row_count = lax.axis_size("row")
    col_count = lax.axis_size("col")
    row_index = lax.axis_index("row")
    col_index = lax.axis_index("col")
    piece_rows = lower_panel.shape[1]
    band_rows = ancestor_inverse.shape[0]
    strip_cols = ancestor_inverse.shape[1]
    piece_start = (row_index * col_count + col_index) * piece_rows
    panel_list = []
    diag_list = []
    for snode in range(NS):
        pattern_part = pattern[snode : snode + 1]
        local_mask = mask_rows(pattern_part, piece_start, piece_rows)
        normed = (
            jnp.einsum(
                "spw,swv->spv",
                lower_panel[snode : snode + 1],
                diag_factor[snode : snode + 1],
                precision=HIGHEST_PREC,
            )
            * local_mask[:, :, None]
        )
        gathered = lax.all_gather(normed, "col", axis=1, tiled=True)
        ratio = col_count // row_count
        offset = col_index % ratio * strip_cols
        selected = lax.dynamic_slice_in_dim(gathered, offset, strip_cols, 1)
        root_row = col_index * row_count // col_count
        transposed = from_root(selected, "row", root_row)
        term = -jnp.einsum("ij,sjw->isw", ancestor_inverse, transposed, precision=HIGHEST_PREC)
        totals = lax.psum(term, "col")
        band_mask = mask_rows(pattern_part, row_index * band_rows, band_rows)
        band_inverse = jnp.transpose(totals, (1, 0, 2)) * band_mask[:, :, None]
        panel_result = lax.dynamic_slice_in_dim(band_inverse, col_index * piece_rows, piece_rows, 1)
        partial_value = jnp.einsum("spw,spv->swv", gathered, band_inverse, precision=HIGHEST_PREC)
        update = lax.psum(partial_value, "row")
        diag_one = diag_block[snode : snode + 1] - update
        panel_list.append(panel_result)
        diag_list.append(diag_one)
    panel_inverse = jnp.concatenate(panel_list, axis=0)
    diag_inverse = jnp.concatenate(diag_list, axis=0)
    return (panel_inverse, diag_inverse)


def solution(mesh):
    return jax.shard_map(
        local,
        mesh=mesh,
        in_specs=(P("row", "col"), P(None, ("row", "col"), None), P(), P(), P()),
        out_specs=(P(None, ("row", "col"), None), P()),
        check_vma=False,
    )
```

profile of v0, /device:TPU:0, one launch (start us, length us, event | category | flops | bytes accessed | tf_op | source)
XLA Modules:
  0.0 577.2 jit_solution(4160613363360111562)
XLA Ops:
  7.2 0.0 all-gather.5.cloned.1.call-start
  7.2 0.8 fusion.32
  8.0 0.1 fusion.25
  8.1 0.1 broadcast_in_dim.16
  8.1 0.1 convert_element_type.66
  8.2 2.1 convolution_multiply_fusion.1
  10.3 0.0 all-gather.5.cloned.1.call-update
  10.3 0.0 all-gather.7.cloned.1.call-start
  10.4 0.1 broadcast_in_dim.18
  10.4 0.1 convert_element_type.72
  10.5 2.1 convolution_multiply_fusion
  12.6 0.0 all-gather.7.cloned.1.call-update
  12.6 0.0 all-reduce.11.cloned.1.call-start
  12.7 36.3 %all-gather.5.cloned.1.call-done = f32[3072,256]{1,0:T(8,128)} async-done(((f32[192,256]{1,0:T(8,128)}), f32[3072,256]{1,0:T(8,128)}) %all-gather.5.cloned.1.call-update) | async-done | bytes 3145744 | tf_op jit(solution)/shard_map/all_gather | solution.py:46
  49.0 2.7 dynamic-slice_select_fusion.1
  51.7 35.6 %all-gather.7.cloned.1.call-done = f32[3072,256]{1,0:T(8,128)} async-done(((f32[192,256]{1,0:T(8,128)}), f32[3072,256]{1,0:T(8,128)}) %all-gather.7.cloned.1.call-update) | async-done | bytes 3145744 | tf_op jit(solution)/shard_map/all_gather | solution.py:46
  87.3 2.7 dynamic-slice_select_fusion
  89.9 0.0 all-reduce.11.cloned.1.call-update
  89.9 0.0 all-reduce.7.cloned.1.call-start
  90.0 146.5 %all-reduce.11.cloned.1.call-done = (f32[1536,256]{1,0:T(8,128)}, f32[1536,256]{1,0:T(8,128)}) async-done(((f32[1536,256]{1,0:T(8,128)}, f32[1536,256]{1,0:T(8,128)}), (f32[1536,256]{1,0:T(8,128)}, f32[1536,256]{1,0:T(8,128)})) %all-reduce.11.cloned.1.call-update) | async-done | bytes 3145744 | tf_op jit(solution)/shard_map/psum | solution.py:15
  236.5 35.6 %fusion = f32[3072,1,256]{0,2,1:T(8,128)} fusion(f32[1536,256]{1,0:T(8,128)} %get-tuple-element.8, f32[3072,1536]{1,0:T(8,128)} %param.5), kind=kOutput, calls=%fused_computation.1 | convolution fusion | flops 14496301056 | bytes 23592960 | tf_op jit(solution)/shard_map/ij,sjw->isw/dot_general | solution.py:52
  272.1 0.0 slice-done
  272.1 0.0 slice-done.1
  272.1 0.0 slice-done.3
  272.2 0.0 slice-done.4
  272.2 0.0 copy-done.3
  272.2 43.1 %fusion.1 = f32[3072,1,256]{0,2,1:T(8,128)} fusion(f32[1536,256]{1,0:T(8,128)S(1)} %copy-done.3, f32[3072,1536]{1,0:T(8,128)S(1)} %bitcast.51), kind=kOutput, calls=%fused_computation.3 | convolution fusion | flops 14496301056 | bytes 23592960 | tf_op jit(solution)/shard_map/ij,sjw->isw/dot_general | solution.py:52
  315.3 0.0 all-reduce.7.cloned.1.call-update
  315.3 0.0 all-reduce.9.cloned.1.call-start
  315.4 0.1 fusion.27
  315.5 0.1 broadcast_in_dim.17
  315.6 0.1 convert_element_type.69
  315.6 0.1 broadcast_in_dim.19
  315.7 0.1 convert_element_type.75
  315.8 0.1 dynamic-slice.2
  315.9 0.1 dynamic-slice.3
  315.9 153.4 %all-reduce.7.cloned.1.call-done = (f32[3072,1,256]{0,2,1:T(8,128)}, f32[3072,1,256]{0,2,1:T(8,128)}) async-done(((f32[3072,1,256]{0,2,1:T(8,128)}, f32[3072,1,256]{0,2,1:T(8,128)}), (f32[3072,1,256]{0,2,1:T(8,128)}, f32[3072,1,256]{0,2,1:T(8,128)})) %all-reduce.7.cloned.1.call-update) | async-done | bytes 6291472 | tf_op jit(solution)/shard_map/psum | solution.py:53
  469.3 0.0 copy-done
  469.3 7.9 %fusion.10 = f32[1,256,256]{2,1,0:T(8,128)} fusion(f32[3072,256]{1,0:T(8,128)S(1)} %copy-done, f32[3072,1,256]{0,2,1:T(8,128)} %get-tuple-element.5, f32[3072]{0:T(1024)S(1)} %convert_element_type.69), kind=kOutput, calls=%fused_computation.14 | convolution fusion | flops 2416705536 | bytes 6565888 | tf_op jit(solution)/shard_map/spw,spv->swv/dot_general | solution.py:57
  477.2 0.0 copy-done.2
  477.2 6.0 %fusion.13 = f32[1,256,256]{2,1,0:T(8,128)} fusion(f32[3072,256]{1,0:T(8,128)S(1)} %copy-done.1, f32[3072,1,256]{0,2,1:T(8,128)S(1)} %copy-done.2, f32[3072]{0:T(1024)S(1)} %convert_element_type.75), kind=kOutput, calls=%fused_computation.15 | convolution fusion | flops 2416705536 | bytes 6565888 | tf_op jit(solution)/shard_map/spw,spv->swv/dot_general | solution.py:57
  483.2 0.0 all-reduce.9.cloned.1.call-update
  483.2 1.2 dynamic-slice_multiply_fusion.1
  484.4 1.1 dynamic-slice_multiply_fusion
  485.6 0.9 copy.7
  486.6 81.8 %all-reduce.9.cloned.1.call-done = (f32[1,256,256]{2,1,0:T(8,128)}, f32[1,256,256]{2,1,0:T(8,128)}) async-done(((f32[1,256,256]{2,1,0:T(8,128)}, f32[1,256,256]{2,1,0:T(8,128)}), (f32[1,256,256]{2,1,0:T(8,128)}, f32[1,256,256]{2,1,0:T(8,128)})) %all-reduce.9.cloned.1.call-update) | async-done | bytes 524304 | tf_op jit(solution)/shard_map/psum | solution.py:58
  568.4 1.1 slice_subtract_fusion.1
  569.5 0.8 pad_maximum_fusion.1
  (15 shorter events, 0.1 us)
Async XLA Ops:
  7.2 41.8 %all-gather.5.cloned.1.call-start = ((), (), s32[]{:S(2)}) async-start(), calls=%async_computation | async-start | bytes 3342336 | tf_op jit(solution)/shard_map/all_gather | solution.py:46
  10.3 76.9 %all-gather.7.cloned.1.call-start = ((), (), s32[]{:S(2)}) async-start(), calls=%async_computation.1 | async-start | bytes 3342336 | tf_op jit(solution)/shard_map/all_gather | solution.py:46
  12.6 223.9 %all-reduce.11.cloned.1.call-start = ((), (), s32[]{:S(2)}) async-start(), calls=%async_computation.4 | async-start | bytes 6291456 | tf_op jit(solution)/shard_map/psum | solution.py:15
  89.9 182.2 %slice-start = ((s8[18874368]{0:T(1024)(128)(4,1)}), s8[2097152]{0:T(1024)(128)(4,1)S(1)}, s32[]{:S(2)}) async-start(s8[18874368]{0:T(1024)(128)(4,1)} %bitcast.50), calls=%async_computation.5 | async-start | bytes 4194304
  89.9 379.4 %all-reduce.7.cloned.1.call-start = ((), (), s32[]{:S(2)}) async-start(), calls=%async_computation.2 | async-start | bytes 12582912 | tf_op jit(solution)/shard_map/psum | solution.py:53
  236.5 35.7 %slice-start.1 = ((s8[18874368]{0:T(1024)(128)(4,1)}), s8[4194304]{0:T(1024)(128)(4,1)S(1)}, s32[]{:S(2)}) async-start(s8[18874368]{0:T(1024)(128)(4,1)} %bitcast.50), calls=%async_computation.6 | async-start | bytes 8388608
  236.5 35.7 %slice-start.2 = ((s8[18874368]{0:T(1024)(128)(4,1)}), s8[4194304]{0:T(1024)(128)(4,1)S(1)}, s32[]{:S(2)}) async-start(s8[18874368]{0:T(1024)(128)(4,1)} %bitcast.50), calls=%async_computation.7 | async-start | bytes 8388608
  236.5 35.7 %slice-start.3 = ((s8[18874368]{0:T(1024)(128)(4,1)}), s8[4194304]{0:T(1024)(128)(4,1)S(1)}, s32[]{:S(2)}) async-start(s8[18874368]{0:T(1024)(128)(4,1)} %bitcast.50), calls=%async_computation.8 | async-start | bytes 8388608
  236.5 35.7 %slice-start.4 = ((s8[18874368]{0:T(1024)(128)(4,1)}), s8[4194304]{0:T(1024)(128)(4,1)S(1)}, s32[]{:S(2)}) async-start(s8[18874368]{0:T(1024)(128)(4,1)} %bitcast.50), calls=%async_computation.9 | async-start | bytes 8388608
  236.5 35.7 %copy-start.3 = (f32[1536,256]{1,0:T(8,128)S(1)}, f32[1536,256]{1,0:T(8,128)}, u32[]{:S(2)}) copy-start(f32[1536,256]{1,0:T(8,128)} %get-tuple-element.9) | copy-start | bytes 4718596
  315.3 154.0 %copy-start = (f32[3072,256]{1,0:T(8,128)S(1)}, f32[3072,256]{1,0:T(8,128)}, u32[]{:S(2)}) copy-start(f32[3072,256]{1,0:T(8,128)} %all-gather.5.cloned.1.call-done) | copy-start | bytes 9437188
  315.3 253.0 %all-reduce.9.cloned.1.call-start = ((), (), s32[]{:S(2)}) async-start(), calls=%async_computation.3 | async-start | bytes 1048576 | tf_op jit(solution)/shard_map/psum | solution.py:58
  469.3 7.9 %copy-start.1 = (f32[3072,256]{1,0:T(8,128)S(1)}, f32[3072,256]{1,0:T(8,128)}, u32[]{:S(2)}) copy-start(f32[3072,256]{1,0:T(8,128)} %all-gather.7.cloned.1.call-done) | copy-start | bytes 9437188
  469.3 7.9 %copy-start.2 = (f32[3072,1,256]{0,2,1:T(8,128)S(1)}, f32[3072,1,256]{0,2,1:T(8,128)}, u32[]{:S(2)}) copy-start(f32[3072,1,256]{0,2,1:T(8,128)} %get-tuple-element.4) | copy-start | bytes 9437188
  483.2 85.2 %copy-start.4 = (f32[2,256,256]{2,1,0:T(8,128)S(1)}, f32[2,256,256]{2,1,0:T(8,128)}, u32[]{:S(2)}) copy-start(f32[2,256,256]{2,1,0:T(8,128)} %param.8) | copy-start | bytes 1572868
Sparse Core Ops, SparseCore 0:
  10.4 38.5 all-gather.4
  51.3 35.9 all-gather.6
  90.1 146.3 all-reduce.10
  315.5 153.8 all-reduce.6
  483.4 84.9 all-reduce.8
where the time goes:
time: 586 us; the launch traced here: 577 us
  waiting for transfers between devices  454 us (77%)
  matrix products  96.8 us (17%)
  between operations  14.3 us (2%)
  other arithmetic  9.8 us (2%)
    psum x1, waiting for transfers between devices, local(): totals = lax.psum(term, 'col')  153 us
    psum x1, waiting for transfers between devices, from_root(): return lax.psum(block, axis)  146 us
    psum x1, waiting for transfers between devices, local(): update = lax.psum(partial_value, 'row')  81.8 us
    dot_general x2, matrix products, local(): jnp.einsum('ij,sjw->isw', ancestor_inverse, transposed, precision=HIGHEST...  78.8 us
    all_gather x2, waiting for transfers between devices, local(): gathered = lax.all_gather(normed, 'col', axis=1, tiled=True)  71.9 us
    dot_general x2, matrix products, local(): jnp.einsum('spw,spv->swv', gathered, band_inverse, precision=HIGHEST_PREC)  13.9 us
  transfers between devices with their start and end apart: 5, of which 5 were waited for; matrix products, arithmetic and copies ran while one was open for 2% of the time, Pallas kernels for 0%

commit v1 on v0

v1 whole, which is shorter than its diff:
```python
import jax
import jax.numpy as jnp
from jax import lax
from jax.sharding import Mesh, PartitionSpec as P

BS = 64
NS = 2
HIGH = lax.Precision.HIGH
ALL = ("y", "xh", "z", "xl", "k")


def send(x, axis, size, to):
    return lax.ppermute(x, axis, [(i, to(i)) for i in range(size)])


def transpose_pairs():
    return [(8 * c + r, 16 * r + c) for r in range(8) for c in range(16)]


def tile_mask(pattern, snode, start, length):
    tiles = lax.dynamic_slice_in_dim(pattern[snode], start // BS, length // BS, 0)
    return jnp.repeat(tiles, BS).astype(jnp.float32)[:, None]


def scatter_four(x, axis):
    me = lax.axis_index(axis)
    rows = x.shape[0] // 4
    part = lambda i: lax.dynamic_slice_in_dim(x, lax.rem(i, 4) * rows, rows, 0)
    got = [send(part(me + d), axis, 4, lambda i, d=d: (i + d) % 4) for d in (1, 2, 3)]
    return part(me) + got[0] + got[1] + got[2]


def others_four(x, axis):
    return [send(x, axis, 4, lambda i, d=d: (i + d) % 4) for d in (1, 2, 3)]


def sum_four(x, axis):
    got = others_four(x, axis)
    return x + got[0] + got[1] + got[2]


def gather_four(x, axis):
    me = lax.axis_index(axis)
    one, two, three = others_four(x, axis)
    twice = jnp.concatenate([three, two, one, x, three, two, one], axis=0)
    return lax.dynamic_slice_in_dim(twice, (3 - me) * x.shape[0], 4 * x.shape[0], 0)


def swap_core(x):
    return send(x, "k", 2, lambda i: i ^ 1)


def total(x):
    k = lax.axis_index("k")
    half = x.shape[0] // 2
    mine = lax.dynamic_slice_in_dim(x, k * half, half, 0)
    theirs = lax.dynamic_slice_in_dim(x, (1 - k) * half, half, 0)
    mine = mine + swap_core(theirs)
    mine = scatter_four(mine, "y")
    mine = sum_four(mine, "z")
    mine = mine + send(mine, "xl", 2, lambda i: i ^ 1)
    mine = mine + send(mine, "xh", 2, lambda i: i ^ 1)
    mine = gather_four(mine, "y")
    other = swap_core(mine)
    low = jnp.where(k == 0, mine, other)
    high = jnp.where(k == 0, other, mine)
    return jnp.concatenate([low, high], axis=0)


def local(ancestor_inverse, lower_panel, diag_factor, diag_block, pattern):
    y, xh, z, xl, k = (lax.axis_index(a) for a in ALL)
    row, col = y * 2 + xh, z * 4 + xl * 2 + k
    piece = lower_panel.shape[1]
    cols = ancestor_inverse.shape[1]
    width = lower_panel.shape[2]
    panels, diags = [], []
    for snode in range(NS):
        one = lower_panel[snode]
        factor = diag_factor[snode]
        piece_mask = tile_mask(pattern, snode, (row * 16 + col) * piece, piece)
        normed = jnp.dot(one, factor, precision=HIGH) * piece_mask

        mine = lax.ppermute(one, ALL, transpose_pairs())
        pair = send(mine, "xh", 2, lambda i: i ^ 1)
        mine1 = send(mine, "y", 4, lambda i: i ^ 1)
        pair3 = send(pair, "y", 4, lambda i: i ^ 3)
        both = jnp.stack([mine, mine1])
        mine32 = send(both, "y", 4, lambda i: i ^ 3)
        both = jnp.stack([pair, pair3])
        pair12 = send(both, "y", 4, lambda i: i ^ 1)
        parts = jnp.stack([mine, pair, mine1, pair12[0], mine32[1], pair12[1], mine32[0], pair3])
        places = jnp.arange(8)
        order = ((places // 2) ^ y) * 2 + ((places % 2) ^ xh)
        block = parts[order].reshape(cols, width)
        x = jnp.dot(block, factor, precision=HIGH) * tile_mask(pattern, snode, col * cols, cols)

        out = jnp.dot(ancestor_inverse, x, precision=HIGH)
        out = out.reshape(4, 2, 2, piece, width)
        keep = lax.dynamic_slice_in_dim(out, k, 1, 2)[:, :, 0]
        give = lax.dynamic_slice_in_dim(out, 1 - k, 1, 2)[:, :, 0]
        summed = keep + swap_core(give)
        summed = lax.psum_scatter(summed, "z", scatter_dimension=0, tiled=False)
        keep = lax.dynamic_slice_in_dim(summed, xl, 1, 0)[0]
        give = lax.dynamic_slice_in_dim(summed, 1 - xl, 1, 0)[0]
        summed = keep + send(give, "xl", 2, lambda i: i ^ 1)
        panel = -piece_mask * summed
        panels.append(panel)
        update = lax.dot_general(normed, panel, (((0,), (0,)), ((), ())), precision=HIGH)
        diags.append(diag_block[snode] - total(update))
    return jnp.stack(panels), jnp.stack(diags)


def solution(mesh):
    fine = Mesh(mesh.devices.reshape(4, 2, 4, 2, 2), ALL)
    rows, cols = ("y", "xh"), ("z", "xl", "k")
    return jax.shard_map(
        local,
        mesh=fine,
        in_specs=(P(rows, cols), P(None, ALL, None), P(), P(), P()),
        out_specs=(P(None, ALL, None), P()),
        check_vma=False,
    )
```

time: 586 us -> 231 us (0.39); the launches traced: 577 us -> 229 us
  waiting for transfers between devices: 454 us -> 63.6 us
  starting transfers between devices: 0.21 us -> 64.4 us
  matrix products: 96.8 us -> 45.3 us
  local copies, waits for them, and re-layouts: 2.48 us -> 32.6 us
    psum x3 -> x0, waiting for transfers between devices: 382 us -> none  [the longest x1 153 us: local(): totals = lax.psum(term, 'col')]
    all_gather x2 -> x0, waiting for transfers between devices: 71.9 us -> none  [local(): gathered = lax.all_gather(normed, 'col', axis=1, tiled=True)]
    ppermute x0 -> x42, starting transfers between devices: none -> 64.2 us  [the longest x40 62.8 us: send(): return lax.ppermute(x, axis, [(i, to(i)) for i in range(size)])]
    dot_general x6 -> x8, matrix products: 96.8 us -> 45.3 us  [the longest x2 41.3 us: local(): out = jnp.dot(ancestor_inverse, x, precision=HIGH)]
    ppermute x0 -> x42, waiting for transfers between devices: none -> 41.6 us  [the longest x40 41.6 us: send(): return lax.ppermute(x, axis, [(i, to(i)) for i in range(size)])]
    reduce_scatter x0 -> x2, waiting for transfers between devices: none -> 21.9 us  [local(): summed = lax.psum_scatter(summed, 'z', scatter_dimension=0, tiled=False)]
    unnamed x21 -> x46, local copies, waits for them, and re-layouts: 0.97 us -> 15.1 us
  transfers between devices with their start and end apart: 5 -> 44, of which waited for: 5 -> 17; matrix products, arithmetic and copies ran while one was open for 2% -> 35% of each run, Pallas kernels for 0% -> 0%
where the time goes in v1:
time: 231 us; the launch traced here: 229 us
  starting transfers between devices  64.4 us (28%)
  waiting for transfers between devices  63.6 us (28%)
  matrix products  45.3 us (20%)
  local copies, waits for them, and re-layouts  32.6 us (14%)
  between operations  14.6 us (6%)
  other arithmetic  8.72 us (4%)
    ppermute x40, starting transfers between devices, send(): return lax.ppermute(x, axis, [(i, to(i)) for i in range(size)])  62.8 us
    ppermute x40, waiting for transfers between devices, send(): return lax.ppermute(x, axis, [(i, to(i)) for i in range(size)])  41.6 us
    dot_general x2, matrix products, local(): out = jnp.dot(ancestor_inverse, x, precision=HIGH)  41.3 us
    reduce_scatter x2, waiting for transfers between devices, local(): summed = lax.psum_scatter(summed, 'z', scatter_dimension=0, tiled=False)  21.9 us
    unnamed x46, local copies, waits for them, and re-layouts  15.1 us
    gather x2, local copies, waits for them, and re-layouts, local(): block = parts[order].reshape(cols, width)  5.35 us
    dot_general x2, local copies, waits for them, and re-layouts, local(): out = jnp.dot(ancestor_inverse, x, precision=HIGH)  4.79 us
  transfers between devices with their start and end apart: 44, of which 17 were waited for; matrix products, arithmetic and copies ran while one was open for 35% of the time, Pallas kernels for 0%

profile of v1, /device:TPU:0, one launch (start us, length us, event | category | flops | bytes accessed | tf_op | source)
XLA Modules:
  0.0 229.3 jit_solution(6872172298410164351)
XLA Ops:
  7.2 1.1 slice_bitcast_fusion.1
  11.3 8.6 %collective-permute-start.9 = (f32[192,256]{1,0:T(8,128)S(1)}, f32[192,256]{1,0:T(8,128)S(1)}, u32[]{:S(2)}, u32[]{:S(2)}) collective-permute-start(f32[192,256]{1,0:T(8,128)S(1)} %collective-permute-done.8), channel_id=1, source_target_pairs={{0,16},{16,0},{1,17},{17,1},{2,18},{18,2},{3,19},{19,3},{4,20},{20... | collective-permute-start | bytes 589832 | tf_op jit(solution)/shard_map/ppermute | solution.py:13
  20.0 5.1 %collective-permute-start.10 = (f32[192,256]{1,0:T(8,128)S(1)}, f32[192,256]{1,0:T(8,128)S(1)}, u32[]{:S(2)}, u32[]{:S(2)}) collective-permute-start(f32[192,256]{1,0:T(8,128)S(1)} %collective-permute-done.8), channel_id=1, source_target_pairs={{0,32},{32,0},{64,96},{96,64},{1,33},{33,1},{65,97},{97,65},{2,34}... | collective-permute-start | bytes 589832 | tf_op jit(solution)/shard_map/ppermute | solution.py:13
  25.9 5.6 %collective-permute-start.2 = (f32[192,256]{1,0:T(8,128)S(1)}, f32[192,256]{1,0:T(8,128)S(1)}, u32[]{:S(2)}, u32[]{:S(2)}) collective-permute-start(f32[192,256]{1,0:T(8,128)S(1)} %collective-permute-done), channel_id=1, source_target_pairs={{0,32},{32,0},{64,96},{96,64},{1,33},{33,1},{65,97},{97,65},{2,34}... | collective-permute-start | bytes 589832 | tf_op jit(solution)/shard_map/ppermute | solution.py:13
  32.2 2.8 %collective-permute-done.1 = f32[192,256]{1,0:T(8,128)S(1)} collective-permute-done((f32[192,256]{1,0:T(8,128)S(1)}, f32[192,256]{1,0:T(8,128)S(1)}, u32[]{:S(2)}, u32[]{:S(2)}) %collective-permute-start.1) | collective-permute-done | bytes 196640 | tf_op jit(solution)/shard_map/ppermute | solution.py:13
  35.0 2.5 %collective-permute-start.3 = (f32[192,256]{1,0:T(8,128)S(1)}, f32[192,256]{1,0:T(8,128)S(1)}, u32[]{:S(2)}, u32[]{:S(2)}) collective-permute-start(f32[192,256]{1,0:T(8,128)S(1)} %collective-permute-done.1), channel_id=1, source_target_pairs={{0,96},{32,64},{64,32},{96,0},{1,97},{33,65},{65,33},{97,1},{2,98}... | collective-permute-start | bytes 589832 | tf_op jit(solution)/shard_map/ppermute | solution.py:13
  39.0 2.6 %collective-permute-start.5 = (f32[2,192,256]{2,1,0:T(8,128)S(1)}, f32[2,192,256]{2,1,0:T(8,128)S(1)}, u32[]{:S(2)}, u32[]{:S(2)}) collective-permute-start(f32[2,192,256]{2,1,0:T(8,128)S(1)} %pad_maximum_fusion.2), channel_id=1, source_target_pairs={{0,96},{32,64},{64,32},{96,0},{1,97},{33,65},{65,33},{97,1},{2,98}... | collective-permute-start | bytes 1179656 | tf_op jit(solution)/shard_map/ppermute | solution.py:13
  42.3 1.6 collective-permute-done.3
  46.3 18.6 %collective-permute-done.11 = f32[192,256]{1,0:T(8,128)S(1)} collective-permute-done((f32[192,256]{1,0:T(8,128)S(1)}, f32[192,256]{1,0:T(8,128)S(1)}, u32[]{:S(2)}, u32[]{:S(2)}) %collective-permute-start.11) | collective-permute-done | bytes 196640 | tf_op jit(solution)/shard_map/ppermute | solution.py:13
  69.6 2.1 gather_fusion
  72.5 20.7 %convolution_bitcast_fusion.1 = f32[3072,256]{0,1:T(8,128)} fusion(f32[1536,256]{1,0:T(8,128)S(1)} %convolution_multiply_fusion.1, f32[3072,1536]{1,0:T(8,128)} %param.5), kind=kOutput, calls=%fused_computation.3 | convolution fusion | flops 7247757312 | bytes 23592960 | tf_op jit(solution)/shard_map/dot_general | solution.py:97
  93.2 2.4 %copy.7 = f32[3072,256]{1,0:T(8,128)S(1)} copy(f32[3072,256]{0,1:T(8,128)} %convolution_bitcast_fusion.1) | data formatting | bytes 6291456 | tf_op jit(solution)/shard_map/dot_general | solution.py:97
  95.6 1.3 dynamic-slice_bitcast_fusion.1
  98.3 1.6 slice_dynamic-update-slice_fusion.3
  99.9 1.6 slice_dynamic-update-slice_fusion.2
  101.5 1.6 slice_dynamic-update-slice_fusion.1
  103.1 1.6 slice_dynamic-update-slice_fusion
  105.5 3.2 %gather_fusion.1 = f32[8,192,256]{2,1,0:T(8,128)} fusion(f32[8,192,256]{2,1,0:T(8,128)} %constant_dynamic-update-slice_fusion.4, s32[1024]{0:T(1024)S(1)} %pad_clamp_fusion), kind=kCustom, calls=%fused_computation.1 | custom fusion | bytes 3145760 | tf_op jit(solution)/shard_map/gather | solution.py:94
  108.7 2.8 %bitcast_add_fusion.1 = f32[4,2,192,256]{3,2,1,0:T(8,128)} fusion(f32[4,2,192,256]{3,2,1,0:T(8,128)} %collective-permute-done.6, f32[4,2,2,192,256]{4,3,2,1,0:T(8,128)S(1)} %bitcast.97, s32[]{:T(128)S(6)} %select_n.128), kind=kLoop, calls=%fused_computation.7 | loop fusion | flops 393216 | bytes 4718596 | tf_op jit(solution)/shard_map/add | solution.py:101
  111.7 1.2 copy-done
  112.9 1.7 convolution_multiply_fusion
  114.7 20.7 %convolution_bitcast_fusion = f32[3072,256]{0,1:T(8,128)} fusion(f32[1536,256]{1,0:T(8,128)S(1)} %convolution_multiply_fusion, f32[3072,1536]{1,0:T(8,128)} %param.5), kind=kOutput, calls=%fused_computation.2 | convolution fusion | flops 7247757312 | bytes 23592960 | tf_op jit(solution)/shard_map/dot_general | solution.py:97
  135.3 2.4 %copy.8 = f32[3072,256]{1,0:T(8,128)S(1)} copy(f32[3072,256]{0,1:T(8,128)} %convolution_bitcast_fusion) | data formatting | bytes 6291456 | tf_op jit(solution)/shard_map/dot_general | solution.py:97
  138.4 3.0 %collective-permute-done.14 = f32[4,2,192,256]{3,2,1,0:T(8,128)S(1)} collective-permute-done((f32[4,2,192,256]{3,2,1,0:T(8,128)S(1)}, f32[4,2,192,256]{3,2,1,0:T(8,128)S(1)}, u32[]{:S(2)}, u32[]{:S(2)}) %collective-permute-start.14) | collective-permute-done | bytes 1572896 | tf_op jit(solution)/shard_map/ppermute | solution.py:13
  141.5 1.4 bitcast_add_fusion
  144.3 1.0 dynamic-slice_bitcast_fusion.3
  145.4 1.5 collective-permute-start.7
  147.2 21.9 %reduce-scatter.5.cloned.1.call-done = f32[1,2,192,256]{3,2,1,0:T(8,128)} async-done(((f32[4,2,192,256]{3,2,1,0:T(8,128)}), f32[1,2,192,256]{3,2,1,0:T(8,128)}) %reduce-scatter.5.cloned.1.call-update) | async-done | bytes 393232 | tf_op jit(solution)/shard_map/reduce_scatter | solution.py:102
  169.1 1.0 dynamic-slice_bitcast_fusion.2
  170.1 1.6 collective-permute-start.15
  172.3 3.8 %collective-permute-done.15 = f32[192,256]{1,0:T(8,128)S(1)} collective-permute-done((f32[192,256]{1,0:T(8,128)S(1)}, f32[192,256]{1,0:T(8,128)S(1)}, u32[]{:S(2)}, u32[]{:S(2)}) %collective-permute-start.15) | collective-permute-done | bytes 196640 | tf_op jit(solution)/shard_map/ppermute | solution.py:13
  176.8 2.8 %collective-permute-start.19 = (f32[32,256]{1,0:T(8,128)S(1)}, f32[32,256]{1,0:T(8,128)S(1)}, u32[]{:S(2)}, u32[]{:S(2)}) collective-permute-start(f32[32,256]{1,0:T(8,128)S(1)} %get-tuple-element.11), channel_id=1, source_target_pairs={{0,96},{32,0},{64,32},{96,64},{1,97},{33,1},{65,33},{97,65},{2,98}... | collective-permute-start | bytes 98312 | tf_op jit(solution)/shard_map/ppermute | solution.py:13
  181.4 2.4 %collective-permute-start.32 = (f32[32,256]{1,0:T(8,128)S(1)}, f32[32,256]{1,0:T(8,128)S(1)}, u32[]{:S(2)}, u32[]{:S(2)}) collective-permute-start(f32[32,256]{1,0:T(8,128)S(1)} %get-tuple-element.14), channel_id=1, source_target_pairs={{0,96},{32,0},{64,32},{96,64},{1,97},{33,1},{65,33},{97,65},{2,98}... | collective-permute-start | bytes 98312 | tf_op jit(solution)/shard_map/ppermute | solution.py:13
  183.8 1.5 collective-permute-start.31
  185.6 1.9 collective-permute-start.22
  189.3 1.2 collective-permute-done.30
  190.5 1.9 collective-permute-start.35
  193.6 1.6 collective-permute-start.23
  195.2 2.6 %collective-permute-done.34 = f32[32,256]{1,0:T(8,128)S(1)} collective-permute-done((f32[32,256]{1,0:T(8,128)S(1)}, f32[32,256]{1,0:T(8,128)S(1)}, u32[]{:S(2)}, u32[]{:S(2)}) %collective-permute-start.34) | collective-permute-done | bytes 32800 | tf_op jit(solution)/shard_map/ppermute | solution.py:13
  198.5 1.6 collective-permute-start.36
  200.1 2.8 %collective-permute-start.24 = (f32[32,256]{1,0:T(8,128)S(1)}, f32[32,256]{1,0:T(8,128)S(1)}, u32[]{:S(2)}, u32[]{:S(2)}) collective-permute-start(f32[32,256]{1,0:T(8,128)S(1)} %add.229), channel_id=1, source_target_pairs={{0,16},{16,0},{1,17},{17,1},{2,18},{18,2},{3,19},{19,3},{4,20},{20... | collective-permute-start | bytes 98312 | tf_op jit(solution)/shard_map/ppermute | solution.py:13
  203.0 2.5 %collective-permute-start.37 = (f32[32,256]{1,0:T(8,128)S(1)}, f32[32,256]{1,0:T(8,128)S(1)}, u32[]{:S(2)}, u32[]{:S(2)}) collective-permute-start(f32[32,256]{1,0:T(8,128)S(1)} %add.239), channel_id=1, source_target_pairs={{0,16},{16,0},{1,17},{17,1},{2,18},{18,2},{3,19},{19,3},{4,20},{20... | collective-permute-start | bytes 98312 | tf_op jit(solution)/shard_map/ppermute | solution.py:13
  205.6 2.9 %collective-permute-start.25 = (f32[32,256]{1,0:T(8,128)S(1)}, f32[32,256]{1,0:T(8,128)S(1)}, u32[]{:S(2)}, u32[]{:S(2)}) collective-permute-start(f32[32,256]{1,0:T(8,128)S(1)} %add.230), channel_id=1, source_target_pairs={{0,96},{32,0},{64,32},{96,64},{1,97},{33,1},{65,33},{97,65},{2,98}... | collective-permute-start | bytes 98312 | tf_op jit(solution)/shard_map/ppermute | solution.py:13
  210.1 3.3 %collective-permute-start.38 = (f32[32,256]{1,0:T(8,128)S(1)}, f32[32,256]{1,0:T(8,128)S(1)}, u32[]{:S(2)}, u32[]{:S(2)}) collective-permute-start(f32[32,256]{1,0:T(8,128)S(1)} %add.240), channel_id=1, source_target_pairs={{0,96},{32,0},{64,32},{96,64},{1,97},{33,1},{65,33},{97,65},{2,98}... | collective-permute-start | bytes 98312 | tf_op jit(solution)/shard_map/ppermute | solution.py:13
  213.4 1.5 collective-permute-start.39
  215.4 3.4 %collective-permute-done.39 = f32[32,256]{1,0:T(8,128)S(1)} collective-permute-done((f32[32,256]{1,0:T(8,128)S(1)}, f32[32,256]{1,0:T(8,128)S(1)}, u32[]{:S(2)}, u32[]{:S(2)}) %collective-permute-start.39) | collective-permute-done | bytes 32800 | tf_op jit(solution)/shard_map/ppermute | solution.py:13
  218.8 1.2 collective-permute-done.40
  220.2 1.3 collective-permute-done.41
  (153 shorter events, 29.6 us)
Async XLA Ops:
  7.2 137.2 %reduce-scatter.3.cloned.1.call-start = ((), (), s32[]{:S(2)}) async-start(), calls=%async_computation.2 | async-start | bytes 1966080 | tf_op jit(solution)/shard_map/reduce_scatter | solution.py:102
  8.3 3.1 %collective-permute-start.8 = (f32[192,256]{1,0:T(8,128)S(1)}, f32[192,256]{1,0:T(8,128)S(1)}, u32[]{:S(2)}, u32[]{:S(2)}) collective-permute-start(f32[192,256]{1,0:T(8,128)S(1)} %get-tuple-element.5), channel_id=1, source_target_pairs={{0,0},{8,1},{16,2},{24,3},{32,4},{40,5},{48,6},{56,7},{64,8},{72,9... | collective-permute-start | bytes 589832 | tf_op jit(solution)/shard_map/ppermute | solution.py:83
  8.9 16.8 %collective-permute-start = (f32[192,256]{1,0:T(8,128)S(1)}, f32[192,256]{1,0:T(8,128)S(1)}, u32[]{:S(2)}, u32[]{:S(2)}) collective-permute-start(f32[192,256]{1,0:T(8,128)S(1)} %get-tuple-element.4), channel_id=1, source_target_pairs={{0,0},{8,1},{16,2},{24,3},{32,4},{40,5},{48,6},{56,7},{64,8},{72,9... | collective-permute-start | bytes 589832 | tf_op jit(solution)/shard_map/ppermute | solution.py:83
  11.3 30.3 %collective-permute-start.9 = (f32[192,256]{1,0:T(8,128)S(1)}, f32[192,256]{1,0:T(8,128)S(1)}, u32[]{:S(2)}, u32[]{:S(2)}) collective-permute-start(f32[192,256]{1,0:T(8,128)S(1)} %collective-permute-done.8), channel_id=1, source_target_pairs={{0,16},{16,0},{1,17},{17,1},{2,18},{18,2},{3,19},{19,3},{4,20},{20... | collective-permute-start | bytes 589832 | tf_op jit(solution)/shard_map/ppermute | solution.py:13
  20.0 17.5 %collective-permute-start.10 = (f32[192,256]{1,0:T(8,128)S(1)}, f32[192,256]{1,0:T(8,128)S(1)}, u32[]{:S(2)}, u32[]{:S(2)}) collective-permute-start(f32[192,256]{1,0:T(8,128)S(1)} %collective-permute-done.8), channel_id=1, source_target_pairs={{0,32},{32,0},{64,96},{96,64},{1,33},{33,1},{65,97},{97,65},{2,34}... | collective-permute-start | bytes 589832 | tf_op jit(solution)/shard_map/ppermute | solution.py:13
  25.7 9.2 %collective-permute-start.1 = (f32[192,256]{1,0:T(8,128)S(1)}, f32[192,256]{1,0:T(8,128)S(1)}, u32[]{:S(2)}, u32[]{:S(2)}) collective-permute-start(f32[192,256]{1,0:T(8,128)S(1)} %collective-permute-done), channel_id=1, source_target_pairs={{0,16},{16,0},{1,17},{17,1},{2,18},{18,2},{3,19},{19,3},{4,20},{20... | collective-permute-start | bytes 589832 | tf_op jit(solution)/shard_map/ppermute | solution.py:13
  25.9 13.1 %collective-permute-start.2 = (f32[192,256]{1,0:T(8,128)S(1)}, f32[192,256]{1,0:T(8,128)S(1)}, u32[]{:S(2)}, u32[]{:S(2)}) collective-permute-start(f32[192,256]{1,0:T(8,128)S(1)} %collective-permute-done), channel_id=1, source_target_pairs={{0,32},{32,0},{64,96},{96,64},{1,33},{33,1},{65,97},{97,65},{2,34}... | collective-permute-start | bytes 589832 | tf_op jit(solution)/shard_map/ppermute | solution.py:13
  35.0 9.0 %collective-permute-start.3 = (f32[192,256]{1,0:T(8,128)S(1)}, f32[192,256]{1,0:T(8,128)S(1)}, u32[]{:S(2)}, u32[]{:S(2)}) collective-permute-start(f32[192,256]{1,0:T(8,128)S(1)} %collective-permute-done.1), channel_id=1, source_target_pairs={{0,96},{32,64},{64,32},{96,0},{1,97},{33,65},{65,33},{97,1},{2,98}... | collective-permute-start | bytes 589832 | tf_op jit(solution)/shard_map/ppermute | solution.py:13
  38.3 61.6 %collective-permute-start.13 = (f32[2,192,256]{2,1,0:T(8,128)}, f32[2,192,256]{2,1,0:T(8,128)}, u32[]{:S(2)}, u32[]{:S(2)}) collective-permute-start(f32[2,192,256]{2,1,0:T(8,128)} %pad_maximum_fusion.4), channel_id=1, source_target_pairs={{0,96},{32,64},{64,32},{96,0},{1,97},{33,65},{65,33},{97,1},{2,98}... | collective-permute-start | bytes 1179656 | tf_op jit(solution)/shard_map/ppermute | solution.py:13
  39.0 27.8 %collective-permute-start.5 = (f32[2,192,256]{2,1,0:T(8,128)S(1)}, f32[2,192,256]{2,1,0:T(8,128)S(1)}, u32[]{:S(2)}, u32[]{:S(2)}) collective-permute-start(f32[2,192,256]{2,1,0:T(8,128)S(1)} %pad_maximum_fusion.2), channel_id=1, source_target_pairs={{0,96},{32,64},{64,32},{96,0},{1,97},{33,65},{65,33},{97,1},{2,98}... | collective-permute-start | bytes 1179656 | tf_op jit(solution)/shard_map/ppermute | solution.py:13
  41.6 23.3 %collective-permute-start.11 = (f32[192,256]{1,0:T(8,128)S(1)}, f32[192,256]{1,0:T(8,128)S(1)}, u32[]{:S(2)}, u32[]{:S(2)}) collective-permute-start(f32[192,256]{1,0:T(8,128)S(1)} %collective-permute-done.9), channel_id=1, source_target_pairs={{0,96},{32,64},{64,32},{96,0},{1,97},{33,65},{65,33},{97,1},{2,98}... | collective-permute-start | bytes 589832 | tf_op jit(solution)/shard_map/ppermute | solution.py:13
  44.0 22.2 %collective-permute-start.4 = (f32[2,192,256]{2,1,0:T(8,128)S(1)}, f32[2,192,256]{2,1,0:T(8,128)S(1)}, u32[]{:S(2)}, u32[]{:S(2)}) collective-permute-start(f32[2,192,256]{2,1,0:T(8,128)S(1)} %pad_maximum_fusion.1), channel_id=1, source_target_pairs={{0,32},{32,0},{64,96},{96,64},{1,33},{33,1},{65,97},{97,65},{2,34}... | collective-permute-start | bytes 1179656 | tf_op jit(solution)/shard_map/ppermute | solution.py:13
  65.7 32.6 %collective-permute-start.12 = (f32[2,192,256]{2,1,0:T(8,128)}, f32[2,192,256]{2,1,0:T(8,128)}, u32[]{:S(2)}, u32[]{:S(2)}) collective-permute-start(f32[2,192,256]{2,1,0:T(8,128)} %pad_maximum_fusion.3), channel_id=1, source_target_pairs={{0,32},{32,0},{64,96},{96,64},{1,33},{33,1},{65,97},{97,65},{2,34}... | collective-permute-start | bytes 1179656 | tf_op jit(solution)/shard_map/ppermute | solution.py:13
  96.9 7.9 %copy-start.7 = (f32[192,256]{1,0:T(8,128)S(1)}, f32[192,256]{1,0:T(8,128)}, u32[]{:S(2)}) copy-start(f32[192,256]{1,0:T(8,128)} %copy-done.6) | copy-start | bytes 589828
  96.9 11.8 %collective-permute-start.6 = (f32[4,2,192,256]{3,2,1,0:T(8,128)}, f32[4,2,192,256]{3,2,1,0:T(8,128)}, u32[]{:S(2)}, u32[]{:S(2)}) collective-permute-start(f32[4,2,192,256]{3,2,1,0:T(8,128)} %dynamic-slice_bitcast_fusion.1), channel_id=1, source_target_pairs={{0,1},{1,0},{2,3},{3,2},{4,5},{5,4},{6,7},{7,6},{8,9},{9,8},{10,11... | collective-permute-start | bytes 4718600 | tf_op jit(solution)/shard_map/ppermute | solution.py:13
  111.5 57.6 %reduce-scatter.5.cloned.1.call-start = ((), (), s32[]{:S(2)}) async-start(), calls=%async_computation.3 | async-start | bytes 1966080 | tf_op jit(solution)/shard_map/reduce_scatter | solution.py:102
  137.9 3.6 %collective-permute-start.14 = (f32[4,2,192,256]{3,2,1,0:T(8,128)S(1)}, f32[4,2,192,256]{3,2,1,0:T(8,128)S(1)}, u32[]{:S(2)}, u32[]{:S(2)}) collective-permute-start(f32[4,2,192,256]{3,2,1,0:T(8,128)S(1)} %dynamic-slice_bitcast_fusion), channel_id=1, source_target_pairs={{0,1},{1,0},{2,3},{3,2},{4,5},{5,4},{6,7},{7,6},{8,9},{9,8},{10,11... | collective-permute-start | bytes 4718600 | tf_op jit(solution)/shard_map/ppermute | solution.py:13
  144.3 27.4 %copy-start.4 = (f32[1,2,192,256]{3,2,1,0:T(8,128)S(1)}, f32[1,2,192,256]{3,2,1,0:T(8,128)}, u32[]{:S(2)}) copy-start(f32[1,2,192,256]{3,2,1,0:T(8,128)} %reduce-scatter.3.cloned.1.call-done) | copy-start | bytes 1179652
  145.4 26.3 %collective-permute-start.7 = (f32[192,256]{1,0:T(8,128)S(1)}, f32[192,256]{1,0:T(8,128)S(1)}, u32[]{:S(2)}, u32[]{:S(2)}) collective-permute-start(f32[192,256]{1,0:T(8,128)S(1)} %dynamic-slice_bitcast_fusion.3), channel_id=1, source_target_pairs={{0,2},{2,0},{1,3},{3,1},{4,6},{6,4},{5,7},{7,5},{8,10},{10,8},{9,1... | collective-permute-start | bytes 589832 | tf_op jit(solution)/shard_map/ppermute | solution.py:13
  169.1 7.0 %copy-start.5 = (f32[1,2,192,256]{3,2,1,0:T(8,128)S(1)}, f32[1,2,192,256]{3,2,1,0:T(8,128)}, u32[]{:S(2)}) copy-start(f32[1,2,192,256]{3,2,1,0:T(8,128)} %reduce-scatter.5.cloned.1.call-done) | copy-start | bytes 1179652
  170.1 6.0 %collective-permute-start.15 = (f32[192,256]{1,0:T(8,128)S(1)}, f32[192,256]{1,0:T(8,128)S(1)}, u32[]{:S(2)}, u32[]{:S(2)}) collective-permute-start(f32[192,256]{1,0:T(8,128)S(1)} %dynamic-slice_bitcast_fusion.2), channel_id=1, source_target_pairs={{0,2},{2,0},{1,3},{3,1},{4,6},{6,4},{5,7},{7,5},{8,10},{10,8},{9,1... | collective-permute-start | bytes 589832 | tf_op jit(solution)/shard_map/ppermute | solution.py:13
  172.2 4.6 %collective-permute-start.16 = (f32[128,256]{1,0:T(8,128)S(1)}, f32[128,256]{1,0:T(8,128)S(1)}, u32[]{:S(2)}, u32[]{:S(2)}) collective-permute-start(f32[128,256]{1,0:T(8,128)S(1)} %constant_dynamic-slice_fusion.9), channel_id=1, source_target_pairs={{0,1},{1,0},{2,3},{3,2},{4,5},{5,4},{6,7},{7,6},{8,9},{9,8},{10,11... | collective-permute-start | bytes 393224 | tf_op jit(solution)/shard_map/ppermute | solution.py:13
  176.6 4.8 %collective-permute-start.29 = (f32[128,256]{1,0:T(8,128)S(1)}, f32[128,256]{1,0:T(8,128)S(1)}, u32[]{:S(2)}, u32[]{:S(2)}) collective-permute-start(f32[128,256]{1,0:T(8,128)S(1)} %constant_dynamic-slice_fusion.4), channel_id=1, source_target_pairs={{0,1},{1,0},{2,3},{3,2},{4,5},{5,4},{6,7},{7,6},{8,9},{9,8},{10,11... | collective-permute-start | bytes 393224 | tf_op jit(solution)/shard_map/ppermute | solution.py:13
  176.8 8.5 %collective-permute-start.19 = (f32[32,256]{1,0:T(8,128)S(1)}, f32[32,256]{1,0:T(8,128)S(1)}, u32[]{:S(2)}, u32[]{:S(2)}) collective-permute-start(f32[32,256]{1,0:T(8,128)S(1)} %get-tuple-element.11), channel_id=1, source_target_pairs={{0,96},{32,0},{64,32},{96,64},{1,97},{33,1},{65,33},{97,65},{2,98}... | collective-permute-start | bytes 98312 | tf_op jit(solution)/shard_map/ppermute | solution.py:13
  179.7 5.7 %collective-permute-start.18 = (f32[32,256]{1,0:T(8,128)S(1)}, f32[32,256]{1,0:T(8,128)S(1)}, u32[]{:S(2)}, u32[]{:S(2)}) collective-permute-start(f32[32,256]{1,0:T(8,128)S(1)} %get-tuple-element.12), channel_id=1, source_target_pairs={{0,64},{32,96},{64,0},{96,32},{1,65},{33,97},{65,1},{97,33},{2,66}... | collective-permute-start | bytes 98312 | tf_op jit(solution)/shard_map/ppermute | solution.py:13
  180.5 5.1 %collective-permute-start.17 = (f32[32,256]{1,0:T(8,128)S(1)}, f32[32,256]{1,0:T(8,128)S(1)}, u32[]{:S(2)}, u32[]{:S(2)}) collective-permute-start(f32[32,256]{1,0:T(8,128)S(1)} %get-tuple-element.10), channel_id=1, source_target_pairs={{0,32},{32,64},{64,96},{96,0},{1,33},{33,65},{65,97},{97,1},{2,34}... | collective-permute-start | bytes 98312 | tf_op jit(solution)/shard_map/ppermute | solution.py:13
  181.4 7.1 %collective-permute-start.32 = (f32[32,256]{1,0:T(8,128)S(1)}, f32[32,256]{1,0:T(8,128)S(1)}, u32[]{:S(2)}, u32[]{:S(2)}) collective-permute-start(f32[32,256]{1,0:T(8,128)S(1)} %get-tuple-element.14), channel_id=1, source_target_pairs={{0,96},{32,0},{64,32},{96,64},{1,97},{33,1},{65,33},{97,65},{2,98}... | collective-permute-start | bytes 98312 | tf_op jit(solution)/shard_map/ppermute | solution.py:13
  183.8 5.4 %collective-permute-start.31 = (f32[32,256]{1,0:T(8,128)S(1)}, f32[32,256]{1,0:T(8,128)S(1)}, u32[]{:S(2)}, u32[]{:S(2)}) collective-permute-start(f32[32,256]{1,0:T(8,128)S(1)} %get-tuple-element.15), channel_id=1, source_target_pairs={{0,64},{32,96},{64,0},{96,32},{1,65},{33,97},{65,1},{97,33},{2,66}... | collective-permute-start | bytes 98312 | tf_op jit(solution)/shard_map/ppermute | solution.py:13
  185.4 5.1 %collective-permute-start.30 = (f32[32,256]{1,0:T(8,128)S(1)}, f32[32,256]{1,0:T(8,128)S(1)}, u32[]{:S(2)}, u32[]{:S(2)}) collective-permute-start(f32[32,256]{1,0:T(8,128)S(1)} %get-tuple-element.13), channel_id=1, source_target_pairs={{0,32},{32,64},{64,96},{96,0},{1,33},{33,65},{65,97},{97,1},{2,34}... | collective-permute-start | bytes 98312 | tf_op jit(solution)/shard_map/ppermute | solution.py:13
  185.6 7.7 %collective-permute-start.22 = (f32[32,256]{1,0:T(8,128)S(1)}, f32[32,256]{1,0:T(8,128)S(1)}, u32[]{:S(2)}, u32[]{:S(2)}) collective-permute-start(f32[32,256]{1,0:T(8,128)S(1)} %add_add_fusion.3), channel_id=1, source_target_pairs={{0,12},{4,0},{8,4},{12,8},{1,13},{5,1},{9,5},{13,9},{2,14},{6,2},{... | collective-permute-start | bytes 98312 | tf_op jit(solution)/shard_map/ppermute | solution.py:13
  187.5 5.9 %collective-permute-start.21 = (f32[32,256]{1,0:T(8,128)S(1)}, f32[32,256]{1,0:T(8,128)S(1)}, u32[]{:S(2)}, u32[]{:S(2)}) collective-permute-start(f32[32,256]{1,0:T(8,128)S(1)} %add_add_fusion.3), channel_id=1, source_target_pairs={{0,8},{4,12},{8,0},{12,4},{1,9},{5,13},{9,1},{13,5},{2,10},{6,14},... | collective-permute-start | bytes 98312 | tf_op jit(solution)/shard_map/ppermute | solution.py:13
  188.5 5.1 %collective-permute-start.20 = (f32[32,256]{1,0:T(8,128)S(1)}, f32[32,256]{1,0:T(8,128)S(1)}, u32[]{:S(2)}, u32[]{:S(2)}) collective-permute-start(f32[32,256]{1,0:T(8,128)S(1)} %add_add_fusion.3), channel_id=1, source_target_pairs={{0,4},{4,8},{8,12},{12,0},{1,5},{5,9},{9,13},{13,1},{2,6},{6,10},{... | collective-permute-start | bytes 98312 | tf_op jit(solution)/shard_map/ppermute | solution.py:13
  190.5 4.7 %collective-permute-start.35 = (f32[32,256]{1,0:T(8,128)S(1)}, f32[32,256]{1,0:T(8,128)S(1)}, u32[]{:S(2)}, u32[]{:S(2)}) collective-permute-start(f32[32,256]{1,0:T(8,128)S(1)} %add_add_fusion.1), channel_id=1, source_target_pairs={{0,12},{4,0},{8,4},{12,8},{1,13},{5,1},{9,5},{13,9},{2,14},{6,2},{... | collective-permute-start | bytes 98312 | tf_op jit(solution)/shard_map/ppermute | solution.py:13
  192.4 5.4 %collective-permute-start.34 = (f32[32,256]{1,0:T(8,128)S(1)}, f32[32,256]{1,0:T(8,128)S(1)}, u32[]{:S(2)}, u32[]{:S(2)}) collective-permute-start(f32[32,256]{1,0:T(8,128)S(1)} %add_add_fusion.1), channel_id=1, source_target_pairs={{0,8},{4,12},{8,0},{12,4},{1,9},{5,13},{9,1},{13,5},{2,10},{6,14},... | collective-permute-start | bytes 98312 | tf_op jit(solution)/shard_map/ppermute | solution.py:13
  193.3 5.1 %collective-permute-start.33 = (f32[32,256]{1,0:T(8,128)S(1)}, f32[32,256]{1,0:T(8,128)S(1)}, u32[]{:S(2)}, u32[]{:S(2)}) collective-permute-start(f32[32,256]{1,0:T(8,128)S(1)} %add_add_fusion.1), channel_id=1, source_target_pairs={{0,4},{4,8},{8,12},{12,0},{1,5},{5,9},{9,13},{13,1},{2,6},{6,10},{... | collective-permute-start | bytes 98312 | tf_op jit(solution)/shard_map/ppermute | solution.py:13
  193.6 6.5 %collective-permute-start.23 = (f32[32,256]{1,0:T(8,128)S(1)}, f32[32,256]{1,0:T(8,128)S(1)}, u32[]{:S(2)}, u32[]{:S(2)}) collective-permute-start(f32[32,256]{1,0:T(8,128)S(1)} %add_add_fusion.2), channel_id=1, source_target_pairs={{0,2},{2,0},{1,3},{3,1},{4,6},{6,4},{5,7},{7,5},{8,10},{10,8},{9,1... | collective-permute-start | bytes 98312 | tf_op jit(solution)/shard_map/ppermute | solution.py:13
  198.5 4.5 %collective-permute-start.36 = (f32[32,256]{1,0:T(8,128)S(1)}, f32[32,256]{1,0:T(8,128)S(1)}, u32[]{:S(2)}, u32[]{:S(2)}) collective-permute-start(f32[32,256]{1,0:T(8,128)S(1)} %add_add_fusion), channel_id=1, source_target_pairs={{0,2},{2,0},{1,3},{3,1},{4,6},{6,4},{5,7},{7,5},{8,10},{10,8},{9,1... | collective-permute-start | bytes 98312 | tf_op jit(solution)/shard_map/ppermute | solution.py:13
  200.1 5.5 %collective-permute-start.24 = (f32[32,256]{1,0:T(8,128)S(1)}, f32[32,256]{1,0:T(8,128)S(1)}, u32[]{:S(2)}, u32[]{:S(2)}) collective-permute-start(f32[32,256]{1,0:T(8,128)S(1)} %add.229), channel_id=1, source_target_pairs={{0,16},{16,0},{1,17},{17,1},{2,18},{18,2},{3,19},{19,3},{4,20},{20... | collective-permute-start | bytes 98312 | tf_op jit(solution)/shard_map/ppermute | solution.py:13
  203.0 7.2 %collective-permute-start.37 = (f32[32,256]{1,0:T(8,128)S(1)}, f32[32,256]{1,0:T(8,128)S(1)}, u32[]{:S(2)}, u32[]{:S(2)}) collective-permute-start(f32[32,256]{1,0:T(8,128)S(1)} %add.239), channel_id=1, source_target_pairs={{0,16},{16,0},{1,17},{17,1},{2,18},{18,2},{3,19},{19,3},{4,20},{20... | collective-permute-start | bytes 98312 | tf_op jit(solution)/shard_map/ppermute | solution.py:13
  205.6 16.0 %copy-start.8 = (f32[2,256,256]{2,1,0:T(8,128)S(1)}, f32[2,256,256]{2,1,0:T(8,128)}, u32[]{:S(2)}) copy-start(f32[2,256,256]{2,1,0:T(8,128)} %param.8) | copy-start | bytes 1572868
  205.6 9.3 %collective-permute-start.25 = (f32[32,256]{1,0:T(8,128)S(1)}, f32[32,256]{1,0:T(8,128)S(1)}, u32[]{:S(2)}, u32[]{:S(2)}) collective-permute-start(f32[32,256]{1,0:T(8,128)S(1)} %add.230), channel_id=1, source_target_pairs={{0,96},{32,0},{64,32},{96,64},{1,97},{33,1},{65,33},{97,65},{2,98}... | collective-permute-start | bytes 98312 | tf_op jit(solution)/shard_map/ppermute | solution.py:13
  209.2 5.7 %collective-permute-start.26 = (f32[32,256]{1,0:T(8,128)S(1)}, f32[32,256]{1,0:T(8,128)S(1)}, u32[]{:S(2)}, u32[]{:S(2)}) collective-permute-start(f32[32,256]{1,0:T(8,128)S(1)} %add.230), channel_id=1, source_target_pairs={{0,64},{32,96},{64,0},{96,32},{1,65},{33,97},{65,1},{97,33},{2,66}... | collective-permute-start | bytes 98312 | tf_op jit(solution)/shard_map/ppermute | solution.py:13
  210.1 5.1 %collective-permute-start.27 = (f32[32,256]{1,0:T(8,128)S(1)}, f32[32,256]{1,0:T(8,128)S(1)}, u32[]{:S(2)}, u32[]{:S(2)}) collective-permute-start(f32[32,256]{1,0:T(8,128)S(1)} %add.230), channel_id=1, source_target_pairs={{0,32},{32,64},{64,96},{96,0},{1,33},{33,65},{65,97},{97,1},{2,34}... | collective-permute-start | bytes 98312 | tf_op jit(solution)/shard_map/ppermute | solution.py:13
  210.1 5.2 %collective-permute-start.38 = (f32[32,256]{1,0:T(8,128)S(1)}, f32[32,256]{1,0:T(8,128)S(1)}, u32[]{:S(2)}, u32[]{:S(2)}) collective-permute-start(f32[32,256]{1,0:T(8,128)S(1)} %add.240), channel_id=1, source_target_pairs={{0,96},{32,0},{64,32},{96,64},{1,97},{33,1},{65,33},{97,65},{2,98}... | collective-permute-start | bytes 98312 | tf_op jit(solution)/shard_map/ppermute | solution.py:13
  213.4 5.4 %collective-permute-start.39 = (f32[32,256]{1,0:T(8,128)S(1)}, f32[32,256]{1,0:T(8,128)S(1)}, u32[]{:S(2)}, u32[]{:S(2)}) collective-permute-start(f32[32,256]{1,0:T(8,128)S(1)} %add.240), channel_id=1, source_target_pairs={{0,64},{32,96},{64,0},{96,32},{1,65},{33,97},{65,1},{97,33},{2,66}... | collective-permute-start | bytes 98312 | tf_op jit(solution)/shard_map/ppermute | solution.py:13
  214.9 5.1 %collective-permute-start.40 = (f32[32,256]{1,0:T(8,128)S(1)}, f32[32,256]{1,0:T(8,128)S(1)}, u32[]{:S(2)}, u32[]{:S(2)}) collective-permute-start(f32[32,256]{1,0:T(8,128)S(1)} %add.240), channel_id=1, source_target_pairs={{0,32},{32,64},{64,96},{96,0},{1,33},{33,65},{65,97},{97,1},{2,34}... | collective-permute-start | bytes 98312 | tf_op jit(solution)/shard_map/ppermute | solution.py:13
  215.3 4.9 %collective-permute-start.28 = (f32[128,256]{1,0:T(8,128)S(1)}, f32[128,256]{1,0:T(8,128)S(1)}, u32[]{:S(2)}, u32[]{:S(2)}) collective-permute-start(f32[128,256]{1,0:T(8,128)S(1)} %constant_dynamic-slice_fusion.5), channel_id=1, source_target_pairs={{0,1},{1,0},{2,3},{3,2},{4,5},{5,4},{6,7},{7,6},{8,9},{9,8},{10,11... | collective-permute-start | bytes 393224 | tf_op jit(solution)/shard_map/ppermute | solution.py:13
  220.1 1.4 collective-permute-start.41
  (6 other events, 10.5 us)
Sparse Core Ops, SparseCore 0:
  111.6 26.0 reduce-scatter.2
  143.0 26.0 reduce-scatter.4

commit v2 on v1

v2 whole, which is shorter than its diff:
```python
import jax
import jax.numpy as jnp
from jax import lax
from jax.experimental import pallas as pl
from jax.experimental.pallas import tpu as pltpu
from jax.sharding import Mesh, PartitionSpec as P

BS = 64
NS = 2
HIGH = lax.Precision.HIGH
HIGHEST = lax.Precision.HIGHEST
ALL = ("y", "xh", "z", "xl", "k")
BF = jnp.bfloat16
F32 = jnp.float32


def send(x, axis, size, to):
    return lax.ppermute(x, axis, [(i, to(i)) for i in range(size)])


def swap(x, axis):
    return send(x, axis, 2, lambda i: i ^ 1)


def transpose_pairs():
    return [(8 * c + r, 16 * r + c) for r in range(8) for c in range(16)]


def tile_mask(pattern, snode, start, length):
    tiles = lax.dynamic_slice_in_dim(pattern[snode], start // BS, length // BS, 0)
    return jnp.repeat(tiles, BS).astype(F32)[:, None]


def scatter_four(x, axis):
    me = lax.axis_index(axis)
    rows = x.shape[0] // 4
    part = lambda i: lax.dynamic_slice_in_dim(x, lax.rem(i, 4) * rows, rows, 0)
    got = [send(part(me + d), axis, 4, lambda i, d=d: (i + d) % 4) for d in (1, 2, 3)]
    return part(me) + got[0] + got[1] + got[2]


def others_four(x, axis):
    return [send(x, axis, 4, lambda i, d=d: (i + d) % 4) for d in (1, 2, 3)]


def sum_four(x, axis):
    got = others_four(x, axis)
    return x + got[0] + got[1] + got[2]


def gather_four(x, axis):
    me = lax.axis_index(axis)
    one, two, three = others_four(x, axis)
    twice = jnp.concatenate([three, two, one, x, three, two, one], axis=0)
    return lax.dynamic_slice_in_dim(twice, (3 - me) * x.shape[0], 4 * x.shape[0], 0)


def total(first, second):
    k = lax.axis_index("k")
    mine = jnp.where(k == 0, first, second) + swap(jnp.where(k == 0, second, first), "k")
    mine = scatter_four(mine, "y")
    mine = sum_four(mine, "z")
    mine = mine + swap(mine, "xl")
    mine = mine + swap(mine, "xh")
    mine = gather_four(mine, "y")
    other = swap(mine, "k")
    return jnp.where(k == 0, mine, other), jnp.where(k == 0, other, mine)


def halves(x):
    high = x.astype(BF)
    return high, (x - high.astype(F32)).astype(BF)


def dot3(a, b, dims):
    ah, al = halves(a)
    bh, bl = halves(b)
    f = lambda p, q: lax.dot_general(p, q, (dims, ((), ())), preferred_element_type=F32)
    return f(ah, bh) + (f(ah, bl) + f(al, bh))


def product_kernel(place_ref, a_ref, *refs):
    pieces, (keep_ref, give_ref, high, low) = refs[:8], refs[8:]
    piece = pieces[0].shape[0]

    @pl.when(pl.program_id(0) == 0)
    def _():
        for j in range(8):
            rows = pl.ds(pl.multiple_of(place_ref[j] * piece, BS), piece)
            xh, xl = halves(pieces[j][...])
            high[rows, :] = xh
            low[rows, :] = xl

    ah, al = halves(a_ref[...])
    f = lambda p, q: jnp.dot(p, q, preferred_element_type=F32)
    out = f(ah, high[...]) + (f(ah, low[...]) + f(al, high[...]))
    first, second = out[:piece], out[piece:]
    lower = place_ref[8] == 0
    keep_ref[0] = jnp.where(lower, first, second)
    give_ref[0] = jnp.where(lower, second, first)


def product(a, pieces, places):
    rows, cols = a.shape
    piece, width = pieces[0].shape
    blocks = rows // (2 * piece)
    whole = pl.BlockSpec((piece, width), lambda i, p: (0, 0))
    out = pl.BlockSpec((1, piece, width), lambda i, p: (i, 0, 0))
    return pl.pallas_call(
        product_kernel,
        grid_spec=pltpu.PrefetchScalarGridSpec(
            num_scalar_prefetch=1,
            grid=(blocks,),
            in_specs=[pl.BlockSpec((2 * piece, cols), lambda i, p: (i, 0))] + [whole] * 8,
            out_specs=[out, out],
            scratch_shapes=[pltpu.VMEM((cols, width), BF)] * 2,
        ),
        out_shape=[jax.ShapeDtypeStruct((blocks, piece, width), F32)] * 2,
        compiler_params=pltpu.CompilerParams(vmem_limit_bytes=40 << 20),
        cost_estimate=pl.CostEstimate(
            flops=6 * rows * cols * width, bytes_accessed=4 * (rows * cols + (rows + cols) * width), transcendentals=0
        ),
    )(places, a, *pieces)


def add_kernel(keep_ref, got_ref, x_ref, sum_ref, update_ref):
    @pl.when(pl.program_id(0) == 0)
    def _():
        update_ref[...] = jnp.zeros_like(update_ref)

    both = keep_ref[0] + got_ref[0]
    sum_ref[0] = both
    update_ref[...] += dot3(x_ref[0], both, ((0,), (0,)))


def add_and_update(keep, got, x):
    blocks, piece, width = keep.shape
    spec = pl.BlockSpec((1, piece, width), lambda i: (i, 0, 0))
    return pl.pallas_call(
        add_kernel,
        grid=(blocks,),
        in_specs=[spec] * 3,
        out_specs=[spec, pl.BlockSpec((width, width), lambda i: (0, 0))],
        out_shape=[jax.ShapeDtypeStruct(keep.shape, F32), jax.ShapeDtypeStruct((width, width), F32)],
        compiler_params=pltpu.CompilerParams(vmem_limit_bytes=16 << 20),
        cost_estimate=pl.CostEstimate(
            flops=6 * blocks * piece * width * width, bytes_accessed=16 * blocks * piece * width, transcendentals=0
        ),
    )(keep, got, x)


def gather_column(mine):
    pair = swap(mine, "xh")
    one, three = (lambda i: i ^ 1), (lambda i: i ^ 3)
    mine1 = send(mine, "y", 4, one)
    mine3 = send(mine, "y", 4, three)
    pair3 = send(pair, "y", 4, three)
    mine2 = send(mine1, "y", 4, three)
    pair1 = send(pair, "y", 4, one)
    pair2 = send(pair3, "y", 4, one)
    return [mine, pair, mine1, pair1, mine2, pair2, mine3, pair3]


def local(ancestor_inverse, lower_panel, diag_factor, diag_block, pattern):
    y, xh, z, xl, k = (lax.axis_index(a) for a in ALL)
    row, col = y * 2 + xh, z * 4 + xl * 2 + k
    piece = lower_panel.shape[1]
    start = (row * 16 + col) * piece
    masks = [tile_mask(pattern, s, start, piece) for s in range(NS)]
    normed = [jnp.dot(lower_panel[s], diag_factor[s], precision=HIGHEST) * masks[s] for s in range(NS)]
    spots = jnp.arange(8, dtype=jnp.int32)
    places = jnp.concatenate([((spots // 2) ^ y) * 2 + ((spots % 2) ^ xh), k[None]])

    near = swap(normed[1], "xl")
    pair = jnp.stack([jnp.where(xl == 0, normed[1], near), jnp.where(xl == 0, near, normed[1])])
    band = lax.all_gather(pair, "z", axis=0, tiled=True)

    panels, updates = [], []
    for snode in range(NS):
        mine = lax.ppermute(normed[snode], ALL, transpose_pairs())
        keep, give = product(ancestor_inverse, gather_column(mine), places)
        got = swap(give, "k")
        if snode == 0:
            summed = keep + got
        else:
            summed, early = add_and_update(keep, got, band)
        summed = lax.psum_scatter(summed.reshape(4, 2, *summed.shape[1:]), "z", scatter_dimension=0, tiled=False)
        kept = lax.dynamic_slice_in_dim(summed, xl, 1, 0)[0]
        given = lax.dynamic_slice_in_dim(summed, 1 - xl, 1, 0)[0]
        whole = masks[snode] * (kept + swap(given, "xl"))
        panels.append(-whole)
        if snode == 0:
            late = lax.dot_general(normed[0], whole, (((0,), (0,)), ((), ())), precision=HIGH)
    first, second = total(late, early)
    return jnp.stack(panels), jnp.stack([diag_block[0] + first, diag_block[1] + second])


def solution(mesh):
    fine = Mesh(mesh.devices.reshape(4, 2, 4, 2, 2), ALL)
    rows, cols = ("y", "xh"), ("z", "xl", "k")
    return jax.shard_map(
        local,
        mesh=fine,
        in_specs=(P(rows, cols), P(None, ALL, None), P(), P(), P()),
        out_specs=(P(None, ALL, None), P()),
        check_vma=False,
    )
```

time: 231 us -> 185 us (0.80)
  matrix products: 45.3 us -> 4.18 us
  Pallas kernels: 0 us -> 29.9 us
  local copies, waits for them, and re-layouts: 32.6 us -> 4.59 us
  waiting for transfers between devices: 63.6 us -> 56.6 us
  starting transfers between devices: 64.4 us -> 69.2 us
  other arithmetic: 8.72 us -> 4.3 us
    dot_general x8 -> x3, matrix products: 45.3 us -> 4.18 us  [the longest x2 2.77 us: local(): jnp.dot(lower_panel[s], diag_factor[s], precision=HIGHEST) * masks[s]]
    pallas_call x0 -> x3, Pallas kernels: none -> 29.9 us  [the longest x2 26.7 us: product(): pl.pallas_call(product_kernel, grid_spec=pltpu.PrefetchScalarGridSpec(num...]
    reduce_scatter x2, waiting for transfers between devices: 21.9 us -> 0.02 us  [local(): lax.psum_scatter(summed.reshape(4, 2, *summed.shape[1:]), 'z', scatter_di...]
    ppermute x40 -> x32, waiting for transfers between devices: 41.6 us -> 56.5 us  [send(): return lax.ppermute(x, axis, [(i, to(i)) for i in range(size)])]
    unnamed x46 -> x18, local copies, waits for them, and re-layouts: 15.1 us -> 1.47 us
    gather x2 -> x0, local copies, waits for them, and re-layouts: 5.35 us -> none  [local(): block = parts[order].reshape(cols, width)]
    ppermute x40 -> x32, starting transfers between devices: 62.8 us -> 67.7 us  [send(): return lax.ppermute(x, axis, [(i, to(i)) for i in range(size)])]
    dot_general x2 -> x0, local copies, waits for them, and re-layouts: 4.79 us -> none  [local(): out = jnp.dot(ancestor_inverse, x, precision=HIGH)]
  transfers between devices with their start and end apart: 44 -> 37, of which waited for: 17 -> 23; matrix products, arithmetic and copies ran while one was open for 35% -> 5% of each run, Pallas kernels for 0% -> 16%
where the time goes in v2:
time: 185 us; the launch traced here: 183 us
  starting transfers between devices  69.2 us (37%)
  waiting for transfers between devices  56.6 us (31%)
  Pallas kernels  29.9 us (16%)
  between operations  14.1 us (8%)
  local copies, waits for them, and re-layouts  4.59 us (2%)
  other arithmetic  4.3 us (2%)
  matrix products  4.18 us (2%)
    ppermute x32, starting transfers between devices, send(): return lax.ppermute(x, axis, [(i, to(i)) for i in range(size)])  67.7 us
    ppermute x32, waiting for transfers between devices, send(): return lax.ppermute(x, axis, [(i, to(i)) for i in range(size)])  56.5 us
    pallas_call x2, Pallas kernels, product(): pl.pallas_call(product_kernel, grid_spec=pltpu.PrefetchScalarGridSpec(num...  26.7 us
  transfers between devices with their start and end apart: 37, of which 23 were waited for; matrix products, arithmetic and copies ran while one was open for 5% of the time, Pallas kernels for 16%

profile of v2, /device:TPU:0, one launch (start us, length us, event | category | flops | bytes accessed | tf_op | source)
XLA Modules:
  0.0 182.9 jit_solution(16356219886086084071)
XLA Ops:
  8.2 1.4 convolution_multiply_fusion.1
  10.5 10.9 %collective-permute-start.1 = (f32[192,256]{1,0:T(8,128)S(1)}, f32[192,256]{1,0:T(8,128)S(1)}, u32[]{:S(2)}, u32[]{:S(2)}) collective-permute-start(f32[192,256]{1,0:T(8,128)S(1)} %collective-permute-done.refs_0_), channel_id=1, source_target_pairs={{0,16},{16,0},{1,17},{17,1},{2,18},{18,2},{3,19},{19,3},{4,20},{20... | collective-permute-start | bytes 589832 | tf_op jit(solution)/shard_map/ppermute | solution.py:18
  21.3 1.4 convolution_multiply_fusion
  22.8 3.1 %collective-permute-start.2 = (f32[192,256]{1,0:T(8,128)S(1)}, f32[192,256]{1,0:T(8,128)S(1)}, u32[]{:S(2)}, u32[]{:S(2)}) collective-permute-start(f32[192,256]{1,0:T(8,128)S(1)} %collective-permute-done.refs_0_), channel_id=1, source_target_pairs={{0,32},{32,0},{64,96},{96,64},{1,33},{33,1},{65,97},{97,65},{2,34}... | collective-permute-start | bytes 589832 | tf_op jit(solution)/shard_map/ppermute | solution.py:18
  25.9 5.9 %collective-permute-start.7 = (f32[192,256]{1,0:T(8,128)S(1)}, f32[192,256]{1,0:T(8,128)S(1)}, u32[]{:S(2)}, u32[]{:S(2)}) collective-permute-start(f32[192,256]{1,0:T(8,128)S(1)} %collective-permute-done.refs_0_), channel_id=1, source_target_pairs={{0,96},{32,64},{64,32},{96,0},{1,97},{33,65},{65,33},{97,1},{2,98}... | collective-permute-start | bytes 589832 | tf_op jit(solution)/shard_map/ppermute | solution.py:18
  31.8 1.9 %collective-permute-start.5 = (f32[192,256]{1,0:T(8,128)S(1)}, f32[192,256]{1,0:T(8,128)S(1)}, u32[]{:S(2)}, u32[]{:S(2)}) collective-permute-start(f32[192,256]{1,0:T(8,128)S(1)} %collective-permute-done.1.refs_1_), channel_id=1, source_target_pairs={{0,96},{32,64},{64,32},{96,0},{1,97},{33,65},{65,33},{97,1},{2,98}... | collective-permute-start | bytes 589832 | tf_op jit(solution)/shard_map/ppermute | solution.py:18
  33.7 1.8 collective-permute-start.3
  35.5 4.0 %collective-permute-start.4 = (f32[192,256]{1,0:T(8,128)S(1)}, f32[192,256]{1,0:T(8,128)S(1)}, u32[]{:S(2)}, u32[]{:S(2)}) collective-permute-start(f32[192,256]{1,0:T(8,128)S(1)} %collective-permute-done.2.refs_2_), channel_id=1, source_target_pairs={{0,96},{32,64},{64,32},{96,0},{1,97},{33,65},{65,33},{97,1},{2,98}... | collective-permute-start | bytes 589832 | tf_op jit(solution)/shard_map/ppermute | solution.py:18
  39.5 2.3 %collective-permute-done.5.refs_7_ = f32[192,256]{1,0:T(8,128)S(1)} collective-permute-done((f32[192,256]{1,0:T(8,128)S(1)}, f32[192,256]{1,0:T(8,128)S(1)}, u32[]{:S(2)}, u32[]{:S(2)}) %collective-permute-start.5) | collective-permute-done | bytes 196640 | tf_op jit(solution)/shard_map/ppermute | solution.py:18
  42.7 2.7 %collective-permute-done.4.refs_4_ = f32[192,256]{1,0:T(8,128)S(1)} collective-permute-done((f32[192,256]{1,0:T(8,128)S(1)}, f32[192,256]{1,0:T(8,128)S(1)}, u32[]{:S(2)}, u32[]{:S(2)}) %collective-permute-start.4) | collective-permute-done | bytes 196640 | tf_op jit(solution)/shard_map/ppermute | solution.py:18
  45.3 2.1 %collective-permute-done.6.refs_5_ = f32[192,256]{1,0:T(8,128)S(1)} collective-permute-done((f32[192,256]{1,0:T(8,128)S(1)}, f32[192,256]{1,0:T(8,128)S(1)}, u32[]{:S(2)}, u32[]{:S(2)}) %collective-permute-start.6) | collective-permute-done | bytes 196640 | tf_op jit(solution)/shard_map/ppermute | solution.py:18
  47.4 13.4 %shard_map.68 = (f32[8,192,256]{2,1,0:T(8,128)S(1)}, f32[8,192,256]{2,1,0:T(8,128)S(1)}) custom-call(s32[9]{0:T(128)S(1)} %pad_add_fusion.place_ref, f32[3072,1536]{1,0:T(8,128)} %a_ref.3, f32[192,256]{1,0:T(8,128)S(1)} %collective-permute-done.refs_0_, f32[192,256]{1,0:T(8,128)S(1)} %collective-permute-done.1.refs_1_, ...), custom_call_target="tpu_custom_call" | custom-call | flops 7247757312 | bytes 23592960 | tf_op jit(solution)/shard_map/pallas_call | solution.py:109
  60.9 3.4 %collective-permute-done.8 = f32[8,192,256]{2,1,0:T(8,128)S(1)} collective-permute-done((f32[8,192,256]{2,1,0:T(8,128)S(1)}, f32[8,192,256]{2,1,0:T(8,128)S(1)}, u32[]{:S(2)}, u32[]{:S(2)}) %collective-permute-start.8) | collective-permute-done | bytes 1572896 | tf_op jit(solution)/shard_map/ppermute | solution.py:18
  64.3 1.4 add.113
  66.5 9.9 %collective-permute-start.11 = (f32[192,256]{1,0:T(8,128)S(1)}, f32[192,256]{1,0:T(8,128)S(1)}, u32[]{:S(2)}, u32[]{:S(2)}) collective-permute-start(f32[192,256]{1,0:T(8,128)S(1)} %collective-permute-done.10.refs_0_), channel_id=1, source_target_pairs={{0,16},{16,0},{1,17},{17,1},{2,18},{18,2},{3,19},{19,3},{4,20},{20... | collective-permute-start | bytes 589832 | tf_op jit(solution)/shard_map/ppermute | solution.py:18
  76.4 2.2 %collective-permute-start.12 = (f32[192,256]{1,0:T(8,128)S(1)}, f32[192,256]{1,0:T(8,128)S(1)}, u32[]{:S(2)}, u32[]{:S(2)}) collective-permute-start(f32[192,256]{1,0:T(8,128)S(1)} %collective-permute-done.10.refs_0_), channel_id=1, source_target_pairs={{0,32},{32,0},{64,96},{96,64},{1,33},{33,1},{65,97},{97,65},{2,34}... | collective-permute-start | bytes 589832 | tf_op jit(solution)/shard_map/ppermute | solution.py:18
  78.6 2.9 %collective-permute-done.11.refs_1_ = f32[192,256]{1,0:T(8,128)S(1)} collective-permute-done((f32[192,256]{1,0:T(8,128)S(1)}, f32[192,256]{1,0:T(8,128)S(1)}, u32[]{:S(2)}, u32[]{:S(2)}) %collective-permute-start.11) | collective-permute-done | bytes 196640 | tf_op jit(solution)/shard_map/ppermute | solution.py:18
  81.6 8.7 %collective-permute-start.15 = (f32[192,256]{1,0:T(8,128)S(1)}, f32[192,256]{1,0:T(8,128)S(1)}, u32[]{:S(2)}, u32[]{:S(2)}) collective-permute-start(f32[192,256]{1,0:T(8,128)S(1)} %collective-permute-done.11.refs_1_), channel_id=1, source_target_pairs={{0,96},{32,64},{64,32},{96,0},{1,97},{33,65},{65,33},{97,1},{2,98}... | collective-permute-start | bytes 589832 | tf_op jit(solution)/shard_map/ppermute | solution.py:18
  90.3 3.2 %collective-permute-start.14 = (f32[192,256]{1,0:T(8,128)S(1)}, f32[192,256]{1,0:T(8,128)S(1)}, u32[]{:S(2)}, u32[]{:S(2)}) collective-permute-start(f32[192,256]{1,0:T(8,128)S(1)} %collective-permute-done.12.refs_2_), channel_id=1, source_target_pairs={{0,96},{32,64},{64,32},{96,0},{1,97},{33,65},{65,33},{97,1},{2,98}... | collective-permute-start | bytes 589832 | tf_op jit(solution)/shard_map/ppermute | solution.py:18
  93.5 2.5 %collective-permute-done.15.refs_7_ = f32[192,256]{1,0:T(8,128)S(1)} collective-permute-done((f32[192,256]{1,0:T(8,128)S(1)}, f32[192,256]{1,0:T(8,128)S(1)}, u32[]{:S(2)}, u32[]{:S(2)}) %collective-permute-start.15) | collective-permute-done | bytes 196640 | tf_op jit(solution)/shard_map/ppermute | solution.py:18
  96.0 4.2 %collective-permute-done.17.refs_6_ = f32[192,256]{1,0:T(8,128)S(1)} collective-permute-done((f32[192,256]{1,0:T(8,128)S(1)}, f32[192,256]{1,0:T(8,128)S(1)}, u32[]{:S(2)}, u32[]{:S(2)}) %collective-permute-start.17) | collective-permute-done | bytes 196640 | tf_op jit(solution)/shard_map/ppermute | solution.py:18
  100.2 3.2 %collective-permute-done.14.refs_4_ = f32[192,256]{1,0:T(8,128)S(1)} collective-permute-done((f32[192,256]{1,0:T(8,128)S(1)}, f32[192,256]{1,0:T(8,128)S(1)}, u32[]{:S(2)}, u32[]{:S(2)}) %collective-permute-start.14) | collective-permute-done | bytes 196640 | tf_op jit(solution)/shard_map/ppermute | solution.py:18
  103.4 13.3 %shard_map.69 = (f32[8,192,256]{2,1,0:T(8,128)S(1)}, f32[8,192,256]{2,1,0:T(8,128)S(1)}) custom-call(s32[9]{0:T(128)S(1)} %pad_add_fusion.place_ref, f32[3072,1536]{1,0:T(8,128)} %a_ref.3, f32[192,256]{1,0:T(8,128)S(1)} %collective-permute-done.10.refs_0_, f32[192,256]{1,0:T(8,128)S(1)} %collective-permute-done.11.refs_1_, ...), custom_call_target="tpu_custom_call" | custom-call | flops 7247757312 | bytes 23592960 | tf_op jit(solution)/shard_map/pallas_call | solution.py:109
  116.8 3.4 %collective-permute-done.18.got_ref = f32[8,192,256]{2,1,0:T(8,128)S(1)} collective-permute-done((f32[8,192,256]{2,1,0:T(8,128)S(1)}, f32[8,192,256]{2,1,0:T(8,128)S(1)}, u32[]{:S(2)}, u32[]{:S(2)}) %collective-permute-start.18) | collective-permute-done | bytes 1572896 | tf_op jit(solution)/shard_map/ppermute | solution.py:18
  120.2 1.4 copy-done
  121.6 3.3 %shard_map.70 = (f32[8,192,256]{2,1,0:T(8,128)}, f32[256,256]{1,0:T(8,128)S(1)}) custom-call(f32[8,192,256]{2,1,0:T(8,128)S(1)} %get-tuple-element.10.keep_ref, f32[8,192,256]{2,1,0:T(8,128)S(1)} %collective-permute-done.18.got_ref, f32[8,192,256]{2,1,0:T(8,128)S(1)} %copy-done), custom_call_target="tpu_custom_call" | custom-call | flops 603979776 | bytes 6291456 | tf_op jit(solution)/shard_map/pallas_call | solution.py:139
  124.9 1.0 dynamic-slice_bitcast_fusion.1
  125.9 2.4 %collective-permute-start.9 = (f32[192,256]{1,0:T(8,128)S(1)}, f32[192,256]{1,0:T(8,128)S(1)}, u32[]{:S(2)}, u32[]{:S(2)}) collective-permute-start(f32[192,256]{1,0:T(8,128)S(1)} %dynamic-slice_bitcast_fusion.1), channel_id=1, source_target_pairs={{0,2},{2,0},{1,3},{3,1},{4,6},{6,4},{5,7},{7,5},{8,10},{10,8},{9,1... | collective-permute-start | bytes 589832 | tf_op jit(solution)/shard_map/ppermute | solution.py:18
  128.3 5.2 %collective-permute-done.9 = f32[192,256]{1,0:T(8,128)S(1)} collective-permute-done((f32[192,256]{1,0:T(8,128)S(1)}, f32[192,256]{1,0:T(8,128)S(1)}, u32[]{:S(2)}, u32[]{:S(2)}) %collective-permute-start.9) | collective-permute-done | bytes 196640 | tf_op jit(solution)/shard_map/ppermute | solution.py:18
  133.5 1.4 broadcast_select_fusion
  135.0 1.5 collective-permute-done.21
  136.6 3.0 %collective-permute-start.24 = (f32[64,256]{1,0:T(8,128)S(1)}, f32[64,256]{1,0:T(8,128)S(1)}, u32[]{:S(2)}, u32[]{:S(2)}) collective-permute-start(f32[64,256]{1,0:T(8,128)S(1)} %get-tuple-element.19), channel_id=1, source_target_pairs={{0,96},{32,0},{64,32},{96,64},{1,97},{33,1},{65,33},{97,65},{2,98}... | collective-permute-start | bytes 196616 | tf_op jit(solution)/shard_map/ppermute | solution.py:18
  139.6 0.9 collective-permute-start.22
  140.6 2.1 %collective-permute-done.24 = f32[64,256]{1,0:T(8,128)S(1)} collective-permute-done((f32[64,256]{1,0:T(8,128)S(1)}, f32[64,256]{1,0:T(8,128)S(1)}, u32[]{:S(2)}, u32[]{:S(2)}) %collective-permute-start.24) | collective-permute-done | bytes 65568 | tf_op jit(solution)/shard_map/ppermute | solution.py:18
  142.7 3.0 %collective-permute-done.23 = f32[64,256]{1,0:T(8,128)S(1)} collective-permute-done((f32[64,256]{1,0:T(8,128)S(1)}, f32[64,256]{1,0:T(8,128)S(1)}, u32[]{:S(2)}, u32[]{:S(2)}) %collective-permute-start.23) | collective-permute-done | bytes 65568 | tf_op jit(solution)/shard_map/ppermute | solution.py:18
  146.5 3.3 %collective-permute-start.26 = (f32[64,256]{1,0:T(8,128)S(1)}, f32[64,256]{1,0:T(8,128)S(1)}, u32[]{:S(2)}, u32[]{:S(2)}) collective-permute-start(f32[64,256]{1,0:T(8,128)S(1)} %add_add_fusion.1), channel_id=1, source_target_pairs={{0,8},{4,12},{8,0},{12,4},{1,9},{5,13},{9,1},{13,5},{2,10},{6,14},... | collective-permute-start | bytes 196616 | tf_op jit(solution)/shard_map/ppermute | solution.py:18
  150.5 2.3 %collective-permute-done.26 = f32[64,256]{1,0:T(8,128)S(1)} collective-permute-done((f32[64,256]{1,0:T(8,128)S(1)}, f32[64,256]{1,0:T(8,128)S(1)}, u32[]{:S(2)}, u32[]{:S(2)}) %collective-permute-start.26) | collective-permute-done | bytes 65568 | tf_op jit(solution)/shard_map/ppermute | solution.py:18
  152.8 2.5 %collective-permute-done.25 = f32[64,256]{1,0:T(8,128)S(1)} collective-permute-done((f32[64,256]{1,0:T(8,128)S(1)}, f32[64,256]{1,0:T(8,128)S(1)}, u32[]{:S(2)}, u32[]{:S(2)}) %collective-permute-start.25) | collective-permute-done | bytes 65568 | tf_op jit(solution)/shard_map/ppermute | solution.py:18
  155.3 1.8 collective-permute-start.28
  157.1 3.2 %collective-permute-done.28 = f32[64,256]{1,0:T(8,128)S(1)} collective-permute-done((f32[64,256]{1,0:T(8,128)S(1)}, f32[64,256]{1,0:T(8,128)S(1)}, u32[]{:S(2)}, u32[]{:S(2)}) %collective-permute-start.28) | collective-permute-done | bytes 65568 | tf_op jit(solution)/shard_map/ppermute | solution.py:18
  160.8 1.0 dynamic-slice_bitcast_fusion
  161.8 0.8 collective-permute-start.20
  162.6 3.8 %collective-permute-done.29 = f32[64,256]{1,0:T(8,128)S(1)} collective-permute-done((f32[64,256]{1,0:T(8,128)S(1)}, f32[64,256]{1,0:T(8,128)S(1)}, u32[]{:S(2)}, u32[]{:S(2)}) %collective-permute-start.29) | collective-permute-done | bytes 65568 | tf_op jit(solution)/shard_map/ppermute | solution.py:18
  167.8 1.4 collective-permute-start.32
  169.2 1.5 collective-permute-done.30
  170.8 2.3 %collective-permute-done.31 = f32[64,256]{1,0:T(8,128)S(1)} collective-permute-done((f32[64,256]{1,0:T(8,128)S(1)}, f32[64,256]{1,0:T(8,128)S(1)}, u32[]{:S(2)}, u32[]{:S(2)}) %collective-permute-start.31) | collective-permute-done | bytes 65568 | tf_op jit(solution)/shard_map/ppermute | solution.py:18
  174.1 0.8 pad_maximum_fusion.2
  175.6 0.8 pad_maximum_fusion
  (79 shorter events, 9.0 us)
Async XLA Ops:
  7.2 113.0 %all-gather.2.cloned.1.call-start = ((), (), s32[]{:S(2)}) async-start(), calls=%async_computation.3 | async-start | bytes 1966080 | tf_op jit(solution)/shard_map/all_gather | solution.py:176
  9.6 0.9 copy-start.2
  9.6 0.8 collective-permute-start
  10.5 21.3 %collective-permute-start.1 = (f32[192,256]{1,0:T(8,128)S(1)}, f32[192,256]{1,0:T(8,128)S(1)}, u32[]{:S(2)}, u32[]{:S(2)}) collective-permute-start(f32[192,256]{1,0:T(8,128)S(1)} %collective-permute-done.refs_0_), channel_id=1, source_target_pairs={{0,16},{16,0},{1,17},{17,1},{2,18},{18,2},{3,19},{19,3},{4,20},{20... | collective-permute-start | bytes 589832 | tf_op jit(solution)/shard_map/ppermute | solution.py:18
  22.7 11.0 %collective-permute-start.19 = (f32[192,256]{1,0:T(8,128)S(1)}, f32[192,256]{1,0:T(8,128)S(1)}, u32[]{:S(2)}, u32[]{:S(2)}) collective-permute-start(f32[192,256]{1,0:T(8,128)S(1)} %convolution_multiply_fusion), channel_id=1, source_target_pairs={{0,2},{2,0},{1,3},{3,1},{4,6},{6,4},{5,7},{7,5},{8,10},{10,8},{9,1... | collective-permute-start | bytes 589832 | tf_op jit(solution)/shard_map/ppermute | solution.py:18
  22.8 12.7 %collective-permute-start.2 = (f32[192,256]{1,0:T(8,128)S(1)}, f32[192,256]{1,0:T(8,128)S(1)}, u32[]{:S(2)}, u32[]{:S(2)}) collective-permute-start(f32[192,256]{1,0:T(8,128)S(1)} %collective-permute-done.refs_0_), channel_id=1, source_target_pairs={{0,32},{32,0},{64,96},{96,64},{1,33},{33,1},{65,97},{97,65},{2,34}... | collective-permute-start | bytes 589832 | tf_op jit(solution)/shard_map/ppermute | solution.py:18
  25.9 16.8 %collective-permute-start.7 = (f32[192,256]{1,0:T(8,128)S(1)}, f32[192,256]{1,0:T(8,128)S(1)}, u32[]{:S(2)}, u32[]{:S(2)}) collective-permute-start(f32[192,256]{1,0:T(8,128)S(1)} %collective-permute-done.refs_0_), channel_id=1, source_target_pairs={{0,96},{32,64},{64,32},{96,0},{1,97},{33,65},{65,33},{97,1},{2,98}... | collective-permute-start | bytes 589832 | tf_op jit(solution)/shard_map/ppermute | solution.py:18
  31.8 9.9 %collective-permute-start.5 = (f32[192,256]{1,0:T(8,128)S(1)}, f32[192,256]{1,0:T(8,128)S(1)}, u32[]{:S(2)}, u32[]{:S(2)}) collective-permute-start(f32[192,256]{1,0:T(8,128)S(1)} %collective-permute-done.1.refs_1_), channel_id=1, source_target_pairs={{0,96},{32,64},{64,32},{96,0},{1,97},{33,65},{65,33},{97,1},{2,98}... | collective-permute-start | bytes 589832 | tf_op jit(solution)/shard_map/ppermute | solution.py:18
  33.7 8.9 %collective-permute-start.3 = (f32[192,256]{1,0:T(8,128)S(1)}, f32[192,256]{1,0:T(8,128)S(1)}, u32[]{:S(2)}, u32[]{:S(2)}) collective-permute-start(f32[192,256]{1,0:T(8,128)S(1)} %collective-permute-done.1.refs_1_), channel_id=1, source_target_pairs={{0,32},{32,0},{64,96},{96,64},{1,33},{33,1},{65,97},{97,65},{2,34}... | collective-permute-start | bytes 589832 | tf_op jit(solution)/shard_map/ppermute | solution.py:18
  35.5 9.8 %collective-permute-start.4 = (f32[192,256]{1,0:T(8,128)S(1)}, f32[192,256]{1,0:T(8,128)S(1)}, u32[]{:S(2)}, u32[]{:S(2)}) collective-permute-start(f32[192,256]{1,0:T(8,128)S(1)} %collective-permute-done.2.refs_2_), channel_id=1, source_target_pairs={{0,96},{32,64},{64,32},{96,0},{1,97},{33,65},{65,33},{97,1},{2,98}... | collective-permute-start | bytes 589832 | tf_op jit(solution)/shard_map/ppermute | solution.py:18
  41.7 5.7 %collective-permute-start.6 = (f32[192,256]{1,0:T(8,128)S(1)}, f32[192,256]{1,0:T(8,128)S(1)}, u32[]{:S(2)}, u32[]{:S(2)}) collective-permute-start(f32[192,256]{1,0:T(8,128)S(1)} %collective-permute-done.5.refs_7_), channel_id=1, source_target_pairs={{0,32},{32,0},{64,96},{96,64},{1,33},{33,1},{65,97},{97,65},{2,34}... | collective-permute-start | bytes 589832 | tf_op jit(solution)/shard_map/ppermute | solution.py:18
  42.5 82.4 %reduce-scatter.3.cloned.1.call-start = ((), (), s32[]{:S(2)}) async-start(), calls=%async_computation.2 | async-start | bytes 1966080 | tf_op jit(solution)/shard_map/reduce_scatter | solution.py:187
  60.8 3.5 %collective-permute-start.8 = (f32[8,192,256]{2,1,0:T(8,128)S(1)}, f32[8,192,256]{2,1,0:T(8,128)S(1)}, u32[]{:S(2)}, u32[]{:S(2)}) collective-permute-start(f32[8,192,256]{2,1,0:T(8,128)S(1)} %get-tuple-element.9), channel_id=1, source_target_pairs={{0,1},{1,0},{2,3},{3,2},{4,5},{5,4},{6,7},{7,6},{8,9},{9,8},{10,11... | collective-permute-start | bytes 4718600 | tf_op jit(solution)/shard_map/ppermute | solution.py:18
  65.7 95.0 %reduce-scatter.5.cloned.1.call-start = ((), (), s32[]{:S(2)}) async-start(), calls=%async_computation.4 | async-start | bytes 1966080 | tf_op jit(solution)/shard_map/reduce_scatter | solution.py:187
  65.8 0.7 collective-permute-start.10
  66.5 15.1 %collective-permute-start.11 = (f32[192,256]{1,0:T(8,128)S(1)}, f32[192,256]{1,0:T(8,128)S(1)}, u32[]{:S(2)}, u32[]{:S(2)}) collective-permute-start(f32[192,256]{1,0:T(8,128)S(1)} %collective-permute-done.10.refs_0_), channel_id=1, source_target_pairs={{0,16},{16,0},{1,17},{17,1},{2,18},{18,2},{3,19},{19,3},{4,20},{20... | collective-permute-start | bytes 589832 | tf_op jit(solution)/shard_map/ppermute | solution.py:18
  76.4 13.9 %collective-permute-start.12 = (f32[192,256]{1,0:T(8,128)S(1)}, f32[192,256]{1,0:T(8,128)S(1)}, u32[]{:S(2)}, u32[]{:S(2)}) collective-permute-start(f32[192,256]{1,0:T(8,128)S(1)} %collective-permute-done.10.refs_0_), channel_id=1, source_target_pairs={{0,32},{32,0},{64,96},{96,64},{1,33},{33,1},{65,97},{97,65},{2,34}... | collective-permute-start | bytes 589832 | tf_op jit(solution)/shard_map/ppermute | solution.py:18
  81.6 14.4 %collective-permute-start.15 = (f32[192,256]{1,0:T(8,128)S(1)}, f32[192,256]{1,0:T(8,128)S(1)}, u32[]{:S(2)}, u32[]{:S(2)}) collective-permute-start(f32[192,256]{1,0:T(8,128)S(1)} %collective-permute-done.11.refs_1_), channel_id=1, source_target_pairs={{0,96},{32,64},{64,32},{96,0},{1,97},{33,65},{65,33},{97,1},{2,98}... | collective-permute-start | bytes 589832 | tf_op jit(solution)/shard_map/ppermute | solution.py:18
  90.3 10.0 %collective-permute-start.17 = (f32[192,256]{1,0:T(8,128)S(1)}, f32[192,256]{1,0:T(8,128)S(1)}, u32[]{:S(2)}, u32[]{:S(2)}) collective-permute-start(f32[192,256]{1,0:T(8,128)S(1)} %collective-permute-done.10.refs_0_), channel_id=1, source_target_pairs={{0,96},{32,64},{64,32},{96,0},{1,97},{33,65},{65,33},{97,1},{2,98}... | collective-permute-start | bytes 589832 | tf_op jit(solution)/shard_map/ppermute | solution.py:18
  90.3 9.9 %collective-permute-start.13 = (f32[192,256]{1,0:T(8,128)S(1)}, f32[192,256]{1,0:T(8,128)S(1)}, u32[]{:S(2)}, u32[]{:S(2)}) collective-permute-start(f32[192,256]{1,0:T(8,128)S(1)} %collective-permute-done.11.refs_1_), channel_id=1, source_target_pairs={{0,32},{32,0},{64,96},{96,64},{1,33},{33,1},{65,97},{97,65},{2,34}... | collective-permute-start | bytes 589832 | tf_op jit(solution)/shard_map/ppermute | solution.py:18
  90.3 13.1 %collective-permute-start.14 = (f32[192,256]{1,0:T(8,128)S(1)}, f32[192,256]{1,0:T(8,128)S(1)}, u32[]{:S(2)}, u32[]{:S(2)}) collective-permute-start(f32[192,256]{1,0:T(8,128)S(1)} %collective-permute-done.12.refs_2_), channel_id=1, source_target_pairs={{0,96},{32,64},{64,32},{96,0},{1,97},{33,65},{65,33},{97,1},{2,98}... | collective-permute-start | bytes 589832 | tf_op jit(solution)/shard_map/ppermute | solution.py:18
  96.0 7.4 %collective-permute-start.16 = (f32[192,256]{1,0:T(8,128)S(1)}, f32[192,256]{1,0:T(8,128)S(1)}, u32[]{:S(2)}, u32[]{:S(2)}) collective-permute-start(f32[192,256]{1,0:T(8,128)S(1)} %collective-permute-done.15.refs_7_), channel_id=1, source_target_pairs={{0,32},{32,0},{64,96},{96,64},{1,33},{33,1},{65,97},{97,65},{2,34}... | collective-permute-start | bytes 589832 | tf_op jit(solution)/shard_map/ppermute | solution.py:18
  116.7 3.5 %collective-permute-start.18 = (f32[8,192,256]{2,1,0:T(8,128)S(1)}, f32[8,192,256]{2,1,0:T(8,128)S(1)}, u32[]{:S(2)}, u32[]{:S(2)}) collective-permute-start(f32[8,192,256]{2,1,0:T(8,128)S(1)} %get-tuple-element.11), channel_id=1, source_target_pairs={{0,1},{1,0},{2,3},{3,2},{4,5},{5,4},{6,7},{7,6},{8,9},{9,8},{10,11... | collective-permute-start | bytes 4718600 | tf_op jit(solution)/shard_map/ppermute | solution.py:18
  120.2 1.4 copy-start
  124.8 8.7 %copy-start.3 = (f32[192,256]{1,0:T(8,128)S(1)}, f32[192,256]{1,0:T(8,128)}, u32[]{:S(2)}) copy-start(f32[192,256]{1,0:T(8,128)} %copy-done.2) | copy-start | bytes 589828
  125.9 7.6 %collective-permute-start.9 = (f32[192,256]{1,0:T(8,128)S(1)}, f32[192,256]{1,0:T(8,128)S(1)}, u32[]{:S(2)}, u32[]{:S(2)}) collective-permute-start(f32[192,256]{1,0:T(8,128)S(1)} %dynamic-slice_bitcast_fusion.1), channel_id=1, source_target_pairs={{0,2},{2,0},{1,3},{3,1},{4,6},{6,4},{5,7},{7,5},{8,10},{10,8},{9,1... | collective-permute-start | bytes 589832 | tf_op jit(solution)/shard_map/ppermute | solution.py:18
  134.9 32.2 %copy-start.1 = (f32[1,2,192,256]{3,2,1,0:T(8,128)S(1)}, f32[1,2,192,256]{3,2,1,0:T(8,128)}, u32[]{:S(2)}) copy-start(f32[1,2,192,256]{3,2,1,0:T(8,128)} %reduce-scatter.3.cloned.1.call-done) | copy-start | bytes 1179652
  134.9 1.6 collective-permute-start.21
  136.6 6.1 %collective-permute-start.24 = (f32[64,256]{1,0:T(8,128)S(1)}, f32[64,256]{1,0:T(8,128)S(1)}, u32[]{:S(2)}, u32[]{:S(2)}) collective-permute-start(f32[64,256]{1,0:T(8,128)S(1)} %get-tuple-element.19), channel_id=1, source_target_pairs={{0,96},{32,0},{64,32},{96,64},{1,97},{33,1},{65,33},{97,65},{2,98}... | collective-permute-start | bytes 196616 | tf_op jit(solution)/shard_map/ppermute | solution.py:18
  139.6 6.1 %collective-permute-start.23 = (f32[64,256]{1,0:T(8,128)S(1)}, f32[64,256]{1,0:T(8,128)S(1)}, u32[]{:S(2)}, u32[]{:S(2)}) collective-permute-start(f32[64,256]{1,0:T(8,128)S(1)} %get-tuple-element.20), channel_id=1, source_target_pairs={{0,64},{32,96},{64,0},{96,32},{1,65},{33,97},{65,1},{97,33},{2,66}... | collective-permute-start | bytes 196616 | tf_op jit(solution)/shard_map/ppermute | solution.py:18
  139.6 6.5 %collective-permute-start.22 = (f32[64,256]{1,0:T(8,128)S(1)}, f32[64,256]{1,0:T(8,128)S(1)}, u32[]{:S(2)}, u32[]{:S(2)}) collective-permute-start(f32[64,256]{1,0:T(8,128)S(1)} %get-tuple-element.18), channel_id=1, source_target_pairs={{0,32},{32,64},{64,96},{96,0},{1,33},{33,65},{65,97},{97,1},{2,34}... | collective-permute-start | bytes 196616 | tf_op jit(solution)/shard_map/ppermute | solution.py:18
  146.1 4.3 %collective-permute-start.27 = (f32[64,256]{1,0:T(8,128)S(1)}, f32[64,256]{1,0:T(8,128)S(1)}, u32[]{:S(2)}, u32[]{:S(2)}) collective-permute-start(f32[64,256]{1,0:T(8,128)S(1)} %add_add_fusion.1), channel_id=1, source_target_pairs={{0,12},{4,0},{8,4},{12,8},{1,13},{5,1},{9,5},{13,9},{2,14},{6,2},{... | collective-permute-start | bytes 196616 | tf_op jit(solution)/shard_map/ppermute | solution.py:18
  146.5 6.3 %collective-permute-start.26 = (f32[64,256]{1,0:T(8,128)S(1)}, f32[64,256]{1,0:T(8,128)S(1)}, u32[]{:S(2)}, u32[]{:S(2)}) collective-permute-start(f32[64,256]{1,0:T(8,128)S(1)} %add_add_fusion.1), channel_id=1, source_target_pairs={{0,8},{4,12},{8,0},{12,4},{1,9},{5,13},{9,1},{13,5},{2,10},{6,14},... | collective-permute-start | bytes 196616 | tf_op jit(solution)/shard_map/ppermute | solution.py:18
  149.8 5.5 %collective-permute-start.25 = (f32[64,256]{1,0:T(8,128)S(1)}, f32[64,256]{1,0:T(8,128)S(1)}, u32[]{:S(2)}, u32[]{:S(2)}) collective-permute-start(f32[64,256]{1,0:T(8,128)S(1)} %add_add_fusion.1), channel_id=1, source_target_pairs={{0,4},{4,8},{8,12},{12,0},{1,5},{5,9},{9,13},{13,1},{2,6},{6,10},{... | collective-permute-start | bytes 196616 | tf_op jit(solution)/shard_map/ppermute | solution.py:18
  155.3 5.0 %collective-permute-start.28 = (f32[64,256]{1,0:T(8,128)S(1)}, f32[64,256]{1,0:T(8,128)S(1)}, u32[]{:S(2)}, u32[]{:S(2)}) collective-permute-start(f32[64,256]{1,0:T(8,128)S(1)} %add_add_fusion), channel_id=1, source_target_pairs={{0,2},{2,0},{1,3},{3,1},{4,6},{6,4},{5,7},{7,5},{8,10},{10,8},{9,1... | collective-permute-start | bytes 196616 | tf_op jit(solution)/shard_map/ppermute | solution.py:18
  160.3 6.1 %collective-permute-start.29 = (f32[64,256]{1,0:T(8,128)S(1)}, f32[64,256]{1,0:T(8,128)S(1)}, u32[]{:S(2)}, u32[]{:S(2)}) collective-permute-start(f32[64,256]{1,0:T(8,128)S(1)} %add.132), channel_id=1, source_target_pairs={{0,16},{16,0},{1,17},{17,1},{2,18},{18,2},{3,19},{19,3},{4,20},{20... | collective-permute-start | bytes 196616 | tf_op jit(solution)/shard_map/ppermute | solution.py:18
  160.8 13.2 %copy-start.5 = (f32[1,2,192,256]{3,2,1,0:T(8,128)S(1)}, f32[1,2,192,256]{3,2,1,0:T(8,128)}, u32[]{:S(2)}) copy-start(f32[1,2,192,256]{3,2,1,0:T(8,128)} %reduce-scatter.5.cloned.1.call-done) | copy-start | bytes 1179652
  161.8 12.2 %collective-permute-start.20 = (f32[192,256]{1,0:T(8,128)S(1)}, f32[192,256]{1,0:T(8,128)S(1)}, u32[]{:S(2)}, u32[]{:S(2)}) collective-permute-start(f32[192,256]{1,0:T(8,128)S(1)} %dynamic-slice_bitcast_fusion), channel_id=1, source_target_pairs={{0,2},{2,0},{1,3},{3,1},{4,6},{6,4},{5,7},{7,5},{8,10},{10,8},{9,1... | collective-permute-start | bytes 589832 | tf_op jit(solution)/shard_map/ppermute | solution.py:18
  166.4 9.1 %copy-start.4 = (f32[2,256,256]{2,1,0:T(8,128)S(1)}, f32[2,256,256]{2,1,0:T(8,128)}, u32[]{:S(2)}) copy-start(f32[2,256,256]{2,1,0:T(8,128)} %param.8) | copy-start | bytes 1572868
  166.4 4.3 %collective-permute-start.30 = (f32[64,256]{1,0:T(8,128)S(1)}, f32[64,256]{1,0:T(8,128)S(1)}, u32[]{:S(2)}, u32[]{:S(2)}) collective-permute-start(f32[64,256]{1,0:T(8,128)S(1)} %add.133), channel_id=1, source_target_pairs={{0,96},{32,0},{64,32},{96,64},{1,97},{33,1},{65,33},{97,65},{2,98}... | collective-permute-start | bytes 196616 | tf_op jit(solution)/shard_map/ppermute | solution.py:18
  167.2 5.9 %collective-permute-start.31 = (f32[64,256]{1,0:T(8,128)S(1)}, f32[64,256]{1,0:T(8,128)S(1)}, u32[]{:S(2)}, u32[]{:S(2)}) collective-permute-start(f32[64,256]{1,0:T(8,128)S(1)} %add.133), channel_id=1, source_target_pairs={{0,64},{32,96},{64,0},{96,32},{1,65},{33,97},{65,1},{97,33},{2,66}... | collective-permute-start | bytes 196616 | tf_op jit(solution)/shard_map/ppermute | solution.py:18
  167.8 5.9 %collective-permute-start.32 = (f32[64,256]{1,0:T(8,128)S(1)}, f32[64,256]{1,0:T(8,128)S(1)}, u32[]{:S(2)}, u32[]{:S(2)}) collective-permute-start(f32[64,256]{1,0:T(8,128)S(1)} %add.133), channel_id=1, source_target_pairs={{0,32},{32,64},{64,96},{96,0},{1,33},{33,65},{65,97},{97,1},{2,34}... | collective-permute-start | bytes 196616 | tf_op jit(solution)/shard_map/ppermute | solution.py:18
  173.9 1.6 collective-permute-start.33
Sparse Core Ops, SparseCore 0:
  42.7 27.3 all-gather.1
  72.5 27.5 reduce-scatter.2
  125.0 24.7 reduce-scatter.4

commit v3 on v2

v3 whole, which is shorter than its diff:
```python
import jax
import jax.numpy as jnp
from jax import lax
from jax.experimental import pallas as pl
from jax.experimental.pallas import tpu as pltpu
from jax.sharding import Mesh, PartitionSpec as P

BS = 64
NS = 2
HIGH = lax.Precision.HIGH
HIGHEST = lax.Precision.HIGHEST
ALL = ("y", "xh", "z", "xl", "k")
BF = jnp.bfloat16
F32 = jnp.float32
LIMIT = 16


def send(x, axis, size, to):
    return lax.ppermute(x, axis, [(i, to(i)) for i in range(size)])


def swap(x, axis):
    return send(x, axis, 2, lambda i: i ^ 1)


def transpose_pairs():
    return [(8 * c + r, 16 * r + c) for r in range(8) for c in range(16)]


def tile_mask(pattern, snode, start, length):
    tiles = lax.dynamic_slice_in_dim(pattern[snode], start // BS, length // BS, 0)
    return jnp.repeat(tiles, BS).astype(F32)[:, None]


def pick(bit, x, y):
    return jnp.where(bit == 0, x, y)


def total(first, second):
    k, y = lax.axis_index("k"), lax.axis_index("y")
    mine = pick(k, first, second) + swap(pick(k, second, first), "k")
    for flip, bit in ((1, (y ^ (y >> 1)) & 1), (3, y >> 1)):
        half = mine.shape[0] // 2
        low, high = mine[:half], mine[half:]
        mine = pick(bit, low, high) + send(pick(bit, high, low), "y", 4, lambda i: i ^ flip)
    for flip in (1, 3):
        mine = mine + send(mine, "z", 4, lambda i: i ^ flip)
    mine = mine + swap(mine, "xl")
    mine = mine + swap(mine, "xh")
    for flip, bit in ((3, y >> 1), (1, (y ^ (y >> 1)) & 1)):
        other = send(mine, "y", 4, lambda i: i ^ flip)
        mine = jnp.concatenate([pick(bit, mine, other), pick(bit, other, mine)])
    other = swap(mine, "k")
    return pick(k, mine, other), pick(k, other, mine)


def halves(x):
    high = x.astype(BF)
    return high, (x - high.astype(F32)).astype(BF)


def dot3(a, b, dims):
    ah, al = halves(a)
    bh, bl = halves(b)
    f = lambda p, q: lax.dot_general(p, q, (dims, ((), ())), preferred_element_type=F32)
    return f(ah, bh) + (f(ah, bl) + f(al, bh))


def split_kernel(a_ref, high_ref, low_ref):
    high_ref[...], low_ref[...] = halves(a_ref[...])


def split(a, step):
    rows, cols = a.shape
    spec = pl.BlockSpec((step, cols), lambda i: (i, 0))
    return pl.pallas_call(
        split_kernel,
        grid=(rows // step,),
        in_specs=[spec],
        out_specs=[spec, spec],
        out_shape=[jax.ShapeDtypeStruct(a.shape, BF)] * 2,
        compiler_params=pltpu.CompilerParams(vmem_limit_bytes=24 << 20),
        cost_estimate=pl.CostEstimate(flops=4 * rows * cols, bytes_accessed=8 * rows * cols, transcendentals=0),
    )(a)


def later(xs, after):
    anywhere = pl.BlockSpec(memory_space=pl.ANY)
    return pl.pallas_call(
        lambda *refs: None,
        in_specs=[anywhere] * (len(xs) + 1),
        out_specs=[anywhere] * len(xs),
        out_shape=[jax.ShapeDtypeStruct(x.shape, x.dtype) for x in xs],
        input_output_aliases={i: i for i in range(len(xs))},
        cost_estimate=pl.CostEstimate(flops=0, bytes_accessed=0, transcendentals=0),
    )(*xs, after)


def product_kernel(place_ref, ah_ref, al_ref, *refs):
    pieces, (keep_ref, give_ref, high, low) = refs[:8], refs[-4:]
    piece = pieces[0].shape[0]

    @pl.when(pl.program_id(0) == 0)
    def _():
        for j in range(8):
            rows = pl.ds(pl.multiple_of(place_ref[j] * piece, BS), piece)
            xh, xl = halves(pieces[j][...])
            high[rows, :] = xh
            low[rows, :] = xl

    ah, al = ah_ref[...], al_ref[...]
    f = lambda p, q: jnp.dot(p, q, preferred_element_type=F32)
    out = f(ah, high[...]) + (f(ah, low[...]) + f(al, high[...]))
    first, second = out[:piece], out[piece:]
    lower = place_ref[8] == 0
    keep_ref[0] = jnp.where(lower, first, second)
    give_ref[0] = jnp.where(lower, second, first)


def product(parts, pieces, places, after=()):
    rows, cols = parts[0].shape
    piece, width = pieces[0].shape
    blocks = rows // (2 * piece)
    whole = pl.BlockSpec((piece, width), lambda i, p: (0, 0))
    out = pl.BlockSpec((1, piece, width), lambda i, p: (i, 0, 0))
    return pl.pallas_call(
        product_kernel,
        grid_spec=pltpu.PrefetchScalarGridSpec(
            num_scalar_prefetch=1,
            grid=(blocks,),
            in_specs=[pl.BlockSpec((2 * piece, cols), lambda i, p: (i, 0))] * 2
            + [whole] * 8
            + [pl.BlockSpec(memory_space=pl.ANY)] * len(after),
            out_specs=[out, out],
            scratch_shapes=[pltpu.VMEM((cols, width), BF)] * 2,
        ),
        out_shape=[jax.ShapeDtypeStruct((blocks, piece, width), F32)] * 2,
        compiler_params=pltpu.CompilerParams(vmem_limit_bytes=LIMIT << 20),
        cost_estimate=pl.CostEstimate(
            flops=6 * rows * cols * width, bytes_accessed=4 * (rows * cols + (rows + cols) * width), transcendentals=0
        ),
    )(places, *parts, *pieces, *after)


def add_kernel(block_ref, keep_ref, got_ref, x_ref, *refs):
    outs, update_ref = refs[:-1], refs[-1]
    step = pl.program_id(0)

    @pl.when(step == 0)
    def _():
        update_ref[...] = jnp.zeros_like(update_ref)

    both = keep_ref[0] + got_ref[0]
    each = pl.num_programs(0) // len(outs)
    for j, out in enumerate(outs):

        @pl.when(step // each == j)
        def _():
            out[0] = both

    update_ref[...] += dot3(x_ref[0], both, ((0,), (0,)))


def add_and_update(keep, got, x, blocks, parts):
    count, piece, width = keep.shape
    each = count // parts
    spec = pl.BlockSpec((1, piece, width), lambda i, b: (b[i], 0, 0))
    outs = [
        pl.BlockSpec((1, piece, width), lambda i, b, j=j: (jnp.clip(i - j * each, 0, each - 1), 0, 0)) for j in range(parts)
    ]
    *sums, update = pl.pallas_call(
        add_kernel,
        grid_spec=pltpu.PrefetchScalarGridSpec(
            num_scalar_prefetch=1,
            grid=(count,),
            in_specs=[spec] * 3,
            out_specs=[*outs, pl.BlockSpec((width, width), lambda i, b: (0, 0))],
        ),
        out_shape=[jax.ShapeDtypeStruct((each, piece, width), F32)] * parts + [jax.ShapeDtypeStruct((width, width), F32)],
        compiler_params=pltpu.CompilerParams(vmem_limit_bytes=16 << 20),
        cost_estimate=pl.CostEstimate(
            flops=6 * count * piece * width * width, bytes_accessed=16 * count * piece * width, transcendentals=0
        ),
    )(blocks, keep, got, x)
    return sums, update


def near_pieces(mine):
    return swap(mine, "xh"), send(mine, "y", 4, lambda i: i ^ 1), send(mine, "y", 4, lambda i: i ^ 3)


def gather_column(mine, pair, mine1, mine3):
    one, three = (lambda i: i ^ 1), (lambda i: i ^ 3)
    pair3 = send(pair, "y", 4, three)
    pair1 = send(pair, "y", 4, one)
    mine2 = send(mine1, "y", 4, three)
    pair2 = send(pair3, "y", 4, one)
    return [mine, pair, mine1, pair1, mine2, pair2, mine3, pair3]


def sum_scattered(sums, z):
    give_a, give_b, keep_a, keep_b = sums
    one, three = (lambda i: i ^ 1), (lambda i: i ^ 3)
    got_a = send(give_a, "z", 4, one)
    got_b = send(give_b, "z", 4, three)
    next_a = send(keep_a[1] + got_a[1], "z", 4, three)
    next_b = send(keep_b[1] + got_b[1], "z", 4, one)
    return (keep_a[0] + got_a[0]) + next_a, (keep_b[0] + got_b[0]) + next_b


def local(ancestor_inverse, lower_panel, diag_factor, diag_block, pattern):
    y, xh, z, xl, k = (lax.axis_index(a) for a in ALL)
    row, col = y * 2 + xh, z * 4 + xl * 2 + k
    piece = lower_panel.shape[1]
    start = (row * 16 + col) * piece
    masks = [tile_mask(pattern, s, start, piece) for s in range(NS)]
    normed = [jnp.dot(lower_panel[s], diag_factor[s], precision=HIGHEST) * masks[s] for s in range(NS)]
    spots = jnp.arange(8, dtype=jnp.int32)
    places = jnp.concatenate([((spots // 2) ^ y) * 2 + ((spots % 2) ^ xh), k[None]])

    mine = [lax.ppermute(n, ALL, transpose_pairs()) for n in normed]

    near = [swap(n, "xl") for n in normed]
    pairs = [jnp.stack([pick(xl, n, m), pick(xl, m, n)]) for n, m in zip(normed, near)]
    bands = [lax.all_gather(p, "z", axis=0, tiled=True) for p in pairs]
    apart = jnp.array([1, 2, 3, 2, 0, 3, 0, 1], jnp.int32)
    half = jnp.array([0, 0, 1, 1, 0, 0, 1, 1], jnp.int32)
    halving = (apart ^ z) * 2 + half

    parts = split(ancestor_inverse, 2 * piece)
    near = [near_pieces(m) for m in mine]
    panels, updates = [], []
    for snode in range(NS):
        if snode == 0:
            after = (mine[1], *pairs)
            around = near[0]
        else:
            after = ()
            around = later(near[1], keep)
        keep, give = product(parts, gather_column(mine[snode], *around), places, after)
        got = swap(give, "k")
        if snode == 0:
            (summed,), update = add_and_update(keep, got, bands[0], spots, 1)
            summed = lax.psum_scatter(summed.reshape(4, 2, *summed.shape[1:]), "z", scatter_dimension=0, tiled=False)
            first, second = summed[0], summed[1]
        else:
            sums, update = add_and_update(keep, got, bands[1], halving, 4)
            first, second = sum_scattered(sums, z)
        kept, given = pick(xl, first, second), pick(xl, second, first)
        panels.append(-masks[snode] * (kept + swap(given, "xl")))
        updates.append(update)
    first, second = total(*updates)
    return jnp.stack(panels), jnp.stack([diag_block[0] + first, diag_block[1] + second])


def solution(mesh):
    fine = Mesh(mesh.devices.reshape(4, 2, 4, 2, 2), ALL)
    rows, cols = ("y", "xh"), ("z", "xl", "k")
    return jax.shard_map(
        local,
        mesh=fine,
        in_specs=(P(rows, cols), P(None, ALL, None), P(), P(), P()),
        out_specs=(P(None, ALL, None), P()),
        check_vma=False,
    )
```

time: 185 us -> 225 us (1.22)
  local copies, waits for them, and re-layouts: 4.59 us -> 36.3 us
  Pallas kernels: 29.9 us -> 42.9 us
  starting transfers between devices: 69.2 us -> 65.6 us
  matrix products: 4.18 us -> 1.71 us
    unnamed x18 -> x66, local copies, waits for them, and re-layouts: 1.47 us -> 35.3 us
    pallas_call x1 -> x4, Pallas kernels: 3.27 us -> 22.3 us  [the longest x2 12.9 us: add_and_update(): pl.pallas_call(add_kernel, grid_spec=pltpu.PrefetchScalarGridSpec(num_sca...]
    pallas_call x2, Pallas kernels: 26.7 us -> 20.6 us  [product(): pl.pallas_call(product_kernel, grid_spec=pltpu.PrefetchScalarGridSpec(num...]
    ppermute x32 -> x34, starting transfers between devices: 67.7 us -> 64.2 us  [send(): return lax.ppermute(x, axis, [(i, to(i)) for i in range(size)])]
    ppermute x32 -> x34, waiting for transfers between devices: 56.5 us -> 58.1 us  [send(): return lax.ppermute(x, axis, [(i, to(i)) for i in range(size)])]
  transfers between devices with their start and end apart: 37 -> 39, of which waited for: 23 -> 15; matrix products, arithmetic and copies ran while one was open for 5% -> 2% of each run, Pallas kernels for 16% -> 16%
where the time goes in v3:
time: 225 us; the launch traced here: 224 us
  starting transfers between devices  65.6 us (29%)
  waiting for transfers between devices  58.2 us (26%)
  Pallas kernels  42.9 us (19%)
  local copies, waits for them, and re-layouts  36.3 us (16%)
  between operations  14.2 us (6%)
  other arithmetic  5.01 us (2%)
    ppermute x34, starting transfers between devices, send(): return lax.ppermute(x, axis, [(i, to(i)) for i in range(size)])  64.2 us
    ppermute x34, waiting for transfers between devices, send(): return lax.ppermute(x, axis, [(i, to(i)) for i in range(size)])  58.1 us
    unnamed x66, local copies, waits for them, and re-layouts  35.3 us
    pallas_call x2, Pallas kernels, product(): pl.pallas_call(product_kernel, grid_spec=pltpu.PrefetchScalarGridSpec(num...  20.6 us
    pallas_call x2, Pallas kernels, add_and_update(): pl.pallas_call(add_kernel, grid_spec=pltpu.PrefetchScalarGridSpec(num_sca...  12.9 us
    pallas_call x1, Pallas kernels, split(): pl.pallas_call(split_kernel, grid=(rows // step,), in_specs=[spec], out_s...  9.39 us
  transfers between devices with their start and end apart: 39, of which 15 were waited for; matrix products, arithmetic and copies ran while one was open for 2% of the time, Pallas kernels for 16%

profile of v3, /device:TPU:0, one launch (start us, length us, event | category | flops | bytes accessed | tf_op | source)
XLA Modules:
  0.0 223.9 jit_solution(10463295008221156064)
XLA Ops:
  8.3 1.4 convolution_multiply_fusion.1
  9.7 1.7 collective-permute-start.9
  11.3 4.9 %collective-permute-done.9 = f32[192,256]{1,0:T(8,128)S(1)} collective-permute-done((f32[192,256]{1,0:T(8,128)S(1)}, f32[192,256]{1,0:T(8,128)S(1)}, u32[]{:S(2)}, u32[]{:S(2)}) %collective-permute-start.9) | collective-permute-done | bytes 196640 | tf_op jit(solution)/shard_map/ppermute | solution.py:19
  17.9 11.0 %collective-permute-start.1 = (f32[192,256]{1,0:T(8,128)S(1)}, f32[192,256]{1,0:T(8,128)S(1)}, u32[]{:S(2)}, u32[]{:S(2)}) collective-permute-start(f32[192,256]{1,0:T(8,128)S(1)} %collective-permute-done.refs_0_), channel_id=1, source_target_pairs={{0,16},{16,0},{1,17},{17,1},{2,18},{18,2},{3,19},{19,3},{4,20},{20... | collective-permute-start | bytes 589832 | tf_op jit(solution)/shard_map/ppermute | solution.py:19
  30.1 9.4 %shard_map.86 = (bf16[3072,1536]{1,0:T(8,128)(2,1)S(1)}, bf16[3072,1536]{1,0:T(8,128)(2,1)S(1)}) custom-call(f32[3072,1536]{1,0:T(8,128)} %a_ref.1), custom_call_target="tpu_custom_call" | custom-call | flops 18874368 | bytes 37748736 | tf_op jit(solution)/shard_map/pallas_call | solution.py:76
  39.5 3.7 %copy-done.12 = bf16[3072,1536]{1,0:T(8,128)(2,1)} copy-done((bf16[3072,1536]{1,0:T(8,128)(2,1)}, bf16[3072,1536]{1,0:T(8,128)(2,1)S(1)}, u32[]{:S(2)}) %copy-start.12) | copy-done | bytes 9437208
  43.2 3.6 %copy-done.15 = bf16[3072,1536]{1,0:T(8,128)(2,1)} copy-done((bf16[3072,1536]{1,0:T(8,128)(2,1)}, bf16[3072,1536]{1,0:T(8,128)(2,1)S(1)}, u32[]{:S(2)}) %copy-start.15) | copy-done | bytes 9437208
  46.8 6.4 %collective-permute-start.2 = (f32[192,256]{1,0:T(8,128)S(1)}, f32[192,256]{1,0:T(8,128)S(1)}, u32[]{:S(2)}, u32[]{:S(2)}) collective-permute-start(f32[192,256]{1,0:T(8,128)S(1)} %collective-permute-done.refs_0_), channel_id=1, source_target_pairs={{0,32},{32,0},{64,96},{96,64},{1,33},{33,1},{65,97},{97,65},{2,34}... | collective-permute-start | bytes 589832 | tf_op jit(solution)/shard_map/ppermute | solution.py:19
  53.2 9.0 %collective-permute-start.5 = (f32[192,256]{1,0:T(8,128)S(1)}, f32[192,256]{1,0:T(8,128)S(1)}, u32[]{:S(2)}, u32[]{:S(2)}) collective-permute-start(f32[192,256]{1,0:T(8,128)S(1)} %collective-permute-done.1.refs_1_), channel_id=1, source_target_pairs={{0,96},{32,64},{64,32},{96,0},{1,97},{33,65},{65,33},{97,1},{2,98}... | collective-permute-start | bytes 589832 | tf_op jit(solution)/shard_map/ppermute | solution.py:19
  62.5 5.3 %collective-permute-start.4 = (f32[192,256]{1,0:T(8,128)S(1)}, f32[192,256]{1,0:T(8,128)S(1)}, u32[]{:S(2)}, u32[]{:S(2)}) collective-permute-start(f32[192,256]{1,0:T(8,128)S(1)} %collective-permute-done.2.refs_2_), channel_id=1, source_target_pairs={{0,96},{32,64},{64,32},{96,0},{1,97},{33,65},{65,33},{97,1},{2,98}... | collective-permute-start | bytes 589832 | tf_op jit(solution)/shard_map/ppermute | solution.py:19
  67.8 1.2 collective-permute-start.6
  69.0 3.9 %collective-permute-start.13 = (f32[192,256]{1,0:T(8,128)S(1)}, f32[192,256]{1,0:T(8,128)S(1)}, u32[]{:S(2)}, u32[]{:S(2)}) collective-permute-start(f32[192,256]{1,0:T(8,128)S(1)} %collective-permute-done.8.refs_8_.refs_0_), channel_id=1, source_target_pairs={{0,16},{16,0},{1,17},{17,1},{2,18},{18,2},{3,19},{19,3},{4,20},{20... | collective-permute-start | bytes 589832 | tf_op jit(solution)/shard_map/ppermute | solution.py:19
  73.7 3.3 %collective-permute-start.15 = (f32[192,256]{1,0:T(8,128)S(1)}, f32[192,256]{1,0:T(8,128)S(1)}, u32[]{:S(2)}, u32[]{:S(2)}) collective-permute-start(f32[192,256]{1,0:T(8,128)S(1)} %collective-permute-done.8.refs_8_.refs_0_), channel_id=1, source_target_pairs={{0,96},{32,64},{64,32},{96,0},{1,97},{33,65},{65,33},{97,1},{2,98}... | collective-permute-start | bytes 589832 | tf_op jit(solution)/shard_map/ppermute | solution.py:19
  77.0 3.7 %copy-done.13 = bf16[3072,1536]{1,0:T(8,128)(2,1)S(1)} copy-done((bf16[3072,1536]{1,0:T(8,128)(2,1)S(1)}, bf16[3072,1536]{1,0:T(8,128)(2,1)}, u32[]{:S(2)}) %copy-start.13) | copy-done | bytes 9437208
  80.7 3.7 %copy-done.16 = bf16[3072,1536]{1,0:T(8,128)(2,1)S(1)} copy-done((bf16[3072,1536]{1,0:T(8,128)(2,1)S(1)}, bf16[3072,1536]{1,0:T(8,128)(2,1)}, u32[]{:S(2)}) %copy-start.16) | copy-done | bytes 9437208
  84.4 10.3 %shard_map.87 = (f32[8,192,256]{2,1,0:T(8,128)S(1)}, f32[8,192,256]{2,1,0:T(8,128)}) custom-call(s32[9]{0:T(128)S(1)} %pad_add_fusion.place_ref, bf16[3072,1536]{1,0:T(8,128)(2,1)S(1)} %copy-done.13, bf16[3072,1536]{1,0:T(8,128)(2,1)S(1)} %copy-done.16, f32[192,256]{1,0:T(8,128)S(1)} %collective-permute-done.refs_0_, ...), custom_call_target="tpu_custom_call" | custom-call | flops 7247757312 | bytes 23592960 | tf_op jit(solution)/shard_map/pallas_call | solution.py:126
  94.7 1.1 copy-done
  96.6 2.5 %collective-permute-start.18 = (f32[192,256]{1,0:T(8,128)}, f32[192,256]{1,0:T(8,128)S(1)}, u32[]{:S(2)}, u32[]{:S(2)}) collective-permute-start(f32[192,256]{1,0:T(8,128)} %get-tuple-element.23.refs_1_), channel_id=1, source_target_pairs={{0,96},{32,64},{64,32},{96,0},{1,97},{33,65},{65,33},{97,1},{2,98}... | collective-permute-start | bytes 589832 | tf_op jit(solution)/shard_map/ppermute | solution.py:19
  99.9 6.0 %collective-permute-done.18.refs_7_ = f32[192,256]{1,0:T(8,128)S(1)} collective-permute-done((f32[192,256]{1,0:T(8,128)}, f32[192,256]{1,0:T(8,128)S(1)}, u32[]{:S(2)}, u32[]{:S(2)}) %collective-permute-start.18) | collective-permute-done | bytes 196640 | tf_op jit(solution)/shard_map/ppermute | solution.py:19
  106.7 2.1 collective-permute-done.17.refs_4_
  109.5 2.0 collective-permute-done.19.refs_5_
  115.0 3.7 %copy-done.14 = bf16[3072,1536]{1,0:T(8,128)(2,1)S(1)} copy-done((bf16[3072,1536]{1,0:T(8,128)(2,1)S(1)}, bf16[3072,1536]{1,0:T(8,128)(2,1)}, u32[]{:S(2)}) %copy-start.14) | copy-done | bytes 9437208
  118.7 3.8 %copy-done.17 = bf16[3072,1536]{1,0:T(8,128)(2,1)S(1)} copy-done((bf16[3072,1536]{1,0:T(8,128)(2,1)S(1)}, bf16[3072,1536]{1,0:T(8,128)(2,1)}, u32[]{:S(2)}) %copy-start.17) | copy-done | bytes 9437208
  125.3 10.3 %shard_map.90 = (f32[8,192,256]{2,1,0:T(8,128)S(1)}, f32[8,192,256]{2,1,0:T(8,128)}) custom-call(s32[9]{0:T(128)S(1)} %pad_add_fusion.place_ref, bf16[3072,1536]{1,0:T(8,128)(2,1)S(1)} %copy-done.14, bf16[3072,1536]{1,0:T(8,128)(2,1)S(1)} %copy-done.17, f32[192,256]{1,0:T(8,128)S(1)} %copy-done.21, f32[192,256]{1,0:T(8,128)S(1)} %copy-done.7, ...), custom_call_target="tpu_custom_call" | custom-call | flops 7247757312 | bytes 23592960 | tf_op jit(solution)/shard_map/pallas_call | solution.py:126
  136.3 1.4 copy-done.2
  137.7 6.7 %shard_map.88 = (f32[8,192,256]{2,1,0:T(8,128)}, f32[256,256]{1,0:T(8,128)S(1)}) custom-call(s32[8]{0:T(128)S(1)} %iota.7.block_ref, f32[8,192,256]{2,1,0:T(8,128)S(1)} %copy-done.1, f32[8,192,256]{2,1,0:T(8,128)} %collective-permute-done.11.got_ref, f32[8,192,256]{2,1,0:T(8,128)S(1)} %copy-done.2), custom_call_target="tpu_custom_call" | custom-call | flops 603979776 | bytes 6291456 | tf_op jit(solution)/shard_map/pallas_call | solution.py:171
  144.4 1.4 copy-done.3
  145.8 6.2 %shard_map.91 = (f32[2,192,256]{2,1,0:T(8,128)S(1)}, f32[2,192,256]{2,1,0:T(8,128)S(1)}, f32[2,192,256]{2,1,0:T(8,128)S(1)}, f32[2,192,256]{2,1,0:T(8,128)S(1)}, f32[256,256]{1,0:T(8,128)S(1)}) custom-call(s32[8]{0:T(128)S(1)} %multiply_add_fusion.block_ref, f32[8,192,256]{2,1,0:T(8,128)S(1)} %get-tuple-element.26.keep_ref, ...), custom_call_target="tpu_custom_call" | custom-call | flops 603979776 | bytes 6291456 | tf_op jit(solution)/shard_map/pallas_call | solution.py:171
  153.4 1.1 collective-permute-done.26
  154.7 5.8 %collective-permute-done.27 = f32[128,256]{1,0:T(8,128)S(1)} collective-permute-done((f32[128,256]{1,0:T(8,128)S(1)}, f32[128,256]{1,0:T(8,128)S(1)}, u32[]{:S(2)}, u32[]{:S(2)}) %collective-permute-start.27) | collective-permute-done | bytes 131104 | tf_op jit(solution)/shard_map/ppermute | solution.py:19
  160.5 2.5 %collective-permute-start.28 = (f32[64,256]{1,0:T(8,128)S(1)}, f32[64,256]{1,0:T(8,128)S(1)}, u32[]{:S(2)}, u32[]{:S(2)}) collective-permute-start(f32[64,256]{1,0:T(8,128)S(1)} %slice_select_fusion.1), channel_id=1, source_target_pairs={{0,96},{32,64},{64,32},{96,0},{1,97},{33,65},{65,33},{97,1},{2,98}... | collective-permute-start | bytes 196616 | tf_op jit(solution)/shard_map/ppermute | solution.py:19
  163.0 3.0 %collective-permute-done.28 = f32[64,256]{1,0:T(8,128)S(1)} collective-permute-done((f32[64,256]{1,0:T(8,128)S(1)}, f32[64,256]{1,0:T(8,128)S(1)}, u32[]{:S(2)}, u32[]{:S(2)}) %collective-permute-start.28) | collective-permute-done | bytes 65568 | tf_op jit(solution)/shard_map/ppermute | solution.py:19
  166.2 2.0 collective-permute-start.21
  168.2 3.9 %collective-permute-done.29 = f32[64,256]{1,0:T(8,128)S(1)} collective-permute-done((f32[64,256]{1,0:T(8,128)S(1)}, f32[64,256]{1,0:T(8,128)S(1)}, u32[]{:S(2)}, u32[]{:S(2)}) %collective-permute-start.29) | collective-permute-done | bytes 65568 | tf_op jit(solution)/shard_map/ppermute | solution.py:19
  172.1 1.1 collective-permute-start.30
  173.2 10.5 %collective-permute-done.30 = f32[64,256]{1,0:T(8,128)S(1)} collective-permute-done((f32[64,256]{1,0:T(8,128)S(1)}, f32[64,256]{1,0:T(8,128)S(1)}, u32[]{:S(2)}, u32[]{:S(2)}) %collective-permute-start.30) | collective-permute-done | bytes 65568 | tf_op jit(solution)/shard_map/ppermute | solution.py:19
  183.7 1.5 collective-permute-start.31
  185.2 2.8 %collective-permute-done.31 = f32[64,256]{1,0:T(8,128)S(1)} collective-permute-done((f32[64,256]{1,0:T(8,128)S(1)}, f32[64,256]{1,0:T(8,128)S(1)}, u32[]{:S(2)}, u32[]{:S(2)}) %collective-permute-start.31) | collective-permute-done | bytes 65568 | tf_op jit(solution)/shard_map/ppermute | solution.py:19
  188.0 3.1 %collective-permute-start.32 = (f32[64,256]{1,0:T(8,128)S(1)}, f32[64,256]{1,0:T(8,128)S(1)}, u32[]{:S(2)}, u32[]{:S(2)}) collective-permute-start(f32[64,256]{1,0:T(8,128)S(1)} %add.120), channel_id=1, source_target_pairs={{0,16},{16,0},{1,17},{17,1},{2,18},{18,2},{3,19},{19,3},{4,20},{20... | collective-permute-start | bytes 196616 | tf_op jit(solution)/shard_map/ppermute | solution.py:19
  191.2 2.7 %collective-permute-done.32 = f32[64,256]{1,0:T(8,128)S(1)} collective-permute-done((f32[64,256]{1,0:T(8,128)S(1)}, f32[64,256]{1,0:T(8,128)S(1)}, u32[]{:S(2)}, u32[]{:S(2)}) %collective-permute-start.32) | collective-permute-done | bytes 65568 | tf_op jit(solution)/shard_map/ppermute | solution.py:19
  193.9 2.8 %collective-permute-start.33 = (f32[64,256]{1,0:T(8,128)S(1)}, f32[64,256]{1,0:T(8,128)S(1)}, u32[]{:S(2)}, u32[]{:S(2)}) collective-permute-start(f32[64,256]{1,0:T(8,128)S(1)} %add.121), channel_id=1, source_target_pairs={{0,96},{32,64},{64,32},{96,0},{1,97},{33,65},{65,33},{97,1},{2,98}... | collective-permute-start | bytes 196616 | tf_op jit(solution)/shard_map/ppermute | solution.py:19
  197.1 2.3 %collective-permute-done.33 = f32[64,256]{1,0:T(8,128)S(1)} collective-permute-done((f32[64,256]{1,0:T(8,128)S(1)}, f32[64,256]{1,0:T(8,128)S(1)}, u32[]{:S(2)}, u32[]{:S(2)}) %collective-permute-start.33) | collective-permute-done | bytes 65568 | tf_op jit(solution)/shard_map/ppermute | solution.py:19
  200.0 3.7 %collective-permute-done.22 = f32[192,256]{1,0:T(8,128)S(1)} collective-permute-done((f32[192,256]{1,0:T(8,128)S(1)}, f32[192,256]{1,0:T(8,128)S(1)}, u32[]{:S(2)}, u32[]{:S(2)}) %collective-permute-start.22) | collective-permute-done | bytes 196640 | tf_op jit(solution)/shard_map/ppermute | solution.py:19
  203.8 1.4 collective-permute-start.25
  205.4 4.2 %collective-permute-done.25 = f32[192,256]{1,0:T(8,128)S(1)} collective-permute-done((f32[192,256]{1,0:T(8,128)S(1)}, f32[192,256]{1,0:T(8,128)S(1)}, u32[]{:S(2)}, u32[]{:S(2)}) %collective-permute-start.25) | collective-permute-done | bytes 196640 | tf_op jit(solution)/shard_map/ppermute | solution.py:19
  209.7 1.1 select_bitcast_fusion
  210.8 1.7 collective-permute-start.12
  213.4 3.1 %collective-permute-done.12 = f32[192,256]{1,0:T(8,128)S(1)} collective-permute-done((f32[192,256]{1,0:T(8,128)S(1)}, f32[192,256]{1,0:T(8,128)S(1)}, u32[]{:S(2)}, u32[]{:S(2)}) %collective-permute-start.12) | collective-permute-done | bytes 196640 | tf_op jit(solution)/shard_map/ppermute | solution.py:19
  (146 shorter events, 19.8 us)
Async XLA Ops:
  7.2 21.8 %copy-start.31 = (f32[2,192,256]{2,1,0:T(8,128)S(1)}, f32[2,192,256]{2,1,0:T(8,128)}, u32[]{:S(2)}) copy-start(f32[2,192,256]{2,1,0:T(8,128)} %param.8) | copy-start | bytes 1179652
  7.2 21.8 %copy-start.29 = (f32[2,256,256]{2,1,0:T(8,128)S(1)}, f32[2,256,256]{2,1,0:T(8,128)}, u32[]{:S(2)}) copy-start(f32[2,256,256]{2,1,0:T(8,128)} %param.9) | copy-start | bytes 1572868
  7.2 129.1 %all-gather.3.cloned.1.call-start = ((), (), s32[]{:S(2)}) async-start(), calls=%async_computation.1 | async-start | bytes 1966080 | tf_op jit(solution)/shard_map/all_gather | solution.py:225
  9.7 6.6 %collective-permute-start.9 = (f32[192,256]{1,0:T(8,128)S(1)}, f32[192,256]{1,0:T(8,128)S(1)}, u32[]{:S(2)}, u32[]{:S(2)}) collective-permute-start(f32[192,256]{1,0:T(8,128)S(1)} %convolution_multiply_fusion.1), channel_id=1, source_target_pairs={{0,2},{2,0},{1,3},{3,1},{4,6},{6,4},{5,7},{7,5},{8,10},{10,8},{9,1... | collective-permute-start | bytes 589832 | tf_op jit(solution)/shard_map/ppermute | solution.py:19
  17.0 127.3 %all-gather.5.cloned.1.call-start = ((), (), s32[]{:S(2)}) async-start(), calls=%async_computation.3 | async-start | bytes 1966080 | tf_op jit(solution)/shard_map/all_gather | solution.py:225
  17.1 0.8 collective-permute-start
  17.9 35.2 %collective-permute-start.1 = (f32[192,256]{1,0:T(8,128)S(1)}, f32[192,256]{1,0:T(8,128)S(1)}, u32[]{:S(2)}, u32[]{:S(2)}) collective-permute-start(f32[192,256]{1,0:T(8,128)S(1)} %collective-permute-done.refs_0_), channel_id=1, source_target_pairs={{0,16},{16,0},{1,17},{17,1},{2,18},{18,2},{3,19},{19,3},{4,20},{20... | collective-permute-start | bytes 589832 | tf_op jit(solution)/shard_map/ppermute | solution.py:19
  29.3 33.0 %collective-permute-start.10 = (f32[192,256]{1,0:T(8,128)S(1)}, f32[192,256]{1,0:T(8,128)S(1)}, u32[]{:S(2)}, u32[]{:S(2)}) collective-permute-start(f32[192,256]{1,0:T(8,128)S(1)} %convolution_multiply_fusion), channel_id=1, source_target_pairs={{0,2},{2,0},{1,3},{3,1},{4,6},{6,4},{5,7},{7,5},{8,10},{10,8},{9,1... | collective-permute-start | bytes 589832 | tf_op jit(solution)/shard_map/ppermute | solution.py:19
  29.4 39.6 %collective-permute-start.8 = (f32[192,256]{1,0:T(8,128)S(1)}, f32[192,256]{1,0:T(8,128)S(1)}, u32[]{:S(2)}, u32[]{:S(2)}) collective-permute-start(f32[192,256]{1,0:T(8,128)S(1)} %convolution_multiply_fusion), channel_id=1, source_target_pairs={{0,0},{8,1},{16,2},{24,3},{32,4},{40,5},{48,6},{56,7},{64,8},{72,9... | collective-permute-start | bytes 589832 | tf_op jit(solution)/shard_map/ppermute | solution.py:221
  46.8 30.2 %copy-start.4 = (f32[2,192,256]{2,1,0:T(8,128)S(1)}, f32[2,192,256]{2,1,0:T(8,128)}, u32[]{:S(2)}) copy-start(f32[2,192,256]{2,1,0:T(8,128)} %pad_maximum_fusion.1.refs_9_) | copy-start | bytes 1179652
  46.8 15.7 %collective-permute-start.2 = (f32[192,256]{1,0:T(8,128)S(1)}, f32[192,256]{1,0:T(8,128)S(1)}, u32[]{:S(2)}, u32[]{:S(2)}) collective-permute-start(f32[192,256]{1,0:T(8,128)S(1)} %collective-permute-done.refs_0_), channel_id=1, source_target_pairs={{0,32},{32,0},{64,96},{96,64},{1,33},{33,1},{65,97},{97,65},{2,34}... | collective-permute-start | bytes 589832 | tf_op jit(solution)/shard_map/ppermute | solution.py:19
  53.2 14.6 %collective-permute-start.5 = (f32[192,256]{1,0:T(8,128)S(1)}, f32[192,256]{1,0:T(8,128)S(1)}, u32[]{:S(2)}, u32[]{:S(2)}) collective-permute-start(f32[192,256]{1,0:T(8,128)S(1)} %collective-permute-done.1.refs_1_), channel_id=1, source_target_pairs={{0,96},{32,64},{64,32},{96,0},{1,97},{33,65},{65,33},{97,1},{2,98}... | collective-permute-start | bytes 589832 | tf_op jit(solution)/shard_map/ppermute | solution.py:19
  62.3 10.7 %collective-permute-start.7 = (f32[192,256]{1,0:T(8,128)S(1)}, f32[192,256]{1,0:T(8,128)S(1)}, u32[]{:S(2)}, u32[]{:S(2)}) collective-permute-start(f32[192,256]{1,0:T(8,128)S(1)} %collective-permute-done.refs_0_), channel_id=1, source_target_pairs={{0,96},{32,64},{64,32},{96,0},{1,97},{33,65},{65,33},{97,1},{2,98}... | collective-permute-start | bytes 589832 | tf_op jit(solution)/shard_map/ppermute | solution.py:19
  62.3 11.4 %collective-permute-start.3 = (f32[192,256]{1,0:T(8,128)S(1)}, f32[192,256]{1,0:T(8,128)S(1)}, u32[]{:S(2)}, u32[]{:S(2)}) collective-permute-start(f32[192,256]{1,0:T(8,128)S(1)} %collective-permute-done.1.refs_1_), channel_id=1, source_target_pairs={{0,32},{32,0},{64,96},{96,64},{1,33},{33,1},{65,97},{97,65},{2,34}... | collective-permute-start | bytes 589832 | tf_op jit(solution)/shard_map/ppermute | solution.py:19
  62.5 14.5 %collective-permute-start.4 = (f32[192,256]{1,0:T(8,128)S(1)}, f32[192,256]{1,0:T(8,128)S(1)}, u32[]{:S(2)}, u32[]{:S(2)}) collective-permute-start(f32[192,256]{1,0:T(8,128)S(1)} %collective-permute-done.2.refs_2_), channel_id=1, source_target_pairs={{0,96},{32,64},{64,32},{96,0},{1,97},{33,65},{65,33},{97,1},{2,98}... | collective-permute-start | bytes 589832 | tf_op jit(solution)/shard_map/ppermute | solution.py:19
  67.8 9.2 %collective-permute-start.6 = (f32[192,256]{1,0:T(8,128)S(1)}, f32[192,256]{1,0:T(8,128)S(1)}, u32[]{:S(2)}, u32[]{:S(2)}) collective-permute-start(f32[192,256]{1,0:T(8,128)S(1)} %collective-permute-done.5.refs_7_), channel_id=1, source_target_pairs={{0,32},{32,0},{64,96},{96,64},{1,33},{33,1},{65,97},{97,65},{2,34}... | collective-permute-start | bytes 589832 | tf_op jit(solution)/shard_map/ppermute | solution.py:19
  69.0 25.6 %copy-start.20 = (f32[192,256]{1,0:T(8,128)}, f32[192,256]{1,0:T(8,128)S(1)}, u32[]{:S(2)}) copy-start(f32[192,256]{1,0:T(8,128)S(1)} %collective-permute-done.8.refs_8_.refs_0_) | copy-start | bytes 589828
  69.0 26.7 %collective-permute-start.13 = (f32[192,256]{1,0:T(8,128)S(1)}, f32[192,256]{1,0:T(8,128)S(1)}, u32[]{:S(2)}, u32[]{:S(2)}) collective-permute-start(f32[192,256]{1,0:T(8,128)S(1)} %collective-permute-done.8.refs_8_.refs_0_), channel_id=1, source_target_pairs={{0,16},{16,0},{1,17},{17,1},{2,18},{18,2},{3,19},{19,3},{4,20},{20... | collective-permute-start | bytes 589832 | tf_op jit(solution)/shard_map/ppermute | solution.py:19
  73.0 21.7 %copy-start.5 = (f32[2,192,256]{2,1,0:T(8,128)}, f32[2,192,256]{2,1,0:T(8,128)S(1)}, u32[]{:S(2)}) copy-start(f32[2,192,256]{2,1,0:T(8,128)S(1)} %pad_maximum_fusion.2.refs_10_) | copy-start | bytes 1179652
  73.0 22.8 %collective-permute-start.14 = (f32[192,256]{1,0:T(8,128)S(1)}, f32[192,256]{1,0:T(8,128)S(1)}, u32[]{:S(2)}, u32[]{:S(2)}) collective-permute-start(f32[192,256]{1,0:T(8,128)S(1)} %collective-permute-done.8.refs_8_.refs_0_), channel_id=1, source_target_pairs={{0,32},{32,0},{64,96},{96,64},{1,33},{33,1},{65,97},{97,65},{2,34}... | collective-permute-start | bytes 589832 | tf_op jit(solution)/shard_map/ppermute | solution.py:19
  73.7 22.1 %collective-permute-start.15 = (f32[192,256]{1,0:T(8,128)S(1)}, f32[192,256]{1,0:T(8,128)S(1)}, u32[]{:S(2)}, u32[]{:S(2)}) collective-permute-start(f32[192,256]{1,0:T(8,128)S(1)} %collective-permute-done.8.refs_8_.refs_0_), channel_id=1, source_target_pairs={{0,96},{32,64},{64,32},{96,0},{1,97},{33,65},{65,33},{97,1},{2,98}... | collective-permute-start | bytes 589832 | tf_op jit(solution)/shard_map/ppermute | solution.py:19
  95.8 16.4 %copy-start.21 = (f32[192,256]{1,0:T(8,128)S(1)}, f32[192,256]{1,0:T(8,128)}, u32[]{:S(2)}) copy-start(f32[192,256]{1,0:T(8,128)} %copy-done.20) | copy-start | bytes 589828
  96.6 9.2 %collective-permute-start.18 = (f32[192,256]{1,0:T(8,128)}, f32[192,256]{1,0:T(8,128)S(1)}, u32[]{:S(2)}, u32[]{:S(2)}) collective-permute-start(f32[192,256]{1,0:T(8,128)} %get-tuple-element.23.refs_1_), channel_id=1, source_target_pairs={{0,96},{32,64},{64,32},{96,0},{1,97},{33,65},{65,33},{97,1},{2,98}... | collective-permute-start | bytes 589832 | tf_op jit(solution)/shard_map/ppermute | solution.py:19
  99.1 6.9 %collective-permute-start.16 = (f32[192,256]{1,0:T(8,128)}, f32[192,256]{1,0:T(8,128)S(1)}, u32[]{:S(2)}, u32[]{:S(2)}) collective-permute-start(f32[192,256]{1,0:T(8,128)} %get-tuple-element.23.refs_1_), channel_id=1, source_target_pairs={{0,32},{32,0},{64,96},{96,64},{1,33},{33,1},{65,97},{97,65},{2,34}... | collective-permute-start | bytes 589832 | tf_op jit(solution)/shard_map/ppermute | solution.py:19
  99.1 9.7 %collective-permute-start.17 = (f32[192,256]{1,0:T(8,128)}, f32[192,256]{1,0:T(8,128)S(1)}, u32[]{:S(2)}, u32[]{:S(2)}) collective-permute-start(f32[192,256]{1,0:T(8,128)} %get-tuple-element.24.refs_2_), channel_id=1, source_target_pairs={{0,96},{32,64},{64,32},{96,0},{1,97},{33,65},{65,33},{97,1},{2,98}... | collective-permute-start | bytes 589832 | tf_op jit(solution)/shard_map/ppermute | solution.py:19
  105.8 5.7 %collective-permute-start.19 = (f32[192,256]{1,0:T(8,128)S(1)}, f32[192,256]{1,0:T(8,128)S(1)}, u32[]{:S(2)}, u32[]{:S(2)}) collective-permute-start(f32[192,256]{1,0:T(8,128)S(1)} %collective-permute-done.18.refs_7_), channel_id=1, source_target_pairs={{0,32},{32,0},{64,96},{96,64},{1,33},{33,1},{65,97},{97,65},{2,34}... | collective-permute-start | bytes 589832 | tf_op jit(solution)/shard_map/ppermute | solution.py:19
  105.9 103.8 %reduce-scatter.2.cloned.1.call-start = ((), (), s32[]{:S(2)}) async-start(), calls=%async_computation.2 | async-start | bytes 1966080 | tf_op jit(solution)/shard_map/reduce_scatter | solution.py:244
  105.9 30.3 %collective-permute-start.11 = (f32[8,192,256]{2,1,0:T(8,128)}, f32[8,192,256]{2,1,0:T(8,128)}, u32[]{:S(2)}, u32[]{:S(2)}) collective-permute-start(f32[8,192,256]{2,1,0:T(8,128)} %get-tuple-element.21), channel_id=1, source_target_pairs={{0,1},{1,0},{2,3},{3,2},{4,5},{5,4},{6,7},{7,6},{8,9},{9,8},{10,11... | collective-permute-start | bytes 4718600 | tf_op jit(solution)/shard_map/ppermute | solution.py:19
  125.3 10.3 %copy-start.32 = (s32[8]{0:T(128)S(1)}, s32[8]{0:T(128)}, u32[]{:S(2)}) copy-start(s32[8]{0:T(128)} %constant.80.clone) | copy-start | bytes 100
  125.3 11.0 %copy-start.1 = (f32[8,192,256]{2,1,0:T(8,128)S(1)}, f32[8,192,256]{2,1,0:T(8,128)}, u32[]{:S(2)}) copy-start(f32[8,192,256]{2,1,0:T(8,128)} %copy-done) | copy-start | bytes 4718596
  135.6 8.8 %collective-permute-start.20 = (f32[8,192,256]{2,1,0:T(8,128)}, f32[8,192,256]{2,1,0:T(8,128)}, u32[]{:S(2)}, u32[]{:S(2)}) collective-permute-start(f32[8,192,256]{2,1,0:T(8,128)} %get-tuple-element.27), channel_id=1, source_target_pairs={{0,1},{1,0},{2,3},{3,2},{4,5},{5,4},{6,7},{7,6},{8,9},{9,8},{10,11... | collective-permute-start | bytes 4718600 | tf_op jit(solution)/shard_map/ppermute | solution.py:19
  152.8 1.8 collective-permute-start.26
  153.3 9.7 %copy-start.19 = (f32[2,192,256]{2,1,0:T(8,128)S(1)}, f32[2,192,256]{2,1,0:T(8,128)}, u32[]{:S(2)}) copy-start(f32[2,192,256]{2,1,0:T(8,128)} %copy-done.18) | copy-start | bytes 1179652
  154.6 5.9 %collective-permute-start.27 = (f32[128,256]{1,0:T(8,128)S(1)}, f32[128,256]{1,0:T(8,128)S(1)}, u32[]{:S(2)}, u32[]{:S(2)}) collective-permute-start(f32[128,256]{1,0:T(8,128)S(1)} %slice_select_fusion), channel_id=1, source_target_pairs={{0,32},{32,0},{64,96},{96,64},{1,33},{33,1},{65,97},{97,65},{2,34}... | collective-permute-start | bytes 393224 | tf_op jit(solution)/shard_map/ppermute | solution.py:19
  160.5 5.6 %collective-permute-start.28 = (f32[64,256]{1,0:T(8,128)S(1)}, f32[64,256]{1,0:T(8,128)S(1)}, u32[]{:S(2)}, u32[]{:S(2)}) collective-permute-start(f32[64,256]{1,0:T(8,128)S(1)} %slice_select_fusion.1), channel_id=1, source_target_pairs={{0,96},{32,64},{64,32},{96,0},{1,97},{33,65},{65,33},{97,1},{2,98}... | collective-permute-start | bytes 196616 | tf_op jit(solution)/shard_map/ppermute | solution.py:19
  163.0 28.1 %collective-permute-start.23 = (f32[2,192,256]{2,1,0:T(8,128)S(1)}, f32[2,192,256]{2,1,0:T(8,128)S(1)}, u32[]{:S(2)}, u32[]{:S(2)}) collective-permute-start(f32[2,192,256]{2,1,0:T(8,128)S(1)} %copy-done.19), channel_id=1, source_target_pairs={{0,12},{4,8},{8,4},{12,0},{1,13},{5,9},{9,5},{13,1},{2,14},{6,10},... | collective-permute-start | bytes 1179656 | tf_op jit(solution)/shard_map/ppermute | solution.py:19
  166.1 6.0 %collective-permute-start.29 = (f32[64,256]{1,0:T(8,128)S(1)}, f32[64,256]{1,0:T(8,128)S(1)}, u32[]{:S(2)}, u32[]{:S(2)}) collective-permute-start(f32[64,256]{1,0:T(8,128)S(1)} %select_add_fusion.2), channel_id=1, source_target_pairs={{0,4},{4,0},{8,12},{12,8},{1,5},{5,1},{9,13},{13,9},{2,6},{6,2},{1... | collective-permute-start | bytes 196616 | tf_op jit(solution)/shard_map/ppermute | solution.py:19
  166.2 30.5 %collective-permute-start.21 = (f32[2,192,256]{2,1,0:T(8,128)S(1)}, f32[2,192,256]{2,1,0:T(8,128)S(1)}, u32[]{:S(2)}, u32[]{:S(2)}) collective-permute-start(f32[2,192,256]{2,1,0:T(8,128)S(1)} %get-tuple-element.29), channel_id=1, source_target_pairs={{0,4},{4,0},{8,12},{12,8},{1,5},{5,1},{9,13},{13,9},{2,6},{6,2},{1... | collective-permute-start | bytes 1179656 | tf_op jit(solution)/shard_map/ppermute | solution.py:19
  172.1 11.6 %collective-permute-start.30 = (f32[64,256]{1,0:T(8,128)S(1)}, f32[64,256]{1,0:T(8,128)S(1)}, u32[]{:S(2)}, u32[]{:S(2)}) collective-permute-start(f32[64,256]{1,0:T(8,128)S(1)} %add.118), channel_id=1, source_target_pairs={{0,12},{4,8},{8,4},{12,0},{1,13},{5,9},{9,5},{13,1},{2,14},{6,10},... | collective-permute-start | bytes 196616 | tf_op jit(solution)/shard_map/ppermute | solution.py:19
  183.7 4.3 %collective-permute-start.31 = (f32[64,256]{1,0:T(8,128)S(1)}, f32[64,256]{1,0:T(8,128)S(1)}, u32[]{:S(2)}, u32[]{:S(2)}) collective-permute-start(f32[64,256]{1,0:T(8,128)S(1)} %add.119), channel_id=1, source_target_pairs={{0,2},{2,0},{1,3},{3,1},{4,6},{6,4},{5,7},{7,5},{8,10},{10,8},{9,1... | collective-permute-start | bytes 196616 | tf_op jit(solution)/shard_map/ppermute | solution.py:19
  188.0 5.8 %collective-permute-start.32 = (f32[64,256]{1,0:T(8,128)S(1)}, f32[64,256]{1,0:T(8,128)S(1)}, u32[]{:S(2)}, u32[]{:S(2)}) collective-permute-start(f32[64,256]{1,0:T(8,128)S(1)} %add.120), channel_id=1, source_target_pairs={{0,16},{16,0},{1,17},{17,1},{2,18},{18,2},{3,19},{19,3},{4,20},{20... | collective-permute-start | bytes 196616 | tf_op jit(solution)/shard_map/ppermute | solution.py:19
  191.1 8.9 %collective-permute-start.24 = (f32[192,256]{1,0:T(8,128)S(1)}, f32[192,256]{1,0:T(8,128)S(1)}, u32[]{:S(2)}, u32[]{:S(2)}) collective-permute-start(f32[192,256]{1,0:T(8,128)S(1)} %fusion.6), channel_id=1, source_target_pairs={{0,4},{4,0},{8,12},{12,8},{1,5},{5,1},{9,13},{13,9},{2,6},{6,2},{1... | collective-permute-start | bytes 589832 | tf_op jit(solution)/shard_map/ppermute | solution.py:19
  193.9 5.6 %collective-permute-start.33 = (f32[64,256]{1,0:T(8,128)S(1)}, f32[64,256]{1,0:T(8,128)S(1)}, u32[]{:S(2)}, u32[]{:S(2)}) collective-permute-start(f32[64,256]{1,0:T(8,128)S(1)} %add.121), channel_id=1, source_target_pairs={{0,96},{32,64},{64,32},{96,0},{1,97},{33,65},{65,33},{97,1},{2,98}... | collective-permute-start | bytes 196616 | tf_op jit(solution)/shard_map/ppermute | solution.py:19
  196.7 7.0 %collective-permute-start.22 = (f32[192,256]{1,0:T(8,128)S(1)}, f32[192,256]{1,0:T(8,128)S(1)}, u32[]{:S(2)}, u32[]{:S(2)}) collective-permute-start(f32[192,256]{1,0:T(8,128)S(1)} %fusion.9), channel_id=1, source_target_pairs={{0,12},{4,8},{8,4},{12,0},{1,13},{5,9},{9,5},{13,1},{2,14},{6,10},... | collective-permute-start | bytes 589832 | tf_op jit(solution)/shard_map/ppermute | solution.py:19
  199.5 5.8 %collective-permute-start.34 = (f32[128,256]{1,0:T(8,128)S(1)}, f32[128,256]{1,0:T(8,128)S(1)}, u32[]{:S(2)}, u32[]{:S(2)}) collective-permute-start(f32[128,256]{1,0:T(8,128)S(1)} %pad_maximum_fusion.5), channel_id=1, source_target_pairs={{0,32},{32,0},{64,96},{96,64},{1,33},{33,1},{65,97},{97,65},{2,34}... | collective-permute-start | bytes 393224 | tf_op jit(solution)/shard_map/ppermute | solution.py:19
  203.8 5.7 %collective-permute-start.25 = (f32[192,256]{1,0:T(8,128)S(1)}, f32[192,256]{1,0:T(8,128)S(1)}, u32[]{:S(2)}, u32[]{:S(2)}) collective-permute-start(f32[192,256]{1,0:T(8,128)S(1)} %broadcast_select_fusion.1), channel_id=1, source_target_pairs={{0,2},{2,0},{1,3},{3,1},{4,6},{6,4},{5,7},{7,5},{8,10},{10,8},{9,1... | collective-permute-start | bytes 589832 | tf_op jit(solution)/shard_map/ppermute | solution.py:19
  205.3 7.2 %collective-permute-start.35 = (f32[256,256]{1,0:T(8,128)S(1)}, f32[256,256]{1,0:T(8,128)S(1)}, u32[]{:S(2)}, u32[]{:S(2)}) collective-permute-start(f32[256,256]{1,0:T(8,128)S(1)} %pad_maximum_fusion.4), channel_id=1, source_target_pairs={{0,1},{1,0},{2,3},{3,2},{4,5},{5,4},{6,7},{7,6},{8,9},{9,8},{10,11... | collective-permute-start | bytes 786440 | tf_op jit(solution)/shard_map/ppermute | solution.py:19
  210.8 5.7 %collective-permute-start.12 = (f32[192,256]{1,0:T(8,128)S(1)}, f32[192,256]{1,0:T(8,128)S(1)}, u32[]{:S(2)}, u32[]{:S(2)}) collective-permute-start(f32[192,256]{1,0:T(8,128)S(1)} %select_bitcast_fusion), channel_id=1, source_target_pairs={{0,2},{2,0},{1,3},{3,1},{4,6},{6,4},{5,7},{7,5},{8,10},{10,8},{9,1... | collective-permute-start | bytes 589832 | tf_op jit(solution)/shard_map/ppermute | solution.py:19
  (24 other events, 52.3 us)
Sparse Core Ops, SparseCore 0:
  17.2 31.2 all-gather.2
  106.0 23.9 all-gather.4
  153.5 28.4 reduce-scatter.1

commit v4 on v2

--- a/solution.py
+++ b/solution.py
@@ -79,48 +79,89 @@
     return f(ah, bh) + (f(ah, bl) + f(al, bh))
 
 
+def later(xs, after):
+    anywhere = pl.BlockSpec(memory_space=pl.ANY)
+    return pl.pallas_call(
+        lambda *refs: None,
+        in_specs=[anywhere] * (len(xs) + 1),
+        out_specs=[anywhere] * len(xs),
+        out_shape=[jax.ShapeDtypeStruct(x.shape, x.dtype) for x in xs],
+        input_output_aliases={i: i for i in range(len(xs))},
+        cost_estimate=pl.CostEstimate(flops=0, bytes_accessed=0, transcendentals=0),
+    )(*xs, after)
+
+
 def product_kernel(place_ref, a_ref, *refs):
-    pieces, (keep_ref, give_ref, high, low) = refs[:8], refs[8:]
-    piece = pieces[0].shape[0]
-
-    @pl.when(pl.program_id(0) == 0)
-    def _():
-        for j in range(8):
-            rows = pl.ds(pl.multiple_of(place_ref[j] * piece, BS), piece)
-            xh, xl = halves(pieces[j][...])
-            high[rows, :] = xh
-            low[rows, :] = xl
-
-    ah, al = halves(a_ref[...])
+    pieces, (keep_ref, give_ref) = refs[:8], refs[-10:-8]
+    rows_in, a_in, high, low, kept, given, sems, outs = refs[-8:]
+    blocks = kept.shape[0]
+    piece = kept.shape[1]
+
+    def block_copy(i):
+        return pltpu.make_async_copy(a_ref.at[pl.ds(i * 2 * piece, 2 * piece)], a_in.at[i], sems.at[8 + i])
+
+    copies = [pltpu.make_async_copy(pieces[j], rows_in.at[j], sems.at[j]) for j in range(8)]
+    for c in copies:
+        c.start()
+    for i in range(blocks):
+        block_copy(i).start()
+    for j, c in enumerate(copies):
+        c.wait()
+        rows = pl.ds(pl.multiple_of(place_ref[j] * piece, BS), piece)
+        xh, xl = halves(rows_in[j])
+        high[rows, :] = xh
+        low[rows, :] = xl
+    lower = place_ref[8] == 0
     f = lambda p, q: jnp.dot(p, q, preferred_element_type=F32)
-    out = f(ah, high[...]) + (f(ah, low[...]) + f(al, high[...]))
-    first, second = out[:piece], out[piece:]
-    lower = place_ref[8] == 0
-    keep_ref[0] = jnp.where(lower, first, second)
-    give_ref[0] = jnp.where(lower, second, first)
-
-
-def product(a, pieces, places):
+
+    def out_copies(i):
+        return (
+            pltpu.make_async_copy(kept.at[i], keep_ref.at[i], outs.at[0, i]),
+            pltpu.make_async_copy(given.at[i], give_ref.at[i], outs.at[1, i]),
+        )
+
+    def body(i, _):
+        block_copy(i).wait()
+        ah, al = halves(a_in[i])
+        out = f(ah, high[...]) + (f(ah, low[...]) + f(al, high[...]))
+        first, second = out[:piece], out[piece:]
+        kept[i] = jnp.where(lower, first, second)
+        given[i] = jnp.where(lower, second, first)
+        for c in out_copies(i):
+            c.start()
+        return 0
+
+    lax.fori_loop(0, blocks, body, 0)
+    for i in range(blocks):
+        for c in out_copies(i):
+            c.wait()
+
+
+def product(a, pieces, places, after=()):
     rows, cols = a.shape
     piece, width = pieces[0].shape
     blocks = rows // (2 * piece)
-    whole = pl.BlockSpec((piece, width), lambda i, p: (0, 0))
-    out = pl.BlockSpec((1, piece, width), lambda i, p: (i, 0, 0))
+    anywhere = pl.BlockSpec(memory_space=pl.ANY)
     return pl.pallas_call(
         product_kernel,
-        grid_spec=pltpu.PrefetchScalarGridSpec(
-            num_scalar_prefetch=1,
-            grid=(blocks,),
-            in_specs=[pl.BlockSpec((2 * piece, cols), lambda i, p: (i, 0))] + [whole] * 8,
-            out_specs=[out, out],
-            scratch_shapes=[pltpu.VMEM((cols, width), BF)] * 2,
-        ),
+        in_specs=[pl.BlockSpec(memory_space=pltpu.SMEM)] + [anywhere] * (9 + len(after)),
+        out_specs=[anywhere] * 2,
+        scratch_shapes=[
+            pltpu.VMEM((8, piece, width), F32),
+            pltpu.VMEM((blocks, 2 * piece, cols), F32),
+            pltpu.VMEM((cols, width), BF),
+            pltpu.VMEM((cols, width), BF),
+            pltpu.VMEM((blocks, piece, width), F32),
+            pltpu.VMEM((blocks, piece, width), F32),
+            pltpu.SemaphoreType.DMA((8 + blocks,)),
+            pltpu.SemaphoreType.DMA((2, blocks)),
+        ],
         out_shape=[jax.ShapeDtypeStruct((blocks, piece, width), F32)] * 2,
-        compiler_params=pltpu.CompilerParams(vmem_limit_bytes=40 << 20),
+        compiler_params=pltpu.CompilerParams(vmem_limit_bytes=48 << 20),
         cost_estimate=pl.CostEstimate(
             flops=6 * rows * cols * width, bytes_accessed=4 * (rows * cols + (rows + cols) * width), transcendentals=0
         ),
-    )(places, a, *pieces)
+    )(places, a, *pieces, *after)
 
 
 def add_kernel(keep_ref, got_ref, x_ref, sum_ref, update_ref):
@@ -149,14 +190,15 @@
     )(keep, got, x)
 
 
-def gather_column(mine):
-    pair = swap(mine, "xh")
+def near_pieces(mine):
+    return swap(mine, "xh"), send(mine, "y", 4, lambda i: i ^ 1), send(mine, "y", 4, lambda i: i ^ 3)
+
+
+def gather_column(mine, pair, mine1, mine3):
     one, three = (lambda i: i ^ 1), (lambda i: i ^ 3)
-    mine1 = send(mine, "y", 4, one)
-    mine3 = send(mine, "y", 4, three)
     pair3 = send(pair, "y", 4, three)
+    pair1 = send(pair, "y", 4, one)
     mine2 = send(mine1, "y", 4, three)
-    pair1 = send(pair, "y", 4, one)
     pair2 = send(pair3, "y", 4, one)
     return [mine, pair, mine1, pair1, mine2, pair2, mine3, pair3]
 
@@ -175,10 +217,15 @@
     pair = jnp.stack([jnp.where(xl == 0, normed[1], near), jnp.where(xl == 0, near, normed[1])])
     band = lax.all_gather(pair, "z", axis=0, tiled=True)
 
-    panels, updates = [], []
+    mine = [lax.ppermute(n, ALL, transpose_pairs()) for n in normed]
+    panels = []
     for snode in range(NS):
-        mine = lax.ppermute(normed[snode], ALL, transpose_pairs())
-        keep, give = product(ancestor_inverse, gather_column(mine), places)
+        near = near_pieces(mine[snode])
+        if snode == 0:
+            after = (mine[1],)
+        else:
+            near, after = later(near, keep), ()
+        keep, give = product(ancestor_inverse, gather_column(mine[snode], *near), places, after)
         got = swap(give, "k")
         if snode == 0:
             summed = keep + got

time: 185 us -> 192 us (1.038)
  starting transfers between devices: 69.2 us -> 54.9 us
  waiting for transfers between devices: 56.6 us -> 68.1 us
  Pallas kernels: 29.9 us -> 36.6 us
  local copies, waits for them, and re-layouts: 4.59 us -> 8.05 us
    ppermute x32, starting transfers between devices: 67.7 us -> 53.4 us  [send(): return lax.ppermute(x, axis, [(i, to(i)) for i in range(size)])]
    ppermute x32, waiting for transfers between devices: 56.5 us -> 68 us  [send(): return lax.ppermute(x, axis, [(i, to(i)) for i in range(size)])]
    pallas_call x2 -> x3, Pallas kernels: 26.7 us -> 33.3 us  [the longest x2 33.3 us: product(): pl.pallas_call(product_kernel, in_specs=[pl.BlockSpec(memory_space=pltpu....]
    unnamed x18 -> x32, local copies, waits for them, and re-layouts: 1.47 us -> 4.93 us
  transfers between devices with their start and end apart: 37 -> 37, of which waited for: 23 -> 22; matrix products, arithmetic and copies ran while one was open for 5% -> 4% of each run, Pallas kernels for 16% -> 19%
where the time goes in v4:
time: 192 us; the launch traced here: 190 us
  waiting for transfers between devices  68.1 us (35%)
  starting transfers between devices  54.9 us (29%)
  Pallas kernels  36.6 us (19%)
  between operations  14.1 us (7%)
  local copies, waits for them, and re-layouts  8.05 us (4%)
  other arithmetic  4.31 us (2%)
  matrix products  4.24 us (2%)
    ppermute x32, waiting for transfers between devices, send(): return lax.ppermute(x, axis, [(i, to(i)) for i in range(size)])  68 us
    ppermute x32, starting transfers between devices, send(): return lax.ppermute(x, axis, [(i, to(i)) for i in range(size)])  53.4 us
    pallas_call x2, Pallas kernels, product(): pl.pallas_call(product_kernel, in_specs=[pl.BlockSpec(memory_space=pltpu....  33.3 us
    unnamed x32, local copies, waits for them, and re-layouts  4.93 us
  transfers between devices with their start and end apart: 37, of which 22 were waited for; matrix products, arithmetic and copies ran while one was open for 4% of the time, Pallas kernels for 19%

profile of v4, /device:TPU:0, one launch (start us, length us, event | category | flops | bytes accessed | tf_op | source)
XLA Modules:
  0.0 190.3 jit_solution(9639827591096349429)
XLA Ops:
  7.2 0.8 fusion.25
  8.2 1.4 convolution_multiply_fusion.1
  10.5 10.9 %collective-permute-start.1 = (f32[192,256]{1,0:T(8,128)S(1)}, f32[192,256]{1,0:T(8,128)S(1)}, u32[]{:S(2)}, u32[]{:S(2)}) collective-permute-start(f32[192,256]{1,0:T(8,128)S(1)} %collective-permute-done.refs_0_), channel_id=1, source_target_pairs={{0,16},{16,0},{1,17},{17,1},{2,18},{18,2},{3,19},{19,3},{4,20},{20... | collective-permute-start | bytes 589832 | tf_op jit(solution)/shard_map/ppermute | solution.py:18
  21.3 1.4 convolution_multiply_fusion
  23.5 6.5 %collective-permute-start.2 = (f32[192,256]{1,0:T(8,128)S(1)}, f32[192,256]{1,0:T(8,128)S(1)}, u32[]{:S(2)}, u32[]{:S(2)}) collective-permute-start(f32[192,256]{1,0:T(8,128)S(1)} %collective-permute-done.refs_0_), channel_id=1, source_target_pairs={{0,32},{32,0},{64,96},{96,64},{1,33},{33,1},{65,97},{97,65},{2,34}... | collective-permute-start | bytes 589832 | tf_op jit(solution)/shard_map/ppermute | solution.py:18
  30.0 9.0 %collective-permute-start.7 = (f32[192,256]{1,0:T(8,128)S(1)}, f32[192,256]{1,0:T(8,128)S(1)}, u32[]{:S(2)}, u32[]{:S(2)}) collective-permute-start(f32[192,256]{1,0:T(8,128)S(1)} %collective-permute-done.refs_0_), channel_id=1, source_target_pairs={{0,96},{32,64},{64,32},{96,0},{1,97},{33,65},{65,33},{97,1},{2,98}... | collective-permute-start | bytes 589832 | tf_op jit(solution)/shard_map/ppermute | solution.py:18
  39.3 7.8 %collective-permute-start.4 = (f32[192,256]{1,0:T(8,128)S(1)}, f32[192,256]{1,0:T(8,128)S(1)}, u32[]{:S(2)}, u32[]{:S(2)}) collective-permute-start(f32[192,256]{1,0:T(8,128)S(1)} %collective-permute-done.2.refs_2_), channel_id=1, source_target_pairs={{0,96},{32,64},{64,32},{96,0},{1,97},{33,65},{65,33},{97,1},{2,98}... | collective-permute-start | bytes 589832 | tf_op jit(solution)/shard_map/ppermute | solution.py:18
  47.1 5.9 %collective-permute-done.5.refs_7_ = f32[192,256]{1,0:T(8,128)S(1)} collective-permute-done((f32[192,256]{1,0:T(8,128)S(1)}, f32[192,256]{1,0:T(8,128)S(1)}, u32[]{:S(2)}, u32[]{:S(2)}) %collective-permute-start.5) | collective-permute-done | bytes 196640 | tf_op jit(solution)/shard_map/ppermute | solution.py:18
  53.0 0.8 pad_maximum_fusion.1
  54.0 2.1 %collective-permute-done.4.refs_4_ = f32[192,256]{1,0:T(8,128)S(1)} collective-permute-done((f32[192,256]{1,0:T(8,128)S(1)}, f32[192,256]{1,0:T(8,128)S(1)}, u32[]{:S(2)}, u32[]{:S(2)}) %collective-permute-start.4) | collective-permute-done | bytes 196640 | tf_op jit(solution)/shard_map/ppermute | solution.py:18
  56.0 2.7 %collective-permute-done.6.refs_5_ = f32[192,256]{1,0:T(8,128)S(1)} collective-permute-done((f32[192,256]{1,0:T(8,128)S(1)}, f32[192,256]{1,0:T(8,128)S(1)}, u32[]{:S(2)}, u32[]{:S(2)}) %collective-permute-start.6) | collective-permute-done | bytes 196640 | tf_op jit(solution)/shard_map/ppermute | solution.py:18
  58.7 17.4 %shard_map.68 = (f32[8,192,256]{2,1,0:T(8,128)S(1)}, f32[8,192,256]{2,1,0:T(8,128)S(1)}) custom-call(s32[9]{0:T(128)S(1)} %pad_add_fusion.place_ref, f32[3072,1536]{1,0:T(8,128)} %a_ref.3, f32[192,256]{1,0:T(8,128)S(1)} %collective-permute-done.refs_0_, f32[192,256]{1,0:T(8,128)S(1)} %collective-permute-done.1.refs_1_, ...), custom_call_target="tpu_custom_call" | custom-call | flops 7247757312 | bytes 23592960 | tf_op jit(solution)/shard_map/pallas_call | solution.py:145
  76.2 3.4 %collective-permute-done.9 = f32[8,192,256]{2,1,0:T(8,128)S(1)} collective-permute-done((f32[8,192,256]{2,1,0:T(8,128)S(1)}, f32[8,192,256]{2,1,0:T(8,128)S(1)}, u32[]{:S(2)}, u32[]{:S(2)}) %collective-permute-start.9) | collective-permute-done | bytes 1572896 | tf_op jit(solution)/shard_map/ppermute | solution.py:18
  79.6 1.4 add.113
  81.1 3.1 %collective-permute-start.11 = (f32[192,256]{1,0:T(8,128)S(1)}, f32[192,256]{1,0:T(8,128)S(1)}, u32[]{:S(2)}, u32[]{:S(2)}) collective-permute-start(f32[192,256]{1,0:T(8,128)S(1)} %collective-permute-done.8.refs_8_.refs_0_), channel_id=1, source_target_pairs={{0,16},{16,0},{1,17},{17,1},{2,18},{18,2},{3,19},{19,3},{4,20},{20... | collective-permute-start | bytes 589832 | tf_op jit(solution)/shard_map/ppermute | solution.py:18
  84.2 5.4 %collective-permute-done.11.refs_0_ = f32[192,256]{1,0:T(8,128)S(1)} collective-permute-done((f32[192,256]{1,0:T(8,128)S(1)}, f32[192,256]{1,0:T(8,128)S(1)}, u32[]{:S(2)}, u32[]{:S(2)}) %collective-permute-start.11) | collective-permute-done | bytes 196640 | tf_op jit(solution)/shard_map/ppermute | solution.py:18
  89.6 1.3 collective-permute-done.12.refs_1_
  90.9 1.2 collective-permute-done.13.refs_2_
  93.6 2.4 %collective-permute-start.15 = (f32[192,256]{1,0:T(8,128)}, f32[192,256]{1,0:T(8,128)S(1)}, u32[]{:S(2)}, u32[]{:S(2)}) collective-permute-start(f32[192,256]{1,0:T(8,128)} %get-tuple-element.14.refs_2_), channel_id=1, source_target_pairs={{0,96},{32,64},{64,32},{96,0},{1,97},{33,65},{65,33},{97,1},{2,98}... | collective-permute-start | bytes 589832 | tf_op jit(solution)/shard_map/ppermute | solution.py:18
  96.0 6.0 %collective-permute-done.16.refs_7_ = f32[192,256]{1,0:T(8,128)S(1)} collective-permute-done((f32[192,256]{1,0:T(8,128)}, f32[192,256]{1,0:T(8,128)S(1)}, u32[]{:S(2)}, u32[]{:S(2)}) %collective-permute-start.16) | collective-permute-done | bytes 196640 | tf_op jit(solution)/shard_map/ppermute | solution.py:18
  102.0 2.2 %collective-permute-done.15.refs_4_ = f32[192,256]{1,0:T(8,128)S(1)} collective-permute-done((f32[192,256]{1,0:T(8,128)}, f32[192,256]{1,0:T(8,128)S(1)}, u32[]{:S(2)}, u32[]{:S(2)}) %collective-permute-start.15) | collective-permute-done | bytes 196640 | tf_op jit(solution)/shard_map/ppermute | solution.py:18
  104.2 3.5 %collective-permute-done.17.refs_5_ = f32[192,256]{1,0:T(8,128)S(1)} collective-permute-done((f32[192,256]{1,0:T(8,128)S(1)}, f32[192,256]{1,0:T(8,128)S(1)}, u32[]{:S(2)}, u32[]{:S(2)}) %collective-permute-start.17) | collective-permute-done | bytes 196640 | tf_op jit(solution)/shard_map/ppermute | solution.py:18
  107.7 0.9 copy-done.3
  108.6 0.9 copy-done.5
  109.6 0.9 copy-done.7
  110.5 15.9 %shard_map.70 = (f32[8,192,256]{2,1,0:T(8,128)S(1)}, f32[8,192,256]{2,1,0:T(8,128)}) custom-call(s32[9]{0:T(128)S(1)} %pad_add_fusion.place_ref, f32[3072,1536]{1,0:T(8,128)} %a_ref.3, f32[192,256]{1,0:T(8,128)S(1)} %collective-permute-done.8.refs_8_.refs_0_, f32[192,256]{1,0:T(8,128)S(1)} %copy-done.3, f32[192,256]{1,0:T(8,128)S(1)} %copy-done.5, ...), custom_call_target="tpu_custom_call" | custom-call | flops 7247757312 | bytes 23592960 | tf_op jit(solution)/shard_map/pallas_call | solution.py:145
  126.5 3.6 %collective-permute-done.18.got_ref = f32[8,192,256]{2,1,0:T(8,128)S(1)} collective-permute-done((f32[8,192,256]{2,1,0:T(8,128)}, f32[8,192,256]{2,1,0:T(8,128)S(1)}, u32[]{:S(2)}, u32[]{:S(2)}) %collective-permute-start.18) | collective-permute-done | bytes 1572896 | tf_op jit(solution)/shard_map/ppermute | solution.py:18
  130.1 1.4 copy-done.1
  131.5 3.3 %shard_map.71 = (f32[8,192,256]{2,1,0:T(8,128)}, f32[256,256]{1,0:T(8,128)S(1)}) custom-call(f32[8,192,256]{2,1,0:T(8,128)S(1)} %get-tuple-element.16.keep_ref, f32[8,192,256]{2,1,0:T(8,128)S(1)} %collective-permute-done.18.got_ref, f32[8,192,256]{2,1,0:T(8,128)S(1)} %copy-done.1), custom_call_target="tpu_custom_call" | custom-call | flops 603979776 | bytes 6291456 | tf_op jit(solution)/shard_map/pallas_call | solution.py:180
  134.9 1.0 dynamic-slice_bitcast_fusion.1
  136.1 6.8 %collective-permute-done.10 = f32[192,256]{1,0:T(8,128)S(1)} collective-permute-done((f32[192,256]{1,0:T(8,128)S(1)}, f32[192,256]{1,0:T(8,128)S(1)}, u32[]{:S(2)}, u32[]{:S(2)}) %collective-permute-start.10) | collective-permute-done | bytes 196640 | tf_op jit(solution)/shard_map/ppermute | solution.py:18
  142.9 1.5 broadcast_select_fusion
  144.5 1.5 collective-permute-done.21
  146.2 1.7 collective-permute-start.23
  147.9 1.5 collective-permute-start.24
  149.4 3.5 %collective-permute-done.22 = f32[64,256]{1,0:T(8,128)S(1)} collective-permute-done((f32[64,256]{1,0:T(8,128)S(1)}, f32[64,256]{1,0:T(8,128)S(1)}, u32[]{:S(2)}, u32[]{:S(2)}) %collective-permute-start.22) | collective-permute-done | bytes 65568 | tf_op jit(solution)/shard_map/ppermute | solution.py:18
  153.8 3.0 %collective-permute-start.27 = (f32[64,256]{1,0:T(8,128)S(1)}, f32[64,256]{1,0:T(8,128)S(1)}, u32[]{:S(2)}, u32[]{:S(2)}) collective-permute-start(f32[64,256]{1,0:T(8,128)S(1)} %add_add_fusion.1), channel_id=1, source_target_pairs={{0,12},{4,0},{8,4},{12,8},{1,13},{5,1},{9,5},{13,9},{2,14},{6,2},{... | collective-permute-start | bytes 196616 | tf_op jit(solution)/shard_map/ppermute | solution.py:18
  156.8 2.9 %collective-permute-done.25 = f32[64,256]{1,0:T(8,128)S(1)} collective-permute-done((f32[64,256]{1,0:T(8,128)S(1)}, f32[64,256]{1,0:T(8,128)S(1)}, u32[]{:S(2)}, u32[]{:S(2)}) %collective-permute-start.25) | collective-permute-done | bytes 65568 | tf_op jit(solution)/shard_map/ppermute | solution.py:18
  159.7 0.9 collective-permute-done.27
  161.0 4.0 %collective-permute-done.28 = f32[64,256]{1,0:T(8,128)S(1)} collective-permute-done((f32[64,256]{1,0:T(8,128)S(1)}, f32[64,256]{1,0:T(8,128)S(1)}, u32[]{:S(2)}, u32[]{:S(2)}) %collective-permute-start.28) | collective-permute-done | bytes 65568 | tf_op jit(solution)/shard_map/ppermute | solution.py:18
  165.0 1.3 collective-permute-start.29
  166.5 4.4 %collective-permute-done.29 = f32[64,256]{1,0:T(8,128)S(1)} collective-permute-done((f32[64,256]{1,0:T(8,128)S(1)}, f32[64,256]{1,0:T(8,128)S(1)}, u32[]{:S(2)}, u32[]{:S(2)}) %collective-permute-start.29) | collective-permute-done | bytes 65568 | tf_op jit(solution)/shard_map/ppermute | solution.py:18
  170.9 2.4 %collective-permute-start.30 = (f32[64,256]{1,0:T(8,128)S(1)}, f32[64,256]{1,0:T(8,128)S(1)}, u32[]{:S(2)}, u32[]{:S(2)}) collective-permute-start(f32[64,256]{1,0:T(8,128)S(1)} %add.133), channel_id=1, source_target_pairs={{0,96},{32,0},{64,32},{96,64},{1,97},{33,1},{65,33},{97,65},{2,98}... | collective-permute-start | bytes 196616 | tf_op jit(solution)/shard_map/ppermute | solution.py:18
  173.3 1.0 dynamic-slice_bitcast_fusion
  174.7 0.7 collective-permute-start.31
  175.6 4.9 %collective-permute-done.31 = f32[64,256]{1,0:T(8,128)S(1)} collective-permute-done((f32[64,256]{1,0:T(8,128)S(1)}, f32[64,256]{1,0:T(8,128)S(1)}, u32[]{:S(2)}, u32[]{:S(2)}) %collective-permute-start.31) | collective-permute-done | bytes 65568 | tf_op jit(solution)/shard_map/ppermute | solution.py:18
  181.5 0.8 pad_maximum_fusion.2
  182.9 0.8 pad_maximum_fusion
  (94 shorter events, 8.2 us)
Async XLA Ops:
  7.2 119.4 %all-gather.2.cloned.1.call-start = ((), (), s32[]{:S(2)}) async-start(), calls=%async_computation.3 | async-start | bytes 1966080 | tf_op jit(solution)/shard_map/all_gather | solution.py:218
  9.6 13.1 %copy-start.9 = (f32[192,256]{1,0:T(8,128)}, f32[192,256]{1,0:T(8,128)S(1)}, u32[]{:S(2)}) copy-start(f32[192,256]{1,0:T(8,128)S(1)} %convolution_multiply_fusion.1) | copy-start | bytes 589828
  9.6 0.8 collective-permute-start
  10.5 28.6 %collective-permute-start.1 = (f32[192,256]{1,0:T(8,128)S(1)}, f32[192,256]{1,0:T(8,128)S(1)}, u32[]{:S(2)}, u32[]{:S(2)}) collective-permute-start(f32[192,256]{1,0:T(8,128)S(1)} %collective-permute-done.refs_0_), channel_id=1, source_target_pairs={{0,16},{16,0},{1,17},{17,1},{2,18},{18,2},{3,19},{19,3},{4,20},{20... | collective-permute-start | bytes 589832 | tf_op jit(solution)/shard_map/ppermute | solution.py:18
  22.7 16.3 %collective-permute-start.19 = (f32[192,256]{1,0:T(8,128)S(1)}, f32[192,256]{1,0:T(8,128)S(1)}, u32[]{:S(2)}, u32[]{:S(2)}) collective-permute-start(f32[192,256]{1,0:T(8,128)S(1)} %convolution_multiply_fusion), channel_id=1, source_target_pairs={{0,2},{2,0},{1,3},{3,1},{4,6},{6,4},{5,7},{7,5},{8,10},{10,8},{9,1... | collective-permute-start | bytes 589832 | tf_op jit(solution)/shard_map/ppermute | solution.py:18
  22.8 31.1 %collective-permute-start.8 = (f32[192,256]{1,0:T(8,128)S(1)}, f32[192,256]{1,0:T(8,128)S(1)}, u32[]{:S(2)}, u32[]{:S(2)}) collective-permute-start(f32[192,256]{1,0:T(8,128)S(1)} %convolution_multiply_fusion), channel_id=1, source_target_pairs={{0,0},{8,1},{16,2},{24,3},{32,4},{40,5},{48,6},{56,7},{64,8},{72,9... | collective-permute-start | bytes 589832 | tf_op jit(solution)/shard_map/ppermute | solution.py:220
  23.5 15.8 %collective-permute-start.2 = (f32[192,256]{1,0:T(8,128)S(1)}, f32[192,256]{1,0:T(8,128)S(1)}, u32[]{:S(2)}, u32[]{:S(2)}) collective-permute-start(f32[192,256]{1,0:T(8,128)S(1)} %collective-permute-done.refs_0_), channel_id=1, source_target_pairs={{0,32},{32,0},{64,96},{96,64},{1,33},{33,1},{65,97},{97,65},{2,34}... | collective-permute-start | bytes 589832 | tf_op jit(solution)/shard_map/ppermute | solution.py:18
  30.0 23.9 %collective-permute-start.7 = (f32[192,256]{1,0:T(8,128)S(1)}, f32[192,256]{1,0:T(8,128)S(1)}, u32[]{:S(2)}, u32[]{:S(2)}) collective-permute-start(f32[192,256]{1,0:T(8,128)S(1)} %collective-permute-done.refs_0_), channel_id=1, source_target_pairs={{0,96},{32,64},{64,32},{96,0},{1,97},{33,65},{65,33},{97,1},{2,98}... | collective-permute-start | bytes 589832 | tf_op jit(solution)/shard_map/ppermute | solution.py:18
  39.0 14.0 %collective-permute-start.5 = (f32[192,256]{1,0:T(8,128)S(1)}, f32[192,256]{1,0:T(8,128)S(1)}, u32[]{:S(2)}, u32[]{:S(2)}) collective-permute-start(f32[192,256]{1,0:T(8,128)S(1)} %collective-permute-done.1.refs_1_), channel_id=1, source_target_pairs={{0,96},{32,64},{64,32},{96,0},{1,97},{33,65},{65,33},{97,1},{2,98}... | collective-permute-start | bytes 589832 | tf_op jit(solution)/shard_map/ppermute | solution.py:18
  39.1 14.9 %collective-permute-start.3 = (f32[192,256]{1,0:T(8,128)S(1)}, f32[192,256]{1,0:T(8,128)S(1)}, u32[]{:S(2)}, u32[]{:S(2)}) collective-permute-start(f32[192,256]{1,0:T(8,128)S(1)} %collective-permute-done.1.refs_1_), channel_id=1, source_target_pairs={{0,32},{32,0},{64,96},{96,64},{1,33},{33,1},{65,97},{97,65},{2,34}... | collective-permute-start | bytes 589832 | tf_op jit(solution)/shard_map/ppermute | solution.py:18
  39.3 16.7 %collective-permute-start.4 = (f32[192,256]{1,0:T(8,128)S(1)}, f32[192,256]{1,0:T(8,128)S(1)}, u32[]{:S(2)}, u32[]{:S(2)}) collective-permute-start(f32[192,256]{1,0:T(8,128)S(1)} %collective-permute-done.2.refs_2_), channel_id=1, source_target_pairs={{0,96},{32,64},{64,32},{96,0},{1,97},{33,65},{65,33},{97,1},{2,98}... | collective-permute-start | bytes 589832 | tf_op jit(solution)/shard_map/ppermute | solution.py:18
  53.0 5.7 %collective-permute-start.6 = (f32[192,256]{1,0:T(8,128)S(1)}, f32[192,256]{1,0:T(8,128)S(1)}, u32[]{:S(2)}, u32[]{:S(2)}) collective-permute-start(f32[192,256]{1,0:T(8,128)S(1)} %collective-permute-done.5.refs_7_), channel_id=1, source_target_pairs={{0,32},{32,0},{64,96},{96,64},{1,33},{33,1},{65,97},{97,65},{2,34}... | collective-permute-start | bytes 589832 | tf_op jit(solution)/shard_map/ppermute | solution.py:18
  53.8 81.0 %reduce-scatter.3.cloned.1.call-start = ((), (), s32[]{:S(2)}) async-start(), calls=%async_computation.2 | async-start | bytes 1966080 | tf_op jit(solution)/shard_map/reduce_scatter | solution.py:234
  76.1 4.9 %copy-start = (f32[8,192,256]{2,1,0:T(8,128)}, f32[8,192,256]{2,1,0:T(8,128)S(1)}, u32[]{:S(2)}) copy-start(f32[8,192,256]{2,1,0:T(8,128)S(1)} %get-tuple-element.11.refs_3_) | copy-start | bytes 4718596
  76.1 3.5 %collective-permute-start.9 = (f32[8,192,256]{2,1,0:T(8,128)S(1)}, f32[8,192,256]{2,1,0:T(8,128)S(1)}, u32[]{:S(2)}, u32[]{:S(2)}) collective-permute-start(f32[8,192,256]{2,1,0:T(8,128)S(1)} %get-tuple-element.12), channel_id=1, source_target_pairs={{0,1},{1,0},{2,3},{3,2},{4,5},{5,4},{6,7},{7,6},{8,9},{9,8},{10,11... | collective-permute-start | bytes 4718600 | tf_op jit(solution)/shard_map/ppermute | solution.py:18
  81.0 92.3 %reduce-scatter.5.cloned.1.call-start = ((), (), s32[]{:S(2)}) async-start(), calls=%async_computation.4 | async-start | bytes 1966080 | tf_op jit(solution)/shard_map/reduce_scatter | solution.py:234
  81.1 8.5 %collective-permute-start.11 = (f32[192,256]{1,0:T(8,128)S(1)}, f32[192,256]{1,0:T(8,128)S(1)}, u32[]{:S(2)}, u32[]{:S(2)}) collective-permute-start(f32[192,256]{1,0:T(8,128)S(1)} %collective-permute-done.8.refs_8_.refs_0_), channel_id=1, source_target_pairs={{0,16},{16,0},{1,17},{17,1},{2,18},{18,2},{3,19},{19,3},{4,20},{20... | collective-permute-start | bytes 589832 | tf_op jit(solution)/shard_map/ppermute | solution.py:18
  84.2 6.7 %collective-permute-start.12 = (f32[192,256]{1,0:T(8,128)S(1)}, f32[192,256]{1,0:T(8,128)S(1)}, u32[]{:S(2)}, u32[]{:S(2)}) collective-permute-start(f32[192,256]{1,0:T(8,128)S(1)} %collective-permute-done.8.refs_8_.refs_0_), channel_id=1, source_target_pairs={{0,32},{32,0},{64,96},{96,64},{1,33},{33,1},{65,97},{97,65},{2,34}... | collective-permute-start | bytes 589832 | tf_op jit(solution)/shard_map/ppermute | solution.py:18
  84.2 7.9 %collective-permute-start.13 = (f32[192,256]{1,0:T(8,128)S(1)}, f32[192,256]{1,0:T(8,128)S(1)}, u32[]{:S(2)}, u32[]{:S(2)}) collective-permute-start(f32[192,256]{1,0:T(8,128)S(1)} %collective-permute-done.8.refs_8_.refs_0_), channel_id=1, source_target_pairs={{0,96},{32,64},{64,32},{96,0},{1,97},{33,65},{65,33},{97,1},{2,98}... | collective-permute-start | bytes 589832 | tf_op jit(solution)/shard_map/ppermute | solution.py:18
  89.6 2.5 %copy-start.2 = (f32[192,256]{1,0:T(8,128)}, f32[192,256]{1,0:T(8,128)S(1)}, u32[]{:S(2)}) copy-start(f32[192,256]{1,0:T(8,128)S(1)} %collective-permute-done.11.refs_0_) | copy-start | bytes 589828
  90.9 1.2 copy-start.4
  92.8 9.3 %collective-permute-start.16 = (f32[192,256]{1,0:T(8,128)}, f32[192,256]{1,0:T(8,128)S(1)}, u32[]{:S(2)}, u32[]{:S(2)}) collective-permute-start(f32[192,256]{1,0:T(8,128)} %get-tuple-element.13.refs_1_), channel_id=1, source_target_pairs={{0,96},{32,64},{64,32},{96,0},{1,97},{33,65},{65,33},{97,1},{2,98}... | collective-permute-start | bytes 589832 | tf_op jit(solution)/shard_map/ppermute | solution.py:18
  93.0 9.0 %collective-permute-start.14 = (f32[192,256]{1,0:T(8,128)}, f32[192,256]{1,0:T(8,128)S(1)}, u32[]{:S(2)}, u32[]{:S(2)}) collective-permute-start(f32[192,256]{1,0:T(8,128)} %get-tuple-element.13.refs_1_), channel_id=1, source_target_pairs={{0,32},{32,0},{64,96},{96,64},{1,33},{33,1},{65,97},{97,65},{2,34}... | collective-permute-start | bytes 589832 | tf_op jit(solution)/shard_map/ppermute | solution.py:18
  93.6 10.6 %collective-permute-start.15 = (f32[192,256]{1,0:T(8,128)}, f32[192,256]{1,0:T(8,128)S(1)}, u32[]{:S(2)}, u32[]{:S(2)}) collective-permute-start(f32[192,256]{1,0:T(8,128)} %get-tuple-element.14.refs_2_), channel_id=1, source_target_pairs={{0,96},{32,64},{64,32},{96,0},{1,97},{33,65},{65,33},{97,1},{2,98}... | collective-permute-start | bytes 589832 | tf_op jit(solution)/shard_map/ppermute | solution.py:18
  102.0 5.7 %collective-permute-start.17 = (f32[192,256]{1,0:T(8,128)S(1)}, f32[192,256]{1,0:T(8,128)S(1)}, u32[]{:S(2)}, u32[]{:S(2)}) collective-permute-start(f32[192,256]{1,0:T(8,128)S(1)} %collective-permute-done.16.refs_7_), channel_id=1, source_target_pairs={{0,32},{32,0},{64,96},{96,64},{1,33},{33,1},{65,97},{97,65},{2,34}... | collective-permute-start | bytes 589832 | tf_op jit(solution)/shard_map/ppermute | solution.py:18
  107.7 0.9 copy-start.3
  108.6 0.9 copy-start.5
  126.4 3.7 %collective-permute-start.18 = (f32[8,192,256]{2,1,0:T(8,128)}, f32[8,192,256]{2,1,0:T(8,128)S(1)}, u32[]{:S(2)}, u32[]{:S(2)}) collective-permute-start(f32[8,192,256]{2,1,0:T(8,128)} %get-tuple-element.17), channel_id=1, source_target_pairs={{0,1},{1,0},{2,3},{3,2},{4,5},{5,4},{6,7},{7,6},{8,9},{9,8},{10,11... | collective-permute-start | bytes 4718600 | tf_op jit(solution)/shard_map/ppermute | solution.py:18
  130.1 1.4 copy-start.1
  134.8 8.1 %copy-start.10 = (f32[192,256]{1,0:T(8,128)S(1)}, f32[192,256]{1,0:T(8,128)}, u32[]{:S(2)}) copy-start(f32[192,256]{1,0:T(8,128)} %copy-done.9) | copy-start | bytes 589828
  135.9 7.0 %collective-permute-start.10 = (f32[192,256]{1,0:T(8,128)S(1)}, f32[192,256]{1,0:T(8,128)S(1)}, u32[]{:S(2)}, u32[]{:S(2)}) collective-permute-start(f32[192,256]{1,0:T(8,128)S(1)} %dynamic-slice_bitcast_fusion.1), channel_id=1, source_target_pairs={{0,2},{2,0},{1,3},{3,1},{4,6},{6,4},{5,7},{7,5},{8,10},{10,8},{9,1... | collective-permute-start | bytes 589832 | tf_op jit(solution)/shard_map/ppermute | solution.py:18
  142.9 23.5 %copy-start.8 = (f32[1,2,192,256]{3,2,1,0:T(8,128)S(1)}, f32[1,2,192,256]{3,2,1,0:T(8,128)}, u32[]{:S(2)}) copy-start(f32[1,2,192,256]{3,2,1,0:T(8,128)} %reduce-scatter.3.cloned.1.call-done) | copy-start | bytes 1179652
  144.4 1.6 collective-permute-start.21
  146.1 6.8 %collective-permute-start.22 = (f32[64,256]{1,0:T(8,128)S(1)}, f32[64,256]{1,0:T(8,128)S(1)}, u32[]{:S(2)}, u32[]{:S(2)}) collective-permute-start(f32[64,256]{1,0:T(8,128)S(1)} %get-tuple-element.24), channel_id=1, source_target_pairs={{0,32},{32,64},{64,96},{96,0},{1,33},{33,65},{65,97},{97,1},{2,34}... | collective-permute-start | bytes 196616 | tf_op jit(solution)/shard_map/ppermute | solution.py:18
  146.2 6.7 %collective-permute-start.23 = (f32[64,256]{1,0:T(8,128)S(1)}, f32[64,256]{1,0:T(8,128)S(1)}, u32[]{:S(2)}, u32[]{:S(2)}) collective-permute-start(f32[64,256]{1,0:T(8,128)S(1)} %get-tuple-element.26), channel_id=1, source_target_pairs={{0,64},{32,96},{64,0},{96,32},{1,65},{33,97},{65,1},{97,33},{2,66}... | collective-permute-start | bytes 196616 | tf_op jit(solution)/shard_map/ppermute | solution.py:18
  147.9 5.6 %collective-permute-start.24 = (f32[64,256]{1,0:T(8,128)S(1)}, f32[64,256]{1,0:T(8,128)S(1)}, u32[]{:S(2)}, u32[]{:S(2)}) collective-permute-start(f32[64,256]{1,0:T(8,128)S(1)} %get-tuple-element.25), channel_id=1, source_target_pairs={{0,96},{32,0},{64,32},{96,64},{1,97},{33,1},{65,33},{97,65},{2,98}... | collective-permute-start | bytes 196616 | tf_op jit(solution)/shard_map/ppermute | solution.py:18
  153.5 6.2 %collective-permute-start.25 = (f32[64,256]{1,0:T(8,128)S(1)}, f32[64,256]{1,0:T(8,128)S(1)}, u32[]{:S(2)}, u32[]{:S(2)}) collective-permute-start(f32[64,256]{1,0:T(8,128)S(1)} %add_add_fusion.1), channel_id=1, source_target_pairs={{0,4},{4,8},{8,12},{12,0},{1,5},{5,9},{9,13},{13,1},{2,6},{6,10},{... | collective-permute-start | bytes 196616 | tf_op jit(solution)/shard_map/ppermute | solution.py:18
  153.6 6.2 %collective-permute-start.26 = (f32[64,256]{1,0:T(8,128)S(1)}, f32[64,256]{1,0:T(8,128)S(1)}, u32[]{:S(2)}, u32[]{:S(2)}) collective-permute-start(f32[64,256]{1,0:T(8,128)S(1)} %add_add_fusion.1), channel_id=1, source_target_pairs={{0,8},{4,12},{8,0},{12,4},{1,9},{5,13},{9,1},{13,5},{2,10},{6,14},... | collective-permute-start | bytes 196616 | tf_op jit(solution)/shard_map/ppermute | solution.py:18
  153.8 6.7 %collective-permute-start.27 = (f32[64,256]{1,0:T(8,128)S(1)}, f32[64,256]{1,0:T(8,128)S(1)}, u32[]{:S(2)}, u32[]{:S(2)}) collective-permute-start(f32[64,256]{1,0:T(8,128)S(1)} %add_add_fusion.1), channel_id=1, source_target_pairs={{0,12},{4,0},{8,4},{12,8},{1,13},{5,1},{9,5},{13,9},{2,14},{6,2},{... | collective-permute-start | bytes 196616 | tf_op jit(solution)/shard_map/ppermute | solution.py:18
  160.6 4.4 %collective-permute-start.28 = (f32[64,256]{1,0:T(8,128)S(1)}, f32[64,256]{1,0:T(8,128)S(1)}, u32[]{:S(2)}, u32[]{:S(2)}) collective-permute-start(f32[64,256]{1,0:T(8,128)S(1)} %add_add_fusion), channel_id=1, source_target_pairs={{0,2},{2,0},{1,3},{3,1},{4,6},{6,4},{5,7},{7,5},{8,10},{10,8},{9,1... | collective-permute-start | bytes 196616 | tf_op jit(solution)/shard_map/ppermute | solution.py:18
  165.0 5.8 %collective-permute-start.29 = (f32[64,256]{1,0:T(8,128)S(1)}, f32[64,256]{1,0:T(8,128)S(1)}, u32[]{:S(2)}, u32[]{:S(2)}) collective-permute-start(f32[64,256]{1,0:T(8,128)S(1)} %add.132), channel_id=1, source_target_pairs={{0,16},{16,0},{1,17},{17,1},{2,18},{18,2},{3,19},{19,3},{4,20},{20... | collective-permute-start | bytes 196616 | tf_op jit(solution)/shard_map/ppermute | solution.py:18
  170.9 12.0 %copy-start.11 = (f32[2,256,256]{2,1,0:T(8,128)S(1)}, f32[2,256,256]{2,1,0:T(8,128)}, u32[]{:S(2)}) copy-start(f32[2,256,256]{2,1,0:T(8,128)} %param.8) | copy-start | bytes 1572868
  170.9 4.7 %collective-permute-start.30 = (f32[64,256]{1,0:T(8,128)S(1)}, f32[64,256]{1,0:T(8,128)S(1)}, u32[]{:S(2)}, u32[]{:S(2)}) collective-permute-start(f32[64,256]{1,0:T(8,128)S(1)} %add.133), channel_id=1, source_target_pairs={{0,96},{32,0},{64,32},{96,64},{1,97},{33,1},{65,33},{97,65},{2,98}... | collective-permute-start | bytes 196616 | tf_op jit(solution)/shard_map/ppermute | solution.py:18
  173.3 8.1 %copy-start.12 = (f32[1,2,192,256]{3,2,1,0:T(8,128)S(1)}, f32[1,2,192,256]{3,2,1,0:T(8,128)}, u32[]{:S(2)}) copy-start(f32[1,2,192,256]{3,2,1,0:T(8,128)} %reduce-scatter.5.cloned.1.call-done) | copy-start | bytes 1179652
  174.3 7.0 %collective-permute-start.20 = (f32[192,256]{1,0:T(8,128)S(1)}, f32[192,256]{1,0:T(8,128)S(1)}, u32[]{:S(2)}, u32[]{:S(2)}) collective-permute-start(f32[192,256]{1,0:T(8,128)S(1)} %dynamic-slice_bitcast_fusion), channel_id=1, source_target_pairs={{0,2},{2,0},{1,3},{3,1},{4,6},{6,4},{5,7},{7,5},{8,10},{10,8},{9,1... | collective-permute-start | bytes 589832 | tf_op jit(solution)/shard_map/ppermute | solution.py:18
  174.7 5.8 %collective-permute-start.31 = (f32[64,256]{1,0:T(8,128)S(1)}, f32[64,256]{1,0:T(8,128)S(1)}, u32[]{:S(2)}, u32[]{:S(2)}) collective-permute-start(f32[64,256]{1,0:T(8,128)S(1)} %add.133), channel_id=1, source_target_pairs={{0,64},{32,96},{64,0},{96,32},{1,65},{33,97},{65,1},{97,33},{2,66}... | collective-permute-start | bytes 196616 | tf_op jit(solution)/shard_map/ppermute | solution.py:18
  175.4 5.8 %collective-permute-start.32 = (f32[64,256]{1,0:T(8,128)S(1)}, f32[64,256]{1,0:T(8,128)S(1)}, u32[]{:S(2)}, u32[]{:S(2)}) collective-permute-start(f32[64,256]{1,0:T(8,128)S(1)} %add.133), channel_id=1, source_target_pairs={{0,32},{32,64},{64,96},{96,0},{1,33},{33,65},{65,97},{97,1},{2,34}... | collective-permute-start | bytes 196616 | tf_op jit(solution)/shard_map/ppermute | solution.py:18
  181.2 1.6 collective-permute-start.33
  (2 other events, 1.6 us)
Sparse Core Ops, SparseCore 0:
  54.0 24.5 all-gather.1
  81.1 25.5 reduce-scatter.2
  135.0 20.7 reduce-scatter.4

commit v5 on v2

--- a/solution.py
+++ b/solution.py
@@ -104,7 +104,7 @@
     rows, cols = a.shape
     piece, width = pieces[0].shape
     blocks = rows // (2 * piece)
-    whole = pl.BlockSpec((piece, width), lambda i, p: (0, 0))
+    whole = pl.BlockSpec((piece, width), lambda i, p: (0, 0), pipeline_mode=pl.Buffered(1))
     out = pl.BlockSpec((1, piece, width), lambda i, p: (i, 0, 0))
     return pl.pallas_call(
         product_kernel,
@@ -123,30 +123,34 @@
     )(places, a, *pieces)
 
 
-def add_kernel(keep_ref, got_ref, x_ref, sum_ref, update_ref):
+def update_kernel(sum_ref, x_ref, first_ref, second_ref):
     @pl.when(pl.program_id(0) == 0)
     def _():
-        update_ref[...] = jnp.zeros_like(update_ref)
-
-    both = keep_ref[0] + got_ref[0]
-    sum_ref[0] = both
-    update_ref[...] += dot3(x_ref[0], both, ((0,), (0,)))
-
-
-def add_and_update(keep, got, x):
-    blocks, piece, width = keep.shape
+        first_ref[...] = jnp.zeros_like(first_ref)
+        second_ref[...] = jnp.zeros_like(second_ref)
+
+    both, x = sum_ref[0], x_ref[0]
+    wide = first_ref.shape[0]
+    first_ref[...] += dot3(x[:, :wide], both[:, :wide], ((0,), (0,)))
+    second_ref[...] += dot3(x[:, wide:], both[:, wide:], ((0,), (0,)))
+
+
+def updates(summed, x):
+    blocks, piece, width = summed.shape
+    wide = width // NS
     spec = pl.BlockSpec((1, piece, width), lambda i: (i, 0, 0))
+    update = pl.BlockSpec((wide, wide), lambda i: (0, 0))
     return pl.pallas_call(
-        add_kernel,
+        update_kernel,
         grid=(blocks,),
-        in_specs=[spec] * 3,
-        out_specs=[spec, pl.BlockSpec((width, width), lambda i: (0, 0))],
-        out_shape=[jax.ShapeDtypeStruct(keep.shape, F32), jax.ShapeDtypeStruct((width, width), F32)],
+        in_specs=[spec] * 2,
+        out_specs=[update, update],
+        out_shape=[jax.ShapeDtypeStruct((wide, wide), F32)] * 2,
         compiler_params=pltpu.CompilerParams(vmem_limit_bytes=16 << 20),
         cost_estimate=pl.CostEstimate(
-            flops=6 * blocks * piece * width * width, bytes_accessed=16 * blocks * piece * width, transcendentals=0
+            flops=6 * blocks * piece * width * wide, bytes_accessed=8 * blocks * piece * width, transcendentals=0
         ),
-    )(keep, got, x)
+    )(summed, x)
 
 
 def gather_column(mine):
@@ -164,34 +168,28 @@
 def local(ancestor_inverse, lower_panel, diag_factor, diag_block, pattern):
     y, xh, z, xl, k = (lax.axis_index(a) for a in ALL)
     row, col = y * 2 + xh, z * 4 + xl * 2 + k
-    piece = lower_panel.shape[1]
+    piece, wide = lower_panel.shape[1:]
     start = (row * 16 + col) * piece
     masks = [tile_mask(pattern, s, start, piece) for s in range(NS)]
-    normed = [jnp.dot(lower_panel[s], diag_factor[s], precision=HIGHEST) * masks[s] for s in range(NS)]
+    normed = jnp.concatenate(
+        [jnp.dot(lower_panel[s], diag_factor[s], precision=HIGHEST) * masks[s] for s in range(NS)], axis=1
+    )
     spots = jnp.arange(8, dtype=jnp.int32)
     places = jnp.concatenate([((spots // 2) ^ y) * 2 + ((spots % 2) ^ xh), k[None]])
-
-    near = swap(normed[1], "xl")
-    pair = jnp.stack([jnp.where(xl == 0, normed[1], near), jnp.where(xl == 0, near, normed[1])])
-    band = lax.all_gather(pair, "z", axis=0, tiled=True)
-
-    panels, updates = [], []
-    for snode in range(NS):
-        mine = lax.ppermute(normed[snode], ALL, transpose_pairs())
-        keep, give = product(ancestor_inverse, gather_column(mine), places)
-        got = swap(give, "k")
-        if snode == 0:
-            summed = keep + got
-        else:
-            summed, early = add_and_update(keep, got, band)
-        summed = lax.psum_scatter(summed.reshape(4, 2, *summed.shape[1:]), "z", scatter_dimension=0, tiled=False)
-        kept = lax.dynamic_slice_in_dim(summed, xl, 1, 0)[0]
-        given = lax.dynamic_slice_in_dim(summed, 1 - xl, 1, 0)[0]
-        whole = masks[snode] * (kept + swap(given, "xl"))
-        panels.append(-whole)
-        if snode == 0:
-            late = lax.dot_general(normed[0], whole, (((0,), (0,)), ((), ())), precision=HIGH)
-    first, second = total(late, early)
+    mine = lax.ppermute(normed, ALL, transpose_pairs())
+
+    band = lax.all_gather(normed, ("z", "xl"), axis=0, tiled=False)
+
+    keep, give = product(ancestor_inverse, gather_column(mine), places)
+    got = swap(give, "k")
+    summed = keep + got
+    first, second = updates(summed, band)
+    summed = lax.psum_scatter(summed.reshape(4, 2, *summed.shape[1:]), "z", scatter_dimension=0, tiled=False)
+    kept = lax.dynamic_slice_in_dim(summed, xl, 1, 0)[0]
+    given = lax.dynamic_slice_in_dim(summed, 1 - xl, 1, 0)[0]
+    whole = kept + swap(given, "xl")
+    panels = [-masks[s] * whole[:, s * wide : (s + 1) * wide] for s in range(NS)]
+    first, second = total(first, second)
     return jnp.stack(panels), jnp.stack([diag_block[0] + first, diag_block[1] + second])
 
 

time: 185 us -> 173 us (0.935)
  starting transfers between devices: 69.2 us -> 47.9 us
  waiting for transfers between devices: 56.6 us -> 73.6 us
  Pallas kernels: 29.9 us -> 22.6 us
    ppermute x32 -> x22, starting transfers between devices: 67.7 us -> 47.1 us  [send(): return lax.ppermute(x, axis, [(i, to(i)) for i in range(size)])]
    ppermute x32 -> x22, waiting for transfers between devices: 56.5 us -> 65.6 us  [send(): return lax.ppermute(x, axis, [(i, to(i)) for i in range(size)])]
    all_gather x1, waiting for transfers between devices: 0.01 us -> 7.95 us  [local(): band = lax.all_gather(normed, ('z', 'xl'), axis=0, tiled=False)]
    pallas_call x2 -> x1, Pallas kernels: 26.7 us -> 18.9 us  [product(): pl.pallas_call(product_kernel, grid_spec=pltpu.PrefetchScalarGridSpec(num...]
  transfers between devices with their start and end apart: 37 -> 25, of which waited for: 23 -> 19; matrix products, arithmetic and copies ran while one was open for 5% -> 3% of each run, Pallas kernels for 16% -> 13%
where the time goes in v5:
time: 173 us; the launch traced here: 172 us
  waiting for transfers between devices  73.6 us (43%)
  starting transfers between devices  47.9 us (28%)
  Pallas kernels  22.6 us (13%)
  between operations  15.8 us (9%)
  local copies, waits for them, and re-layouts  4.86 us (3%)
  other arithmetic  4.62 us (3%)
  matrix products  2.77 us (2%)
    ppermute x22, waiting for transfers between devices, send(): return lax.ppermute(x, axis, [(i, to(i)) for i in range(size)])  65.6 us
    ppermute x22, starting transfers between devices, send(): return lax.ppermute(x, axis, [(i, to(i)) for i in range(size)])  47.1 us
    pallas_call x1, Pallas kernels, product(): pl.pallas_call(product_kernel, grid_spec=pltpu.PrefetchScalarGridSpec(num...  18.9 us
    all_gather x1, waiting for transfers between devices, local(): band = lax.all_gather(normed, ('z', 'xl'), axis=0, tiled=False)  7.95 us
    pallas_call x1, Pallas kernels, updates(): pl.pallas_call(update_kernel, grid=(blocks,), in_specs=[spec] * 2, out_sp...  3.62 us
  transfers between devices with their start and end apart: 25, of which 19 were waited for; matrix products, arithmetic and copies ran while one was open for 3% of the time, Pallas kernels for 13%

profile of v5, /device:TPU:0, one launch (start us, length us, event | category | flops | bytes accessed | tf_op | source)
XLA Modules:
  0.0 172.1 jit_solution(1774670125788479653)
XLA Ops:
  8.1 0.8 fusion.20
  9.2 1.4 convolution_multiply_fusion
  10.6 1.4 convolution_multiply_fusion.1
  12.1 0.7 collective-permute-start
  12.8 14.3 %collective-permute-start.1 = (f32[192,512]{1,0:T(8,128)S(1)}, f32[192,512]{1,0:T(8,128)S(1)}, u32[]{:S(2)}, u32[]{:S(2)}) collective-permute-start(f32[192,512]{1,0:T(8,128)S(1)} %collective-permute-done.refs_0_), channel_id=1, source_target_pairs={{0,16},{16,0},{1,17},{17,1},{2,18},{18,2},{3,19},{19,3},{4,20},{20... | collective-permute-start | bytes 1179656 | tf_op jit(solution)/shard_map/ppermute | solution.py:18
  27.2 3.9 %collective-permute-start.2 = (f32[192,512]{1,0:T(8,128)S(1)}, f32[192,512]{1,0:T(8,128)S(1)}, u32[]{:S(2)}, u32[]{:S(2)}) collective-permute-start(f32[192,512]{1,0:T(8,128)S(1)} %collective-permute-done.refs_0_), channel_id=1, source_target_pairs={{0,32},{32,0},{64,96},{96,64},{1,33},{33,1},{65,97},{97,65},{2,34}... | collective-permute-start | bytes 1179656 | tf_op jit(solution)/shard_map/ppermute | solution.py:18
  31.1 5.8 %collective-permute-done.1.refs_1_ = f32[192,512]{1,0:T(8,128)S(1)} collective-permute-done((f32[192,512]{1,0:T(8,128)S(1)}, f32[192,512]{1,0:T(8,128)S(1)}, u32[]{:S(2)}, u32[]{:S(2)}) %collective-permute-start.1) | collective-permute-done | bytes 393248 | tf_op jit(solution)/shard_map/ppermute | solution.py:18
  36.9 7.5 %collective-permute-start.5 = (f32[192,512]{1,0:T(8,128)S(1)}, f32[192,512]{1,0:T(8,128)S(1)}, u32[]{:S(2)}, u32[]{:S(2)}) collective-permute-start(f32[192,512]{1,0:T(8,128)S(1)} %collective-permute-done.1.refs_1_), channel_id=1, source_target_pairs={{0,96},{32,64},{64,32},{96,0},{1,97},{33,65},{65,33},{97,1},{2,98}... | collective-permute-start | bytes 1179656 | tf_op jit(solution)/shard_map/ppermute | solution.py:18
  44.5 1.8 %collective-permute-start.3 = (f32[192,512]{1,0:T(8,128)S(1)}, f32[192,512]{1,0:T(8,128)S(1)}, u32[]{:S(2)}, u32[]{:S(2)}) collective-permute-start(f32[192,512]{1,0:T(8,128)S(1)} %collective-permute-done.1.refs_1_), channel_id=1, source_target_pairs={{0,32},{32,0},{64,96},{96,64},{1,33},{33,1},{65,97},{97,65},{2,34}... | collective-permute-start | bytes 1179656 | tf_op jit(solution)/shard_map/ppermute | solution.py:18
  46.3 2.6 %collective-permute-start.4 = (f32[192,512]{1,0:T(8,128)S(1)}, f32[192,512]{1,0:T(8,128)S(1)}, u32[]{:S(2)}, u32[]{:S(2)}) collective-permute-start(f32[192,512]{1,0:T(8,128)S(1)} %collective-permute-done.2.refs_2_), channel_id=1, source_target_pairs={{0,96},{32,64},{64,32},{96,0},{1,97},{33,65},{65,33},{97,1},{2,98}... | collective-permute-start | bytes 1179656 | tf_op jit(solution)/shard_map/ppermute | solution.py:18
  48.9 5.6 %collective-permute-done.5.refs_7_ = f32[192,512]{1,0:T(8,128)S(1)} collective-permute-done((f32[192,512]{1,0:T(8,128)S(1)}, f32[192,512]{1,0:T(8,128)S(1)}, u32[]{:S(2)}, u32[]{:S(2)}) %collective-permute-start.5) | collective-permute-done | bytes 393248 | tf_op jit(solution)/shard_map/ppermute | solution.py:18
  54.5 1.8 %collective-permute-start.6 = (f32[192,512]{1,0:T(8,128)S(1)}, f32[192,512]{1,0:T(8,128)S(1)}, u32[]{:S(2)}, u32[]{:S(2)}) collective-permute-start(f32[192,512]{1,0:T(8,128)S(1)} %collective-permute-done.5.refs_7_), channel_id=1, source_target_pairs={{0,32},{32,0},{64,96},{96,64},{1,33},{33,1},{65,97},{97,65},{2,34}... | collective-permute-start | bytes 1179656 | tf_op jit(solution)/shard_map/ppermute | solution.py:18
  56.4 6.5 %collective-permute-done.7.refs_6_ = f32[192,512]{1,0:T(8,128)S(1)} collective-permute-done((f32[192,512]{1,0:T(8,128)S(1)}, f32[192,512]{1,0:T(8,128)S(1)}, u32[]{:S(2)}, u32[]{:S(2)}) %collective-permute-start.7) | collective-permute-done | bytes 393248 | tf_op jit(solution)/shard_map/ppermute | solution.py:18
  62.9 6.6 %collective-permute-done.4.refs_4_ = f32[192,512]{1,0:T(8,128)S(1)} collective-permute-done((f32[192,512]{1,0:T(8,128)S(1)}, f32[192,512]{1,0:T(8,128)S(1)}, u32[]{:S(2)}, u32[]{:S(2)}) %collective-permute-start.4) | collective-permute-done | bytes 393248 | tf_op jit(solution)/shard_map/ppermute | solution.py:18
  69.5 18.9 %shard_map.68 = (f32[8,192,512]{2,1,0:T(8,128)S(1)}, f32[8,192,512]{2,1,0:T(8,128)S(1)}) custom-call(s32[9]{0:T(128)S(1)} %pad_add_fusion.place_ref, f32[3072,1536]{1,0:T(8,128)} %a_ref.1, f32[192,512]{1,0:T(8,128)S(1)} %collective-permute-done.refs_0_, f32[192,512]{1,0:T(8,128)S(1)} %collective-permute-done.1.refs_1_, ...), custom_call_target="tpu_custom_call" | custom-call | flops 14495514624 | bytes 28311552 | tf_op jit(solution)/shard_map/pallas_call | solution.py:109
  88.6 5.6 %collective-permute-done.8 = f32[8,192,512]{2,1,0:T(8,128)S(1)} collective-permute-done((f32[8,192,512]{2,1,0:T(8,128)S(1)}, f32[8,192,512]{2,1,0:T(8,128)S(1)}, u32[]{:S(2)}, u32[]{:S(2)}) %collective-permute-start.8) | collective-permute-done | bytes 3145760 | tf_op jit(solution)/shard_map/ppermute | solution.py:18
  94.2 2.4 %add.106.sum_ref = f32[8,192,512]{2,1,0:T(8,128)} add(f32[8,192,512]{2,1,0:T(8,128)S(1)} %get-tuple-element.6, f32[8,192,512]{2,1,0:T(8,128)S(1)} %collective-permute-done.8) | non-fusion elementwise | flops 786432 | bytes 9437184 | tf_op jit(solution)/shard_map/add | solution.py:185
  96.7 7.9 %all-gather.3.cloned.1.call-done = f32[1536,512]{1,0:T(8,128)} async-done(((f32[192,512]{1,0:T(8,128)}), f32[1536,512]{1,0:T(8,128)}) %all-gather.3.cloned.1.call-update) | async-done | bytes 3145744 | tf_op jit(solution)/shard_map/all_gather | solution.py:181
  104.7 1.9 %copy-done.1 = f32[1536,512]{1,0:T(8,128)S(1)} copy-done((f32[1536,512]{1,0:T(8,128)S(1)}, f32[1536,512]{1,0:T(8,128)}, u32[]{:S(2)}) %copy-start.1) | copy-done | bytes 3145752
  106.5 3.6 %shard_map.69 = (f32[256,256]{1,0:T(8,128)S(1)}, f32[256,256]{1,0:T(8,128)S(1)}) custom-call(f32[8,192,512]{2,1,0:T(8,128)S(1)} %copy-done, f32[8,192,512]{2,1,0:T(8,128)S(1)} %bitcast.40), custom_call_target="tpu_custom_call" | custom-call | flops 1207959552 | bytes 6291456 | tf_op jit(solution)/shard_map/pallas_call | solution.py:143
  110.2 0.7 copy-done.2
  111.0 1.5 collective-permute-done.10
  112.6 2.8 %collective-permute-start.13 = (f32[64,256]{1,0:T(8,128)S(1)}, f32[64,256]{1,0:T(8,128)S(1)}, u32[]{:S(2)}, u32[]{:S(2)}) collective-permute-start(f32[64,256]{1,0:T(8,128)S(1)} %get-tuple-element.15), channel_id=1, source_target_pairs={{0,96},{32,0},{64,32},{96,64},{1,97},{33,1},{65,33},{97,65},{2,98}... | collective-permute-start | bytes 196616 | tf_op jit(solution)/shard_map/ppermute | solution.py:18
  115.4 0.8 collective-permute-start.12
  116.2 0.9 collective-permute-start.11
  117.7 4.2 %collective-permute-done.12 = f32[64,256]{1,0:T(8,128)S(1)} collective-permute-done((f32[64,256]{1,0:T(8,128)S(1)}, f32[64,256]{1,0:T(8,128)S(1)}, u32[]{:S(2)}, u32[]{:S(2)}) %collective-permute-start.12) | collective-permute-done | bytes 65568 | tf_op jit(solution)/shard_map/ppermute | solution.py:18
  121.9 1.2 collective-permute-done.11
  123.2 1.4 collective-permute-start.16
  124.6 0.7 collective-permute-start.15
  125.3 0.9 collective-permute-start.14
  126.2 3.4 %collective-permute-done.16 = f32[64,256]{1,0:T(8,128)S(1)} collective-permute-done((f32[64,256]{1,0:T(8,128)S(1)}, f32[64,256]{1,0:T(8,128)S(1)}, u32[]{:S(2)}, u32[]{:S(2)}) %collective-permute-start.16) | collective-permute-done | bytes 65568 | tf_op jit(solution)/shard_map/ppermute | solution.py:18
  129.6 2.8 %collective-permute-done.15 = f32[64,256]{1,0:T(8,128)S(1)} collective-permute-done((f32[64,256]{1,0:T(8,128)S(1)}, f32[64,256]{1,0:T(8,128)S(1)}, u32[]{:S(2)}, u32[]{:S(2)}) %collective-permute-start.15) | collective-permute-done | bytes 65568 | tf_op jit(solution)/shard_map/ppermute | solution.py:18
  132.5 1.0 collective-permute-done.14
  133.5 1.1 collective-permute-start.17
  134.6 3.3 %collective-permute-done.17 = f32[64,256]{1,0:T(8,128)S(1)} collective-permute-done((f32[64,256]{1,0:T(8,128)S(1)}, f32[64,256]{1,0:T(8,128)S(1)}, u32[]{:S(2)}, u32[]{:S(2)}) %collective-permute-start.17) | collective-permute-done | bytes 65568 | tf_op jit(solution)/shard_map/ppermute | solution.py:18
  137.9 2.8 %collective-permute-start.18 = (f32[64,256]{1,0:T(8,128)S(1)}, f32[64,256]{1,0:T(8,128)S(1)}, u32[]{:S(2)}, u32[]{:S(2)}) collective-permute-start(f32[64,256]{1,0:T(8,128)S(1)} %add.124), channel_id=1, source_target_pairs={{0,16},{16,0},{1,17},{17,1},{2,18},{18,2},{3,19},{19,3},{4,20},{20... | collective-permute-start | bytes 196616 | tf_op jit(solution)/shard_map/ppermute | solution.py:18
  140.6 3.1 %collective-permute-done.18 = f32[64,256]{1,0:T(8,128)S(1)} collective-permute-done((f32[64,256]{1,0:T(8,128)S(1)}, f32[64,256]{1,0:T(8,128)S(1)}, u32[]{:S(2)}, u32[]{:S(2)}) %collective-permute-start.18) | collective-permute-done | bytes 65568 | tf_op jit(solution)/shard_map/ppermute | solution.py:18
  143.7 0.6 collective-permute-start.19
  144.3 0.8 collective-permute-start.20
  145.1 0.9 collective-permute-start.21
  146.1 2.0 %collective-permute-done.19 = f32[64,256]{1,0:T(8,128)S(1)} collective-permute-done((f32[64,256]{1,0:T(8,128)S(1)}, f32[64,256]{1,0:T(8,128)S(1)}, u32[]{:S(2)}, u32[]{:S(2)}) %collective-permute-start.19) | collective-permute-done | bytes 65568 | tf_op jit(solution)/shard_map/ppermute | solution.py:18
  148.1 2.0 %collective-permute-done.20 = f32[64,256]{1,0:T(8,128)S(1)} collective-permute-done((f32[64,256]{1,0:T(8,128)S(1)}, f32[64,256]{1,0:T(8,128)S(1)}, u32[]{:S(2)}, u32[]{:S(2)}) %collective-permute-start.20) | collective-permute-done | bytes 65568 | tf_op jit(solution)/shard_map/ppermute | solution.py:18
  150.1 0.7 collective-permute-done.21
  151.0 1.1 dynamic-slice_bitcast_fusion
  152.2 1.1 collective-permute-start.9
  153.3 0.8 pad_maximum_fusion
  154.2 9.5 %collective-permute-done.9 = f32[192,512]{1,0:T(8,128)S(1)} collective-permute-done((f32[192,512]{1,0:T(8,128)S(1)}, f32[192,512]{1,0:T(8,128)S(1)}, u32[]{:S(2)}, u32[]{:S(2)}) %collective-permute-start.9) | collective-permute-done | bytes 393248 | tf_op jit(solution)/shard_map/ppermute | solution.py:18
  163.9 0.8 pad_maximum_fusion.2
  (53 shorter events, 2.0 us)
Async XLA Ops:
  8.0 96.7 %all-gather.3.cloned.1.call-start = ((), (), s32[]{:S(2)}) async-start(), calls=%async_computation.2 | async-start | bytes 3538944 | tf_op jit(solution)/shard_map/all_gather | solution.py:181
  12.0 15.1 %copy-start.3 = (f32[192,512]{1,0:T(8,128)}, f32[192,512]{1,0:T(8,128)S(1)}, u32[]{:S(2)}) copy-start(f32[192,512]{1,0:T(8,128)S(1)} %pad_maximum_fusion.1) | copy-start | bytes 1179652
  12.1 0.7 collective-permute-start
  12.8 24.1 %collective-permute-start.1 = (f32[192,512]{1,0:T(8,128)S(1)}, f32[192,512]{1,0:T(8,128)S(1)}, u32[]{:S(2)}, u32[]{:S(2)}) collective-permute-start(f32[192,512]{1,0:T(8,128)S(1)} %collective-permute-done.refs_0_), channel_id=1, source_target_pairs={{0,16},{16,0},{1,17},{17,1},{2,18},{18,2},{3,19},{19,3},{4,20},{20... | collective-permute-start | bytes 1179656 | tf_op jit(solution)/shard_map/ppermute | solution.py:18
  27.1 123.9 %reduce-scatter.2.cloned.1.call-start = ((), (), s32[]{:S(2)}) async-start(), calls=%async_computation.1 | async-start | bytes 3932160 | tf_op jit(solution)/shard_map/reduce_scatter | solution.py:187
  27.2 19.1 %collective-permute-start.2 = (f32[192,512]{1,0:T(8,128)S(1)}, f32[192,512]{1,0:T(8,128)S(1)}, u32[]{:S(2)}, u32[]{:S(2)}) collective-permute-start(f32[192,512]{1,0:T(8,128)S(1)} %collective-permute-done.refs_0_), channel_id=1, source_target_pairs={{0,32},{32,0},{64,96},{96,64},{1,33},{33,1},{65,97},{97,65},{2,34}... | collective-permute-start | bytes 1179656 | tf_op jit(solution)/shard_map/ppermute | solution.py:18
  36.9 17.6 %collective-permute-start.5 = (f32[192,512]{1,0:T(8,128)S(1)}, f32[192,512]{1,0:T(8,128)S(1)}, u32[]{:S(2)}, u32[]{:S(2)}) collective-permute-start(f32[192,512]{1,0:T(8,128)S(1)} %collective-permute-done.1.refs_1_), channel_id=1, source_target_pairs={{0,96},{32,64},{64,32},{96,0},{1,97},{33,65},{65,33},{97,1},{2,98}... | collective-permute-start | bytes 1179656 | tf_op jit(solution)/shard_map/ppermute | solution.py:18
  44.4 18.5 %collective-permute-start.7 = (f32[192,512]{1,0:T(8,128)S(1)}, f32[192,512]{1,0:T(8,128)S(1)}, u32[]{:S(2)}, u32[]{:S(2)}) collective-permute-start(f32[192,512]{1,0:T(8,128)S(1)} %collective-permute-done.refs_0_), channel_id=1, source_target_pairs={{0,96},{32,64},{64,32},{96,0},{1,97},{33,65},{65,33},{97,1},{2,98}... | collective-permute-start | bytes 1179656 | tf_op jit(solution)/shard_map/ppermute | solution.py:18
  44.5 18.4 %collective-permute-start.3 = (f32[192,512]{1,0:T(8,128)S(1)}, f32[192,512]{1,0:T(8,128)S(1)}, u32[]{:S(2)}, u32[]{:S(2)}) collective-permute-start(f32[192,512]{1,0:T(8,128)S(1)} %collective-permute-done.1.refs_1_), channel_id=1, source_target_pairs={{0,32},{32,0},{64,96},{96,64},{1,33},{33,1},{65,97},{97,65},{2,34}... | collective-permute-start | bytes 1179656 | tf_op jit(solution)/shard_map/ppermute | solution.py:18
  46.3 23.2 %collective-permute-start.4 = (f32[192,512]{1,0:T(8,128)S(1)}, f32[192,512]{1,0:T(8,128)S(1)}, u32[]{:S(2)}, u32[]{:S(2)}) collective-permute-start(f32[192,512]{1,0:T(8,128)S(1)} %collective-permute-done.2.refs_2_), channel_id=1, source_target_pairs={{0,96},{32,64},{64,32},{96,0},{1,97},{33,65},{65,33},{97,1},{2,98}... | collective-permute-start | bytes 1179656 | tf_op jit(solution)/shard_map/ppermute | solution.py:18
  54.5 15.1 %collective-permute-start.6 = (f32[192,512]{1,0:T(8,128)S(1)}, f32[192,512]{1,0:T(8,128)S(1)}, u32[]{:S(2)}, u32[]{:S(2)}) collective-permute-start(f32[192,512]{1,0:T(8,128)S(1)} %collective-permute-done.5.refs_7_), channel_id=1, source_target_pairs={{0,32},{32,0},{64,96},{96,64},{1,33},{33,1},{65,97},{97,65},{2,34}... | collective-permute-start | bytes 1179656 | tf_op jit(solution)/shard_map/ppermute | solution.py:18
  88.5 5.7 %collective-permute-start.8 = (f32[8,192,512]{2,1,0:T(8,128)S(1)}, f32[8,192,512]{2,1,0:T(8,128)S(1)}, u32[]{:S(2)}, u32[]{:S(2)}) collective-permute-start(f32[8,192,512]{2,1,0:T(8,128)S(1)} %get-tuple-element.7), channel_id=1, source_target_pairs={{0,1},{1,0},{2,3},{3,2},{4,5},{5,4},{6,7},{7,6},{8,9},{9,8},{10,11... | collective-permute-start | bytes 9437192 | tf_op jit(solution)/shard_map/ppermute | solution.py:18
  96.7 8.0 %copy-start = (f32[8,192,512]{2,1,0:T(8,128)S(1)}, f32[8,192,512]{2,1,0:T(8,128)}, u32[]{:S(2)}) copy-start(f32[8,192,512]{2,1,0:T(8,128)} %add.106.sum_ref) | copy-start | bytes 9437188
  104.7 1.9 %copy-start.1 = (f32[1536,512]{1,0:T(8,128)S(1)}, f32[1536,512]{1,0:T(8,128)}, u32[]{:S(2)}) copy-start(f32[1536,512]{1,0:T(8,128)} %all-gather.3.cloned.1.call-done) | copy-start | bytes 9437188
  110.2 0.7 copy-start.2
  110.2 43.1 %copy-start.5 = (f32[2,256,256]{2,1,0:T(8,128)S(1)}, f32[2,256,256]{2,1,0:T(8,128)}, u32[]{:S(2)}) copy-start(f32[2,256,256]{2,1,0:T(8,128)} %param.8) | copy-start | bytes 1572868
  110.9 1.6 collective-permute-start.10
  112.6 5.1 %collective-permute-start.13 = (f32[64,256]{1,0:T(8,128)S(1)}, f32[64,256]{1,0:T(8,128)S(1)}, u32[]{:S(2)}, u32[]{:S(2)}) collective-permute-start(f32[64,256]{1,0:T(8,128)S(1)} %get-tuple-element.15), channel_id=1, source_target_pairs={{0,96},{32,0},{64,32},{96,64},{1,97},{33,1},{65,33},{97,65},{2,98}... | collective-permute-start | bytes 196616 | tf_op jit(solution)/shard_map/ppermute | solution.py:18
  115.4 6.5 %collective-permute-start.12 = (f32[64,256]{1,0:T(8,128)S(1)}, f32[64,256]{1,0:T(8,128)S(1)}, u32[]{:S(2)}, u32[]{:S(2)}) collective-permute-start(f32[64,256]{1,0:T(8,128)S(1)} %get-tuple-element.16), channel_id=1, source_target_pairs={{0,64},{32,96},{64,0},{96,32},{1,65},{33,97},{65,1},{97,33},{2,66}... | collective-permute-start | bytes 196616 | tf_op jit(solution)/shard_map/ppermute | solution.py:18
  116.2 6.9 %collective-permute-start.11 = (f32[64,256]{1,0:T(8,128)S(1)}, f32[64,256]{1,0:T(8,128)S(1)}, u32[]{:S(2)}, u32[]{:S(2)}) collective-permute-start(f32[64,256]{1,0:T(8,128)S(1)} %get-tuple-element.14), channel_id=1, source_target_pairs={{0,32},{32,64},{64,96},{96,0},{1,33},{33,65},{65,97},{97,1},{2,34}... | collective-permute-start | bytes 196616 | tf_op jit(solution)/shard_map/ppermute | solution.py:18
  123.2 6.4 %collective-permute-start.16 = (f32[64,256]{1,0:T(8,128)S(1)}, f32[64,256]{1,0:T(8,128)S(1)}, u32[]{:S(2)}, u32[]{:S(2)}) collective-permute-start(f32[64,256]{1,0:T(8,128)S(1)} %add_add_fusion.1), channel_id=1, source_target_pairs={{0,12},{4,0},{8,4},{12,8},{1,13},{5,1},{9,5},{13,9},{2,14},{6,2},{... | collective-permute-start | bytes 196616 | tf_op jit(solution)/shard_map/ppermute | solution.py:18
  124.6 7.9 %collective-permute-start.15 = (f32[64,256]{1,0:T(8,128)S(1)}, f32[64,256]{1,0:T(8,128)S(1)}, u32[]{:S(2)}, u32[]{:S(2)}) collective-permute-start(f32[64,256]{1,0:T(8,128)S(1)} %add_add_fusion.1), channel_id=1, source_target_pairs={{0,8},{4,12},{8,0},{12,4},{1,9},{5,13},{9,1},{13,5},{2,10},{6,14},... | collective-permute-start | bytes 196616 | tf_op jit(solution)/shard_map/ppermute | solution.py:18
  125.3 8.2 %collective-permute-start.14 = (f32[64,256]{1,0:T(8,128)S(1)}, f32[64,256]{1,0:T(8,128)S(1)}, u32[]{:S(2)}, u32[]{:S(2)}) collective-permute-start(f32[64,256]{1,0:T(8,128)S(1)} %add_add_fusion.1), channel_id=1, source_target_pairs={{0,4},{4,8},{8,12},{12,0},{1,5},{5,9},{9,13},{13,1},{2,6},{6,10},{... | collective-permute-start | bytes 196616 | tf_op jit(solution)/shard_map/ppermute | solution.py:18
  133.5 4.3 %collective-permute-start.17 = (f32[64,256]{1,0:T(8,128)S(1)}, f32[64,256]{1,0:T(8,128)S(1)}, u32[]{:S(2)}, u32[]{:S(2)}) collective-permute-start(f32[64,256]{1,0:T(8,128)S(1)} %add_add_fusion), channel_id=1, source_target_pairs={{0,2},{2,0},{1,3},{3,1},{4,6},{6,4},{5,7},{7,5},{8,10},{10,8},{9,1... | collective-permute-start | bytes 196616 | tf_op jit(solution)/shard_map/ppermute | solution.py:18
  137.9 5.8 %collective-permute-start.18 = (f32[64,256]{1,0:T(8,128)S(1)}, f32[64,256]{1,0:T(8,128)S(1)}, u32[]{:S(2)}, u32[]{:S(2)}) collective-permute-start(f32[64,256]{1,0:T(8,128)S(1)} %add.124), channel_id=1, source_target_pairs={{0,16},{16,0},{1,17},{17,1},{2,18},{18,2},{3,19},{19,3},{4,20},{20... | collective-permute-start | bytes 196616 | tf_op jit(solution)/shard_map/ppermute | solution.py:18
  143.7 4.3 %collective-permute-start.19 = (f32[64,256]{1,0:T(8,128)S(1)}, f32[64,256]{1,0:T(8,128)S(1)}, u32[]{:S(2)}, u32[]{:S(2)}) collective-permute-start(f32[64,256]{1,0:T(8,128)S(1)} %add.125), channel_id=1, source_target_pairs={{0,96},{32,0},{64,32},{96,64},{1,97},{33,1},{65,33},{97,65},{2,98}... | collective-permute-start | bytes 196616 | tf_op jit(solution)/shard_map/ppermute | solution.py:18
  144.3 5.8 %collective-permute-start.20 = (f32[64,256]{1,0:T(8,128)S(1)}, f32[64,256]{1,0:T(8,128)S(1)}, u32[]{:S(2)}, u32[]{:S(2)}) collective-permute-start(f32[64,256]{1,0:T(8,128)S(1)} %add.125), channel_id=1, source_target_pairs={{0,64},{32,96},{64,0},{96,32},{1,65},{33,97},{65,1},{97,33},{2,66}... | collective-permute-start | bytes 196616 | tf_op jit(solution)/shard_map/ppermute | solution.py:18
  145.1 5.7 %collective-permute-start.21 = (f32[64,256]{1,0:T(8,128)S(1)}, f32[64,256]{1,0:T(8,128)S(1)}, u32[]{:S(2)}, u32[]{:S(2)}) collective-permute-start(f32[64,256]{1,0:T(8,128)S(1)} %add.125), channel_id=1, source_target_pairs={{0,32},{32,64},{64,96},{96,0},{1,33},{33,65},{65,97},{97,1},{2,34}... | collective-permute-start | bytes 196616 | tf_op jit(solution)/shard_map/ppermute | solution.py:18
  150.9 2.3 %collective-permute-start.22 = (f32[256,256]{1,0:T(8,128)S(1)}, f32[256,256]{1,0:T(8,128)S(1)}, u32[]{:S(2)}, u32[]{:S(2)}) collective-permute-start(f32[256,256]{1,0:T(8,128)S(1)} %constant_dynamic-slice_fusion), channel_id=1, source_target_pairs={{0,1},{1,0},{2,3},{3,2},{4,5},{5,4},{6,7},{7,6},{8,9},{9,8},{10,11... | collective-permute-start | bytes 786440 | tf_op jit(solution)/shard_map/ppermute | solution.py:18
  151.0 12.7 %copy-start.4 = (f32[1,2,192,512]{3,2,1,0:T(8,128)S(1)}, f32[1,2,192,512]{3,2,1,0:T(8,128)}, u32[]{:S(2)}) copy-start(f32[1,2,192,512]{3,2,1,0:T(8,128)} %reduce-scatter.2.cloned.1.call-done) | copy-start | bytes 2359300
  152.2 11.6 %collective-permute-start.9 = (f32[192,512]{1,0:T(8,128)S(1)}, f32[192,512]{1,0:T(8,128)S(1)}, u32[]{:S(2)}, u32[]{:S(2)}) collective-permute-start(f32[192,512]{1,0:T(8,128)S(1)} %dynamic-slice_bitcast_fusion), channel_id=1, source_target_pairs={{0,2},{2,0},{1,3},{3,1},{4,6},{6,4},{5,7},{7,5},{8,10},{10,8},{9,1... | collective-permute-start | bytes 1179656 | tf_op jit(solution)/shard_map/ppermute | solution.py:18
Sparse Core Ops, SparseCore 0:
  27.3 77.3 all-gather.2
Sparse Core Ops, SparseCore 1:
  96.8 42.3 reduce-scatter.1

commit v6 on v5

--- a/solution.py
+++ b/solution.py
@@ -55,7 +55,7 @@
     return lax.dynamic_slice_in_dim(twice, (3 - me) * x.shape[0], 4 * x.shape[0], 0)
 
 
-def total(first, second):
+def total(first, second, before):
     k = lax.axis_index("k")
     mine = jnp.where(k == 0, first, second) + swap(jnp.where(k == 0, second, first), "k")
     mine = scatter_four(mine, "y")
@@ -63,6 +63,7 @@
     mine = mine + swap(mine, "xl")
     mine = mine + swap(mine, "xh")
     mine = gather_four(mine, "y")
+    (mine,) = later([mine], [before])
     other = swap(mine, "k")
     return jnp.where(k == 0, mine, other), jnp.where(k == 0, other, mine)
 
@@ -77,6 +78,18 @@
     bh, bl = halves(b)
     f = lambda p, q: lax.dot_general(p, q, (dims, ((), ())), preferred_element_type=F32)
     return f(ah, bh) + (f(ah, bl) + f(al, bh))
+
+
+def later(xs, after):
+    anywhere = pl.BlockSpec(memory_space=pl.ANY)
+    return pl.pallas_call(
+        lambda *refs: None,
+        in_specs=[anywhere] * (len(xs) + len(after)),
+        out_specs=[anywhere] * len(xs),
+        out_shape=[jax.ShapeDtypeStruct(x.shape, x.dtype) for x in xs],
+        input_output_aliases={i: i for i in range(len(xs))},
+        cost_estimate=pl.CostEstimate(flops=0, bytes_accessed=0, transcendentals=0),
+    )(*xs, *after)
 
 
 def product_kernel(place_ref, a_ref, *refs):
@@ -100,8 +113,8 @@
     give_ref[0] = jnp.where(lower, second, first)
 
 
-def product(a, pieces, places):
-    rows, cols = a.shape
+def product(a, pieces, places, part):
+    rows, cols = a.shape[0] // 2, a.shape[1]
     piece, width = pieces[0].shape
     blocks = rows // (2 * piece)
     whole = pl.BlockSpec((piece, width), lambda i, p: (0, 0), pipeline_mode=pl.Buffered(1))
@@ -111,7 +124,7 @@
         grid_spec=pltpu.PrefetchScalarGridSpec(
             num_scalar_prefetch=1,
             grid=(blocks,),
-            in_specs=[pl.BlockSpec((2 * piece, cols), lambda i, p: (i, 0))] + [whole] * 8,
+            in_specs=[pl.BlockSpec((2 * piece, cols), lambda i, p: (2 * i + part, 0))] + [whole] * 8,
             out_specs=[out, out],
             scratch_shapes=[pltpu.VMEM((cols, width), BF)] * 2,
         ),
@@ -123,34 +136,35 @@
     )(places, a, *pieces)
 
 
-def update_kernel(sum_ref, x_ref, first_ref, second_ref):
+def update_kernel(near_ref, far_ref, x_ref, first_ref, second_ref):
     @pl.when(pl.program_id(0) == 0)
     def _():
         first_ref[...] = jnp.zeros_like(first_ref)
         second_ref[...] = jnp.zeros_like(second_ref)
 
-    both, x = sum_ref[0], x_ref[0]
     wide = first_ref.shape[0]
-    first_ref[...] += dot3(x[:, :wide], both[:, :wide], ((0,), (0,)))
-    second_ref[...] += dot3(x[:, wide:], both[:, wide:], ((0,), (0,)))
-
-
-def updates(summed, x):
-    blocks, piece, width = summed.shape
+    for h, ref in enumerate((near_ref, far_ref)):
+        both, x = ref[0], x_ref[h]
+        first_ref[...] += dot3(x[:, :wide], both[:, :wide], ((0,), (0,)))
+        second_ref[...] += dot3(x[:, wide:], both[:, wide:], ((0,), (0,)))
+
+
+def updates(halved, x):
+    blocks, piece, width = halved[0].shape
     wide = width // NS
     spec = pl.BlockSpec((1, piece, width), lambda i: (i, 0, 0))
     update = pl.BlockSpec((wide, wide), lambda i: (0, 0))
     return pl.pallas_call(
         update_kernel,
         grid=(blocks,),
-        in_specs=[spec] * 2,
+        in_specs=[spec, spec, pl.BlockSpec((2, piece, width), lambda i: (i, 0, 0))],
         out_specs=[update, update],
         out_shape=[jax.ShapeDtypeStruct((wide, wide), F32)] * 2,
         compiler_params=pltpu.CompilerParams(vmem_limit_bytes=16 << 20),
         cost_estimate=pl.CostEstimate(
-            flops=6 * blocks * piece * width * wide, bytes_accessed=8 * blocks * piece * width, transcendentals=0
+            flops=12 * blocks * piece * width * wide, bytes_accessed=16 * blocks * piece * width, transcendentals=0
         ),
-    )(summed, x)
+    )(*halved, x)
 
 
 def gather_column(mine):
@@ -178,18 +192,21 @@
     places = jnp.concatenate([((spots // 2) ^ y) * 2 + ((spots % 2) ^ xh), k[None]])
     mine = lax.ppermute(normed, ALL, transpose_pairs())
 
-    band = lax.all_gather(normed, ("z", "xl"), axis=0, tiled=False)
-
-    keep, give = product(ancestor_inverse, gather_column(mine), places)
-    got = swap(give, "k")
-    summed = keep + got
-    first, second = updates(summed, band)
-    summed = lax.psum_scatter(summed.reshape(4, 2, *summed.shape[1:]), "z", scatter_dimension=0, tiled=False)
-    kept = lax.dynamic_slice_in_dim(summed, xl, 1, 0)[0]
-    given = lax.dynamic_slice_in_dim(summed, 1 - xl, 1, 0)[0]
-    whole = kept + swap(given, "xl")
+    (sent,) = later([normed], [mine])
+    band = lax.all_gather(sent, ("z", "xl"), axis=0, tiled=False)
+
+    pieces = gather_column(mine)
+    halved = []
+    for part in range(2):
+        keep, give = product(ancestor_inverse, pieces, places, part)
+        halved.append(keep + swap(give, "k"))
+    first, second = updates(halved, band)
+    sums = [lax.psum_scatter(h, "z", scatter_dimension=0, tiled=False) for h in halved]
+    given = jnp.where(xl == 0, sums[1], sums[0])
+    taken = swap(given, "xl")
+    whole = jnp.where(xl == 0, sums[0], sums[1]) + taken
     panels = [-masks[s] * whole[:, s * wide : (s + 1) * wide] for s in range(NS)]
-    first, second = total(first, second)
+    first, second = total(first, second, taken)
     return jnp.stack(panels), jnp.stack([diag_block[0] + first, diag_block[1] + second])
 
 

time: 173 us -> 170 us (0.983)
  waiting for transfers between devices: 73.6 us -> 46.1 us
  starting transfers between devices: 47.9 us -> 61.7 us
  local copies, waits for them, and re-layouts: 4.86 us -> 9.92 us
  other arithmetic: 4.62 us -> 7.44 us
  Pallas kernels: 22.6 us -> 24.4 us
    ppermute x22 -> x23, waiting for transfers between devices: 65.6 us -> 45.9 us  [send(): return lax.ppermute(x, axis, [(i, to(i)) for i in range(size)])]
    ppermute x22 -> x23, starting transfers between devices: 47.1 us -> 60.9 us  [send(): return lax.ppermute(x, axis, [(i, to(i)) for i in range(size)])]
    all_gather x1, waiting for transfers between devices: 7.95 us -> 0.16 us  [local(): band = lax.all_gather(sent, ('z', 'xl'), axis=0, tiled=False)]
    unnamed x18 -> x30, local copies, waits for them, and re-layouts: 2.63 us -> 8.08 us
    pallas_call x1 -> x2, Pallas kernels: 18.9 us -> 21.7 us  [product(): pl.pallas_call(product_kernel, grid_spec=pltpu.PrefetchScalarGridSpec(num...]
    add x2 -> x3, other arithmetic: 2.5 us -> 4.18 us  [the longest x2 3.02 us: local(): halved.append(keep + swap(give, 'k'))]
    pallas_call x1 -> x3, Pallas kernels: 3.62 us -> 2.68 us  [the longest x1 2.68 us: updates(): pl.pallas_call(update_kernel, grid=(blocks,), in_specs=[spec, spec, pl.Bl...]
  transfers between devices with their start and end apart: 25 -> 27, of which waited for: 19 -> 16; matrix products, arithmetic and copies ran while one was open for 3% -> 4% of each run, Pallas kernels for 13% -> 15%
where the time goes in v6:
time: 170 us; the launch traced here: 168 us
  starting transfers between devices  61.7 us (36%)
  waiting for transfers between devices  46.1 us (27%)
  Pallas kernels  24.4 us (14%)
  between operations  15.7 us (9%)
  local copies, waits for them, and re-layouts  9.92 us (6%)
  other arithmetic  7.44 us (4%)
  matrix products  2.77 us (2%)
    ppermute x23, starting transfers between devices, send(): return lax.ppermute(x, axis, [(i, to(i)) for i in range(size)])  60.9 us
    ppermute x23, waiting for transfers between devices, send(): return lax.ppermute(x, axis, [(i, to(i)) for i in range(size)])  45.9 us
    pallas_call x2, Pallas kernels, product(): pl.pallas_call(product_kernel, grid_spec=pltpu.PrefetchScalarGridSpec(num...  21.7 us
    unnamed x30, local copies, waits for them, and re-layouts  8.08 us
  transfers between devices with their start and end apart: 27, of which 16 were waited for; matrix products, arithmetic and copies ran while one was open for 4% of the time, Pallas kernels for 15%

profile of v6, /device:TPU:0, one launch (start us, length us, event | category | flops | bytes accessed | tf_op | source)
XLA Modules:
  0.0 168.1 jit_solution(12478383989375429900)
XLA Ops:
  8.1 0.8 fusion.20
  9.2 1.4 convolution_multiply_fusion
  10.6 1.4 convolution_multiply_fusion.1
  13.6 14.4 %collective-permute-start.1 = (f32[192,512]{1,0:T(8,128)}, f32[192,512]{1,0:T(8,128)S(1)}, u32[]{:S(2)}, u32[]{:S(2)}) collective-permute-start(f32[192,512]{1,0:T(8,128)} %copy-done.3), channel_id=1, source_target_pairs={{0,16},{16,0},{1,17},{17,1},{2,18},{18,2},{3,19},{19,3},{4,20},{20... | collective-permute-start | bytes 1179656 | tf_op jit(solution)/shard_map/ppermute | solution.py:18
  28.0 3.8 %collective-permute-start.2 = (f32[192,512]{1,0:T(8,128)}, f32[192,512]{1,0:T(8,128)S(1)}, u32[]{:S(2)}, u32[]{:S(2)}) collective-permute-start(f32[192,512]{1,0:T(8,128)} %copy-done.3), channel_id=1, source_target_pairs={{0,32},{32,0},{64,96},{96,64},{1,33},{33,1},{65,97},{97,65},{2,34}... | collective-permute-start | bytes 1179656 | tf_op jit(solution)/shard_map/ppermute | solution.py:18
  31.9 6.2 %collective-permute-done.1.refs_1_ = f32[192,512]{1,0:T(8,128)S(1)} collective-permute-done((f32[192,512]{1,0:T(8,128)}, f32[192,512]{1,0:T(8,128)S(1)}, u32[]{:S(2)}, u32[]{:S(2)}) %collective-permute-start.1) | collective-permute-done | bytes 393248 | tf_op jit(solution)/shard_map/ppermute | solution.py:18
  38.0 7.9 %collective-permute-start.5 = (f32[192,512]{1,0:T(8,128)S(1)}, f32[192,512]{1,0:T(8,128)S(1)}, u32[]{:S(2)}, u32[]{:S(2)}) collective-permute-start(f32[192,512]{1,0:T(8,128)S(1)} %collective-permute-done.1.refs_1_), channel_id=1, source_target_pairs={{0,96},{32,64},{64,32},{96,0},{1,97},{33,65},{65,33},{97,1},{2,98}... | collective-permute-start | bytes 1179656 | tf_op jit(solution)/shard_map/ppermute | solution.py:18
  46.0 3.0 %collective-permute-start.3 = (f32[192,512]{1,0:T(8,128)S(1)}, f32[192,512]{1,0:T(8,128)S(1)}, u32[]{:S(2)}, u32[]{:S(2)}) collective-permute-start(f32[192,512]{1,0:T(8,128)S(1)} %collective-permute-done.1.refs_1_), channel_id=1, source_target_pairs={{0,32},{32,0},{64,96},{96,64},{1,33},{33,1},{65,97},{97,65},{2,34}... | collective-permute-start | bytes 1179656 | tf_op jit(solution)/shard_map/ppermute | solution.py:18
  49.0 2.6 %collective-permute-start.4 = (f32[192,512]{1,0:T(8,128)S(1)}, f32[192,512]{1,0:T(8,128)S(1)}, u32[]{:S(2)}, u32[]{:S(2)}) collective-permute-start(f32[192,512]{1,0:T(8,128)S(1)} %collective-permute-done.2.refs_2_), channel_id=1, source_target_pairs={{0,96},{32,64},{64,32},{96,0},{1,97},{33,65},{65,33},{97,1},{2,98}... | collective-permute-start | bytes 1179656 | tf_op jit(solution)/shard_map/ppermute | solution.py:18
  51.6 4.4 %collective-permute-done.5.refs_7_ = f32[192,512]{1,0:T(8,128)S(1)} collective-permute-done((f32[192,512]{1,0:T(8,128)S(1)}, f32[192,512]{1,0:T(8,128)S(1)}, u32[]{:S(2)}, u32[]{:S(2)}) %collective-permute-start.5) | collective-permute-done | bytes 393248 | tf_op jit(solution)/shard_map/ppermute | solution.py:18
  56.0 3.0 %collective-permute-start.6 = (f32[192,512]{1,0:T(8,128)S(1)}, f32[192,512]{1,0:T(8,128)S(1)}, u32[]{:S(2)}, u32[]{:S(2)}) collective-permute-start(f32[192,512]{1,0:T(8,128)S(1)} %collective-permute-done.5.refs_7_), channel_id=1, source_target_pairs={{0,32},{32,0},{64,96},{96,64},{1,33},{33,1},{65,97},{97,65},{2,34}... | collective-permute-start | bytes 1179656 | tf_op jit(solution)/shard_map/ppermute | solution.py:18
  59.1 5.3 %collective-permute-done.7.refs_6_ = f32[192,512]{1,0:T(8,128)S(1)} collective-permute-done((f32[192,512]{1,0:T(8,128)}, f32[192,512]{1,0:T(8,128)S(1)}, u32[]{:S(2)}, u32[]{:S(2)}) %collective-permute-start.7) | collective-permute-done | bytes 393248 | tf_op jit(solution)/shard_map/ppermute | solution.py:18
  64.4 6.3 %collective-permute-done.4.refs_4_ = f32[192,512]{1,0:T(8,128)S(1)} collective-permute-done((f32[192,512]{1,0:T(8,128)S(1)}, f32[192,512]{1,0:T(8,128)S(1)}, u32[]{:S(2)}, u32[]{:S(2)}) %collective-permute-start.4) | collective-permute-done | bytes 393248 | tf_op jit(solution)/shard_map/ppermute | solution.py:18
  70.7 1.0 copy-done.4
  71.7 10.8 %shard_map.68 = (f32[4,192,512]{2,1,0:T(8,128)S(1)}, f32[4,192,512]{2,1,0:T(8,128)S(1)}) custom-call(s32[9]{0:T(128)S(1)} %pad_add_fusion.place_ref, f32[3072,1536]{1,0:T(8,128)} %a_ref.3, f32[192,512]{1,0:T(8,128)S(1)} %copy-done.4, f32[192,512]{1,0:T(8,128)S(1)} %collective-permute-done.1.refs_1_, f32[192,512]{1,0:T(8,128)S(1)} %collective-permute-done.2.refs_2_, ...), custom_call_target="tpu_custom_call" | custom-call | flops 7247757312 | bytes 15728640 | tf_op jit(solution)/shard_map/pallas_call | solution.py:122
  82.6 3.4 %collective-permute-done.8 = f32[4,192,512]{2,1,0:T(8,128)S(1)} collective-permute-done((f32[4,192,512]{2,1,0:T(8,128)S(1)}, f32[4,192,512]{2,1,0:T(8,128)S(1)}, u32[]{:S(2)}, u32[]{:S(2)}) %collective-permute-start.8) | collective-permute-done | bytes 1572896 | tf_op jit(solution)/shard_map/ppermute | solution.py:18
  86.0 1.5 add.104.near_ref
  87.6 0.9 copy-done.5
  88.5 10.9 %shard_map.69 = (f32[4,192,512]{2,1,0:T(8,128)S(1)}, f32[4,192,512]{2,1,0:T(8,128)S(1)}) custom-call(s32[9]{0:T(128)S(1)} %pad_add_fusion.place_ref, f32[3072,1536]{1,0:T(8,128)} %a_ref.3, f32[192,512]{1,0:T(8,128)S(1)} %copy-done.5, f32[192,512]{1,0:T(8,128)S(1)} %collective-permute-done.1.refs_1_, f32[192,512]{1,0:T(8,128)S(1)} %collective-permute-done.2.refs_2_, ...), custom_call_target="tpu_custom_call" | custom-call | flops 7247757312 | bytes 15728640 | tf_op jit(solution)/shard_map/pallas_call | solution.py:122
  99.6 3.3 %collective-permute-done.9 = f32[4,192,512]{2,1,0:T(8,128)S(1)} collective-permute-done((f32[4,192,512]{2,1,0:T(8,128)S(1)}, f32[4,192,512]{2,1,0:T(8,128)S(1)}, u32[]{:S(2)}, u32[]{:S(2)}) %collective-permute-start.9) | collective-permute-done | bytes 1572896 | tf_op jit(solution)/shard_map/ppermute | solution.py:18
  102.9 1.5 add.105.far_ref
  104.6 1.2 copy-done
  105.8 1.4 copy-done.1
  107.2 1.9 %copy-done.2 = f32[1536,512]{1,0:T(8,128)S(1)} copy-done((f32[1536,512]{1,0:T(8,128)S(1)}, f32[1536,512]{1,0:T(8,128)}, u32[]{:S(2)}) %copy-start.2) | copy-done | bytes 3145752
  109.2 2.7 %shard_map.71 = (f32[256,256]{1,0:T(8,128)S(1)}, f32[256,256]{1,0:T(8,128)S(1)}) custom-call(f32[4,192,512]{2,1,0:T(8,128)S(1)} %copy-done, f32[4,192,512]{2,1,0:T(8,128)S(1)} %copy-done.1, f32[8,192,512]{2,1,0:T(8,128)S(1)} %bitcast.38), custom_call_target="tpu_custom_call" | custom-call | flops 1207959552 | bytes 6291456 | tf_op jit(solution)/shard_map/pallas_call | solution.py:157
  112.1 1.4 collective-permute-done.11
  113.6 2.1 %collective-permute-start.12 = (f32[64,256]{1,0:T(8,128)S(1)}, f32[64,256]{1,0:T(8,128)S(1)}, u32[]{:S(2)}, u32[]{:S(2)}) collective-permute-start(f32[64,256]{1,0:T(8,128)S(1)} %get-tuple-element.18), channel_id=1, source_target_pairs={{0,32},{32,64},{64,96},{96,0},{1,33},{33,65},{65,97},{97,1},{2,34}... | collective-permute-start | bytes 196616 | tf_op jit(solution)/shard_map/ppermute | solution.py:18
  115.7 2.4 %collective-permute-start.13 = (f32[64,256]{1,0:T(8,128)S(1)}, f32[64,256]{1,0:T(8,128)S(1)}, u32[]{:S(2)}, u32[]{:S(2)}) collective-permute-start(f32[64,256]{1,0:T(8,128)S(1)} %get-tuple-element.20), channel_id=1, source_target_pairs={{0,64},{32,96},{64,0},{96,32},{1,65},{33,97},{65,1},{97,33},{2,66}... | collective-permute-start | bytes 196616 | tf_op jit(solution)/shard_map/ppermute | solution.py:18
  118.1 2.0 %collective-permute-start.14 = (f32[64,256]{1,0:T(8,128)S(1)}, f32[64,256]{1,0:T(8,128)S(1)}, u32[]{:S(2)}, u32[]{:S(2)}) collective-permute-start(f32[64,256]{1,0:T(8,128)S(1)} %get-tuple-element.19), channel_id=1, source_target_pairs={{0,96},{32,0},{64,32},{96,64},{1,97},{33,1},{65,33},{97,65},{2,98}... | collective-permute-start | bytes 196616 | tf_op jit(solution)/shard_map/ppermute | solution.py:18
  120.1 1.7 collective-permute-done.13
  122.4 3.2 %collective-permute-start.15 = (f32[64,256]{1,0:T(8,128)S(1)}, f32[64,256]{1,0:T(8,128)S(1)}, u32[]{:S(2)}, u32[]{:S(2)}) collective-permute-start(f32[64,256]{1,0:T(8,128)S(1)} %add_add_fusion.1), channel_id=1, source_target_pairs={{0,4},{4,8},{8,12},{12,0},{1,5},{5,9},{9,13},{13,1},{2,6},{6,10},{... | collective-permute-start | bytes 196616 | tf_op jit(solution)/shard_map/ppermute | solution.py:18
  125.6 2.8 %collective-permute-start.17 = (f32[64,256]{1,0:T(8,128)S(1)}, f32[64,256]{1,0:T(8,128)S(1)}, u32[]{:S(2)}, u32[]{:S(2)}) collective-permute-start(f32[64,256]{1,0:T(8,128)S(1)} %add_add_fusion.1), channel_id=1, source_target_pairs={{0,12},{4,0},{8,4},{12,8},{1,13},{5,1},{9,5},{13,9},{2,14},{6,2},{... | collective-permute-start | bytes 196616 | tf_op jit(solution)/shard_map/ppermute | solution.py:18
  128.4 4.0 %collective-permute-done.16 = f32[64,256]{1,0:T(8,128)S(1)} collective-permute-done((f32[64,256]{1,0:T(8,128)S(1)}, f32[64,256]{1,0:T(8,128)S(1)}, u32[]{:S(2)}, u32[]{:S(2)}) %collective-permute-start.16) | collective-permute-done | bytes 65568 | tf_op jit(solution)/shard_map/ppermute | solution.py:18
  132.4 2.4 %collective-permute-start.18 = (f32[64,256]{1,0:T(8,128)S(1)}, f32[64,256]{1,0:T(8,128)S(1)}, u32[]{:S(2)}, u32[]{:S(2)}) collective-permute-start(f32[64,256]{1,0:T(8,128)S(1)} %add_add_fusion), channel_id=1, source_target_pairs={{0,2},{2,0},{1,3},{3,1},{4,6},{6,4},{5,7},{7,5},{8,10},{10,8},{9,1... | collective-permute-start | bytes 196616 | tf_op jit(solution)/shard_map/ppermute | solution.py:18
  134.8 2.2 %collective-permute-done.18 = f32[64,256]{1,0:T(8,128)S(1)} collective-permute-done((f32[64,256]{1,0:T(8,128)S(1)}, f32[64,256]{1,0:T(8,128)S(1)}, u32[]{:S(2)}, u32[]{:S(2)}) %collective-permute-start.18) | collective-permute-done | bytes 65568 | tf_op jit(solution)/shard_map/ppermute | solution.py:18
  137.1 4.5 %collective-permute-start.19 = (f32[64,256]{1,0:T(8,128)S(1)}, f32[64,256]{1,0:T(8,128)S(1)}, u32[]{:S(2)}, u32[]{:S(2)}) collective-permute-start(f32[64,256]{1,0:T(8,128)S(1)} %add.121), channel_id=1, source_target_pairs={{0,16},{16,0},{1,17},{17,1},{2,18},{18,2},{3,19},{19,3},{4,20},{20... | collective-permute-start | bytes 196616 | tf_op jit(solution)/shard_map/ppermute | solution.py:18
  141.6 2.2 %collective-permute-done.19 = f32[64,256]{1,0:T(8,128)S(1)} collective-permute-done((f32[64,256]{1,0:T(8,128)S(1)}, f32[64,256]{1,0:T(8,128)S(1)}, u32[]{:S(2)}, u32[]{:S(2)}) %collective-permute-start.19) | collective-permute-done | bytes 65568 | tf_op jit(solution)/shard_map/ppermute | solution.py:18
  143.9 2.2 %collective-permute-start.20 = (f32[64,256]{1,0:T(8,128)S(1)}, f32[64,256]{1,0:T(8,128)S(1)}, u32[]{:S(2)}, u32[]{:S(2)}) collective-permute-start(f32[64,256]{1,0:T(8,128)S(1)} %add.122), channel_id=1, source_target_pairs={{0,96},{32,0},{64,32},{96,64},{1,97},{33,1},{65,33},{97,65},{2,98}... | collective-permute-start | bytes 196616 | tf_op jit(solution)/shard_map/ppermute | solution.py:18
  146.1 1.1 select_bitcast_fusion
  147.2 1.9 %collective-permute-start.10 = (f32[192,512]{1,0:T(8,128)S(1)}, f32[192,512]{1,0:T(8,128)S(1)}, u32[]{:S(2)}, u32[]{:S(2)}) collective-permute-start(f32[192,512]{1,0:T(8,128)S(1)} %select_bitcast_fusion), channel_id=1, source_target_pairs={{0,2},{2,0},{1,3},{3,1},{4,6},{6,4},{5,7},{7,5},{8,10},{10,8},{9,1... | collective-permute-start | bytes 1179656 | tf_op jit(solution)/shard_map/ppermute | solution.py:18
  149.1 1.1 collective-permute-start.21
  150.2 0.9 collective-permute-start.22
  151.2 3.7 %collective-permute-done.21 = f32[64,256]{1,0:T(8,128)S(1)} collective-permute-done((f32[64,256]{1,0:T(8,128)S(1)}, f32[64,256]{1,0:T(8,128)S(1)}, u32[]{:S(2)}, u32[]{:S(2)}) %collective-permute-start.21) | collective-permute-done | bytes 65568 | tf_op jit(solution)/shard_map/ppermute | solution.py:18
  154.9 0.8 collective-permute-done.22
  156.9 0.7 copy-done.8
  157.7 1.2 bitcast_add_fusion
  159.0 0.8 pad_maximum_fusion.2
  159.8 0.8 pad_maximum_fusion
  (74 shorter events, 5.1 us)
Async XLA Ops:
  8.0 96.6 %all-gather.3.cloned.1.call-start = ((), (), s32[]{:S(2)}) async-start(), calls=%async_computation.4 | async-start | bytes 3538944 | tf_op jit(solution)/shard_map/all_gather | solution.py:196
  12.1 0.8 copy-start.6
  12.1 0.7 collective-permute-start
  12.8 0.7 copy-start.3
  13.6 132.5 %reduce-scatter.3.cloned.1.call-start = ((), (), s32[]{:S(2)}) async-start(), calls=%async_computation.2 | async-start | bytes 1966080 | tf_op jit(solution)/shard_map/reduce_scatter | solution.py:204
  13.6 24.4 %collective-permute-start.1 = (f32[192,512]{1,0:T(8,128)}, f32[192,512]{1,0:T(8,128)S(1)}, u32[]{:S(2)}, u32[]{:S(2)}) collective-permute-start(f32[192,512]{1,0:T(8,128)} %copy-done.3), channel_id=1, source_target_pairs={{0,16},{16,0},{1,17},{17,1},{2,18},{18,2},{3,19},{19,3},{4,20},{20... | collective-permute-start | bytes 1179656 | tf_op jit(solution)/shard_map/ppermute | solution.py:18
  28.0 21.0 %collective-permute-start.2 = (f32[192,512]{1,0:T(8,128)}, f32[192,512]{1,0:T(8,128)S(1)}, u32[]{:S(2)}, u32[]{:S(2)}) collective-permute-start(f32[192,512]{1,0:T(8,128)} %copy-done.3), channel_id=1, source_target_pairs={{0,32},{32,0},{64,96},{96,64},{1,33},{33,1},{65,97},{97,65},{2,34}... | collective-permute-start | bytes 1179656 | tf_op jit(solution)/shard_map/ppermute | solution.py:18
  38.0 17.9 %collective-permute-start.5 = (f32[192,512]{1,0:T(8,128)S(1)}, f32[192,512]{1,0:T(8,128)S(1)}, u32[]{:S(2)}, u32[]{:S(2)}) collective-permute-start(f32[192,512]{1,0:T(8,128)S(1)} %collective-permute-done.1.refs_1_), channel_id=1, source_target_pairs={{0,96},{32,64},{64,32},{96,0},{1,97},{33,65},{65,33},{97,1},{2,98}... | collective-permute-start | bytes 1179656 | tf_op jit(solution)/shard_map/ppermute | solution.py:18
  45.9 18.5 %collective-permute-start.7 = (f32[192,512]{1,0:T(8,128)}, f32[192,512]{1,0:T(8,128)S(1)}, u32[]{:S(2)}, u32[]{:S(2)}) collective-permute-start(f32[192,512]{1,0:T(8,128)} %copy-done.3), channel_id=1, source_target_pairs={{0,96},{32,64},{64,32},{96,0},{1,97},{33,65},{65,33},{97,1},{2,98}... | collective-permute-start | bytes 1179656 | tf_op jit(solution)/shard_map/ppermute | solution.py:18
  46.0 18.4 %collective-permute-start.3 = (f32[192,512]{1,0:T(8,128)S(1)}, f32[192,512]{1,0:T(8,128)S(1)}, u32[]{:S(2)}, u32[]{:S(2)}) collective-permute-start(f32[192,512]{1,0:T(8,128)S(1)} %collective-permute-done.1.refs_1_), channel_id=1, source_target_pairs={{0,32},{32,0},{64,96},{96,64},{1,33},{33,1},{65,97},{97,65},{2,34}... | collective-permute-start | bytes 1179656 | tf_op jit(solution)/shard_map/ppermute | solution.py:18
  49.0 21.6 %collective-permute-start.4 = (f32[192,512]{1,0:T(8,128)S(1)}, f32[192,512]{1,0:T(8,128)S(1)}, u32[]{:S(2)}, u32[]{:S(2)}) collective-permute-start(f32[192,512]{1,0:T(8,128)S(1)} %collective-permute-done.2.refs_2_), channel_id=1, source_target_pairs={{0,96},{32,64},{64,32},{96,0},{1,97},{33,65},{65,33},{97,1},{2,98}... | collective-permute-start | bytes 1179656 | tf_op jit(solution)/shard_map/ppermute | solution.py:18
  56.0 14.7 %collective-permute-start.6 = (f32[192,512]{1,0:T(8,128)S(1)}, f32[192,512]{1,0:T(8,128)S(1)}, u32[]{:S(2)}, u32[]{:S(2)}) collective-permute-start(f32[192,512]{1,0:T(8,128)S(1)} %collective-permute-done.5.refs_7_), channel_id=1, source_target_pairs={{0,32},{32,0},{64,96},{96,64},{1,33},{33,1},{65,97},{97,65},{2,34}... | collective-permute-start | bytes 1179656 | tf_op jit(solution)/shard_map/ppermute | solution.py:18
  70.7 1.0 copy-start.4
  82.5 3.5 %collective-permute-start.8 = (f32[4,192,512]{2,1,0:T(8,128)S(1)}, f32[4,192,512]{2,1,0:T(8,128)S(1)}, u32[]{:S(2)}, u32[]{:S(2)}) collective-permute-start(f32[4,192,512]{2,1,0:T(8,128)S(1)} %get-tuple-element.9), channel_id=1, source_target_pairs={{0,1},{1,0},{2,3},{3,2},{4,5},{5,4},{6,7},{7,6},{8,9},{9,8},{10,11... | collective-permute-start | bytes 4718600 | tf_op jit(solution)/shard_map/ppermute | solution.py:18
  87.5 1.0 copy-start.5
  87.5 58.5 %reduce-scatter.5.cloned.1.call-start = ((), (), s32[]{:S(2)}) async-start(), calls=%async_computation.3 | async-start | bytes 1966080 | tf_op jit(solution)/shard_map/reduce_scatter | solution.py:204
  99.4 3.5 %collective-permute-start.9 = (f32[4,192,512]{2,1,0:T(8,128)S(1)}, f32[4,192,512]{2,1,0:T(8,128)S(1)}, u32[]{:S(2)}, u32[]{:S(2)}) collective-permute-start(f32[4,192,512]{2,1,0:T(8,128)S(1)} %get-tuple-element.11), channel_id=1, source_target_pairs={{0,1},{1,0},{2,3},{3,2},{4,5},{5,4},{6,7},{7,6},{8,9},{9,8},{10,11... | collective-permute-start | bytes 4718600 | tf_op jit(solution)/shard_map/ppermute | solution.py:18
  104.4 1.4 copy-start
  105.8 1.4 copy-start.1
  107.2 1.9 %copy-start.2 = (f32[1536,512]{1,0:T(8,128)S(1)}, f32[1536,512]{1,0:T(8,128)}, u32[]{:S(2)}) copy-start(f32[1536,512]{1,0:T(8,128)} %all-gather.3.cloned.1.call-done) | copy-start | bytes 9437188
  111.9 1.6 collective-permute-start.11
  113.6 6.5 %collective-permute-start.12 = (f32[64,256]{1,0:T(8,128)S(1)}, f32[64,256]{1,0:T(8,128)S(1)}, u32[]{:S(2)}, u32[]{:S(2)}) collective-permute-start(f32[64,256]{1,0:T(8,128)S(1)} %get-tuple-element.18), channel_id=1, source_target_pairs={{0,32},{32,64},{64,96},{96,0},{1,33},{33,65},{65,97},{97,1},{2,34}... | collective-permute-start | bytes 196616 | tf_op jit(solution)/shard_map/ppermute | solution.py:18
  115.7 6.1 %collective-permute-start.13 = (f32[64,256]{1,0:T(8,128)S(1)}, f32[64,256]{1,0:T(8,128)S(1)}, u32[]{:S(2)}, u32[]{:S(2)}) collective-permute-start(f32[64,256]{1,0:T(8,128)S(1)} %get-tuple-element.20), channel_id=1, source_target_pairs={{0,64},{32,96},{64,0},{96,32},{1,65},{33,97},{65,1},{97,33},{2,66}... | collective-permute-start | bytes 196616 | tf_op jit(solution)/shard_map/ppermute | solution.py:18
  118.1 4.3 %collective-permute-start.14 = (f32[64,256]{1,0:T(8,128)S(1)}, f32[64,256]{1,0:T(8,128)S(1)}, u32[]{:S(2)}, u32[]{:S(2)}) collective-permute-start(f32[64,256]{1,0:T(8,128)S(1)} %get-tuple-element.19), channel_id=1, source_target_pairs={{0,96},{32,0},{64,32},{96,64},{1,97},{33,1},{65,33},{97,65},{2,98}... | collective-permute-start | bytes 196616 | tf_op jit(solution)/shard_map/ppermute | solution.py:18
  122.4 6.0 %collective-permute-start.15 = (f32[64,256]{1,0:T(8,128)S(1)}, f32[64,256]{1,0:T(8,128)S(1)}, u32[]{:S(2)}, u32[]{:S(2)}) collective-permute-start(f32[64,256]{1,0:T(8,128)S(1)} %add_add_fusion.1), channel_id=1, source_target_pairs={{0,4},{4,8},{8,12},{12,0},{1,5},{5,9},{9,13},{13,1},{2,6},{6,10},{... | collective-permute-start | bytes 196616 | tf_op jit(solution)/shard_map/ppermute | solution.py:18
  125.6 6.8 %collective-permute-start.16 = (f32[64,256]{1,0:T(8,128)S(1)}, f32[64,256]{1,0:T(8,128)S(1)}, u32[]{:S(2)}, u32[]{:S(2)}) collective-permute-start(f32[64,256]{1,0:T(8,128)S(1)} %add_add_fusion.1), channel_id=1, source_target_pairs={{0,8},{4,12},{8,0},{12,4},{1,9},{5,13},{9,1},{13,5},{2,10},{6,14},... | collective-permute-start | bytes 196616 | tf_op jit(solution)/shard_map/ppermute | solution.py:18
  125.6 6.8 %collective-permute-start.17 = (f32[64,256]{1,0:T(8,128)S(1)}, f32[64,256]{1,0:T(8,128)S(1)}, u32[]{:S(2)}, u32[]{:S(2)}) collective-permute-start(f32[64,256]{1,0:T(8,128)S(1)} %add_add_fusion.1), channel_id=1, source_target_pairs={{0,12},{4,0},{8,4},{12,8},{1,13},{5,1},{9,5},{13,9},{2,14},{6,2},{... | collective-permute-start | bytes 196616 | tf_op jit(solution)/shard_map/ppermute | solution.py:18
  132.4 4.7 %collective-permute-start.18 = (f32[64,256]{1,0:T(8,128)S(1)}, f32[64,256]{1,0:T(8,128)S(1)}, u32[]{:S(2)}, u32[]{:S(2)}) collective-permute-start(f32[64,256]{1,0:T(8,128)S(1)} %add_add_fusion), channel_id=1, source_target_pairs={{0,2},{2,0},{1,3},{3,1},{4,6},{6,4},{5,7},{7,5},{8,10},{10,8},{9,1... | collective-permute-start | bytes 196616 | tf_op jit(solution)/shard_map/ppermute | solution.py:18
  137.1 6.8 %collective-permute-start.19 = (f32[64,256]{1,0:T(8,128)S(1)}, f32[64,256]{1,0:T(8,128)S(1)}, u32[]{:S(2)}, u32[]{:S(2)}) collective-permute-start(f32[64,256]{1,0:T(8,128)S(1)} %add.121), channel_id=1, source_target_pairs={{0,16},{16,0},{1,17},{17,1},{2,18},{18,2},{3,19},{19,3},{4,20},{20... | collective-permute-start | bytes 196616 | tf_op jit(solution)/shard_map/ppermute | solution.py:18
  143.9 7.3 %collective-permute-start.20 = (f32[64,256]{1,0:T(8,128)S(1)}, f32[64,256]{1,0:T(8,128)S(1)}, u32[]{:S(2)}, u32[]{:S(2)}) collective-permute-start(f32[64,256]{1,0:T(8,128)S(1)} %add.122), channel_id=1, source_target_pairs={{0,96},{32,0},{64,32},{96,64},{1,97},{33,1},{65,33},{97,65},{2,98}... | collective-permute-start | bytes 196616 | tf_op jit(solution)/shard_map/ppermute | solution.py:18
  146.1 11.6 %copy-start.9 = (f32[1,192,512]{2,1,0:T(8,128)S(1)}, f32[1,192,512]{2,1,0:T(8,128)}, u32[]{:S(2)}) copy-start(f32[1,192,512]{2,1,0:T(8,128)} %reduce-scatter.3.cloned.1.call-done) | copy-start | bytes 1179652
  146.1 11.6 %copy-start.10 = (f32[1,192,512]{2,1,0:T(8,128)S(1)}, f32[1,192,512]{2,1,0:T(8,128)}, u32[]{:S(2)}) copy-start(f32[1,192,512]{2,1,0:T(8,128)} %reduce-scatter.5.cloned.1.call-done) | copy-start | bytes 1179652
  147.2 9.7 %collective-permute-start.10 = (f32[192,512]{1,0:T(8,128)S(1)}, f32[192,512]{1,0:T(8,128)S(1)}, u32[]{:S(2)}, u32[]{:S(2)}) collective-permute-start(f32[192,512]{1,0:T(8,128)S(1)} %select_bitcast_fusion), channel_id=1, source_target_pairs={{0,2},{2,0},{1,3},{3,1},{4,6},{6,4},{5,7},{7,5},{8,10},{10,8},{9,1... | collective-permute-start | bytes 1179656 | tf_op jit(solution)/shard_map/ppermute | solution.py:18
  149.1 5.8 %collective-permute-start.21 = (f32[64,256]{1,0:T(8,128)S(1)}, f32[64,256]{1,0:T(8,128)S(1)}, u32[]{:S(2)}, u32[]{:S(2)}) collective-permute-start(f32[64,256]{1,0:T(8,128)S(1)} %add.122), channel_id=1, source_target_pairs={{0,64},{32,96},{64,0},{96,32},{1,65},{33,97},{65,1},{97,33},{2,66}... | collective-permute-start | bytes 196616 | tf_op jit(solution)/shard_map/ppermute | solution.py:18
  150.2 5.5 %collective-permute-start.22 = (f32[64,256]{1,0:T(8,128)S(1)}, f32[64,256]{1,0:T(8,128)S(1)}, u32[]{:S(2)}, u32[]{:S(2)}) collective-permute-start(f32[64,256]{1,0:T(8,128)S(1)} %add.122), channel_id=1, source_target_pairs={{0,32},{32,64},{64,96},{96,0},{1,33},{33,65},{65,97},{97,1},{2,34}... | collective-permute-start | bytes 196616 | tf_op jit(solution)/shard_map/ppermute | solution.py:18
  156.9 0.7 copy-start.8
  157.6 2.1 %copy-start.7 = (f32[256,256]{1,0:T(8,128)S(1)}, f32[256,256]{1,0:T(8,128)}, u32[]{:S(2)}) copy-start(f32[256,256]{1,0:T(8,128)} %shard_map.72) | copy-start | bytes 786436
  157.6 2.1 %copy-start.11 = (f32[2,256,256]{2,1,0:T(8,128)S(1)}, f32[2,256,256]{2,1,0:T(8,128)}, u32[]{:S(2)}) copy-start(f32[2,256,256]{2,1,0:T(8,128)} %param.8) | copy-start | bytes 1572868
  157.7 2.1 %collective-permute-start.23 = (f32[256,256]{1,0:T(8,128)}, f32[256,256]{1,0:T(8,128)S(1)}, u32[]{:S(2)}, u32[]{:S(2)}) collective-permute-start(f32[256,256]{1,0:T(8,128)} %shard_map.72), channel_id=1, source_target_pairs={{0,1},{1,0},{2,3},{3,2},{4,5},{5,4},{6,7},{7,6},{8,9},{9,8},{10,11... | collective-permute-start | bytes 786440 | tf_op jit(solution)/shard_map/ppermute | solution.py:18
Sparse Core Ops, SparseCore 0:
  13.7 90.8 all-gather.2
Sparse Core Ops, SparseCore 1:
  87.6 29.1 reduce-scatter.2
  119.1 25.8 reduce-scatter.4

commit v7 on v5

--- a/solution.py
+++ b/solution.py
@@ -55,7 +55,7 @@
     return lax.dynamic_slice_in_dim(twice, (3 - me) * x.shape[0], 4 * x.shape[0], 0)
 
 
-def total(first, second):
+def total(first, second, before):
     k = lax.axis_index("k")
     mine = jnp.where(k == 0, first, second) + swap(jnp.where(k == 0, second, first), "k")
     mine = scatter_four(mine, "y")
@@ -63,6 +63,7 @@
     mine = mine + swap(mine, "xl")
     mine = mine + swap(mine, "xh")
     mine = gather_four(mine, "y")
+    (mine,) = later([mine], [before])
     other = swap(mine, "k")
     return jnp.where(k == 0, mine, other), jnp.where(k == 0, other, mine)
 
@@ -77,6 +78,19 @@
     bh, bl = halves(b)
     f = lambda p, q: lax.dot_general(p, q, (dims, ((), ())), preferred_element_type=F32)
     return f(ah, bh) + (f(ah, bl) + f(al, bh))
+
+
+def later(xs, after):
+    anywhere = pl.BlockSpec(memory_space=pl.ANY)
+    return pl.pallas_call(
+        lambda *refs: None,
+        grid=(1,),
+        in_specs=[anywhere] * len(xs) + [pl.BlockSpec((8, 128), lambda i: (0, 0)) for _ in after],
+        out_specs=[anywhere] * len(xs),
+        out_shape=[jax.ShapeDtypeStruct(x.shape, x.dtype) for x in xs],
+        input_output_aliases={i: i for i in range(len(xs))},
+        cost_estimate=pl.CostEstimate(flops=0, bytes_accessed=0, transcendentals=0),
+    )(*xs, *after)
 
 
 def product_kernel(place_ref, a_ref, *refs):
@@ -154,13 +168,14 @@
 
 
 def gather_column(mine):
-    pair = swap(mine, "xh")
     one, three = (lambda i: i ^ 1), (lambda i: i ^ 3)
     mine1 = send(mine, "y", 4, one)
     mine3 = send(mine, "y", 4, three)
+    (pair,) = later([swap(mine, "xh")], [mine1, mine3])
     pair3 = send(pair, "y", 4, three)
+    pair1 = send(pair, "y", 4, one)
+    pair3, mine1 = later([pair3, mine1], [pair1])
     mine2 = send(mine1, "y", 4, three)
-    pair1 = send(pair, "y", 4, one)
     pair2 = send(pair3, "y", 4, one)
     return [mine, pair, mine1, pair1, mine2, pair2, mine3, pair3]
 
@@ -187,9 +202,10 @@
     summed = lax.psum_scatter(summed.reshape(4, 2, *summed.shape[1:]), "z", scatter_dimension=0, tiled=False)
     kept = lax.dynamic_slice_in_dim(summed, xl, 1, 0)[0]
     given = lax.dynamic_slice_in_dim(summed, 1 - xl, 1, 0)[0]
-    whole = kept + swap(given, "xl")
+    taken = swap(given, "xl")
+    whole = kept + taken
     panels = [-masks[s] * whole[:, s * wide : (s + 1) * wide] for s in range(NS)]
-    first, second = total(first, second)
+    first, second = total(first, second, taken)
     return jnp.stack(panels), jnp.stack([diag_block[0] + first, diag_block[1] + second])
 
 

time: 173 us -> 178 us (1.029)
  local copies, waits for them, and re-layouts: 4.86 us -> 13.2 us
  starting transfers between devices: 47.9 us -> 42.9 us
  waiting for transfers between devices: 73.6 us -> 70.2 us
  other arithmetic: 4.62 us -> 6.66 us
  Pallas kernels: 22.6 us -> 24.6 us
    unnamed x18 -> x38, local copies, waits for them, and re-layouts: 2.63 us -> 10.3 us
    all_gather x1, waiting for transfers between devices: 7.95 us -> 2.87 us  [local(): band = lax.all_gather(normed, ('z', 'xl'), axis=0, tiled=False)]
    ppermute x22, starting transfers between devices: 47.1 us -> 42.2 us  [send(): return lax.ppermute(x, axis, [(i, to(i)) for i in range(size)])]
    pallas_call x0 -> x3, Pallas kernels: none -> 2.05 us  [later(): pl.pallas_call(lambda *refs: None, grid=(1,), in_specs=[anywhere] * len(x...]
  transfers between devices with their start and end apart: 25 -> 25, of which waited for: 19 -> 20; matrix products, arithmetic and copies ran while one was open for 3% -> 3% of each run, Pallas kernels for 13% -> 14%
where the time goes in v7:
time: 178 us; the launch traced here: 176 us
  waiting for transfers between devices  70.2 us (39%)
  starting transfers between devices  42.9 us (24%)
  Pallas kernels  24.6 us (14%)
  between operations  15.7 us (9%)
  local copies, waits for them, and re-layouts  13.2 us (7%)
  other arithmetic  6.66 us (4%)
  matrix products  2.77 us (2%)
    ppermute x22, waiting for transfers between devices, send(): return lax.ppermute(x, axis, [(i, to(i)) for i in range(size)])  67.3 us
    ppermute x22, starting transfers between devices, send(): return lax.ppermute(x, axis, [(i, to(i)) for i in range(size)])  42.2 us
    pallas_call x1, Pallas kernels, product(): pl.pallas_call(product_kernel, grid_spec=pltpu.PrefetchScalarGridSpec(num...  19 us
    unnamed x38, local copies, waits for them, and re-layouts  10.3 us
    pallas_call x1, Pallas kernels, updates(): pl.pallas_call(update_kernel, grid=(blocks,), in_specs=[spec] * 2, out_sp...  3.62 us
  transfers between devices with their start and end apart: 25, of which 20 were waited for; matrix products, arithmetic and copies ran while one was open for 3% of the time, Pallas kernels for 14%

profile of v7, /device:TPU:0, one launch (start us, length us, event | category | flops | bytes accessed | tf_op | source)
XLA Modules:
  0.0 176.2 jit_solution(1644351708003613548)
XLA Ops:
  8.1 0.8 fusion.20
  9.2 1.4 convolution_multiply_fusion
  10.6 1.4 convolution_multiply_fusion.1
  12.8 14.3 %collective-permute-start.1 = (f32[192,512]{1,0:T(8,128)S(1)}, f32[192,512]{1,0:T(8,128)S(1)}, u32[]{:S(2)}, u32[]{:S(2)}) collective-permute-start(f32[192,512]{1,0:T(8,128)S(1)} %collective-permute-done.refs_0_), channel_id=1, source_target_pairs={{0,16},{16,0},{1,17},{17,1},{2,18},{18,2},{3,19},{19,3},{4,20},{20... | collective-permute-start | bytes 1179656 | tf_op jit(solution)/shard_map/ppermute | solution.py:18
  27.1 3.8 %collective-permute-start.2 = (f32[192,512]{1,0:T(8,128)S(1)}, f32[192,512]{1,0:T(8,128)S(1)}, u32[]{:S(2)}, u32[]{:S(2)}) collective-permute-start(f32[192,512]{1,0:T(8,128)S(1)} %collective-permute-done.refs_0_), channel_id=1, source_target_pairs={{0,32},{32,0},{64,96},{96,64},{1,33},{33,1},{65,97},{97,65},{2,34}... | collective-permute-start | bytes 1179656 | tf_op jit(solution)/shard_map/ppermute | solution.py:18
  30.9 6.2 %collective-permute-start.3 = (f32[192,512]{1,0:T(8,128)S(1)}, f32[192,512]{1,0:T(8,128)S(1)}, u32[]{:S(2)}, u32[]{:S(2)}) collective-permute-start(f32[192,512]{1,0:T(8,128)S(1)} %collective-permute-done.refs_0_), channel_id=1, source_target_pairs={{0,96},{32,64},{64,32},{96,0},{1,97},{33,65},{65,33},{97,1},{2,98}... | collective-permute-start | bytes 1179656 | tf_op jit(solution)/shard_map/ppermute | solution.py:18
  37.3 0.8 collective-permute-done.2.refs_1_
  38.1 8.2 %collective-permute-done.3.refs_2_.refs_6_ = f32[192,512]{1,0:T(8,128)S(1)} collective-permute-done((f32[192,512]{1,0:T(8,128)S(1)}, f32[192,512]{1,0:T(8,128)S(1)}, u32[]{:S(2)}, u32[]{:S(2)}) %collective-permute-start.3) | collective-permute-done | bytes 393248 | tf_op jit(solution)/shard_map/ppermute | solution.py:18
  47.8 2.6 %collective-permute-start.4 = (f32[192,512]{1,0:T(8,128)}, f32[192,512]{1,0:T(8,128)S(1)}, u32[]{:S(2)}, u32[]{:S(2)}) collective-permute-start(f32[192,512]{1,0:T(8,128)} %shard_map.68.refs_1_), channel_id=1, source_target_pairs={{0,96},{32,64},{64,32},{96,0},{1,97},{33,65},{65,33},{97,1},{2,98}... | collective-permute-start | bytes 1179656 | tf_op jit(solution)/shard_map/ppermute | solution.py:18
  50.3 9.2 %collective-permute-done.4.refs_0_ = f32[192,512]{1,0:T(8,128)S(1)} collective-permute-done((f32[192,512]{1,0:T(8,128)}, f32[192,512]{1,0:T(8,128)S(1)}, u32[]{:S(2)}, u32[]{:S(2)}) %collective-permute-start.4) | collective-permute-done | bytes 393248 | tf_op jit(solution)/shard_map/ppermute | solution.py:18
  60.3 0.7 copy-done.7
  61.7 1.8 %collective-permute-start.6 = (f32[192,512]{1,0:T(8,128)}, f32[192,512]{1,0:T(8,128)S(1)}, u32[]{:S(2)}, u32[]{:S(2)}) collective-permute-start(f32[192,512]{1,0:T(8,128)} %get-tuple-element.8.refs_2_), channel_id=1, source_target_pairs={{0,96},{32,64},{64,32},{96,0},{1,97},{33,65},{65,33},{97,1},{2,98}... | collective-permute-start | bytes 1179656 | tf_op jit(solution)/shard_map/ppermute | solution.py:18
  63.6 9.1 %collective-permute-done.6.refs_4_ = f32[192,512]{1,0:T(8,128)S(1)} collective-permute-done((f32[192,512]{1,0:T(8,128)}, f32[192,512]{1,0:T(8,128)S(1)}, u32[]{:S(2)}, u32[]{:S(2)}) %collective-permute-start.6) | collective-permute-done | bytes 393248 | tf_op jit(solution)/shard_map/ppermute | solution.py:18
  72.7 1.0 copy-done.3
  73.7 1.0 copy-done.6
  74.7 1.0 copy-done.8
  75.7 1.0 copy-done.10
  76.7 1.0 copy-done.12
  77.7 19.0 %shard_map.70 = (f32[8,192,512]{2,1,0:T(8,128)S(1)}, f32[8,192,512]{2,1,0:T(8,128)S(1)}) custom-call(s32[9]{0:T(128)S(1)} %pad_add_fusion.place_ref, f32[3072,1536]{1,0:T(8,128)} %a_ref.1, f32[192,512]{1,0:T(8,128)S(1)} %collective-permute-done.refs_0_, f32[192,512]{1,0:T(8,128)S(1)} %copy-done.10, f32[192,512]{1,0:T(8,128)S(1)} %copy-done.3, ...), custom_call_target="tpu_custom_call" | custom-call | flops 14495514624 | bytes 28311552 | tf_op jit(solution)/shard_map/pallas_call | solution.py:123
  96.7 5.6 %collective-permute-done.8 = f32[8,192,512]{2,1,0:T(8,128)S(1)} collective-permute-done((f32[8,192,512]{2,1,0:T(8,128)S(1)}, f32[8,192,512]{2,1,0:T(8,128)S(1)}, u32[]{:S(2)}, u32[]{:S(2)}) %collective-permute-start.8) | collective-permute-done | bytes 3145760 | tf_op jit(solution)/shard_map/ppermute | solution.py:18
  102.4 2.4 %add.106.sum_ref = f32[8,192,512]{2,1,0:T(8,128)} add(f32[8,192,512]{2,1,0:T(8,128)S(1)} %get-tuple-element.10, f32[8,192,512]{2,1,0:T(8,128)S(1)} %collective-permute-done.8) | non-fusion elementwise | flops 786432 | bytes 9437184 | tf_op jit(solution)/shard_map/add | solution.py:200
  104.8 2.9 %all-gather.3.cloned.1.call-done = f32[1536,512]{1,0:T(8,128)} async-done(((f32[192,512]{1,0:T(8,128)}), f32[1536,512]{1,0:T(8,128)}) %all-gather.3.cloned.1.call-update) | async-done | bytes 3145744 | tf_op jit(solution)/shard_map/all_gather | solution.py:196
  107.7 1.9 %copy-done.1 = f32[1536,512]{1,0:T(8,128)S(1)} copy-done((f32[1536,512]{1,0:T(8,128)S(1)}, f32[1536,512]{1,0:T(8,128)}, u32[]{:S(2)}) %copy-start.1) | copy-done | bytes 3145752
  109.6 3.6 %shard_map.71 = (f32[256,256]{1,0:T(8,128)S(1)}, f32[256,256]{1,0:T(8,128)S(1)}) custom-call(f32[8,192,512]{2,1,0:T(8,128)S(1)} %copy-done, f32[8,192,512]{2,1,0:T(8,128)S(1)} %bitcast.40), custom_call_target="tpu_custom_call" | custom-call | flops 1207959552 | bytes 6291456 | tf_op jit(solution)/shard_map/pallas_call | solution.py:157
  114.1 1.5 collective-permute-done.10
  115.7 2.8 %collective-permute-start.13 = (f32[64,256]{1,0:T(8,128)S(1)}, f32[64,256]{1,0:T(8,128)S(1)}, u32[]{:S(2)}, u32[]{:S(2)}) collective-permute-start(f32[64,256]{1,0:T(8,128)S(1)} %get-tuple-element.19), channel_id=1, source_target_pairs={{0,96},{32,0},{64,32},{96,64},{1,97},{33,1},{65,33},{97,65},{2,98}... | collective-permute-start | bytes 196616 | tf_op jit(solution)/shard_map/ppermute | solution.py:18
  118.5 0.8 collective-permute-start.12
  119.3 0.9 collective-permute-start.11
  120.7 4.2 %collective-permute-done.12 = f32[64,256]{1,0:T(8,128)S(1)} collective-permute-done((f32[64,256]{1,0:T(8,128)S(1)}, f32[64,256]{1,0:T(8,128)S(1)}, u32[]{:S(2)}, u32[]{:S(2)}) %collective-permute-start.12) | collective-permute-done | bytes 65568 | tf_op jit(solution)/shard_map/ppermute | solution.py:18
  124.9 1.2 collective-permute-done.11
  126.2 1.4 collective-permute-start.16
  127.6 1.7 collective-permute-start.15
  129.3 3.3 %collective-permute-done.16 = f32[64,256]{1,0:T(8,128)S(1)} collective-permute-done((f32[64,256]{1,0:T(8,128)S(1)}, f32[64,256]{1,0:T(8,128)S(1)}, u32[]{:S(2)}, u32[]{:S(2)}) %collective-permute-start.16) | collective-permute-done | bytes 65568 | tf_op jit(solution)/shard_map/ppermute | solution.py:18
  132.6 2.9 %collective-permute-done.15 = f32[64,256]{1,0:T(8,128)S(1)} collective-permute-done((f32[64,256]{1,0:T(8,128)S(1)}, f32[64,256]{1,0:T(8,128)S(1)}, u32[]{:S(2)}, u32[]{:S(2)}) %collective-permute-start.15) | collective-permute-done | bytes 65568 | tf_op jit(solution)/shard_map/ppermute | solution.py:18
  135.5 1.6 collective-permute-done.14
  137.6 3.8 %collective-permute-done.17 = f32[64,256]{1,0:T(8,128)S(1)} collective-permute-done((f32[64,256]{1,0:T(8,128)S(1)}, f32[64,256]{1,0:T(8,128)S(1)}, u32[]{:S(2)}, u32[]{:S(2)}) %collective-permute-start.17) | collective-permute-done | bytes 65568 | tf_op jit(solution)/shard_map/ppermute | solution.py:18
  141.5 2.2 %collective-permute-start.18 = (f32[64,256]{1,0:T(8,128)S(1)}, f32[64,256]{1,0:T(8,128)S(1)}, u32[]{:S(2)}, u32[]{:S(2)}) collective-permute-start(f32[64,256]{1,0:T(8,128)S(1)} %add.124), channel_id=1, source_target_pairs={{0,16},{16,0},{1,17},{17,1},{2,18},{18,2},{3,19},{19,3},{4,20},{20... | collective-permute-start | bytes 196616 | tf_op jit(solution)/shard_map/ppermute | solution.py:18
  143.7 3.6 %collective-permute-done.18 = f32[64,256]{1,0:T(8,128)S(1)} collective-permute-done((f32[64,256]{1,0:T(8,128)S(1)}, f32[64,256]{1,0:T(8,128)S(1)}, u32[]{:S(2)}, u32[]{:S(2)}) %collective-permute-start.18) | collective-permute-done | bytes 65568 | tf_op jit(solution)/shard_map/ppermute | solution.py:18
  147.9 0.8 collective-permute-start.20
  148.8 0.9 collective-permute-start.21
  149.7 2.0 %collective-permute-done.19 = f32[64,256]{1,0:T(8,128)S(1)} collective-permute-done((f32[64,256]{1,0:T(8,128)S(1)}, f32[64,256]{1,0:T(8,128)S(1)}, u32[]{:S(2)}, u32[]{:S(2)}) %collective-permute-start.19) | collective-permute-done | bytes 65568 | tf_op jit(solution)/shard_map/ppermute | solution.py:18
  151.7 2.0 %collective-permute-done.20 = f32[64,256]{1,0:T(8,128)S(1)} collective-permute-done((f32[64,256]{1,0:T(8,128)S(1)}, f32[64,256]{1,0:T(8,128)S(1)}, u32[]{:S(2)}, u32[]{:S(2)}) %collective-permute-start.20) | collective-permute-done | bytes 65568 | tf_op jit(solution)/shard_map/ppermute | solution.py:18
  154.5 1.0 dynamic-slice_bitcast_fusion
  156.8 6.5 %collective-permute-done.9.refs_1_ = f32[192,512]{1,0:T(8,128)S(1)} collective-permute-done((f32[192,512]{1,0:T(8,128)S(1)}, f32[192,512]{1,0:T(8,128)S(1)}, u32[]{:S(2)}, u32[]{:S(2)}) %collective-permute-start.9) | collective-permute-done | bytes 393248 | tf_op jit(solution)/shard_map/ppermute | solution.py:18
  164.8 1.2 bitcast_add_fusion
  166.1 0.8 pad_maximum_fusion.2
  166.9 1.0 fusion.1
  167.9 0.8 pad_maximum_fusion
  (76 shorter events, 10.5 us)
Async XLA Ops:
  8.0 99.7 %all-gather.3.cloned.1.call-start = ((), (), s32[]{:S(2)}) async-start(), calls=%async_computation.2 | async-start | bytes 3538944 | tf_op jit(solution)/shard_map/all_gather | solution.py:196
  12.0 25.1 %copy-start.13 = (f32[192,512]{1,0:T(8,128)}, f32[192,512]{1,0:T(8,128)S(1)}, u32[]{:S(2)}) copy-start(f32[192,512]{1,0:T(8,128)S(1)} %pad_maximum_fusion.1) | copy-start | bytes 1179652
  12.1 0.7 collective-permute-start
  12.8 24.5 %collective-permute-start.1 = (f32[192,512]{1,0:T(8,128)S(1)}, f32[192,512]{1,0:T(8,128)S(1)}, u32[]{:S(2)}, u32[]{:S(2)}) collective-permute-start(f32[192,512]{1,0:T(8,128)S(1)} %collective-permute-done.refs_0_), channel_id=1, source_target_pairs={{0,16},{16,0},{1,17},{17,1},{2,18},{18,2},{3,19},{19,3},{4,20},{20... | collective-permute-start | bytes 1179656 | tf_op jit(solution)/shard_map/ppermute | solution.py:18
  27.1 11.0 %collective-permute-start.2 = (f32[192,512]{1,0:T(8,128)S(1)}, f32[192,512]{1,0:T(8,128)S(1)}, u32[]{:S(2)}, u32[]{:S(2)}) collective-permute-start(f32[192,512]{1,0:T(8,128)S(1)} %collective-permute-done.refs_0_), channel_id=1, source_target_pairs={{0,32},{32,0},{64,96},{96,64},{1,33},{33,1},{65,97},{97,65},{2,34}... | collective-permute-start | bytes 1179656 | tf_op jit(solution)/shard_map/ppermute | solution.py:18
  30.9 15.4 %collective-permute-start.3 = (f32[192,512]{1,0:T(8,128)S(1)}, f32[192,512]{1,0:T(8,128)S(1)}, u32[]{:S(2)}, u32[]{:S(2)}) collective-permute-start(f32[192,512]{1,0:T(8,128)S(1)} %collective-permute-done.refs_0_), channel_id=1, source_target_pairs={{0,96},{32,64},{64,32},{96,0},{1,97},{33,65},{65,33},{97,1},{2,98}... | collective-permute-start | bytes 1179656 | tf_op jit(solution)/shard_map/ppermute | solution.py:18
  37.2 117.3 %reduce-scatter.2.cloned.1.call-start = ((), (), s32[]{:S(2)}) async-start(), calls=%async_computation.1 | async-start | bytes 3932160 | tf_op jit(solution)/shard_map/reduce_scatter | solution.py:202
  37.3 9.1 %copy-start.9 = (f32[192,512]{1,0:T(8,128)}, f32[192,512]{1,0:T(8,128)S(1)}, u32[]{:S(2)}) copy-start(f32[192,512]{1,0:T(8,128)S(1)} %collective-permute-done.1.refs_0_) | copy-start | bytes 1179652
  38.1 8.2 %copy-start.2 = (f32[192,512]{1,0:T(8,128)}, f32[192,512]{1,0:T(8,128)S(1)}, u32[]{:S(2)}) copy-start(f32[192,512]{1,0:T(8,128)S(1)} %collective-permute-done.2.refs_1_) | copy-start | bytes 1179652
  46.3 0.7 copy-start.5
  47.8 11.8 %collective-permute-start.4 = (f32[192,512]{1,0:T(8,128)}, f32[192,512]{1,0:T(8,128)S(1)}, u32[]{:S(2)}, u32[]{:S(2)}) collective-permute-start(f32[192,512]{1,0:T(8,128)} %shard_map.68.refs_1_), channel_id=1, source_target_pairs={{0,96},{32,64},{64,32},{96,0},{1,97},{33,65},{65,33},{97,1},{2,98}... | collective-permute-start | bytes 1179656 | tf_op jit(solution)/shard_map/ppermute | solution.py:18
  50.3 9.5 %collective-permute-start.5 = (f32[192,512]{1,0:T(8,128)}, f32[192,512]{1,0:T(8,128)S(1)}, u32[]{:S(2)}, u32[]{:S(2)}) collective-permute-start(f32[192,512]{1,0:T(8,128)} %shard_map.68.refs_1_), channel_id=1, source_target_pairs={{0,32},{32,0},{64,96},{96,64},{1,33},{33,1},{65,97},{97,65},{2,34}... | collective-permute-start | bytes 1179656 | tf_op jit(solution)/shard_map/ppermute | solution.py:18
  59.5 0.8 copy-start.11
  60.3 0.7 copy-start.7
  61.7 10.9 %collective-permute-start.6 = (f32[192,512]{1,0:T(8,128)}, f32[192,512]{1,0:T(8,128)S(1)}, u32[]{:S(2)}, u32[]{:S(2)}) collective-permute-start(f32[192,512]{1,0:T(8,128)} %get-tuple-element.8.refs_2_), channel_id=1, source_target_pairs={{0,96},{32,64},{64,32},{96,0},{1,97},{33,65},{65,33},{97,1},{2,98}... | collective-permute-start | bytes 1179656 | tf_op jit(solution)/shard_map/ppermute | solution.py:18
  63.5 9.2 %collective-permute-start.7 = (f32[192,512]{1,0:T(8,128)}, f32[192,512]{1,0:T(8,128)S(1)}, u32[]{:S(2)}, u32[]{:S(2)}) collective-permute-start(f32[192,512]{1,0:T(8,128)} %get-tuple-element.9.refs_7_), channel_id=1, source_target_pairs={{0,32},{32,0},{64,96},{96,64},{1,33},{33,1},{65,97},{97,65},{2,34}... | collective-permute-start | bytes 1179656 | tf_op jit(solution)/shard_map/ppermute | solution.py:18
  72.7 1.0 copy-start.3
  73.7 1.0 copy-start.6
  74.7 1.0 copy-start.8
  75.7 1.0 copy-start.10
  76.7 1.0 copy-start.12
  96.6 5.7 %collective-permute-start.8 = (f32[8,192,512]{2,1,0:T(8,128)S(1)}, f32[8,192,512]{2,1,0:T(8,128)S(1)}, u32[]{:S(2)}, u32[]{:S(2)}) collective-permute-start(f32[8,192,512]{2,1,0:T(8,128)S(1)} %get-tuple-element.11), channel_id=1, source_target_pairs={{0,1},{1,0},{2,3},{3,2},{4,5},{5,4},{6,7},{7,6},{8,9},{9,8},{10,11... | collective-permute-start | bytes 9437192 | tf_op jit(solution)/shard_map/ppermute | solution.py:18
  104.8 2.9 %copy-start = (f32[8,192,512]{2,1,0:T(8,128)S(1)}, f32[8,192,512]{2,1,0:T(8,128)}, u32[]{:S(2)}) copy-start(f32[8,192,512]{2,1,0:T(8,128)} %add.106.sum_ref) | copy-start | bytes 9437188
  107.7 1.9 %copy-start.1 = (f32[1536,512]{1,0:T(8,128)S(1)}, f32[1536,512]{1,0:T(8,128)}, u32[]{:S(2)}) copy-start(f32[1536,512]{1,0:T(8,128)} %all-gather.3.cloned.1.call-done) | copy-start | bytes 9437188
  113.2 0.7 copy-start.4
  114.0 1.6 collective-permute-start.10
  115.7 5.1 %collective-permute-start.13 = (f32[64,256]{1,0:T(8,128)S(1)}, f32[64,256]{1,0:T(8,128)S(1)}, u32[]{:S(2)}, u32[]{:S(2)}) collective-permute-start(f32[64,256]{1,0:T(8,128)S(1)} %get-tuple-element.19), channel_id=1, source_target_pairs={{0,96},{32,0},{64,32},{96,64},{1,97},{33,1},{65,33},{97,65},{2,98}... | collective-permute-start | bytes 196616 | tf_op jit(solution)/shard_map/ppermute | solution.py:18
  118.5 6.5 %collective-permute-start.12 = (f32[64,256]{1,0:T(8,128)S(1)}, f32[64,256]{1,0:T(8,128)S(1)}, u32[]{:S(2)}, u32[]{:S(2)}) collective-permute-start(f32[64,256]{1,0:T(8,128)S(1)} %get-tuple-element.20), channel_id=1, source_target_pairs={{0,64},{32,96},{64,0},{96,32},{1,65},{33,97},{65,1},{97,33},{2,66}... | collective-permute-start | bytes 196616 | tf_op jit(solution)/shard_map/ppermute | solution.py:18
  119.3 6.9 %collective-permute-start.11 = (f32[64,256]{1,0:T(8,128)S(1)}, f32[64,256]{1,0:T(8,128)S(1)}, u32[]{:S(2)}, u32[]{:S(2)}) collective-permute-start(f32[64,256]{1,0:T(8,128)S(1)} %get-tuple-element.18), channel_id=1, source_target_pairs={{0,32},{32,64},{64,96},{96,0},{1,33},{33,65},{65,97},{97,1},{2,34}... | collective-permute-start | bytes 196616 | tf_op jit(solution)/shard_map/ppermute | solution.py:18
  126.2 6.4 %collective-permute-start.16 = (f32[64,256]{1,0:T(8,128)S(1)}, f32[64,256]{1,0:T(8,128)S(1)}, u32[]{:S(2)}, u32[]{:S(2)}) collective-permute-start(f32[64,256]{1,0:T(8,128)S(1)} %add_add_fusion.1), channel_id=1, source_target_pairs={{0,12},{4,0},{8,4},{12,8},{1,13},{5,1},{9,5},{13,9},{2,14},{6,2},{... | collective-permute-start | bytes 196616 | tf_op jit(solution)/shard_map/ppermute | solution.py:18
  127.6 7.9 %collective-permute-start.15 = (f32[64,256]{1,0:T(8,128)S(1)}, f32[64,256]{1,0:T(8,128)S(1)}, u32[]{:S(2)}, u32[]{:S(2)}) collective-permute-start(f32[64,256]{1,0:T(8,128)S(1)} %add_add_fusion.1), channel_id=1, source_target_pairs={{0,8},{4,12},{8,0},{12,4},{1,9},{5,13},{9,1},{13,5},{2,10},{6,14},... | collective-permute-start | bytes 196616 | tf_op jit(solution)/shard_map/ppermute | solution.py:18
  129.3 7.8 %collective-permute-start.14 = (f32[64,256]{1,0:T(8,128)S(1)}, f32[64,256]{1,0:T(8,128)S(1)}, u32[]{:S(2)}, u32[]{:S(2)}) collective-permute-start(f32[64,256]{1,0:T(8,128)S(1)} %add_add_fusion.1), channel_id=1, source_target_pairs={{0,4},{4,8},{8,12},{12,0},{1,5},{5,9},{9,13},{13,1},{2,6},{6,10},{... | collective-permute-start | bytes 196616 | tf_op jit(solution)/shard_map/ppermute | solution.py:18
  137.1 29.8 %copy-start.15 = (f32[2,256,256]{2,1,0:T(8,128)S(1)}, f32[2,256,256]{2,1,0:T(8,128)}, u32[]{:S(2)}) copy-start(f32[2,256,256]{2,1,0:T(8,128)} %param.8) | copy-start | bytes 1572868
  137.1 4.3 %collective-permute-start.17 = (f32[64,256]{1,0:T(8,128)S(1)}, f32[64,256]{1,0:T(8,128)S(1)}, u32[]{:S(2)}, u32[]{:S(2)}) collective-permute-start(f32[64,256]{1,0:T(8,128)S(1)} %add_add_fusion), channel_id=1, source_target_pairs={{0,2},{2,0},{1,3},{3,1},{4,6},{6,4},{5,7},{7,5},{8,10},{10,8},{9,1... | collective-permute-start | bytes 196616 | tf_op jit(solution)/shard_map/ppermute | solution.py:18
  141.5 5.8 %collective-permute-start.18 = (f32[64,256]{1,0:T(8,128)S(1)}, f32[64,256]{1,0:T(8,128)S(1)}, u32[]{:S(2)}, u32[]{:S(2)}) collective-permute-start(f32[64,256]{1,0:T(8,128)S(1)} %add.124), channel_id=1, source_target_pairs={{0,16},{16,0},{1,17},{17,1},{2,18},{18,2},{3,19},{19,3},{4,20},{20... | collective-permute-start | bytes 196616 | tf_op jit(solution)/shard_map/ppermute | solution.py:18
  147.3 4.3 %collective-permute-start.19 = (f32[64,256]{1,0:T(8,128)S(1)}, f32[64,256]{1,0:T(8,128)S(1)}, u32[]{:S(2)}, u32[]{:S(2)}) collective-permute-start(f32[64,256]{1,0:T(8,128)S(1)} %add.125), channel_id=1, source_target_pairs={{0,96},{32,0},{64,32},{96,64},{1,97},{33,1},{65,33},{97,65},{2,98}... | collective-permute-start | bytes 196616 | tf_op jit(solution)/shard_map/ppermute | solution.py:18
  147.9 5.8 %collective-permute-start.20 = (f32[64,256]{1,0:T(8,128)S(1)}, f32[64,256]{1,0:T(8,128)S(1)}, u32[]{:S(2)}, u32[]{:S(2)}) collective-permute-start(f32[64,256]{1,0:T(8,128)S(1)} %add.125), channel_id=1, source_target_pairs={{0,64},{32,96},{64,0},{96,32},{1,65},{33,97},{65,1},{97,33},{2,66}... | collective-permute-start | bytes 196616 | tf_op jit(solution)/shard_map/ppermute | solution.py:18
  148.8 5.6 %collective-permute-start.21 = (f32[64,256]{1,0:T(8,128)S(1)}, f32[64,256]{1,0:T(8,128)S(1)}, u32[]{:S(2)}, u32[]{:S(2)}) collective-permute-start(f32[64,256]{1,0:T(8,128)S(1)} %add.125), channel_id=1, source_target_pairs={{0,32},{32,64},{64,96},{96,0},{1,33},{33,65},{65,97},{97,1},{2,34}... | collective-permute-start | bytes 196616 | tf_op jit(solution)/shard_map/ppermute | solution.py:18
  155.5 7.9 %collective-permute-start.9 = (f32[192,512]{1,0:T(8,128)S(1)}, f32[192,512]{1,0:T(8,128)S(1)}, u32[]{:S(2)}, u32[]{:S(2)}) collective-permute-start(f32[192,512]{1,0:T(8,128)S(1)} %dynamic-slice_bitcast_fusion), channel_id=1, source_target_pairs={{0,2},{2,0},{1,3},{3,1},{4,6},{6,4},{5,7},{7,5},{8,10},{10,8},{9,1... | collective-permute-start | bytes 1179656 | tf_op jit(solution)/shard_map/ppermute | solution.py:18
  163.3 0.7 copy-start.14
  164.8 2.1 %collective-permute-start.22 = (f32[256,256]{1,0:T(8,128)}, f32[256,256]{1,0:T(8,128)S(1)}, u32[]{:S(2)}, u32[]{:S(2)}) collective-permute-start(f32[256,256]{1,0:T(8,128)} %shard_map.72), channel_id=1, source_target_pairs={{0,1},{1,0},{2,3},{3,2},{4,5},{5,4},{6,7},{7,6},{8,9},{9,8},{10,11... | collective-permute-start | bytes 786440 | tf_op jit(solution)/shard_map/ppermute | solution.py:18
Sparse Core Ops, SparseCore 0:
  37.3 70.3 all-gather.2
Sparse Core Ops, SparseCore 1:
  104.9 39.0 reduce-scatter.1

commit v8 on v7

--- a/solution.py
+++ b/solution.py
@@ -1,3 +1,5 @@
+import functools
+
 import jax
 import jax.numpy as jnp
 from jax import lax
@@ -55,15 +57,16 @@
     return lax.dynamic_slice_in_dim(twice, (3 - me) * x.shape[0], 4 * x.shape[0], 0)
 
 
-def total(first, second, before):
+def total(first, second, given, taken):
     k = lax.axis_index("k")
     mine = jnp.where(k == 0, first, second) + swap(jnp.where(k == 0, second, first), "k")
     mine = scatter_four(mine, "y")
     mine = sum_four(mine, "z")
     mine = mine + swap(mine, "xl")
     mine = mine + swap(mine, "xh")
+    (mine,) = later([mine], [given])
     mine = gather_four(mine, "y")
-    (mine,) = later([mine], [before])
+    (mine,) = later([mine], [taken])
     other = swap(mine, "k")
     return jnp.where(k == 0, mine, other), jnp.where(k == 0, other, mine)
 
@@ -84,8 +87,7 @@
     anywhere = pl.BlockSpec(memory_space=pl.ANY)
     return pl.pallas_call(
         lambda *refs: None,
-        grid=(1,),
-        in_specs=[anywhere] * len(xs) + [pl.BlockSpec((8, 128), lambda i: (0, 0)) for _ in after],
+        in_specs=[anywhere] * (len(xs) + len(after)),
         out_specs=[anywhere] * len(xs),
         out_shape=[jax.ShapeDtypeStruct(x.shape, x.dtype) for x in xs],
         input_output_aliases={i: i for i in range(len(xs))},
@@ -93,48 +95,61 @@
     )(*xs, *after)
 
 
-def product_kernel(place_ref, a_ref, *refs):
-    pieces, (keep_ref, give_ref, high, low) = refs[:8], refs[8:]
+def product_kernel(place_ref, *refs, count, adds):
+    strips, pieces = refs[: count // 2], refs[count // 2 : count // 2 + count]
+    before = refs[count // 2 + count : -4]
+    keep_ref, give_ref, high, low = refs[-4:]
     piece = pieces[0].shape[0]
 
     @pl.when(pl.program_id(0) == 0)
     def _():
-        for j in range(8):
-            rows = pl.ds(pl.multiple_of(place_ref[j] * piece, BS), piece)
+        for j in range(count):
+            rows = pl.ds(pl.multiple_of((j // 2) * 2 * piece + place_ref[5 + j % 2] * piece, BS), piece)
             xh, xl = halves(pieces[j][...])
             high[rows, :] = xh
             low[rows, :] = xl
 
-    ah, al = halves(a_ref[...])
     f = lambda p, q: jnp.dot(p, q, preferred_element_type=F32)
-    out = f(ah, high[...]) + (f(ah, low[...]) + f(al, high[...]))
+    out = None
+    for m, strip in enumerate(strips):
+        rows = slice(m * 2 * piece, (m + 1) * 2 * piece)
+        ah, al = halves(strip[...])
+        term = f(ah, high[rows, :]) + (f(ah, low[rows, :]) + f(al, high[rows, :]))
+        out = term if out is None else out + term
     first, second = out[:piece], out[piece:]
-    lower = place_ref[8] == 0
-    keep_ref[0] = jnp.where(lower, first, second)
-    give_ref[0] = jnp.where(lower, second, first)
-
-
-def product(a, pieces, places):
-    rows, cols = a.shape
+    lower = place_ref[4] == 0
+    kept, given = jnp.where(lower, first, second), jnp.where(lower, second, first)
+    if adds:
+        kept, given = kept + before[0][0], given + before[1][0]
+    keep_ref[0] = kept
+    give_ref[0] = given
+
+
+def product(a, pieces, places, start, before=()):
+    rows = a.shape[0]
     piece, width = pieces[0].shape
+    count = len(pieces)
     blocks = rows // (2 * piece)
     whole = pl.BlockSpec((piece, width), lambda i, p: (0, 0), pipeline_mode=pl.Buffered(1))
+    strips = [pl.BlockSpec((2 * piece, 2 * piece), lambda i, p, m=m: (i, p[start + m])) for m in range(count // 2)]
     out = pl.BlockSpec((1, piece, width), lambda i, p: (i, 0, 0))
     return pl.pallas_call(
-        product_kernel,
+        functools.partial(product_kernel, count=count, adds=bool(before)),
         grid_spec=pltpu.PrefetchScalarGridSpec(
             num_scalar_prefetch=1,
             grid=(blocks,),
-            in_specs=[pl.BlockSpec((2 * piece, cols), lambda i, p: (i, 0))] + [whole] * 8,
+            in_specs=[*strips] + [whole] * count + [out] * len(before),
             out_specs=[out, out],
-            scratch_shapes=[pltpu.VMEM((cols, width), BF)] * 2,
+            scratch_shapes=[pltpu.VMEM((count * piece, width), BF)] * 2,
         ),
         out_shape=[jax.ShapeDtypeStruct((blocks, piece, width), F32)] * 2,
         compiler_params=pltpu.CompilerParams(vmem_limit_bytes=40 << 20),
         cost_estimate=pl.CostEstimate(
-            flops=6 * rows * cols * width, bytes_accessed=4 * (rows * cols + (rows + cols) * width), transcendentals=0
+            flops=6 * rows * count * piece * width,
+            bytes_accessed=4 * (rows * count * piece + (rows + count * piece) * width),
+            transcendentals=0,
         ),
-    )(places, a, *pieces)
+    )(places, *[a] * len(strips), *pieces, *before)
 
 
 def update_kernel(sum_ref, x_ref, first_ref, second_ref):
@@ -168,14 +183,13 @@
 
 
 def gather_column(mine):
+    pair = swap(mine, "xh")
     one, three = (lambda i: i ^ 1), (lambda i: i ^ 3)
     mine1 = send(mine, "y", 4, one)
     mine3 = send(mine, "y", 4, three)
-    (pair,) = later([swap(mine, "xh")], [mine1, mine3])
     pair3 = send(pair, "y", 4, three)
+    mine2 = send(mine1, "y", 4, three)
     pair1 = send(pair, "y", 4, one)
-    pair3, mine1 = later([pair3, mine1], [pair1])
-    mine2 = send(mine1, "y", 4, three)
     pair2 = send(pair3, "y", 4, one)
     return [mine, pair, mine1, pair1, mine2, pair2, mine3, pair3]
 
@@ -189,13 +203,15 @@
     normed = jnp.concatenate(
         [jnp.dot(lower_panel[s], diag_factor[s], precision=HIGHEST) * masks[s] for s in range(NS)], axis=1
     )
-    spots = jnp.arange(8, dtype=jnp.int32)
-    places = jnp.concatenate([((spots // 2) ^ y) * 2 + ((spots % 2) ^ xh), k[None]])
+    spots = jnp.arange(4, dtype=jnp.int32)
+    places = jnp.concatenate([spots ^ y, jnp.stack([k, xh, 1 - xh])]).astype(jnp.int32)
     mine = lax.ppermute(normed, ALL, transpose_pairs())
 
     band = lax.all_gather(normed, ("z", "xl"), axis=0, tiled=False)
 
-    keep, give = product(ancestor_inverse, gather_column(mine), places)
+    pieces = gather_column(mine)
+    keep, give = product(ancestor_inverse, pieces[:4], places, 0)
+    keep, give = product(ancestor_inverse, pieces[4:], places, 2, (keep, give))
     got = swap(give, "k")
     summed = keep + got
     first, second = updates(summed, band)
@@ -205,7 +221,7 @@
     taken = swap(given, "xl")
     whole = kept + taken
     panels = [-masks[s] * whole[:, s * wide : (s + 1) * wide] for s in range(NS)]
-    first, second = total(first, second, taken)
+    first, second = total(first, second, given, taken)
     return jnp.stack(panels), jnp.stack([diag_block[0] + first, diag_block[1] + second])
 
 

time: 178 us -> 173 us (0.972)
  waiting for transfers between devices: 70.2 us -> 49 us
  starting transfers between devices: 42.9 us -> 56.5 us
  Pallas kernels: 24.6 us -> 30.6 us
  local copies, waits for them, and re-layouts: 13.2 us -> 9.76 us
    ppermute x22, waiting for transfers between devices: 67.3 us -> 47.7 us  [send(): return lax.ppermute(x, axis, [(i, to(i)) for i in range(size)])]
    ppermute x22, starting transfers between devices: 42.2 us -> 55.7 us  [send(): return lax.ppermute(x, axis, [(i, to(i)) for i in range(size)])]
    pallas_call x4, Pallas kernels: 21 us -> 27 us  [the longest x2 27 us: product(): pl.pallas_call(functools.partial(product_kernel, count=count, adds=bool(b...]
    unnamed x38 -> x20, local copies, waits for them, and re-layouts: 10.3 us -> 6.09 us
    all_gather x1, waiting for transfers between devices: 2.87 us -> 0.02 us  [local(): band = lax.all_gather(normed, ('z', 'xl'), axis=0, tiled=False)]
  transfers between devices with their start and end apart: 25 -> 25, of which waited for: 20 -> 15; matrix products, arithmetic and copies ran while one was open for 3% -> 4% of each run, Pallas kernels for 14% -> 18%
where the time goes in v8:
time: 173 us; the launch traced here: 172 us
  starting transfers between devices  56.5 us (33%)
  waiting for transfers between devices  49 us (28%)
  Pallas kernels  30.6 us (18%)
  between operations  15.7 us (9%)
  local copies, waits for them, and re-layouts  9.76 us (6%)
  other arithmetic  7.19 us (4%)
  matrix products  2.77 us (2%)
    ppermute x22, starting transfers between devices, send(): return lax.ppermute(x, axis, [(i, to(i)) for i in range(size)])  55.7 us
    ppermute x22, waiting for transfers between devices, send(): return lax.ppermute(x, axis, [(i, to(i)) for i in range(size)])  47.7 us
    pallas_call x2, Pallas kernels, product(): pl.pallas_call(functools.partial(product_kernel, count=count, adds=bool(b...  27 us
    unnamed x20, local copies, waits for them, and re-layouts  6.09 us
    pallas_call x1, Pallas kernels, updates(): pl.pallas_call(update_kernel, grid=(blocks,), in_specs=[spec] * 2, out_sp...  3.62 us
  transfers between devices with their start and end apart: 25, of which 15 were waited for; matrix products, arithmetic and copies ran while one was open for 4% of the time, Pallas kernels for 18%

profile of v8, /device:TPU:0, one launch (start us, length us, event | category | flops | bytes accessed | tf_op | source)
XLA Modules:
  0.0 171.6 jit_solution(12541036429494871961)
XLA Ops:
  8.1 0.8 fusion.16
  9.2 1.4 convolution_multiply_fusion
  10.6 1.4 convolution_multiply_fusion.1
  12.9 14.2 %collective-permute-start.3 = (f32[192,512]{1,0:T(8,128)S(1)}, f32[192,512]{1,0:T(8,128)S(1)}, u32[]{:S(2)}, u32[]{:S(2)}) collective-permute-start(f32[192,512]{1,0:T(8,128)S(1)} %collective-permute-done.refs_2_), channel_id=1, source_target_pairs={{0,16},{16,0},{1,17},{17,1},{2,18},{18,2},{3,19},{19,3},{4,20},{20... | collective-permute-start | bytes 1179656 | tf_op jit(solution)/shard_map/ppermute | solution.py:20
  27.1 3.8 %collective-permute-start.1 = (f32[192,512]{1,0:T(8,128)S(1)}, f32[192,512]{1,0:T(8,128)S(1)}, u32[]{:S(2)}, u32[]{:S(2)}) collective-permute-start(f32[192,512]{1,0:T(8,128)S(1)} %collective-permute-done.refs_2_), channel_id=1, source_target_pairs={{0,32},{32,0},{64,96},{96,64},{1,33},{33,1},{65,97},{97,65},{2,34}... | collective-permute-start | bytes 1179656 | tf_op jit(solution)/shard_map/ppermute | solution.py:20
  31.0 13.5 %collective-permute-done.3.refs_3_ = f32[192,512]{1,0:T(8,128)S(1)} collective-permute-done((f32[192,512]{1,0:T(8,128)S(1)}, f32[192,512]{1,0:T(8,128)S(1)}, u32[]{:S(2)}, u32[]{:S(2)}) %collective-permute-start.3) | collective-permute-done | bytes 393248 | tf_op jit(solution)/shard_map/ppermute | solution.py:20
  44.5 9.1 %collective-permute-start.4 = (f32[192,512]{1,0:T(8,128)S(1)}, f32[192,512]{1,0:T(8,128)S(1)}, u32[]{:S(2)}, u32[]{:S(2)}) collective-permute-start(f32[192,512]{1,0:T(8,128)S(1)} %collective-permute-done.3.refs_3_), channel_id=1, source_target_pairs={{0,96},{32,64},{64,32},{96,0},{1,97},{33,65},{65,33},{97,1},{2,98}... | collective-permute-start | bytes 1179656 | tf_op jit(solution)/shard_map/ppermute | solution.py:20
  53.6 1.2 collective-permute-start.7
  55.4 2.6 %collective-permute-start.2 = (f32[192,512]{1,0:T(8,128)S(1)}, f32[192,512]{1,0:T(8,128)S(1)}, u32[]{:S(2)}, u32[]{:S(2)}) collective-permute-start(f32[192,512]{1,0:T(8,128)S(1)} %collective-permute-done.1.refs_4_), channel_id=1, source_target_pairs={{0,96},{32,64},{64,32},{96,0},{1,97},{33,65},{65,33},{97,1},{2,98}... | collective-permute-start | bytes 1179656 | tf_op jit(solution)/shard_map/ppermute | solution.py:20
  58.1 5.5 %collective-permute-done.4.refs_5_ = f32[192,512]{1,0:T(8,128)S(1)} collective-permute-done((f32[192,512]{1,0:T(8,128)S(1)}, f32[192,512]{1,0:T(8,128)S(1)}, u32[]{:S(2)}, u32[]{:S(2)}) %collective-permute-start.4) | collective-permute-done | bytes 393248 | tf_op jit(solution)/shard_map/ppermute | solution.py:20
  63.6 1.1 collective-permute-start.5
  64.7 13.4 %shard_map.68 = (f32[8,192,512]{2,1,0:T(8,128)S(1)}, f32[8,192,512]{2,1,0:T(8,128)S(1)}) custom-call(s32[7]{0:T(128)S(1)} %pad_add_fusion.place_ref, f32[3072,1536]{1,0:T(8,128)} %refs_1_.3, f32[3072,1536]{1,0:T(8,128)} %refs_1_.3, f32[192,512]{1,0:T(8,128)S(1)} %collective-permute-done.refs_2_, f32[192,512]{1,0:T(8,128)S(1)} %collective-permute-done.3.refs_3_, ...), custom_call_target="tpu_custom_call" | custom-call | flops 7247757312 | bytes 17301504 | tf_op jit(solution)/shard_map/pallas_call | solution.py:136
  78.1 0.7 collective-permute-done.2.refs_2_
  78.8 13.6 %shard_map.69 = (f32[8,192,512]{2,1,0:T(8,128)S(1)}, f32[8,192,512]{2,1,0:T(8,128)S(1)}) custom-call(s32[7]{0:T(128)S(1)} %pad_add_fusion.place_ref, f32[3072,1536]{1,0:T(8,128)} %refs_1_.3, f32[3072,1536]{1,0:T(8,128)} %refs_1_.3, f32[192,512]{1,0:T(8,128)S(1)} %collective-permute-done.2.refs_2_, f32[192,512]{1,0:T(8,128)S(1)} %collective-permute-done.5.refs_3_, ...), custom_call_target="tpu_custom_call" | custom-call | flops 7247757312 | bytes 17301504 | tf_op jit(solution)/shard_map/pallas_call | solution.py:136
  92.5 5.6 %collective-permute-done.8 = f32[8,192,512]{2,1,0:T(8,128)S(1)} collective-permute-done((f32[8,192,512]{2,1,0:T(8,128)S(1)}, f32[8,192,512]{2,1,0:T(8,128)S(1)}, u32[]{:S(2)}, u32[]{:S(2)}) %collective-permute-start.8) | collective-permute-done | bytes 3145760 | tf_op jit(solution)/shard_map/ppermute | solution.py:20
  98.2 2.4 %add.94.sum_ref = f32[8,192,512]{2,1,0:T(8,128)} add(f32[8,192,512]{2,1,0:T(8,128)S(1)} %get-tuple-element.10, f32[8,192,512]{2,1,0:T(8,128)S(1)} %collective-permute-done.8) | non-fusion elementwise | flops 786432 | bytes 9437184 | tf_op jit(solution)/shard_map/add | solution.py:216
  100.7 1.8 %copy-done = f32[8,192,512]{2,1,0:T(8,128)S(1)} copy-done((f32[8,192,512]{2,1,0:T(8,128)S(1)}, f32[8,192,512]{2,1,0:T(8,128)}, u32[]{:S(2)}) %copy-start) | copy-done | bytes 3145752
  102.5 1.9 %copy-done.1 = f32[1536,512]{1,0:T(8,128)S(1)} copy-done((f32[1536,512]{1,0:T(8,128)S(1)}, f32[1536,512]{1,0:T(8,128)}, u32[]{:S(2)}) %copy-start.1) | copy-done | bytes 3145752
  104.4 3.6 %shard_map.70 = (f32[256,256]{1,0:T(8,128)S(1)}, f32[256,256]{1,0:T(8,128)S(1)}) custom-call(f32[8,192,512]{2,1,0:T(8,128)S(1)} %copy-done, f32[8,192,512]{2,1,0:T(8,128)S(1)} %bitcast.42), custom_call_target="tpu_custom_call" | custom-call | flops 1207959552 | bytes 6291456 | tf_op jit(solution)/shard_map/pallas_call | solution.py:172
  109.0 1.4 collective-permute-done.10
  110.5 1.7 collective-permute-start.11
  112.2 2.8 %collective-permute-start.12 = (f32[64,256]{1,0:T(8,128)S(1)}, f32[64,256]{1,0:T(8,128)S(1)}, u32[]{:S(2)}, u32[]{:S(2)}) collective-permute-start(f32[64,256]{1,0:T(8,128)S(1)} %get-tuple-element.20), channel_id=1, source_target_pairs={{0,64},{32,96},{64,0},{96,32},{1,65},{33,97},{65,1},{97,33},{2,66}... | collective-permute-start | bytes 196616 | tf_op jit(solution)/shard_map/ppermute | solution.py:20
  115.0 1.6 collective-permute-start.13
  116.6 2.6 %collective-permute-done.12 = f32[64,256]{1,0:T(8,128)S(1)} collective-permute-done((f32[64,256]{1,0:T(8,128)S(1)}, f32[64,256]{1,0:T(8,128)S(1)}, u32[]{:S(2)}, u32[]{:S(2)}) %collective-permute-start.12) | collective-permute-done | bytes 65568 | tf_op jit(solution)/shard_map/ppermute | solution.py:20
  119.6 2.1 %collective-permute-start.14 = (f32[64,256]{1,0:T(8,128)S(1)}, f32[64,256]{1,0:T(8,128)S(1)}, u32[]{:S(2)}, u32[]{:S(2)}) collective-permute-start(f32[64,256]{1,0:T(8,128)S(1)} %add_add_fusion.1), channel_id=1, source_target_pairs={{0,4},{4,8},{8,12},{12,0},{1,5},{5,9},{9,13},{13,1},{2,6},{6,10},{... | collective-permute-start | bytes 196616 | tf_op jit(solution)/shard_map/ppermute | solution.py:20
  121.7 2.3 %collective-permute-start.15 = (f32[64,256]{1,0:T(8,128)S(1)}, f32[64,256]{1,0:T(8,128)S(1)}, u32[]{:S(2)}, u32[]{:S(2)}) collective-permute-start(f32[64,256]{1,0:T(8,128)S(1)} %add_add_fusion.1), channel_id=1, source_target_pairs={{0,8},{4,12},{8,0},{12,4},{1,9},{5,13},{9,1},{13,5},{2,10},{6,14},... | collective-permute-start | bytes 196616 | tf_op jit(solution)/shard_map/ppermute | solution.py:20
  124.0 0.8 collective-permute-start.16
  124.7 2.2 %collective-permute-done.14 = f32[64,256]{1,0:T(8,128)S(1)} collective-permute-done((f32[64,256]{1,0:T(8,128)S(1)}, f32[64,256]{1,0:T(8,128)S(1)}, u32[]{:S(2)}, u32[]{:S(2)}) %collective-permute-start.14) | collective-permute-done | bytes 65568 | tf_op jit(solution)/shard_map/ppermute | solution.py:20
  126.9 3.9 %collective-permute-done.15 = f32[64,256]{1,0:T(8,128)S(1)} collective-permute-done((f32[64,256]{1,0:T(8,128)S(1)}, f32[64,256]{1,0:T(8,128)S(1)}, u32[]{:S(2)}, u32[]{:S(2)}) %collective-permute-start.15) | collective-permute-done | bytes 65568 | tf_op jit(solution)/shard_map/ppermute | solution.py:20
  130.9 2.2 %collective-permute-start.17 = (f32[64,256]{1,0:T(8,128)S(1)}, f32[64,256]{1,0:T(8,128)S(1)}, u32[]{:S(2)}, u32[]{:S(2)}) collective-permute-start(f32[64,256]{1,0:T(8,128)S(1)} %add_add_fusion), channel_id=1, source_target_pairs={{0,2},{2,0},{1,3},{3,1},{4,6},{6,4},{5,7},{7,5},{8,10},{10,8},{9,1... | collective-permute-start | bytes 196616 | tf_op jit(solution)/shard_map/ppermute | solution.py:20
  133.1 2.2 %collective-permute-done.17 = f32[64,256]{1,0:T(8,128)S(1)} collective-permute-done((f32[64,256]{1,0:T(8,128)S(1)}, f32[64,256]{1,0:T(8,128)S(1)}, u32[]{:S(2)}, u32[]{:S(2)}) %collective-permute-start.17) | collective-permute-done | bytes 65568 | tf_op jit(solution)/shard_map/ppermute | solution.py:20
  135.3 3.5 %collective-permute-start.18 = (f32[64,256]{1,0:T(8,128)S(1)}, f32[64,256]{1,0:T(8,128)S(1)}, u32[]{:S(2)}, u32[]{:S(2)}) collective-permute-start(f32[64,256]{1,0:T(8,128)S(1)} %add.112), channel_id=1, source_target_pairs={{0,16},{16,0},{1,17},{17,1},{2,18},{18,2},{3,19},{19,3},{4,20},{20... | collective-permute-start | bytes 196616 | tf_op jit(solution)/shard_map/ppermute | solution.py:20
  138.8 2.4 %collective-permute-done.18 = f32[64,256]{1,0:T(8,128)S(1)} collective-permute-done((f32[64,256]{1,0:T(8,128)S(1)}, f32[64,256]{1,0:T(8,128)S(1)}, u32[]{:S(2)}, u32[]{:S(2)}) %collective-permute-start.18) | collective-permute-done | bytes 65568 | tf_op jit(solution)/shard_map/ppermute | solution.py:20
  141.8 1.3 reduce-scatter.2.cloned.1.call-done
  143.1 1.8 %dynamic-slice_bitcast_fusion.refs_1_ = f32[192,512]{1,0:T(8,128)} fusion(f32[1,2,192,512]{3,2,1,0:T(8,128)} %reduce-scatter.2.cloned.1.call-done, s32[]{:T(128)S(6)} %select_n.54), kind=kLoop, calls=%fused_computation.6 | loop fusion | bytes 786436 | tf_op jit(solution)/shard_map/squeeze | solution.py:220
  144.9 2.7 %collective-permute-start.19 = (f32[64,256]{1,0:T(8,128)}, f32[64,256]{1,0:T(8,128)S(1)}, u32[]{:S(2)}, u32[]{:S(2)}) collective-permute-start(f32[64,256]{1,0:T(8,128)} %shard_map.71), channel_id=1, source_target_pairs={{0,96},{32,0},{64,32},{96,64},{1,97},{33,1},{65,33},{97,65},{2,98}... | collective-permute-start | bytes 196616 | tf_op jit(solution)/shard_map/ppermute | solution.py:20
  147.7 0.8 collective-permute-start.20
  148.5 0.9 collective-permute-start.21
  149.4 1.5 collective-permute-start.9
  150.9 2.8 %collective-permute-done.20 = f32[64,256]{1,0:T(8,128)S(1)} collective-permute-done((f32[64,256]{1,0:T(8,128)}, f32[64,256]{1,0:T(8,128)S(1)}, u32[]{:S(2)}, u32[]{:S(2)}) %collective-permute-start.20) | collective-permute-done | bytes 65568 | tf_op jit(solution)/shard_map/ppermute | solution.py:20
  154.4 0.8 constant_dynamic-update-slice_fusion.3
  155.3 0.7 constant_dynamic-slice_fusion.refs_0_
  156.0 3.6 %collective-permute-done.9.refs_1_ = f32[192,512]{1,0:T(8,128)S(1)} collective-permute-done((f32[192,512]{1,0:T(8,128)}, f32[192,512]{1,0:T(8,128)S(1)}, u32[]{:S(2)}, u32[]{:S(2)}) %collective-permute-start.9) | collective-permute-done | bytes 393248 | tf_op jit(solution)/shard_map/ppermute | solution.py:20
  159.6 0.7 copy-done.4
  160.3 1.0 bitcast_add_fusion
  161.5 0.8 pad_maximum_fusion.2
  162.3 1.0 fusion.1
  163.3 0.8 pad_maximum_fusion
  (58 shorter events, 5.1 us)
Async XLA Ops:
  8.0 92.7 %all-gather.3.cloned.1.call-start = ((), (), s32[]{:S(2)}) async-start(), calls=%async_computation.2 | async-start | bytes 3538944 | tf_op jit(solution)/shard_map/all_gather | solution.py:210
  12.1 0.8 copy-start.3
  12.1 0.8 collective-permute-start
  12.8 130.3 %reduce-scatter.2.cloned.1.call-start = ((), (), s32[]{:S(2)}) async-start(), calls=%async_computation.1 | async-start | bytes 3932160 | tf_op jit(solution)/shard_map/reduce_scatter | solution.py:218
  12.9 31.6 %collective-permute-start.3 = (f32[192,512]{1,0:T(8,128)S(1)}, f32[192,512]{1,0:T(8,128)S(1)}, u32[]{:S(2)}, u32[]{:S(2)}) collective-permute-start(f32[192,512]{1,0:T(8,128)S(1)} %collective-permute-done.refs_2_), channel_id=1, source_target_pairs={{0,16},{16,0},{1,17},{17,1},{2,18},{18,2},{3,19},{19,3},{4,20},{20... | collective-permute-start | bytes 1179656 | tf_op jit(solution)/shard_map/ppermute | solution.py:20
  27.1 28.3 %collective-permute-start.1 = (f32[192,512]{1,0:T(8,128)S(1)}, f32[192,512]{1,0:T(8,128)S(1)}, u32[]{:S(2)}, u32[]{:S(2)}) collective-permute-start(f32[192,512]{1,0:T(8,128)S(1)} %collective-permute-done.refs_2_), channel_id=1, source_target_pairs={{0,32},{32,0},{64,96},{96,64},{1,33},{33,1},{65,97},{97,65},{2,34}... | collective-permute-start | bytes 1179656 | tf_op jit(solution)/shard_map/ppermute | solution.py:20
  44.5 19.1 %collective-permute-start.4 = (f32[192,512]{1,0:T(8,128)S(1)}, f32[192,512]{1,0:T(8,128)S(1)}, u32[]{:S(2)}, u32[]{:S(2)}) collective-permute-start(f32[192,512]{1,0:T(8,128)S(1)} %collective-permute-done.3.refs_3_), channel_id=1, source_target_pairs={{0,96},{32,64},{64,32},{96,0},{1,97},{33,65},{65,33},{97,1},{2,98}... | collective-permute-start | bytes 1179656 | tf_op jit(solution)/shard_map/ppermute | solution.py:20
  53.6 11.1 %collective-permute-start.7 = (f32[192,512]{1,0:T(8,128)S(1)}, f32[192,512]{1,0:T(8,128)S(1)}, u32[]{:S(2)}, u32[]{:S(2)}) collective-permute-start(f32[192,512]{1,0:T(8,128)S(1)} %collective-permute-done.3.refs_3_), channel_id=1, source_target_pairs={{0,32},{32,0},{64,96},{96,64},{1,33},{33,1},{65,97},{97,65},{2,34}... | collective-permute-start | bytes 1179656 | tf_op jit(solution)/shard_map/ppermute | solution.py:20
  54.8 23.3 %collective-permute-start.6 = (f32[192,512]{1,0:T(8,128)S(1)}, f32[192,512]{1,0:T(8,128)S(1)}, u32[]{:S(2)}, u32[]{:S(2)}) collective-permute-start(f32[192,512]{1,0:T(8,128)S(1)} %collective-permute-done.refs_2_), channel_id=1, source_target_pairs={{0,96},{32,64},{64,32},{96,0},{1,97},{33,65},{65,33},{97,1},{2,98}... | collective-permute-start | bytes 1179656 | tf_op jit(solution)/shard_map/ppermute | solution.py:20
  55.4 23.4 %collective-permute-start.2 = (f32[192,512]{1,0:T(8,128)S(1)}, f32[192,512]{1,0:T(8,128)S(1)}, u32[]{:S(2)}, u32[]{:S(2)}) collective-permute-start(f32[192,512]{1,0:T(8,128)S(1)} %collective-permute-done.1.refs_4_), channel_id=1, source_target_pairs={{0,96},{32,64},{64,32},{96,0},{1,97},{33,65},{65,33},{97,1},{2,98}... | collective-permute-start | bytes 1179656 | tf_op jit(solution)/shard_map/ppermute | solution.py:20
  63.6 15.2 %collective-permute-start.5 = (f32[192,512]{1,0:T(8,128)S(1)}, f32[192,512]{1,0:T(8,128)S(1)}, u32[]{:S(2)}, u32[]{:S(2)}) collective-permute-start(f32[192,512]{1,0:T(8,128)S(1)} %collective-permute-done.4.refs_5_), channel_id=1, source_target_pairs={{0,32},{32,0},{64,96},{96,64},{1,33},{33,1},{65,97},{97,65},{2,34}... | collective-permute-start | bytes 1179656 | tf_op jit(solution)/shard_map/ppermute | solution.py:20
  92.4 5.7 %collective-permute-start.8 = (f32[8,192,512]{2,1,0:T(8,128)S(1)}, f32[8,192,512]{2,1,0:T(8,128)S(1)}, u32[]{:S(2)}, u32[]{:S(2)}) collective-permute-start(f32[8,192,512]{2,1,0:T(8,128)S(1)} %get-tuple-element.11), channel_id=1, source_target_pairs={{0,1},{1,0},{2,3},{3,2},{4,5},{5,4},{6,7},{7,6},{8,9},{9,8},{10,11... | collective-permute-start | bytes 9437192 | tf_op jit(solution)/shard_map/ppermute | solution.py:20
  100.6 1.9 %copy-start = (f32[8,192,512]{2,1,0:T(8,128)S(1)}, f32[8,192,512]{2,1,0:T(8,128)}, u32[]{:S(2)}) copy-start(f32[8,192,512]{2,1,0:T(8,128)} %add.94.sum_ref) | copy-start | bytes 9437188
  102.5 1.9 %copy-start.1 = (f32[1536,512]{1,0:T(8,128)S(1)}, f32[1536,512]{1,0:T(8,128)}, u32[]{:S(2)}) copy-start(f32[1536,512]{1,0:T(8,128)} %all-gather.3.cloned.1.call-done) | copy-start | bytes 9437188
  108.0 0.7 copy-start.2
  108.8 1.6 collective-permute-start.10
  110.5 6.1 %collective-permute-start.11 = (f32[64,256]{1,0:T(8,128)S(1)}, f32[64,256]{1,0:T(8,128)S(1)}, u32[]{:S(2)}, u32[]{:S(2)}) collective-permute-start(f32[64,256]{1,0:T(8,128)S(1)} %get-tuple-element.18), channel_id=1, source_target_pairs={{0,32},{32,64},{64,96},{96,0},{1,33},{33,65},{65,97},{97,1},{2,34}... | collective-permute-start | bytes 196616 | tf_op jit(solution)/shard_map/ppermute | solution.py:20
  112.2 7.0 %collective-permute-start.12 = (f32[64,256]{1,0:T(8,128)S(1)}, f32[64,256]{1,0:T(8,128)S(1)}, u32[]{:S(2)}, u32[]{:S(2)}) collective-permute-start(f32[64,256]{1,0:T(8,128)S(1)} %get-tuple-element.20), channel_id=1, source_target_pairs={{0,64},{32,96},{64,0},{96,32},{1,65},{33,97},{65,1},{97,33},{2,66}... | collective-permute-start | bytes 196616 | tf_op jit(solution)/shard_map/ppermute | solution.py:20
  115.0 4.6 %collective-permute-start.13 = (f32[64,256]{1,0:T(8,128)S(1)}, f32[64,256]{1,0:T(8,128)S(1)}, u32[]{:S(2)}, u32[]{:S(2)}) collective-permute-start(f32[64,256]{1,0:T(8,128)S(1)} %get-tuple-element.19), channel_id=1, source_target_pairs={{0,96},{32,0},{64,32},{96,64},{1,97},{33,1},{65,33},{97,65},{2,98}... | collective-permute-start | bytes 196616 | tf_op jit(solution)/shard_map/ppermute | solution.py:20
  119.6 7.4 %collective-permute-start.14 = (f32[64,256]{1,0:T(8,128)S(1)}, f32[64,256]{1,0:T(8,128)S(1)}, u32[]{:S(2)}, u32[]{:S(2)}) collective-permute-start(f32[64,256]{1,0:T(8,128)S(1)} %add_add_fusion.1), channel_id=1, source_target_pairs={{0,4},{4,8},{8,12},{12,0},{1,5},{5,9},{9,13},{13,1},{2,6},{6,10},{... | collective-permute-start | bytes 196616 | tf_op jit(solution)/shard_map/ppermute | solution.py:20
  121.7 9.2 %collective-permute-start.15 = (f32[64,256]{1,0:T(8,128)S(1)}, f32[64,256]{1,0:T(8,128)S(1)}, u32[]{:S(2)}, u32[]{:S(2)}) collective-permute-start(f32[64,256]{1,0:T(8,128)S(1)} %add_add_fusion.1), channel_id=1, source_target_pairs={{0,8},{4,12},{8,0},{12,4},{1,9},{5,13},{9,1},{13,5},{2,10},{6,14},... | collective-permute-start | bytes 196616 | tf_op jit(solution)/shard_map/ppermute | solution.py:20
  124.0 6.9 %collective-permute-start.16 = (f32[64,256]{1,0:T(8,128)S(1)}, f32[64,256]{1,0:T(8,128)S(1)}, u32[]{:S(2)}, u32[]{:S(2)}) collective-permute-start(f32[64,256]{1,0:T(8,128)S(1)} %add_add_fusion.1), channel_id=1, source_target_pairs={{0,12},{4,0},{8,4},{12,8},{1,13},{5,1},{9,5},{13,9},{2,14},{6,2},{... | collective-permute-start | bytes 196616 | tf_op jit(solution)/shard_map/ppermute | solution.py:20
  130.9 4.4 %collective-permute-start.17 = (f32[64,256]{1,0:T(8,128)S(1)}, f32[64,256]{1,0:T(8,128)S(1)}, u32[]{:S(2)}, u32[]{:S(2)}) collective-permute-start(f32[64,256]{1,0:T(8,128)S(1)} %add_add_fusion), channel_id=1, source_target_pairs={{0,2},{2,0},{1,3},{3,1},{4,6},{6,4},{5,7},{7,5},{8,10},{10,8},{9,1... | collective-permute-start | bytes 196616 | tf_op jit(solution)/shard_map/ppermute | solution.py:20
  135.3 5.8 %collective-permute-start.18 = (f32[64,256]{1,0:T(8,128)S(1)}, f32[64,256]{1,0:T(8,128)S(1)}, u32[]{:S(2)}, u32[]{:S(2)}) collective-permute-start(f32[64,256]{1,0:T(8,128)S(1)} %add.112), channel_id=1, source_target_pairs={{0,16},{16,0},{1,17},{17,1},{2,18},{18,2},{3,19},{19,3},{4,20},{20... | collective-permute-start | bytes 196616 | tf_op jit(solution)/shard_map/ppermute | solution.py:20
  141.8 20.4 %copy-start.6 = (f32[2,256,256]{2,1,0:T(8,128)S(1)}, f32[2,256,256]{2,1,0:T(8,128)}, u32[]{:S(2)}) copy-start(f32[2,256,256]{2,1,0:T(8,128)} %param.8) | copy-start | bytes 1572868
  143.1 17.2 %copy-start.5 = (f32[1,2,192,512]{3,2,1,0:T(8,128)S(1)}, f32[1,2,192,512]{3,2,1,0:T(8,128)}, u32[]{:S(2)}) copy-start(f32[1,2,192,512]{3,2,1,0:T(8,128)} %reduce-scatter.2.cloned.1.call-done) | copy-start | bytes 2359300
  144.9 5.9 %collective-permute-start.19 = (f32[64,256]{1,0:T(8,128)}, f32[64,256]{1,0:T(8,128)S(1)}, u32[]{:S(2)}, u32[]{:S(2)}) collective-permute-start(f32[64,256]{1,0:T(8,128)} %shard_map.71), channel_id=1, source_target_pairs={{0,96},{32,0},{64,32},{96,64},{1,97},{33,1},{65,33},{97,65},{2,98}... | collective-permute-start | bytes 196616 | tf_op jit(solution)/shard_map/ppermute | solution.py:20
  147.7 6.0 %collective-permute-start.20 = (f32[64,256]{1,0:T(8,128)}, f32[64,256]{1,0:T(8,128)S(1)}, u32[]{:S(2)}, u32[]{:S(2)}) collective-permute-start(f32[64,256]{1,0:T(8,128)} %shard_map.71), channel_id=1, source_target_pairs={{0,64},{32,96},{64,0},{96,32},{1,65},{33,97},{65,1},{97,33},{2,66}... | collective-permute-start | bytes 196616 | tf_op jit(solution)/shard_map/ppermute | solution.py:20
  148.5 5.9 %collective-permute-start.21 = (f32[64,256]{1,0:T(8,128)}, f32[64,256]{1,0:T(8,128)S(1)}, u32[]{:S(2)}, u32[]{:S(2)}) collective-permute-start(f32[64,256]{1,0:T(8,128)} %shard_map.71), channel_id=1, source_target_pairs={{0,32},{32,64},{64,96},{96,0},{1,33},{33,65},{65,97},{97,1},{2,34}... | collective-permute-start | bytes 196616 | tf_op jit(solution)/shard_map/ppermute | solution.py:20
  149.4 10.2 %collective-permute-start.9 = (f32[192,512]{1,0:T(8,128)}, f32[192,512]{1,0:T(8,128)S(1)}, u32[]{:S(2)}, u32[]{:S(2)}) collective-permute-start(f32[192,512]{1,0:T(8,128)} %dynamic-slice_bitcast_fusion.refs_1_), channel_id=1, source_target_pairs={{0,2},{2,0},{1,3},{3,1},{4,6},{6,4},{5,7},{7,5},{8,10},{10,8},{9,1... | collective-permute-start | bytes 1179656 | tf_op jit(solution)/shard_map/ppermute | solution.py:20
  159.6 0.7 copy-start.4
  160.3 2.0 %collective-permute-start.22 = (f32[256,256]{1,0:T(8,128)}, f32[256,256]{1,0:T(8,128)S(1)}, u32[]{:S(2)}, u32[]{:S(2)}) collective-permute-start(f32[256,256]{1,0:T(8,128)} %shard_map.72), channel_id=1, source_target_pairs={{0,1},{1,0},{2,3},{3,2},{4,5},{5,4},{6,7},{7,6},{8,9},{9,8},{10,11... | collective-permute-start | bytes 786440 | tf_op jit(solution)/shard_map/ppermute | solution.py:20
Sparse Core Ops, SparseCore 0:
  12.9 85.6 all-gather.2
Sparse Core Ops, SparseCore 1:
  100.7 42.3 reduce-scatter.1

commit v9 on v7

--- a/solution.py
+++ b/solution.py
@@ -55,15 +55,16 @@
     return lax.dynamic_slice_in_dim(twice, (3 - me) * x.shape[0], 4 * x.shape[0], 0)
 
 
-def total(first, second, before):
+def total(first, second, given, taken):
     k = lax.axis_index("k")
     mine = jnp.where(k == 0, first, second) + swap(jnp.where(k == 0, second, first), "k")
     mine = scatter_four(mine, "y")
     mine = sum_four(mine, "z")
     mine = mine + swap(mine, "xl")
     mine = mine + swap(mine, "xh")
+    (mine,) = later([mine], [given])
     mine = gather_four(mine, "y")
-    (mine,) = later([mine], [before])
+    (mine,) = later([mine], [taken])
     other = swap(mine, "k")
     return jnp.where(k == 0, mine, other), jnp.where(k == 0, other, mine)
 
@@ -85,7 +86,7 @@
     return pl.pallas_call(
         lambda *refs: None,
         grid=(1,),
-        in_specs=[anywhere] * len(xs) + [pl.BlockSpec((8, 128), lambda i: (0, 0)) for _ in after],
+        in_specs=[anywhere] * len(xs) + [pl.BlockSpec((8, 128), lambda i: (0, 0))] * len(after),
         out_specs=[anywhere] * len(xs),
         out_shape=[jax.ShapeDtypeStruct(x.shape, x.dtype) for x in xs],
         input_output_aliases={i: i for i in range(len(xs))},
@@ -94,7 +95,7 @@
 
 
 def product_kernel(place_ref, a_ref, *refs):
-    pieces, (keep_ref, give_ref, high, low) = refs[:8], refs[8:]
+    pieces, (out_ref, high, low) = refs[:8], refs[-3:]
     piece = pieces[0].shape[0]
 
     @pl.when(pl.program_id(0) == 0)
@@ -107,34 +108,31 @@
 
     ah, al = halves(a_ref[...])
     f = lambda p, q: jnp.dot(p, q, preferred_element_type=F32)
-    out = f(ah, high[...]) + (f(ah, low[...]) + f(al, high[...]))
-    first, second = out[:piece], out[piece:]
-    lower = place_ref[8] == 0
-    keep_ref[0] = jnp.where(lower, first, second)
-    give_ref[0] = jnp.where(lower, second, first)
-
-
-def product(a, pieces, places):
+    out_ref[0] = f(ah, high[...]) + (f(ah, low[...]) + f(al, high[...]))
+
+
+def product(a, pieces, places, core, after=()):
     rows, cols = a.shape
     piece, width = pieces[0].shape
     blocks = rows // (2 * piece)
     whole = pl.BlockSpec((piece, width), lambda i, p: (0, 0), pipeline_mode=pl.Buffered(1))
-    out = pl.BlockSpec((1, piece, width), lambda i, p: (i, 0, 0))
     return pl.pallas_call(
         product_kernel,
         grid_spec=pltpu.PrefetchScalarGridSpec(
             num_scalar_prefetch=1,
             grid=(blocks,),
-            in_specs=[pl.BlockSpec((2 * piece, cols), lambda i, p: (i, 0))] + [whole] * 8,
-            out_specs=[out, out],
+            in_specs=[pl.BlockSpec((piece, cols), lambda i, p: (2 * i + p[core], 0))]
+            + [whole] * 8
+            + [pl.BlockSpec((1, 8, 128), lambda i, p: (0, 0, 0))] * len(after),
+            out_specs=pl.BlockSpec((1, piece, width), lambda i, p: (i, 0, 0)),
             scratch_shapes=[pltpu.VMEM((cols, width), BF)] * 2,
         ),
-        out_shape=[jax.ShapeDtypeStruct((blocks, piece, width), F32)] * 2,
+        out_shape=jax.ShapeDtypeStruct((blocks, piece, width), F32),
         compiler_params=pltpu.CompilerParams(vmem_limit_bytes=40 << 20),
         cost_estimate=pl.CostEstimate(
-            flops=6 * rows * cols * width, bytes_accessed=4 * (rows * cols + (rows + cols) * width), transcendentals=0
+            flops=3 * rows * cols * width, bytes_accessed=2 * (rows * cols + (rows + cols) * width), transcendentals=0
         ),
-    )(places, a, *pieces)
+    )(places, a, *pieces, *after)
 
 
 def update_kernel(sum_ref, x_ref, first_ref, second_ref):
@@ -168,14 +166,13 @@
 
 
 def gather_column(mine):
+    pair = swap(mine, "xh")
     one, three = (lambda i: i ^ 1), (lambda i: i ^ 3)
     mine1 = send(mine, "y", 4, one)
     mine3 = send(mine, "y", 4, three)
-    (pair,) = later([swap(mine, "xh")], [mine1, mine3])
     pair3 = send(pair, "y", 4, three)
+    mine2 = send(mine1, "y", 4, three)
     pair1 = send(pair, "y", 4, one)
-    pair3, mine1 = later([pair3, mine1], [pair1])
-    mine2 = send(mine1, "y", 4, three)
     pair2 = send(pair3, "y", 4, one)
     return [mine, pair, mine1, pair1, mine2, pair2, mine3, pair3]
 
@@ -190,13 +187,16 @@
         [jnp.dot(lower_panel[s], diag_factor[s], precision=HIGHEST) * masks[s] for s in range(NS)], axis=1
     )
     spots = jnp.arange(8, dtype=jnp.int32)
-    places = jnp.concatenate([((spots // 2) ^ y) * 2 + ((spots % 2) ^ xh), k[None]])
+    places = jnp.concatenate([((spots // 2) ^ y) * 2 + ((spots % 2) ^ xh), jnp.stack([k, 1 - k])]).astype(jnp.int32)
     mine = lax.ppermute(normed, ALL, transpose_pairs())
 
-    band = lax.all_gather(normed, ("z", "xl"), axis=0, tiled=False)
-
-    keep, give = product(ancestor_inverse, gather_column(mine), places)
+    (sent,) = later([normed], [mine])
+    band = lax.all_gather(sent, ("z", "xl"), axis=0, tiled=False)
+
+    pieces = gather_column(mine)
+    give = product(ancestor_inverse, pieces, places, 9)
     got = swap(give, "k")
+    keep = product(ancestor_inverse, pieces, places, 8, (give,))
     summed = keep + got
     first, second = updates(summed, band)
     summed = lax.psum_scatter(summed.reshape(4, 2, *summed.shape[1:]), "z", scatter_dimension=0, tiled=False)
@@ -205,7 +205,7 @@
     taken = swap(given, "xl")
     whole = kept + taken
     panels = [-masks[s] * whole[:, s * wide : (s + 1) * wide] for s in range(NS)]
-    first, second = total(first, second, taken)
+    first, second = total(first, second, given, taken)
     return jnp.stack(panels), jnp.stack([diag_block[0] + first, diag_block[1] + second])
 
 

time: 178 us -> 173 us (0.972)
  waiting for transfers between devices: 70.2 us -> 54.9 us
  starting transfers between devices: 42.9 us -> 51.6 us
  Pallas kernels: 24.6 us -> 29.2 us
  local copies, waits for them, and re-layouts: 13.2 us -> 9.71 us
    ppermute x22, waiting for transfers between devices: 67.3 us -> 48.1 us  [send(): return lax.ppermute(x, axis, [(i, to(i)) for i in range(size)])]
    ppermute x22, starting transfers between devices: 42.2 us -> 50.8 us  [send(): return lax.ppermute(x, axis, [(i, to(i)) for i in range(size)])]
    pallas_call x1 -> x2, Pallas kernels: 19 us -> 23.6 us  [product(): pl.pallas_call(product_kernel, grid_spec=pltpu.PrefetchScalarGridSpec(num...]
    unnamed x38 -> x24, local copies, waits for them, and re-layouts: 10.3 us -> 6 us
    all_gather x1, waiting for transfers between devices: 2.87 us -> 6.75 us  [local(): band = lax.all_gather(sent, ('z', 'xl'), axis=0, tiled=False)]
  transfers between devices with their start and end apart: 25 -> 25, of which waited for: 20 -> 18; matrix products, arithmetic and copies ran while one was open for 3% -> 4% of each run, Pallas kernels for 14% -> 16%
where the time goes in v9:
time: 173 us; the launch traced here: 171 us
  waiting for transfers between devices  54.9 us (32%)
  starting transfers between devices  51.6 us (30%)
  Pallas kernels  29.2 us (17%)
  between operations  15.7 us (9%)
  local copies, waits for them, and re-layouts  9.71 us (6%)
  other arithmetic  7.19 us (4%)
  matrix products  2.77 us (2%)
    ppermute x22, starting transfers between devices, send(): return lax.ppermute(x, axis, [(i, to(i)) for i in range(size)])  50.8 us
    ppermute x22, waiting for transfers between devices, send(): return lax.ppermute(x, axis, [(i, to(i)) for i in range(size)])  48.1 us
    pallas_call x2, Pallas kernels, product(): pl.pallas_call(product_kernel, grid_spec=pltpu.PrefetchScalarGridSpec(num...  23.6 us
    all_gather x1, waiting for transfers between devices, local(): band = lax.all_gather(sent, ('z', 'xl'), axis=0, tiled=False)  6.75 us
    unnamed x24, local copies, waits for them, and re-layouts  6 us
    pallas_call x1, Pallas kernels, updates(): pl.pallas_call(update_kernel, grid=(blocks,), in_specs=[spec] * 2, out_sp...  3.62 us
  transfers between devices with their start and end apart: 25, of which 18 were waited for; matrix products, arithmetic and copies ran while one was open for 4% of the time, Pallas kernels for 16%

profile of v9, /device:TPU:0, one launch (start us, length us, event | category | flops | bytes accessed | tf_op | source)
XLA Modules:
  0.0 171.1 jit_solution(595914369665068517)
XLA Ops:
  8.1 0.8 fusion.20
  9.2 1.4 convolution_multiply_fusion
  10.6 1.4 convolution_multiply_fusion.1
  12.8 0.7 copy-done.2
  14.3 14.4 %collective-permute-start.1 = (f32[192,512]{1,0:T(8,128)}, f32[192,512]{1,0:T(8,128)S(1)}, u32[]{:S(2)}, u32[]{:S(2)}) collective-permute-start(f32[192,512]{1,0:T(8,128)} %copy-done.2), channel_id=1, source_target_pairs={{0,16},{16,0},{1,17},{17,1},{2,18},{18,2},{3,19},{19,3},{4,20},{20... | collective-permute-start | bytes 1179656 | tf_op jit(solution)/shard_map/ppermute | solution.py:18
  28.7 3.8 %collective-permute-start.2 = (f32[192,512]{1,0:T(8,128)}, f32[192,512]{1,0:T(8,128)S(1)}, u32[]{:S(2)}, u32[]{:S(2)}) collective-permute-start(f32[192,512]{1,0:T(8,128)} %copy-done.2), channel_id=1, source_target_pairs={{0,32},{32,0},{64,96},{96,64},{1,33},{33,1},{65,97},{97,65},{2,34}... | collective-permute-start | bytes 1179656 | tf_op jit(solution)/shard_map/ppermute | solution.py:18
  32.5 6.2 %collective-permute-done.1.refs_1_ = f32[192,512]{1,0:T(8,128)S(1)} collective-permute-done((f32[192,512]{1,0:T(8,128)}, f32[192,512]{1,0:T(8,128)S(1)}, u32[]{:S(2)}, u32[]{:S(2)}) %collective-permute-start.1) | collective-permute-done | bytes 393248 | tf_op jit(solution)/shard_map/ppermute | solution.py:18
  38.7 7.9 %collective-permute-start.5 = (f32[192,512]{1,0:T(8,128)S(1)}, f32[192,512]{1,0:T(8,128)S(1)}, u32[]{:S(2)}, u32[]{:S(2)}) collective-permute-start(f32[192,512]{1,0:T(8,128)S(1)} %collective-permute-done.1.refs_1_), channel_id=1, source_target_pairs={{0,96},{32,64},{64,32},{96,0},{1,97},{33,65},{65,33},{97,1},{2,98}... | collective-permute-start | bytes 1179656 | tf_op jit(solution)/shard_map/ppermute | solution.py:18
  46.7 3.0 %collective-permute-start.3 = (f32[192,512]{1,0:T(8,128)S(1)}, f32[192,512]{1,0:T(8,128)S(1)}, u32[]{:S(2)}, u32[]{:S(2)}) collective-permute-start(f32[192,512]{1,0:T(8,128)S(1)} %collective-permute-done.1.refs_1_), channel_id=1, source_target_pairs={{0,32},{32,0},{64,96},{96,64},{1,33},{33,1},{65,97},{97,65},{2,34}... | collective-permute-start | bytes 1179656 | tf_op jit(solution)/shard_map/ppermute | solution.py:18
  49.7 2.6 %collective-permute-start.4 = (f32[192,512]{1,0:T(8,128)S(1)}, f32[192,512]{1,0:T(8,128)S(1)}, u32[]{:S(2)}, u32[]{:S(2)}) collective-permute-start(f32[192,512]{1,0:T(8,128)S(1)} %collective-permute-done.2.refs_2_), channel_id=1, source_target_pairs={{0,96},{32,64},{64,32},{96,0},{1,97},{33,65},{65,33},{97,1},{2,98}... | collective-permute-start | bytes 1179656 | tf_op jit(solution)/shard_map/ppermute | solution.py:18
  52.3 4.4 %collective-permute-done.5.refs_7_ = f32[192,512]{1,0:T(8,128)S(1)} collective-permute-done((f32[192,512]{1,0:T(8,128)S(1)}, f32[192,512]{1,0:T(8,128)S(1)}, u32[]{:S(2)}, u32[]{:S(2)}) %collective-permute-start.5) | collective-permute-done | bytes 393248 | tf_op jit(solution)/shard_map/ppermute | solution.py:18
  56.7 3.0 %collective-permute-start.6 = (f32[192,512]{1,0:T(8,128)S(1)}, f32[192,512]{1,0:T(8,128)S(1)}, u32[]{:S(2)}, u32[]{:S(2)}) collective-permute-start(f32[192,512]{1,0:T(8,128)S(1)} %collective-permute-done.5.refs_7_), channel_id=1, source_target_pairs={{0,32},{32,0},{64,96},{96,64},{1,33},{33,1},{65,97},{97,65},{2,34}... | collective-permute-start | bytes 1179656 | tf_op jit(solution)/shard_map/ppermute | solution.py:18
  59.8 5.3 %collective-permute-done.7.refs_6_ = f32[192,512]{1,0:T(8,128)S(1)} collective-permute-done((f32[192,512]{1,0:T(8,128)}, f32[192,512]{1,0:T(8,128)S(1)}, u32[]{:S(2)}, u32[]{:S(2)}) %collective-permute-start.7) | collective-permute-done | bytes 393248 | tf_op jit(solution)/shard_map/ppermute | solution.py:18
  65.1 6.3 %collective-permute-done.4.refs_4_ = f32[192,512]{1,0:T(8,128)S(1)} collective-permute-done((f32[192,512]{1,0:T(8,128)S(1)}, f32[192,512]{1,0:T(8,128)S(1)}, u32[]{:S(2)}, u32[]{:S(2)}) %collective-permute-start.4) | collective-permute-done | bytes 393248 | tf_op jit(solution)/shard_map/ppermute | solution.py:18
  71.3 1.0 copy-done.3
  72.3 11.8 %shard_map.68.refs_8_ = f32[8,192,512]{2,1,0:T(8,128)S(1)} custom-call(s32[10]{0:T(128)S(1)} %pad_add_fusion.place_ref, f32[3072,1536]{1,0:T(8,128)} %a_ref.3, f32[192,512]{1,0:T(8,128)S(1)} %copy-done.3, f32[192,512]{1,0:T(8,128)S(1)} %collective-permute-done.1.refs_1_, f32[192,512]{1,0:T(8,128)S(1)} %collective-permute-done.2.refs_2_, ...), custom_call_target="tpu_custom_call" | custom-call | flops 7247757312 | bytes 14155776 | tf_op jit(solution)/shard_map/pallas_call | solution.py:119
  84.2 11.8 %shard_map.69 = f32[8,192,512]{2,1,0:T(8,128)S(1)} custom-call(s32[10]{0:T(128)S(1)} %pad_add_fusion.place_ref, f32[3072,1536]{1,0:T(8,128)} %a_ref.3, f32[192,512]{1,0:T(8,128)S(1)} %copy-done.3, f32[192,512]{1,0:T(8,128)S(1)} %collective-permute-done.1.refs_1_, f32[192,512]{1,0:T(8,128)S(1)} %collective-permute-done.2.refs_2_, ...), custom_call_target="tpu_custom_call" | custom-call | flops 7247757312 | bytes 14155776 | tf_op jit(solution)/shard_map/pallas_call | solution.py:119
  96.0 2.4 %add.106.sum_ref = f32[8,192,512]{2,1,0:T(8,128)} add(f32[8,192,512]{2,1,0:T(8,128)S(1)} %shard_map.69, f32[8,192,512]{2,1,0:T(8,128)S(1)} %collective-permute-done.8) | non-fusion elementwise | flops 786432 | bytes 9437184 | tf_op jit(solution)/shard_map/add | solution.py:200
  98.5 6.8 %all-gather.3.cloned.1.call-done = f32[1536,512]{1,0:T(8,128)} async-done(((f32[192,512]{1,0:T(8,128)}), f32[1536,512]{1,0:T(8,128)}) %all-gather.3.cloned.1.call-update) | async-done | bytes 3145744 | tf_op jit(solution)/shard_map/all_gather | solution.py:194
  105.3 1.9 %copy-done.1 = f32[1536,512]{1,0:T(8,128)S(1)} copy-done((f32[1536,512]{1,0:T(8,128)S(1)}, f32[1536,512]{1,0:T(8,128)}, u32[]{:S(2)}) %copy-start.1) | copy-done | bytes 3145752
  107.1 3.6 %shard_map.71 = (f32[256,256]{1,0:T(8,128)S(1)}, f32[256,256]{1,0:T(8,128)S(1)}) custom-call(f32[8,192,512]{2,1,0:T(8,128)S(1)} %copy-done, f32[8,192,512]{2,1,0:T(8,128)S(1)} %bitcast.41), custom_call_target="tpu_custom_call" | custom-call | flops 1207959552 | bytes 6291456 | tf_op jit(solution)/shard_map/pallas_call | solution.py:155
  111.6 1.5 collective-permute-done.10
  113.2 2.8 %collective-permute-start.13 = (f32[64,256]{1,0:T(8,128)S(1)}, f32[64,256]{1,0:T(8,128)S(1)}, u32[]{:S(2)}, u32[]{:S(2)}) collective-permute-start(f32[64,256]{1,0:T(8,128)S(1)} %get-tuple-element.11), channel_id=1, source_target_pairs={{0,96},{32,0},{64,32},{96,64},{1,97},{33,1},{65,33},{97,65},{2,98}... | collective-permute-start | bytes 196616 | tf_op jit(solution)/shard_map/ppermute | solution.py:18
  116.0 0.8 collective-permute-start.12
  116.8 0.9 collective-permute-start.11
  118.3 4.2 %collective-permute-done.12 = f32[64,256]{1,0:T(8,128)S(1)} collective-permute-done((f32[64,256]{1,0:T(8,128)S(1)}, f32[64,256]{1,0:T(8,128)S(1)}, u32[]{:S(2)}, u32[]{:S(2)}) %collective-permute-start.12) | collective-permute-done | bytes 65568 | tf_op jit(solution)/shard_map/ppermute | solution.py:18
  122.5 1.2 collective-permute-done.11
  123.8 1.4 collective-permute-start.16
  125.9 1.0 collective-permute-start.14
  126.8 3.4 %collective-permute-done.16 = f32[64,256]{1,0:T(8,128)S(1)} collective-permute-done((f32[64,256]{1,0:T(8,128)S(1)}, f32[64,256]{1,0:T(8,128)S(1)}, u32[]{:S(2)}, u32[]{:S(2)}) %collective-permute-start.16) | collective-permute-done | bytes 65568 | tf_op jit(solution)/shard_map/ppermute | solution.py:18
  130.2 2.9 %collective-permute-done.15 = f32[64,256]{1,0:T(8,128)S(1)} collective-permute-done((f32[64,256]{1,0:T(8,128)S(1)}, f32[64,256]{1,0:T(8,128)S(1)}, u32[]{:S(2)}, u32[]{:S(2)}) %collective-permute-start.15) | collective-permute-done | bytes 65568 | tf_op jit(solution)/shard_map/ppermute | solution.py:18
  133.1 1.0 collective-permute-done.14
  134.1 1.4 collective-permute-start.17
  135.5 3.0 %collective-permute-done.17 = f32[64,256]{1,0:T(8,128)S(1)} collective-permute-done((f32[64,256]{1,0:T(8,128)S(1)}, f32[64,256]{1,0:T(8,128)S(1)}, u32[]{:S(2)}, u32[]{:S(2)}) %collective-permute-start.17) | collective-permute-done | bytes 65568 | tf_op jit(solution)/shard_map/ppermute | solution.py:18
  138.5 2.9 %collective-permute-start.18 = (f32[64,256]{1,0:T(8,128)S(1)}, f32[64,256]{1,0:T(8,128)S(1)}, u32[]{:S(2)}, u32[]{:S(2)}) collective-permute-start(f32[64,256]{1,0:T(8,128)S(1)} %add.124), channel_id=1, source_target_pairs={{0,16},{16,0},{1,17},{17,1},{2,18},{18,2},{3,19},{19,3},{4,20},{20... | collective-permute-start | bytes 196616 | tf_op jit(solution)/shard_map/ppermute | solution.py:18
  141.3 3.0 %collective-permute-done.18 = f32[64,256]{1,0:T(8,128)S(1)} collective-permute-done((f32[64,256]{1,0:T(8,128)S(1)}, f32[64,256]{1,0:T(8,128)S(1)}, u32[]{:S(2)}, u32[]{:S(2)}) %collective-permute-start.18) | collective-permute-done | bytes 65568 | tf_op jit(solution)/shard_map/ppermute | solution.py:18
  145.0 1.9 %dynamic-slice_bitcast_fusion.refs_1_ = f32[192,512]{1,0:T(8,128)} fusion(f32[1,2,192,512]{3,2,1,0:T(8,128)} %reduce-scatter.2.cloned.1.call-done, s32[]{:T(128)S(6)} %select_n.67), kind=kLoop, calls=%fused_computation.6 | loop fusion | bytes 786436 | tf_op jit(solution)/shard_map/squeeze | solution.py:204
  148.1 1.3 collective-permute-start.9
  149.3 1.3 collective-permute-start.20
  150.7 0.9 collective-permute-start.21
  152.2 3.1 %collective-permute-done.20 = f32[64,256]{1,0:T(8,128)S(1)} collective-permute-done((f32[64,256]{1,0:T(8,128)}, f32[64,256]{1,0:T(8,128)S(1)}, u32[]{:S(2)}, u32[]{:S(2)}) %collective-permute-start.20) | collective-permute-done | bytes 65568 | tf_op jit(solution)/shard_map/ppermute | solution.py:18
  155.3 1.0 collective-permute-done.21
  156.4 0.8 constant_dynamic-update-slice_fusion.3
  158.4 0.7 copy-done.6
  159.8 1.0 bitcast_add_fusion
  161.0 0.8 pad_maximum_fusion.2
  161.8 1.0 fusion.1
  162.8 0.8 pad_maximum_fusion
  (63 shorter events, 8.9 us)
Async XLA Ops:
  8.0 97.3 %all-gather.3.cloned.1.call-start = ((), (), s32[]{:S(2)}) async-start(), calls=%async_computation.2 | async-start | bytes 3538944 | tf_op jit(solution)/shard_map/all_gather | solution.py:194
  12.0 0.8 copy-start.5
  12.1 0.7 collective-permute-start
  12.8 0.7 copy-start.2
  14.3 130.7 %reduce-scatter.2.cloned.1.call-start = ((), (), s32[]{:S(2)}) async-start(), calls=%async_computation.1 | async-start | bytes 3932160 | tf_op jit(solution)/shard_map/reduce_scatter | solution.py:202
  14.3 24.4 %collective-permute-start.1 = (f32[192,512]{1,0:T(8,128)}, f32[192,512]{1,0:T(8,128)S(1)}, u32[]{:S(2)}, u32[]{:S(2)}) collective-permute-start(f32[192,512]{1,0:T(8,128)} %copy-done.2), channel_id=1, source_target_pairs={{0,16},{16,0},{1,17},{17,1},{2,18},{18,2},{3,19},{19,3},{4,20},{20... | collective-permute-start | bytes 1179656 | tf_op jit(solution)/shard_map/ppermute | solution.py:18
  28.7 21.0 %collective-permute-start.2 = (f32[192,512]{1,0:T(8,128)}, f32[192,512]{1,0:T(8,128)S(1)}, u32[]{:S(2)}, u32[]{:S(2)}) collective-permute-start(f32[192,512]{1,0:T(8,128)} %copy-done.2), channel_id=1, source_target_pairs={{0,32},{32,0},{64,96},{96,64},{1,33},{33,1},{65,97},{97,65},{2,34}... | collective-permute-start | bytes 1179656 | tf_op jit(solution)/shard_map/ppermute | solution.py:18
  38.7 17.9 %collective-permute-start.5 = (f32[192,512]{1,0:T(8,128)S(1)}, f32[192,512]{1,0:T(8,128)S(1)}, u32[]{:S(2)}, u32[]{:S(2)}) collective-permute-start(f32[192,512]{1,0:T(8,128)S(1)} %collective-permute-done.1.refs_1_), channel_id=1, source_target_pairs={{0,96},{32,64},{64,32},{96,0},{1,97},{33,65},{65,33},{97,1},{2,98}... | collective-permute-start | bytes 1179656 | tf_op jit(solution)/shard_map/ppermute | solution.py:18
  46.6 18.5 %collective-permute-start.7 = (f32[192,512]{1,0:T(8,128)}, f32[192,512]{1,0:T(8,128)S(1)}, u32[]{:S(2)}, u32[]{:S(2)}) collective-permute-start(f32[192,512]{1,0:T(8,128)} %copy-done.2), channel_id=1, source_target_pairs={{0,96},{32,64},{64,32},{96,0},{1,97},{33,65},{65,33},{97,1},{2,98}... | collective-permute-start | bytes 1179656 | tf_op jit(solution)/shard_map/ppermute | solution.py:18
  46.7 18.4 %collective-permute-start.3 = (f32[192,512]{1,0:T(8,128)S(1)}, f32[192,512]{1,0:T(8,128)S(1)}, u32[]{:S(2)}, u32[]{:S(2)}) collective-permute-start(f32[192,512]{1,0:T(8,128)S(1)} %collective-permute-done.1.refs_1_), channel_id=1, source_target_pairs={{0,32},{32,0},{64,96},{96,64},{1,33},{33,1},{65,97},{97,65},{2,34}... | collective-permute-start | bytes 1179656 | tf_op jit(solution)/shard_map/ppermute | solution.py:18
  49.7 21.6 %collective-permute-start.4 = (f32[192,512]{1,0:T(8,128)S(1)}, f32[192,512]{1,0:T(8,128)S(1)}, u32[]{:S(2)}, u32[]{:S(2)}) collective-permute-start(f32[192,512]{1,0:T(8,128)S(1)} %collective-permute-done.2.refs_2_), channel_id=1, source_target_pairs={{0,96},{32,64},{64,32},{96,0},{1,97},{33,65},{65,33},{97,1},{2,98}... | collective-permute-start | bytes 1179656 | tf_op jit(solution)/shard_map/ppermute | solution.py:18
  56.7 14.7 %collective-permute-start.6 = (f32[192,512]{1,0:T(8,128)S(1)}, f32[192,512]{1,0:T(8,128)S(1)}, u32[]{:S(2)}, u32[]{:S(2)}) collective-permute-start(f32[192,512]{1,0:T(8,128)S(1)} %collective-permute-done.5.refs_7_), channel_id=1, source_target_pairs={{0,32},{32,0},{64,96},{96,64},{1,33},{33,1},{65,97},{97,65},{2,34}... | collective-permute-start | bytes 1179656 | tf_op jit(solution)/shard_map/ppermute | solution.py:18
  71.3 1.0 copy-start.3
  84.1 11.9 %collective-permute-start.8 = (f32[8,192,512]{2,1,0:T(8,128)S(1)}, f32[8,192,512]{2,1,0:T(8,128)S(1)}, u32[]{:S(2)}, u32[]{:S(2)}) collective-permute-start(f32[8,192,512]{2,1,0:T(8,128)S(1)} %shard_map.68.refs_8_), channel_id=1, source_target_pairs={{0,1},{1,0},{2,3},{3,2},{4,5},{5,4},{6,7},{7,6},{8,9},{9,8},{10,11... | collective-permute-start | bytes 9437192 | tf_op jit(solution)/shard_map/ppermute | solution.py:18
  98.5 6.8 %copy-start = (f32[8,192,512]{2,1,0:T(8,128)S(1)}, f32[8,192,512]{2,1,0:T(8,128)}, u32[]{:S(2)}) copy-start(f32[8,192,512]{2,1,0:T(8,128)} %add.106.sum_ref) | copy-start | bytes 9437188
  105.3 1.9 %copy-start.1 = (f32[1536,512]{1,0:T(8,128)S(1)}, f32[1536,512]{1,0:T(8,128)}, u32[]{:S(2)}) copy-start(f32[1536,512]{1,0:T(8,128)} %all-gather.3.cloned.1.call-done) | copy-start | bytes 9437188
  110.8 0.7 copy-start.4
  111.5 1.6 collective-permute-start.10
  113.2 5.1 %collective-permute-start.13 = (f32[64,256]{1,0:T(8,128)S(1)}, f32[64,256]{1,0:T(8,128)S(1)}, u32[]{:S(2)}, u32[]{:S(2)}) collective-permute-start(f32[64,256]{1,0:T(8,128)S(1)} %get-tuple-element.11), channel_id=1, source_target_pairs={{0,96},{32,0},{64,32},{96,64},{1,97},{33,1},{65,33},{97,65},{2,98}... | collective-permute-start | bytes 196616 | tf_op jit(solution)/shard_map/ppermute | solution.py:18
  116.0 6.5 %collective-permute-start.12 = (f32[64,256]{1,0:T(8,128)S(1)}, f32[64,256]{1,0:T(8,128)S(1)}, u32[]{:S(2)}, u32[]{:S(2)}) collective-permute-start(f32[64,256]{1,0:T(8,128)S(1)} %get-tuple-element.12), channel_id=1, source_target_pairs={{0,64},{32,96},{64,0},{96,32},{1,65},{33,97},{65,1},{97,33},{2,66}... | collective-permute-start | bytes 196616 | tf_op jit(solution)/shard_map/ppermute | solution.py:18
  116.8 6.9 %collective-permute-start.11 = (f32[64,256]{1,0:T(8,128)S(1)}, f32[64,256]{1,0:T(8,128)S(1)}, u32[]{:S(2)}, u32[]{:S(2)}) collective-permute-start(f32[64,256]{1,0:T(8,128)S(1)} %get-tuple-element.10), channel_id=1, source_target_pairs={{0,32},{32,64},{64,96},{96,0},{1,33},{33,65},{65,97},{97,1},{2,34}... | collective-permute-start | bytes 196616 | tf_op jit(solution)/shard_map/ppermute | solution.py:18
  123.8 6.4 %collective-permute-start.16 = (f32[64,256]{1,0:T(8,128)S(1)}, f32[64,256]{1,0:T(8,128)S(1)}, u32[]{:S(2)}, u32[]{:S(2)}) collective-permute-start(f32[64,256]{1,0:T(8,128)S(1)} %add_add_fusion.1), channel_id=1, source_target_pairs={{0,12},{4,0},{8,4},{12,8},{1,13},{5,1},{9,5},{13,9},{2,14},{6,2},{... | collective-permute-start | bytes 196616 | tf_op jit(solution)/shard_map/ppermute | solution.py:18
  125.2 7.9 %collective-permute-start.15 = (f32[64,256]{1,0:T(8,128)S(1)}, f32[64,256]{1,0:T(8,128)S(1)}, u32[]{:S(2)}, u32[]{:S(2)}) collective-permute-start(f32[64,256]{1,0:T(8,128)S(1)} %add_add_fusion.1), channel_id=1, source_target_pairs={{0,8},{4,12},{8,0},{12,4},{1,9},{5,13},{9,1},{13,5},{2,10},{6,14},... | collective-permute-start | bytes 196616 | tf_op jit(solution)/shard_map/ppermute | solution.py:18
  125.9 8.2 %collective-permute-start.14 = (f32[64,256]{1,0:T(8,128)S(1)}, f32[64,256]{1,0:T(8,128)S(1)}, u32[]{:S(2)}, u32[]{:S(2)}) collective-permute-start(f32[64,256]{1,0:T(8,128)S(1)} %add_add_fusion.1), channel_id=1, source_target_pairs={{0,4},{4,8},{8,12},{12,0},{1,5},{5,9},{9,13},{13,1},{2,6},{6,10},{... | collective-permute-start | bytes 196616 | tf_op jit(solution)/shard_map/ppermute | solution.py:18
  134.1 4.3 %collective-permute-start.17 = (f32[64,256]{1,0:T(8,128)S(1)}, f32[64,256]{1,0:T(8,128)S(1)}, u32[]{:S(2)}, u32[]{:S(2)}) collective-permute-start(f32[64,256]{1,0:T(8,128)S(1)} %add_add_fusion), channel_id=1, source_target_pairs={{0,2},{2,0},{1,3},{3,1},{4,6},{6,4},{5,7},{7,5},{8,10},{10,8},{9,1... | collective-permute-start | bytes 196616 | tf_op jit(solution)/shard_map/ppermute | solution.py:18
  138.5 5.8 %collective-permute-start.18 = (f32[64,256]{1,0:T(8,128)S(1)}, f32[64,256]{1,0:T(8,128)S(1)}, u32[]{:S(2)}, u32[]{:S(2)}) collective-permute-start(f32[64,256]{1,0:T(8,128)S(1)} %add.124), channel_id=1, source_target_pairs={{0,16},{16,0},{1,17},{17,1},{2,18},{18,2},{3,19},{19,3},{4,20},{20... | collective-permute-start | bytes 196616 | tf_op jit(solution)/shard_map/ppermute | solution.py:18
  145.0 16.8 %copy-start.8 = (f32[2,256,256]{2,1,0:T(8,128)S(1)}, f32[2,256,256]{2,1,0:T(8,128)}, u32[]{:S(2)}) copy-start(f32[2,256,256]{2,1,0:T(8,128)} %param.8) | copy-start | bytes 1572868
  145.0 14.9 %copy-start.7 = (f32[1,2,192,512]{3,2,1,0:T(8,128)S(1)}, f32[1,2,192,512]{3,2,1,0:T(8,128)}, u32[]{:S(2)}) copy-start(f32[1,2,192,512]{3,2,1,0:T(8,128)} %reduce-scatter.2.cloned.1.call-done) | copy-start | bytes 2359300
  147.5 4.7 %collective-permute-start.19 = (f32[64,256]{1,0:T(8,128)}, f32[64,256]{1,0:T(8,128)S(1)}, u32[]{:S(2)}, u32[]{:S(2)}) collective-permute-start(f32[64,256]{1,0:T(8,128)} %shard_map.72), channel_id=1, source_target_pairs={{0,96},{32,0},{64,32},{96,64},{1,97},{33,1},{65,33},{97,65},{2,98}... | collective-permute-start | bytes 196616 | tf_op jit(solution)/shard_map/ppermute | solution.py:18
  148.1 10.3 %collective-permute-start.9 = (f32[192,512]{1,0:T(8,128)}, f32[192,512]{1,0:T(8,128)S(1)}, u32[]{:S(2)}, u32[]{:S(2)}) collective-permute-start(f32[192,512]{1,0:T(8,128)} %dynamic-slice_bitcast_fusion.refs_1_), channel_id=1, source_target_pairs={{0,2},{2,0},{1,3},{3,1},{4,6},{6,4},{5,7},{7,5},{8,10},{10,8},{9,1... | collective-permute-start | bytes 1179656 | tf_op jit(solution)/shard_map/ppermute | solution.py:18
  149.3 6.0 %collective-permute-start.20 = (f32[64,256]{1,0:T(8,128)}, f32[64,256]{1,0:T(8,128)S(1)}, u32[]{:S(2)}, u32[]{:S(2)}) collective-permute-start(f32[64,256]{1,0:T(8,128)} %shard_map.72), channel_id=1, source_target_pairs={{0,64},{32,96},{64,0},{96,32},{1,65},{33,97},{65,1},{97,33},{2,66}... | collective-permute-start | bytes 196616 | tf_op jit(solution)/shard_map/ppermute | solution.py:18
  150.7 5.7 %collective-permute-start.21 = (f32[64,256]{1,0:T(8,128)}, f32[64,256]{1,0:T(8,128)S(1)}, u32[]{:S(2)}, u32[]{:S(2)}) collective-permute-start(f32[64,256]{1,0:T(8,128)} %shard_map.72), channel_id=1, source_target_pairs={{0,32},{32,64},{64,96},{96,0},{1,33},{33,65},{65,97},{97,1},{2,34}... | collective-permute-start | bytes 196616 | tf_op jit(solution)/shard_map/ppermute | solution.py:18
  158.4 0.7 copy-start.6
  159.8 2.0 %collective-permute-start.22 = (f32[256,256]{1,0:T(8,128)}, f32[256,256]{1,0:T(8,128)S(1)}, u32[]{:S(2)}, u32[]{:S(2)}) collective-permute-start(f32[256,256]{1,0:T(8,128)} %shard_map.73), channel_id=1, source_target_pairs={{0,1},{1,0},{2,3},{3,2},{4,5},{5,4},{6,7},{7,6},{8,9},{9,8},{10,11... | collective-permute-start | bytes 786440 | tf_op jit(solution)/shard_map/ppermute | solution.py:18
Sparse Core Ops, SparseCore 0:
  14.4 90.8 all-gather.2
Sparse Core Ops, SparseCore 1:
  98.6 43.8 reduce-scatter.1

commit v10 on v7

--- a/solution.py
+++ b/solution.py
@@ -1,3 +1,5 @@
+import functools
+
 import jax
 import jax.numpy as jnp
 from jax import lax
@@ -6,6 +8,8 @@
 from jax.sharding import Mesh, PartitionSpec as P
 
 BS = 64
+CUT = 2
+PARTS = ((0,), (1,))
 NS = 2
 HIGH = lax.Precision.HIGH
 HIGHEST = lax.Precision.HIGHEST
@@ -85,7 +89,7 @@
     return pl.pallas_call(
         lambda *refs: None,
         grid=(1,),
-        in_specs=[anywhere] * len(xs) + [pl.BlockSpec((8, 128), lambda i: (0, 0)) for _ in after],
+        in_specs=[anywhere] * len(xs) + [pl.BlockSpec((8, 128), lambda i: (0, 0))] * len(after),
         out_specs=[anywhere] * len(xs),
         out_shape=[jax.ShapeDtypeStruct(x.shape, x.dtype) for x in xs],
         input_output_aliases={i: i for i in range(len(xs))},
@@ -93,8 +97,9 @@
     )(*xs, *after)
 
 
-def product_kernel(place_ref, a_ref, *refs):
-    pieces, (keep_ref, give_ref, high, low) = refs[:8], refs[8:]
+def product_kernel(place_ref, *refs, count):
+    strips, pieces = refs[:count], refs[count : count + 8]
+    keep_ref, give_ref, high, low = refs[-4:]
     piece = pieces[0].shape[0]
 
     @pl.when(pl.program_id(0) == 0)
@@ -105,77 +110,84 @@
             high[rows, :] = xh
             low[rows, :] = xl
 
-    ah, al = halves(a_ref[...])
+    ah, al = halves(jnp.concatenate([strip[...] for strip in strips], axis=0))
     f = lambda p, q: jnp.dot(p, q, preferred_element_type=F32)
     out = f(ah, high[...]) + (f(ah, low[...]) + f(al, high[...]))
-    first, second = out[:piece], out[piece:]
+    some = out.shape[0] // 2
+    first, second = out[:some], out[some:]
     lower = place_ref[8] == 0
     keep_ref[0] = jnp.where(lower, first, second)
     give_ref[0] = jnp.where(lower, second, first)
 
 
-def product(a, pieces, places):
+def product(a, pieces, places, part, after):
     rows, cols = a.shape
     piece, width = pieces[0].shape
     blocks = rows // (2 * piece)
+    share = piece // CUT
+    some = len(part) * share
+    strips = [
+        pl.BlockSpec((share, cols), lambda i, p, n=CUT * core + t: (2 * CUT * i + n, 0)) for core in range(2) for t in part
+    ]
     whole = pl.BlockSpec((piece, width), lambda i, p: (0, 0), pipeline_mode=pl.Buffered(1))
-    out = pl.BlockSpec((1, piece, width), lambda i, p: (i, 0, 0))
+    out = pl.BlockSpec((1, some, width), lambda i, p: (i, 0, 0))
     return pl.pallas_call(
-        product_kernel,
+        functools.partial(product_kernel, count=len(strips)),
         grid_spec=pltpu.PrefetchScalarGridSpec(
             num_scalar_prefetch=1,
             grid=(blocks,),
-            in_specs=[pl.BlockSpec((2 * piece, cols), lambda i, p: (i, 0))] + [whole] * 8,
+            in_specs=[*strips] + [whole] * 8 + [pl.BlockSpec((1, 8, 128), lambda i, p: (0, 0, 0))] * len(after),
             out_specs=[out, out],
             scratch_shapes=[pltpu.VMEM((cols, width), BF)] * 2,
         ),
-        out_shape=[jax.ShapeDtypeStruct((blocks, piece, width), F32)] * 2,
+        out_shape=[jax.ShapeDtypeStruct((blocks, some, width), F32)] * 2,
         compiler_params=pltpu.CompilerParams(vmem_limit_bytes=40 << 20),
         cost_estimate=pl.CostEstimate(
-            flops=6 * rows * cols * width, bytes_accessed=4 * (rows * cols + (rows + cols) * width), transcendentals=0
+            flops=12 * blocks * some * cols * width,
+            bytes_accessed=8 * blocks * some * (cols + width) + 4 * cols * width,
+            transcendentals=0,
         ),
-    )(places, a, *pieces)
-
-
-def update_kernel(sum_ref, x_ref, first_ref, second_ref):
+    )(places, *[a] * len(strips), *pieces, *after)
+
+
+def update_kernel(one_ref, two_ref, x_ref, first_ref, second_ref):
     @pl.when(pl.program_id(0) == 0)
     def _():
         first_ref[...] = jnp.zeros_like(first_ref)
         second_ref[...] = jnp.zeros_like(second_ref)
 
-    both, x = sum_ref[0], x_ref[0]
+    both, x = jnp.concatenate([one_ref[0], two_ref[0]], axis=0), x_ref[0]
     wide = first_ref.shape[0]
     first_ref[...] += dot3(x[:, :wide], both[:, :wide], ((0,), (0,)))
     second_ref[...] += dot3(x[:, wide:], both[:, wide:], ((0,), (0,)))
 
 
 def updates(summed, x):
-    blocks, piece, width = summed.shape
+    blocks, piece, width = x.shape
     wide = width // NS
-    spec = pl.BlockSpec((1, piece, width), lambda i: (i, 0, 0))
+    specs = [pl.BlockSpec((1, *v.shape[1:]), lambda i: (i, 0, 0)) for v in (*summed, x)]
     update = pl.BlockSpec((wide, wide), lambda i: (0, 0))
     return pl.pallas_call(
         update_kernel,
         grid=(blocks,),
-        in_specs=[spec] * 2,
+        in_specs=specs,
         out_specs=[update, update],
         out_shape=[jax.ShapeDtypeStruct((wide, wide), F32)] * 2,
         compiler_params=pltpu.CompilerParams(vmem_limit_bytes=16 << 20),
         cost_estimate=pl.CostEstimate(
             flops=6 * blocks * piece * width * wide, bytes_accessed=8 * blocks * piece * width, transcendentals=0
         ),
-    )(summed, x)
+    )(*summed, x)
 
 
 def gather_column(mine):
+    pair = swap(mine, "xh")
     one, three = (lambda i: i ^ 1), (lambda i: i ^ 3)
     mine1 = send(mine, "y", 4, one)
     mine3 = send(mine, "y", 4, three)
-    (pair,) = later([swap(mine, "xh")], [mine1, mine3])
     pair3 = send(pair, "y", 4, three)
+    mine2 = send(mine1, "y", 4, three)
     pair1 = send(pair, "y", 4, one)
-    pair3, mine1 = later([pair3, mine1], [pair1])
-    mine2 = send(mine1, "y", 4, three)
     pair2 = send(pair3, "y", 4, one)
     return [mine, pair, mine1, pair1, mine2, pair2, mine3, pair3]
 
@@ -193,17 +205,22 @@
     places = jnp.concatenate([((spots // 2) ^ y) * 2 + ((spots % 2) ^ xh), k[None]])
     mine = lax.ppermute(normed, ALL, transpose_pairs())
 
-    band = lax.all_gather(normed, ("z", "xl"), axis=0, tiled=False)
-
-    keep, give = product(ancestor_inverse, gather_column(mine), places)
-    got = swap(give, "k")
-    summed = keep + got
+    (sent,) = later([normed], [mine])
+    band = lax.all_gather(sent, ("z", "xl"), axis=0, tiled=False)
+
+    pieces = gather_column(mine)
+    summed = []
+    for part in PARTS:
+        keep, give = product(ancestor_inverse, pieces, places, part, summed)
+        summed.append(keep + swap(give, "k"))
     first, second = updates(summed, band)
-    summed = lax.psum_scatter(summed.reshape(4, 2, *summed.shape[1:]), "z", scatter_dimension=0, tiled=False)
-    kept = lax.dynamic_slice_in_dim(summed, xl, 1, 0)[0]
-    given = lax.dynamic_slice_in_dim(summed, 1 - xl, 1, 0)[0]
-    taken = swap(given, "xl")
-    whole = kept + taken
+    whole = []
+    for one in summed:
+        over_z = lax.psum_scatter(one.reshape(4, 2, *one.shape[1:]), "z", scatter_dimension=0, tiled=False)
+        kept = lax.dynamic_slice_in_dim(over_z, xl, 1, 0)[0]
+        taken = swap(lax.dynamic_slice_in_dim(over_z, 1 - xl, 1, 0)[0], "xl")
+        whole.append(kept + taken)
+    whole = jnp.concatenate(whole, axis=0)
     panels = [-masks[s] * whole[:, s * wide : (s + 1) * wide] for s in range(NS)]
     first, second = total(first, second, taken)
     return jnp.stack(panels), jnp.stack([diag_block[0] + first, diag_block[1] + second])

time: 178 us -> 182 us (1.022)
  waiting for transfers between devices: 70.2 us -> 45.8 us
  starting transfers between devices: 42.9 us -> 63.6 us
  Pallas kernels: 24.6 us -> 29.2 us
    ppermute x22 -> x24, waiting for transfers between devices: 67.3 us -> 45.7 us  [send(): return lax.ppermute(x, axis, [(i, to(i)) for i in range(size)])]
    ppermute x22 -> x24, starting transfers between devices: 42.2 us -> 62.7 us  [send(): return lax.ppermute(x, axis, [(i, to(i)) for i in range(size)])]
    pallas_call x2 -> x3, Pallas kernels: 22.6 us -> 27.8 us  [the longest x2 23.5 us: product(): pl.pallas_call(functools.partial(product_kernel, count=len(strips)), grid...]
    all_gather x1, waiting for transfers between devices: 2.87 us -> 0.02 us  [local(): band = lax.all_gather(sent, ('z', 'xl'), axis=0, tiled=False)]
    add x2 -> x4, other arithmetic: 3.58 us -> 4.94 us  [the longest x2 2.99 us: local(): summed.append(keep + swap(give, 'k'))]
    unnamed x38 -> x40, local copies, waits for them, and re-layouts: 10.3 us -> 10.3 us
  transfers between devices with their start and end apart: 25 -> 28, of which waited for: 20 -> 16; matrix products, arithmetic and copies ran while one was open for 3% -> 5% of each run, Pallas kernels for 14% -> 16%
where the time goes in v10:
time: 182 us; the launch traced here: 179 us
  starting transfers between devices  63.6 us (35%)
  waiting for transfers between devices  45.8 us (25%)
  Pallas kernels  29.2 us (16%)
  between operations  15.8 us (9%)
  local copies, waits for them, and re-layouts  14.1 us (8%)
  other arithmetic  8.02 us (4%)
  matrix products  2.77 us (2%)
    ppermute x24, starting transfers between devices, send(): return lax.ppermute(x, axis, [(i, to(i)) for i in range(size)])  62.7 us
    ppermute x24, waiting for transfers between devices, send(): return lax.ppermute(x, axis, [(i, to(i)) for i in range(size)])  45.7 us
    pallas_call x2, Pallas kernels, product(): pl.pallas_call(functools.partial(product_kernel, count=len(strips)), grid...  23.5 us
    unnamed x40, local copies, waits for them, and re-layouts  10.3 us
    pallas_call x1, Pallas kernels, updates(): pl.pallas_call(update_kernel, grid=(blocks,), in_specs=specs, out_specs=[...  4.33 us
  transfers between devices with their start and end apart: 28, of which 16 were waited for; matrix products, arithmetic and copies ran while one was open for 5% of the time, Pallas kernels for 16%

profile of v10, /device:TPU:0, one launch (start us, length us, event | category | flops | bytes accessed | tf_op | source)
XLA Modules:
  0.0 179.2 jit_solution(11878792198596093506)
XLA Ops:
  9.2 1.4 convolution_multiply_fusion
  10.6 1.4 convolution_multiply_fusion.1
  14.3 14.4 %collective-permute-start.1 = (f32[192,512]{1,0:T(8,128)}, f32[192,512]{1,0:T(8,128)S(1)}, u32[]{:S(2)}, u32[]{:S(2)}) collective-permute-start(f32[192,512]{1,0:T(8,128)} %copy-done.2), channel_id=1, source_target_pairs={{0,16},{16,0},{1,17},{17,1},{2,18},{18,2},{3,19},{19,3},{4,20},{20... | collective-permute-start | bytes 1179656 | tf_op jit(solution)/shard_map/ppermute | solution.py:22
  28.7 3.8 %collective-permute-start.2 = (f32[192,512]{1,0:T(8,128)}, f32[192,512]{1,0:T(8,128)S(1)}, u32[]{:S(2)}, u32[]{:S(2)}) collective-permute-start(f32[192,512]{1,0:T(8,128)} %copy-done.2), channel_id=1, source_target_pairs={{0,32},{32,0},{64,96},{96,64},{1,33},{33,1},{65,97},{97,65},{2,34}... | collective-permute-start | bytes 1179656 | tf_op jit(solution)/shard_map/ppermute | solution.py:22
  32.6 6.2 %collective-permute-done.1.refs_3_ = f32[192,512]{1,0:T(8,128)S(1)} collective-permute-done((f32[192,512]{1,0:T(8,128)}, f32[192,512]{1,0:T(8,128)S(1)}, u32[]{:S(2)}, u32[]{:S(2)}) %collective-permute-start.1) | collective-permute-done | bytes 393248 | tf_op jit(solution)/shard_map/ppermute | solution.py:22
  38.7 7.9 %collective-permute-start.5 = (f32[192,512]{1,0:T(8,128)S(1)}, f32[192,512]{1,0:T(8,128)S(1)}, u32[]{:S(2)}, u32[]{:S(2)}) collective-permute-start(f32[192,512]{1,0:T(8,128)S(1)} %collective-permute-done.1.refs_3_), channel_id=1, source_target_pairs={{0,96},{32,64},{64,32},{96,0},{1,97},{33,65},{65,33},{97,1},{2,98}... | collective-permute-start | bytes 1179656 | tf_op jit(solution)/shard_map/ppermute | solution.py:22
  46.7 3.0 %collective-permute-start.3 = (f32[192,512]{1,0:T(8,128)S(1)}, f32[192,512]{1,0:T(8,128)S(1)}, u32[]{:S(2)}, u32[]{:S(2)}) collective-permute-start(f32[192,512]{1,0:T(8,128)S(1)} %collective-permute-done.1.refs_3_), channel_id=1, source_target_pairs={{0,32},{32,0},{64,96},{96,64},{1,33},{33,1},{65,97},{97,65},{2,34}... | collective-permute-start | bytes 1179656 | tf_op jit(solution)/shard_map/ppermute | solution.py:22
  49.7 2.6 %collective-permute-start.4 = (f32[192,512]{1,0:T(8,128)S(1)}, f32[192,512]{1,0:T(8,128)S(1)}, u32[]{:S(2)}, u32[]{:S(2)}) collective-permute-start(f32[192,512]{1,0:T(8,128)S(1)} %collective-permute-done.2.refs_4_), channel_id=1, source_target_pairs={{0,96},{32,64},{64,32},{96,0},{1,97},{33,65},{65,33},{97,1},{2,98}... | collective-permute-start | bytes 1179656 | tf_op jit(solution)/shard_map/ppermute | solution.py:22
  52.3 4.4 %collective-permute-done.5.refs_9_ = f32[192,512]{1,0:T(8,128)S(1)} collective-permute-done((f32[192,512]{1,0:T(8,128)S(1)}, f32[192,512]{1,0:T(8,128)S(1)}, u32[]{:S(2)}, u32[]{:S(2)}) %collective-permute-start.5) | collective-permute-done | bytes 393248 | tf_op jit(solution)/shard_map/ppermute | solution.py:22
  56.7 3.0 %collective-permute-start.6 = (f32[192,512]{1,0:T(8,128)S(1)}, f32[192,512]{1,0:T(8,128)S(1)}, u32[]{:S(2)}, u32[]{:S(2)}) collective-permute-start(f32[192,512]{1,0:T(8,128)S(1)} %collective-permute-done.5.refs_9_), channel_id=1, source_target_pairs={{0,32},{32,0},{64,96},{96,64},{1,33},{33,1},{65,97},{97,65},{2,34}... | collective-permute-start | bytes 1179656 | tf_op jit(solution)/shard_map/ppermute | solution.py:22
  59.8 5.3 %collective-permute-done.7.refs_8_ = f32[192,512]{1,0:T(8,128)S(1)} collective-permute-done((f32[192,512]{1,0:T(8,128)}, f32[192,512]{1,0:T(8,128)S(1)}, u32[]{:S(2)}, u32[]{:S(2)}) %collective-permute-start.7) | collective-permute-done | bytes 393248 | tf_op jit(solution)/shard_map/ppermute | solution.py:22
  65.1 6.2 %collective-permute-done.4.refs_6_ = f32[192,512]{1,0:T(8,128)S(1)} collective-permute-done((f32[192,512]{1,0:T(8,128)S(1)}, f32[192,512]{1,0:T(8,128)S(1)}, u32[]{:S(2)}, u32[]{:S(2)}) %collective-permute-start.4) | collective-permute-done | bytes 393248 | tf_op jit(solution)/shard_map/ppermute | solution.py:22
  71.4 1.1 copy-done.3
  72.5 11.7 %shard_map.68 = (f32[8,96,512]{2,1,0:T(8,128)S(1)}, f32[8,96,512]{2,1,0:T(8,128)S(1)}) custom-call(s32[9]{0:T(128)S(1)} %pad_add_fusion.place_ref, f32[3072,1536]{1,0:T(8,128)} %refs_1_.3, f32[3072,1536]{1,0:T(8,128)} %refs_1_.3, f32[192,512]{1,0:T(8,128)S(1)} %copy-done.3, f32[192,512]{1,0:T(8,128)S(1)} %collective-permute-done.1.refs_3_, ...), custom_call_target="tpu_custom_call" | custom-call | flops 7247757312 | bytes 15728640 | tf_op jit(solution)/shard_map/pallas_call | solution.py:134
  84.3 3.4 %collective-permute-done.8 = f32[8,96,512]{2,1,0:T(8,128)S(1)} collective-permute-done((f32[8,96,512]{2,1,0:T(8,128)S(1)}, f32[8,96,512]{2,1,0:T(8,128)S(1)}, u32[]{:S(2)}, u32[]{:S(2)}) %collective-permute-start.8) | collective-permute-done | bytes 1572896 | tf_op jit(solution)/shard_map/ppermute | solution.py:22
  87.7 1.5 add.116.refs_10_.one_ref
  89.3 1.3 copy-done
  90.7 1.0 copy-done.7
  91.7 1.0 copy-done.9
  92.7 1.0 copy-done.11
  93.7 11.8 %shard_map.69 = (f32[8,96,512]{2,1,0:T(8,128)S(1)}, f32[8,96,512]{2,1,0:T(8,128)S(1)}) custom-call(s32[9]{0:T(128)S(1)} %pad_add_fusion.place_ref, f32[3072,1536]{1,0:T(8,128)} %refs_1_.3, f32[3072,1536]{1,0:T(8,128)} %refs_1_.3, f32[192,512]{1,0:T(8,128)S(1)} %copy-done.4, f32[192,512]{1,0:T(8,128)S(1)} %collective-permute-done.1.refs_3_, ...), custom_call_target="tpu_custom_call" | custom-call | flops 7247757312 | bytes 15728640 | tf_op jit(solution)/shard_map/pallas_call | solution.py:134
  105.7 3.2 %collective-permute-done.10 = f32[8,96,512]{2,1,0:T(8,128)S(1)} collective-permute-done((f32[8,96,512]{2,1,0:T(8,128)S(1)}, f32[8,96,512]{2,1,0:T(8,128)S(1)}, u32[]{:S(2)}, u32[]{:S(2)}) %collective-permute-start.10) | collective-permute-done | bytes 1572896 | tf_op jit(solution)/shard_map/ppermute | solution.py:22
  108.9 1.5 add.120.two_ref
  110.5 1.4 copy-done.1
  111.9 1.9 %copy-done.5 = f32[1536,512]{1,0:T(8,128)S(1)} copy-done((f32[1536,512]{1,0:T(8,128)S(1)}, f32[1536,512]{1,0:T(8,128)}, u32[]{:S(2)}) %copy-start.5) | copy-done | bytes 3145752
  113.8 4.3 %shard_map.71 = (f32[256,256]{1,0:T(8,128)S(1)}, f32[256,256]{1,0:T(8,128)}) custom-call(f32[8,96,512]{2,1,0:T(8,128)S(1)} %copy-done, f32[8,96,512]{2,1,0:T(8,128)S(1)} %copy-done.1, f32[8,192,512]{2,1,0:T(8,128)S(1)} %bitcast.46), custom_call_target="tpu_custom_call" | custom-call | flops 1207959552 | bytes 6291456 | tf_op jit(solution)/shard_map/pallas_call | solution.py:170
  118.1 1.0 broadcast_select_fusion
  119.2 1.5 collective-permute-done.12
  120.8 2.1 %collective-permute-start.13 = (f32[64,256]{1,0:T(8,128)S(1)}, f32[64,256]{1,0:T(8,128)S(1)}, u32[]{:S(2)}, u32[]{:S(2)}) collective-permute-start(f32[64,256]{1,0:T(8,128)S(1)} %get-tuple-element.18), channel_id=1, source_target_pairs={{0,32},{32,64},{64,96},{96,0},{1,33},{33,65},{65,97},{97,1},{2,34}... | collective-permute-start | bytes 196616 | tf_op jit(solution)/shard_map/ppermute | solution.py:22
  122.9 2.4 %collective-permute-start.14 = (f32[64,256]{1,0:T(8,128)S(1)}, f32[64,256]{1,0:T(8,128)S(1)}, u32[]{:S(2)}, u32[]{:S(2)}) collective-permute-start(f32[64,256]{1,0:T(8,128)S(1)} %get-tuple-element.20), channel_id=1, source_target_pairs={{0,64},{32,96},{64,0},{96,32},{1,65},{33,97},{65,1},{97,33},{2,66}... | collective-permute-start | bytes 196616 | tf_op jit(solution)/shard_map/ppermute | solution.py:22
  125.4 1.9 %collective-permute-start.15 = (f32[64,256]{1,0:T(8,128)S(1)}, f32[64,256]{1,0:T(8,128)S(1)}, u32[]{:S(2)}, u32[]{:S(2)}) collective-permute-start(f32[64,256]{1,0:T(8,128)S(1)} %get-tuple-element.19), channel_id=1, source_target_pairs={{0,96},{32,0},{64,32},{96,64},{1,97},{33,1},{65,33},{97,65},{2,98}... | collective-permute-start | bytes 196616 | tf_op jit(solution)/shard_map/ppermute | solution.py:22
  127.3 2.3 %collective-permute-done.14 = f32[64,256]{1,0:T(8,128)S(1)} collective-permute-done((f32[64,256]{1,0:T(8,128)S(1)}, f32[64,256]{1,0:T(8,128)S(1)}, u32[]{:S(2)}, u32[]{:S(2)}) %collective-permute-start.14) | collective-permute-done | bytes 65568 | tf_op jit(solution)/shard_map/ppermute | solution.py:22
  129.9 3.2 %collective-permute-start.16 = (f32[64,256]{1,0:T(8,128)S(1)}, f32[64,256]{1,0:T(8,128)S(1)}, u32[]{:S(2)}, u32[]{:S(2)}) collective-permute-start(f32[64,256]{1,0:T(8,128)S(1)} %add_add_fusion.1), channel_id=1, source_target_pairs={{0,4},{4,8},{8,12},{12,0},{1,5},{5,9},{9,13},{13,1},{2,6},{6,10},{... | collective-permute-start | bytes 196616 | tf_op jit(solution)/shard_map/ppermute | solution.py:22
  133.1 2.8 %collective-permute-start.18 = (f32[64,256]{1,0:T(8,128)S(1)}, f32[64,256]{1,0:T(8,128)S(1)}, u32[]{:S(2)}, u32[]{:S(2)}) collective-permute-start(f32[64,256]{1,0:T(8,128)S(1)} %add_add_fusion.1), channel_id=1, source_target_pairs={{0,12},{4,0},{8,4},{12,8},{1,13},{5,1},{9,5},{13,9},{2,14},{6,2},{... | collective-permute-start | bytes 196616 | tf_op jit(solution)/shard_map/ppermute | solution.py:22
  136.8 2.5 %collective-permute-start.9 = (f32[96,512]{1,0:T(8,128)S(1)}, f32[96,512]{1,0:T(8,128)S(1)}, u32[]{:S(2)}, u32[]{:S(2)}) collective-permute-start(f32[96,512]{1,0:T(8,128)S(1)} %dynamic-slice_bitcast_fusion.1), channel_id=1, source_target_pairs={{0,2},{2,0},{1,3},{3,1},{4,6},{6,4},{5,7},{7,5},{8,10},{10,8},{9,1... | collective-permute-start | bytes 589832 | tf_op jit(solution)/shard_map/ppermute | solution.py:22
  139.3 1.1 collective-permute-done.17
  140.9 2.3 %collective-permute-start.19 = (f32[64,256]{1,0:T(8,128)S(1)}, f32[64,256]{1,0:T(8,128)S(1)}, u32[]{:S(2)}, u32[]{:S(2)}) collective-permute-start(f32[64,256]{1,0:T(8,128)S(1)} %add_add_fusion), channel_id=1, source_target_pairs={{0,2},{2,0},{1,3},{3,1},{4,6},{6,4},{5,7},{7,5},{8,10},{10,8},{9,1... | collective-permute-start | bytes 196616 | tf_op jit(solution)/shard_map/ppermute | solution.py:22
  143.2 2.2 %collective-permute-done.19 = f32[64,256]{1,0:T(8,128)S(1)} collective-permute-done((f32[64,256]{1,0:T(8,128)S(1)}, f32[64,256]{1,0:T(8,128)S(1)}, u32[]{:S(2)}, u32[]{:S(2)}) %collective-permute-start.19) | collective-permute-done | bytes 65568 | tf_op jit(solution)/shard_map/ppermute | solution.py:22
  145.4 3.8 %collective-permute-start.20 = (f32[64,256]{1,0:T(8,128)S(1)}, f32[64,256]{1,0:T(8,128)S(1)}, u32[]{:S(2)}, u32[]{:S(2)}) collective-permute-start(f32[64,256]{1,0:T(8,128)S(1)} %add.136), channel_id=1, source_target_pairs={{0,16},{16,0},{1,17},{17,1},{2,18},{18,2},{3,19},{19,3},{4,20},{20... | collective-permute-start | bytes 196616 | tf_op jit(solution)/shard_map/ppermute | solution.py:22
  149.2 2.2 %collective-permute-done.20 = f32[64,256]{1,0:T(8,128)S(1)} collective-permute-done((f32[64,256]{1,0:T(8,128)S(1)}, f32[64,256]{1,0:T(8,128)S(1)}, u32[]{:S(2)}, u32[]{:S(2)}) %collective-permute-start.20) | collective-permute-done | bytes 65568 | tf_op jit(solution)/shard_map/ppermute | solution.py:22
  151.5 3.1 %collective-permute-start.21 = (f32[64,256]{1,0:T(8,128)S(1)}, f32[64,256]{1,0:T(8,128)S(1)}, u32[]{:S(2)}, u32[]{:S(2)}) collective-permute-start(f32[64,256]{1,0:T(8,128)S(1)} %add.137), channel_id=1, source_target_pairs={{0,96},{32,0},{64,32},{96,64},{1,97},{33,1},{65,33},{97,65},{2,98}... | collective-permute-start | bytes 196616 | tf_op jit(solution)/shard_map/ppermute | solution.py:22
  154.5 1.3 collective-permute-start.23
  155.9 1.0 bitcast_add_fusion.3
  156.8 3.6 %collective-permute-done.22 = f32[64,256]{1,0:T(8,128)S(1)} collective-permute-done((f32[64,256]{1,0:T(8,128)S(1)}, f32[64,256]{1,0:T(8,128)S(1)}, u32[]{:S(2)}, u32[]{:S(2)}) %collective-permute-start.22) | collective-permute-done | bytes 65568 | tf_op jit(solution)/shard_map/ppermute | solution.py:22
  160.8 1.0 dynamic-slice_bitcast_fusion
  161.8 2.1 %collective-permute-start.11 = (f32[96,512]{1,0:T(8,128)S(1)}, f32[96,512]{1,0:T(8,128)S(1)}, u32[]{:S(2)}, u32[]{:S(2)}) collective-permute-start(f32[96,512]{1,0:T(8,128)S(1)} %dynamic-slice_bitcast_fusion), channel_id=1, source_target_pairs={{0,2},{2,0},{1,3},{3,1},{4,6},{6,4},{5,7},{7,5},{8,10},{10,8},{9,1... | collective-permute-start | bytes 589832 | tf_op jit(solution)/shard_map/ppermute | solution.py:22
  164.6 2.9 %collective-permute-done.11.refs_1_ = f32[96,512]{1,0:T(8,128)S(1)} collective-permute-done((f32[96,512]{1,0:T(8,128)S(1)}, f32[96,512]{1,0:T(8,128)S(1)}, u32[]{:S(2)}, u32[]{:S(2)}) %collective-permute-start.11) | collective-permute-done | bytes 196640 | tf_op jit(solution)/shard_map/ppermute | solution.py:22
  168.9 1.0 bitcast_add_fusion.2
  (88 shorter events, 10.2 us)
Async XLA Ops:
  8.0 102.5 %all-gather.3.cloned.1.call-start = ((), (), s32[]{:S(2)}) async-start(), calls=%async_computation.4 | async-start | bytes 3538944 | tf_op jit(solution)/shard_map/all_gather | solution.py:209
  12.1 0.8 copy-start.12
  12.1 0.7 collective-permute-start
  12.8 0.7 copy-start.2
  14.3 121.6 %reduce-scatter.3.cloned.1.call-start = ((), (), s32[]{:S(2)}) async-start(), calls=%async_computation.2 | async-start | bytes 1966080 | tf_op jit(solution)/shard_map/reduce_scatter | solution.py:219
  14.3 24.4 %collective-permute-start.1 = (f32[192,512]{1,0:T(8,128)}, f32[192,512]{1,0:T(8,128)S(1)}, u32[]{:S(2)}, u32[]{:S(2)}) collective-permute-start(f32[192,512]{1,0:T(8,128)} %copy-done.2), channel_id=1, source_target_pairs={{0,16},{16,0},{1,17},{17,1},{2,18},{18,2},{3,19},{19,3},{4,20},{20... | collective-permute-start | bytes 1179656 | tf_op jit(solution)/shard_map/ppermute | solution.py:22
  28.7 21.0 %collective-permute-start.2 = (f32[192,512]{1,0:T(8,128)}, f32[192,512]{1,0:T(8,128)S(1)}, u32[]{:S(2)}, u32[]{:S(2)}) collective-permute-start(f32[192,512]{1,0:T(8,128)} %copy-done.2), channel_id=1, source_target_pairs={{0,32},{32,0},{64,96},{96,64},{1,33},{33,1},{65,97},{97,65},{2,34}... | collective-permute-start | bytes 1179656 | tf_op jit(solution)/shard_map/ppermute | solution.py:22
  38.7 17.9 %collective-permute-start.5 = (f32[192,512]{1,0:T(8,128)S(1)}, f32[192,512]{1,0:T(8,128)S(1)}, u32[]{:S(2)}, u32[]{:S(2)}) collective-permute-start(f32[192,512]{1,0:T(8,128)S(1)} %collective-permute-done.1.refs_3_), channel_id=1, source_target_pairs={{0,96},{32,64},{64,32},{96,0},{1,97},{33,65},{65,33},{97,1},{2,98}... | collective-permute-start | bytes 1179656 | tf_op jit(solution)/shard_map/ppermute | solution.py:22
  46.6 18.5 %collective-permute-start.7 = (f32[192,512]{1,0:T(8,128)}, f32[192,512]{1,0:T(8,128)S(1)}, u32[]{:S(2)}, u32[]{:S(2)}) collective-permute-start(f32[192,512]{1,0:T(8,128)} %copy-done.2), channel_id=1, source_target_pairs={{0,96},{32,64},{64,32},{96,0},{1,97},{33,65},{65,33},{97,1},{2,98}... | collective-permute-start | bytes 1179656 | tf_op jit(solution)/shard_map/ppermute | solution.py:22
  46.7 18.4 %collective-permute-start.3 = (f32[192,512]{1,0:T(8,128)S(1)}, f32[192,512]{1,0:T(8,128)S(1)}, u32[]{:S(2)}, u32[]{:S(2)}) collective-permute-start(f32[192,512]{1,0:T(8,128)S(1)} %collective-permute-done.1.refs_3_), channel_id=1, source_target_pairs={{0,32},{32,0},{64,96},{96,64},{1,33},{33,1},{65,97},{97,65},{2,34}... | collective-permute-start | bytes 1179656 | tf_op jit(solution)/shard_map/ppermute | solution.py:22
  49.7 21.6 %collective-permute-start.4 = (f32[192,512]{1,0:T(8,128)S(1)}, f32[192,512]{1,0:T(8,128)S(1)}, u32[]{:S(2)}, u32[]{:S(2)}) collective-permute-start(f32[192,512]{1,0:T(8,128)S(1)} %collective-permute-done.2.refs_4_), channel_id=1, source_target_pairs={{0,96},{32,64},{64,32},{96,0},{1,97},{33,65},{65,33},{97,1},{2,98}... | collective-permute-start | bytes 1179656 | tf_op jit(solution)/shard_map/ppermute | solution.py:22
  56.7 14.7 %collective-permute-start.6 = (f32[192,512]{1,0:T(8,128)S(1)}, f32[192,512]{1,0:T(8,128)S(1)}, u32[]{:S(2)}, u32[]{:S(2)}) collective-permute-start(f32[192,512]{1,0:T(8,128)S(1)} %collective-permute-done.5.refs_9_), channel_id=1, source_target_pairs={{0,32},{32,0},{64,96},{96,64},{1,33},{33,1},{65,97},{97,65},{2,34}... | collective-permute-start | bytes 1179656 | tf_op jit(solution)/shard_map/ppermute | solution.py:22
  65.1 19.1 %copy-start.6 = (f32[192,512]{1,0:T(8,128)}, f32[192,512]{1,0:T(8,128)S(1)}, u32[]{:S(2)}) copy-start(f32[192,512]{1,0:T(8,128)S(1)} %collective-permute-done.3.refs_5_) | copy-start | bytes 1179652
  71.3 12.9 %copy-start.8 = (f32[192,512]{1,0:T(8,128)}, f32[192,512]{1,0:T(8,128)S(1)}, u32[]{:S(2)}) copy-start(f32[192,512]{1,0:T(8,128)S(1)} %collective-permute-done.4.refs_6_) | copy-start | bytes 1179652
  71.4 1.1 copy-start.3
  72.5 11.7 %copy-start.10 = (f32[192,512]{1,0:T(8,128)}, f32[192,512]{1,0:T(8,128)S(1)}, u32[]{:S(2)}) copy-start(f32[192,512]{1,0:T(8,128)S(1)} %collective-permute-done.6.refs_7_) | copy-start | bytes 1179652
  84.2 3.5 %collective-permute-start.8 = (f32[8,96,512]{2,1,0:T(8,128)S(1)}, f32[8,96,512]{2,1,0:T(8,128)S(1)}, u32[]{:S(2)}, u32[]{:S(2)}) collective-permute-start(f32[8,96,512]{2,1,0:T(8,128)S(1)} %get-tuple-element.9), channel_id=1, source_target_pairs={{0,1},{1,0},{2,3},{3,2},{4,5},{5,4},{6,7},{7,6},{8,9},{9,8},{10,11... | collective-permute-start | bytes 4718600 | tf_op jit(solution)/shard_map/ppermute | solution.py:22
  87.7 1.6 copy-start.4
  89.2 1.4 copy-start
  89.3 71.5 %reduce-scatter.5.cloned.1.call-start = ((), (), s32[]{:S(2)}) async-start(), calls=%async_computation.3 | async-start | bytes 1966080 | tf_op jit(solution)/shard_map/reduce_scatter | solution.py:219
  90.6 1.0 copy-start.7
  91.7 1.0 copy-start.9
  92.7 1.0 copy-start.11
  105.4 3.5 %collective-permute-start.10 = (f32[8,96,512]{2,1,0:T(8,128)S(1)}, f32[8,96,512]{2,1,0:T(8,128)S(1)}, u32[]{:S(2)}, u32[]{:S(2)}) collective-permute-start(f32[8,96,512]{2,1,0:T(8,128)S(1)} %get-tuple-element.11), channel_id=1, source_target_pairs={{0,1},{1,0},{2,3},{3,2},{4,5},{5,4},{6,7},{7,6},{8,9},{9,8},{10,11... | collective-permute-start | bytes 4718600 | tf_op jit(solution)/shard_map/ppermute | solution.py:22
  110.4 1.4 copy-start.1
  111.9 1.9 %copy-start.5 = (f32[1536,512]{1,0:T(8,128)S(1)}, f32[1536,512]{1,0:T(8,128)}, u32[]{:S(2)}) copy-start(f32[1536,512]{1,0:T(8,128)} %all-gather.3.cloned.1.call-done) | copy-start | bytes 9437188
  119.1 1.6 collective-permute-start.12
  120.8 6.4 %collective-permute-start.13 = (f32[64,256]{1,0:T(8,128)S(1)}, f32[64,256]{1,0:T(8,128)S(1)}, u32[]{:S(2)}, u32[]{:S(2)}) collective-permute-start(f32[64,256]{1,0:T(8,128)S(1)} %get-tuple-element.18), channel_id=1, source_target_pairs={{0,32},{32,64},{64,96},{96,0},{1,33},{33,65},{65,97},{97,1},{2,34}... | collective-permute-start | bytes 196616 | tf_op jit(solution)/shard_map/ppermute | solution.py:22
  122.9 6.6 %collective-permute-start.14 = (f32[64,256]{1,0:T(8,128)S(1)}, f32[64,256]{1,0:T(8,128)S(1)}, u32[]{:S(2)}, u32[]{:S(2)}) collective-permute-start(f32[64,256]{1,0:T(8,128)S(1)} %get-tuple-element.20), channel_id=1, source_target_pairs={{0,64},{32,96},{64,0},{96,32},{1,65},{33,97},{65,1},{97,33},{2,66}... | collective-permute-start | bytes 196616 | tf_op jit(solution)/shard_map/ppermute | solution.py:22
  125.4 4.5 %collective-permute-start.15 = (f32[64,256]{1,0:T(8,128)S(1)}, f32[64,256]{1,0:T(8,128)S(1)}, u32[]{:S(2)}, u32[]{:S(2)}) collective-permute-start(f32[64,256]{1,0:T(8,128)S(1)} %get-tuple-element.19), channel_id=1, source_target_pairs={{0,96},{32,0},{64,32},{96,64},{1,97},{33,1},{65,33},{97,65},{2,98}... | collective-permute-start | bytes 196616 | tf_op jit(solution)/shard_map/ppermute | solution.py:22
  129.9 9.4 %collective-permute-start.16 = (f32[64,256]{1,0:T(8,128)S(1)}, f32[64,256]{1,0:T(8,128)S(1)}, u32[]{:S(2)}, u32[]{:S(2)}) collective-permute-start(f32[64,256]{1,0:T(8,128)S(1)} %add_add_fusion.1), channel_id=1, source_target_pairs={{0,4},{4,8},{8,12},{12,0},{1,5},{5,9},{9,13},{13,1},{2,6},{6,10},{... | collective-permute-start | bytes 196616 | tf_op jit(solution)/shard_map/ppermute | solution.py:22
  133.1 7.4 %collective-permute-start.17 = (f32[64,256]{1,0:T(8,128)S(1)}, f32[64,256]{1,0:T(8,128)S(1)}, u32[]{:S(2)}, u32[]{:S(2)}) collective-permute-start(f32[64,256]{1,0:T(8,128)S(1)} %add_add_fusion.1), channel_id=1, source_target_pairs={{0,8},{4,12},{8,0},{12,4},{1,9},{5,13},{9,1},{13,5},{2,10},{6,14},... | collective-permute-start | bytes 196616 | tf_op jit(solution)/shard_map/ppermute | solution.py:22
  133.1 7.8 %collective-permute-start.18 = (f32[64,256]{1,0:T(8,128)S(1)}, f32[64,256]{1,0:T(8,128)S(1)}, u32[]{:S(2)}, u32[]{:S(2)}) collective-permute-start(f32[64,256]{1,0:T(8,128)S(1)} %add_add_fusion.1), channel_id=1, source_target_pairs={{0,12},{4,0},{8,4},{12,8},{1,13},{5,1},{9,5},{13,9},{2,14},{6,2},{... | collective-permute-start | bytes 196616 | tf_op jit(solution)/shard_map/ppermute | solution.py:22
  136.8 19.1 %collective-permute-start.9 = (f32[96,512]{1,0:T(8,128)S(1)}, f32[96,512]{1,0:T(8,128)S(1)}, u32[]{:S(2)}, u32[]{:S(2)}) collective-permute-start(f32[96,512]{1,0:T(8,128)S(1)} %dynamic-slice_bitcast_fusion.1), channel_id=1, source_target_pairs={{0,2},{2,0},{1,3},{3,1},{4,6},{6,4},{5,7},{7,5},{8,10},{10,8},{9,1... | collective-permute-start | bytes 589832 | tf_op jit(solution)/shard_map/ppermute | solution.py:22
  140.9 4.6 %collective-permute-start.19 = (f32[64,256]{1,0:T(8,128)S(1)}, f32[64,256]{1,0:T(8,128)S(1)}, u32[]{:S(2)}, u32[]{:S(2)}) collective-permute-start(f32[64,256]{1,0:T(8,128)S(1)} %add_add_fusion), channel_id=1, source_target_pairs={{0,2},{2,0},{1,3},{3,1},{4,6},{6,4},{5,7},{7,5},{8,10},{10,8},{9,1... | collective-permute-start | bytes 196616 | tf_op jit(solution)/shard_map/ppermute | solution.py:22
  145.4 6.0 %collective-permute-start.20 = (f32[64,256]{1,0:T(8,128)S(1)}, f32[64,256]{1,0:T(8,128)S(1)}, u32[]{:S(2)}, u32[]{:S(2)}) collective-permute-start(f32[64,256]{1,0:T(8,128)S(1)} %add.136), channel_id=1, source_target_pairs={{0,16},{16,0},{1,17},{17,1},{2,18},{18,2},{3,19},{19,3},{4,20},{20... | collective-permute-start | bytes 196616 | tf_op jit(solution)/shard_map/ppermute | solution.py:22
  151.5 5.4 %collective-permute-start.21 = (f32[64,256]{1,0:T(8,128)S(1)}, f32[64,256]{1,0:T(8,128)S(1)}, u32[]{:S(2)}, u32[]{:S(2)}) collective-permute-start(f32[64,256]{1,0:T(8,128)S(1)} %add.137), channel_id=1, source_target_pairs={{0,96},{32,0},{64,32},{96,64},{1,97},{33,1},{65,33},{97,65},{2,98}... | collective-permute-start | bytes 196616 | tf_op jit(solution)/shard_map/ppermute | solution.py:22
  154.5 5.9 %collective-permute-start.22 = (f32[64,256]{1,0:T(8,128)S(1)}, f32[64,256]{1,0:T(8,128)S(1)}, u32[]{:S(2)}, u32[]{:S(2)}) collective-permute-start(f32[64,256]{1,0:T(8,128)S(1)} %add.137), channel_id=1, source_target_pairs={{0,64},{32,96},{64,0},{96,32},{1,65},{33,97},{65,1},{97,33},{2,66}... | collective-permute-start | bytes 196616 | tf_op jit(solution)/shard_map/ppermute | solution.py:22
  154.5 6.2 %collective-permute-start.23 = (f32[64,256]{1,0:T(8,128)S(1)}, f32[64,256]{1,0:T(8,128)S(1)}, u32[]{:S(2)}, u32[]{:S(2)}) collective-permute-start(f32[64,256]{1,0:T(8,128)S(1)} %add.137), channel_id=1, source_target_pairs={{0,32},{32,64},{64,96},{96,0},{1,33},{33,65},{65,97},{97,1},{2,34}... | collective-permute-start | bytes 196616 | tf_op jit(solution)/shard_map/ppermute | solution.py:22
  160.8 8.1 %copy-start.16 = (f32[1,2,96,512]{3,2,1,0:T(8,128)S(1)}, f32[1,2,96,512]{3,2,1,0:T(8,128)}, u32[]{:S(2)}) copy-start(f32[1,2,96,512]{3,2,1,0:T(8,128)} %reduce-scatter.5.cloned.1.call-done) | copy-start | bytes 1179652
  161.8 5.7 %collective-permute-start.11 = (f32[96,512]{1,0:T(8,128)S(1)}, f32[96,512]{1,0:T(8,128)S(1)}, u32[]{:S(2)}, u32[]{:S(2)}) collective-permute-start(f32[96,512]{1,0:T(8,128)S(1)} %dynamic-slice_bitcast_fusion), channel_id=1, source_target_pairs={{0,2},{2,0},{1,3},{3,1},{4,6},{6,4},{5,7},{7,5},{8,10},{10,8},{9,1... | collective-permute-start | bytes 589832 | tf_op jit(solution)/shard_map/ppermute | solution.py:22
  164.6 6.2 %copy-start.15 = (f32[2,256,256]{2,1,0:T(8,128)S(1)}, f32[2,256,256]{2,1,0:T(8,128)}, u32[]{:S(2)}) copy-start(f32[2,256,256]{2,1,0:T(8,128)} %param.8) | copy-start | bytes 1572868
  167.6 0.7 copy-start.14
  168.9 1.9 %copy-start.13 = (f32[256,256]{1,0:T(8,128)S(1)}, f32[256,256]{1,0:T(8,128)}, u32[]{:S(2)}) copy-start(f32[256,256]{1,0:T(8,128)} %shard_map.72) | copy-start | bytes 786436
  168.9 1.9 %collective-permute-start.24 = (f32[256,256]{1,0:T(8,128)}, f32[256,256]{1,0:T(8,128)S(1)}, u32[]{:S(2)}, u32[]{:S(2)}) collective-permute-start(f32[256,256]{1,0:T(8,128)} %shard_map.72), channel_id=1, source_target_pairs={{0,1},{1,0},{2,3},{3,2},{4,5},{5,4},{6,7},{7,6},{8,9},{9,8},{10,11... | collective-permute-start | bytes 786440 | tf_op jit(solution)/shard_map/ppermute | solution.py:22
Sparse Core Ops, SparseCore 0:
  14.4 90.8 all-gather.2
Sparse Core Ops, SparseCore 1:
  89.4 28.6 reduce-scatter.2
  120.3 27.8 reduce-scatter.4

commit v11 on v6

--- a/solution.py
+++ b/solution.py
@@ -92,6 +92,25 @@
     )(*xs, *after)
 
 
+def normed_kernel(panel_ref, factor_ref, mask_ref, out_ref):
+    wide = factor_ref.shape[-1]
+    for s in range(NS):
+        rows = jnp.dot(panel_ref[s], factor_ref[s], precision=HIGHEST, preferred_element_type=F32)
+        out_ref[:, s * wide : (s + 1) * wide] = rows * mask_ref[s]
+
+
+def normed_rows(panel, factor, masks):
+    count, piece, wide = panel.shape
+    return pl.pallas_call(
+        normed_kernel,
+        out_shape=jax.ShapeDtypeStruct((piece, count * wide), F32),
+        compiler_params=pltpu.CompilerParams(vmem_limit_bytes=16 << 20),
+        cost_estimate=pl.CostEstimate(
+            flops=12 * count * piece * wide * wide, bytes_accessed=8 * count * piece * wide, transcendentals=0
+        ),
+    )(panel, factor, masks)
+
+
 def product_kernel(place_ref, a_ref, *refs):
     pieces, (keep_ref, give_ref, high, low) = refs[:8], refs[8:]
     piece = pieces[0].shape[0]
@@ -185,9 +204,7 @@
     piece, wide = lower_panel.shape[1:]
     start = (row * 16 + col) * piece
     masks = [tile_mask(pattern, s, start, piece) for s in range(NS)]
-    normed = jnp.concatenate(
-        [jnp.dot(lower_panel[s], diag_factor[s], precision=HIGHEST) * masks[s] for s in range(NS)], axis=1
-    )
+    normed = normed_rows(lower_panel, diag_factor, jnp.stack(masks))
     spots = jnp.arange(8, dtype=jnp.int32)
     places = jnp.concatenate([((spots // 2) ^ y) * 2 + ((spots % 2) ^ xh), k[None]])
     mine = lax.ppermute(normed, ALL, transpose_pairs())

time: 170 us -> 170 us (level)
  matrix products: 2.77 us -> 0 us
  local copies, waits for them, and re-layouts: 9.92 us -> 12.3 us
    dot_general x2 -> x0, matrix products: 2.77 us -> none  [local(): jnp.dot(lower_panel[s], diag_factor[s], precision=HIGHEST) * masks[s]]
    unnamed x30 -> x34, local copies, waits for them, and re-layouts: 8.08 us -> 10.1 us
  transfers between devices with their start and end apart: 27 -> 27, of which waited for: 16 -> 16; matrix products, arithmetic and copies ran while one was open for 4% -> 5% of each run, Pallas kernels for 15% -> 15%
where the time goes in v11:
time: 170 us; the launch traced here: 168 us
  starting transfers between devices  61.8 us (36%)
  waiting for transfers between devices  45.7 us (27%)
  Pallas kernels  24.9 us (15%)
  between operations  15.8 us (9%)
  local copies, waits for them, and re-layouts  12.3 us (7%)
  other arithmetic  7.48 us (4%)
    ppermute x23, starting transfers between devices, send(): return lax.ppermute(x, axis, [(i, to(i)) for i in range(size)])  61 us
    ppermute x23, waiting for transfers between devices, send(): return lax.ppermute(x, axis, [(i, to(i)) for i in range(size)])  45.5 us
    pallas_call x2, Pallas kernels, product(): pl.pallas_call(product_kernel, grid_spec=pltpu.PrefetchScalarGridSpec(num...  21.7 us
    unnamed x34, local copies, waits for them, and re-layouts  10.1 us
  transfers between devices with their start and end apart: 27, of which 16 were waited for; matrix products, arithmetic and copies ran while one was open for 5% of the time, Pallas kernels for 15%

profile of v11, /device:TPU:0, one launch (start us, length us, event | category | flops | bytes accessed | tf_op | source)
XLA Modules:
  0.0 168.0 jit_solution(7657384972423801944)
XLA Ops:
  8.1 0.8 fusion.12
  9.4 1.0 copy-done.4
  10.4 1.0 copy-done.5
  13.5 14.4 %collective-permute-start.1 = (f32[192,512]{1,0:T(8,128)}, f32[192,512]{1,0:T(8,128)S(1)}, u32[]{:S(2)}, u32[]{:S(2)}) collective-permute-start(f32[192,512]{1,0:T(8,128)} %copy-done.6), channel_id=1, source_target_pairs={{0,16},{16,0},{1,17},{17,1},{2,18},{18,2},{3,19},{19,3},{4,20},{20... | collective-permute-start | bytes 1179656 | tf_op jit(solution)/shard_map/ppermute | solution.py:18
  27.9 3.8 %collective-permute-start.2 = (f32[192,512]{1,0:T(8,128)}, f32[192,512]{1,0:T(8,128)S(1)}, u32[]{:S(2)}, u32[]{:S(2)}) collective-permute-start(f32[192,512]{1,0:T(8,128)} %copy-done.6), channel_id=1, source_target_pairs={{0,32},{32,0},{64,96},{96,64},{1,33},{33,1},{65,97},{97,65},{2,34}... | collective-permute-start | bytes 1179656 | tf_op jit(solution)/shard_map/ppermute | solution.py:18
  31.8 6.2 %collective-permute-done.1.refs_1_ = f32[192,512]{1,0:T(8,128)S(1)} collective-permute-done((f32[192,512]{1,0:T(8,128)}, f32[192,512]{1,0:T(8,128)S(1)}, u32[]{:S(2)}, u32[]{:S(2)}) %collective-permute-start.1) | collective-permute-done | bytes 393248 | tf_op jit(solution)/shard_map/ppermute | solution.py:18
  38.0 7.9 %collective-permute-start.5 = (f32[192,512]{1,0:T(8,128)S(1)}, f32[192,512]{1,0:T(8,128)S(1)}, u32[]{:S(2)}, u32[]{:S(2)}) collective-permute-start(f32[192,512]{1,0:T(8,128)S(1)} %collective-permute-done.1.refs_1_), channel_id=1, source_target_pairs={{0,96},{32,64},{64,32},{96,0},{1,97},{33,65},{65,33},{97,1},{2,98}... | collective-permute-start | bytes 1179656 | tf_op jit(solution)/shard_map/ppermute | solution.py:18
  45.9 3.0 %collective-permute-start.3 = (f32[192,512]{1,0:T(8,128)S(1)}, f32[192,512]{1,0:T(8,128)S(1)}, u32[]{:S(2)}, u32[]{:S(2)}) collective-permute-start(f32[192,512]{1,0:T(8,128)S(1)} %collective-permute-done.1.refs_1_), channel_id=1, source_target_pairs={{0,32},{32,0},{64,96},{96,64},{1,33},{33,1},{65,97},{97,65},{2,34}... | collective-permute-start | bytes 1179656 | tf_op jit(solution)/shard_map/ppermute | solution.py:18
  48.9 2.6 %collective-permute-start.4 = (f32[192,512]{1,0:T(8,128)S(1)}, f32[192,512]{1,0:T(8,128)S(1)}, u32[]{:S(2)}, u32[]{:S(2)}) collective-permute-start(f32[192,512]{1,0:T(8,128)S(1)} %collective-permute-done.2.refs_2_), channel_id=1, source_target_pairs={{0,96},{32,64},{64,32},{96,0},{1,97},{33,65},{65,33},{97,1},{2,98}... | collective-permute-start | bytes 1179656 | tf_op jit(solution)/shard_map/ppermute | solution.py:18
  51.5 4.4 %collective-permute-done.5.refs_7_ = f32[192,512]{1,0:T(8,128)S(1)} collective-permute-done((f32[192,512]{1,0:T(8,128)S(1)}, f32[192,512]{1,0:T(8,128)S(1)}, u32[]{:S(2)}, u32[]{:S(2)}) %collective-permute-start.5) | collective-permute-done | bytes 393248 | tf_op jit(solution)/shard_map/ppermute | solution.py:18
  55.9 3.0 %collective-permute-start.6 = (f32[192,512]{1,0:T(8,128)S(1)}, f32[192,512]{1,0:T(8,128)S(1)}, u32[]{:S(2)}, u32[]{:S(2)}) collective-permute-start(f32[192,512]{1,0:T(8,128)S(1)} %collective-permute-done.5.refs_7_), channel_id=1, source_target_pairs={{0,32},{32,0},{64,96},{96,64},{1,33},{33,1},{65,97},{97,65},{2,34}... | collective-permute-start | bytes 1179656 | tf_op jit(solution)/shard_map/ppermute | solution.py:18
  59.0 5.3 %collective-permute-done.7.refs_6_ = f32[192,512]{1,0:T(8,128)S(1)} collective-permute-done((f32[192,512]{1,0:T(8,128)}, f32[192,512]{1,0:T(8,128)S(1)}, u32[]{:S(2)}, u32[]{:S(2)}) %collective-permute-start.7) | collective-permute-done | bytes 393248 | tf_op jit(solution)/shard_map/ppermute | solution.py:18
  64.3 6.3 %collective-permute-done.4.refs_4_ = f32[192,512]{1,0:T(8,128)S(1)} collective-permute-done((f32[192,512]{1,0:T(8,128)S(1)}, f32[192,512]{1,0:T(8,128)S(1)}, u32[]{:S(2)}, u32[]{:S(2)}) %collective-permute-start.4) | collective-permute-done | bytes 393248 | tf_op jit(solution)/shard_map/ppermute | solution.py:18
  70.6 1.0 copy-done.7
  71.6 10.8 %shard_map.69 = (f32[4,192,512]{2,1,0:T(8,128)S(1)}, f32[4,192,512]{2,1,0:T(8,128)S(1)}) custom-call(s32[9]{0:T(128)S(1)} %pad_add_fusion.place_ref, f32[3072,1536]{1,0:T(8,128)} %a_ref.3, f32[192,512]{1,0:T(8,128)S(1)} %copy-done.7, f32[192,512]{1,0:T(8,128)S(1)} %collective-permute-done.1.refs_1_, f32[192,512]{1,0:T(8,128)S(1)} %collective-permute-done.2.refs_2_, ...), custom_call_target="tpu_custom_call" | custom-call | flops 7247757312 | bytes 15728640 | tf_op jit(solution)/shard_map/pallas_call | solution.py:141
  82.5 3.4 %collective-permute-done.8 = f32[4,192,512]{2,1,0:T(8,128)S(1)} collective-permute-done((f32[4,192,512]{2,1,0:T(8,128)S(1)}, f32[4,192,512]{2,1,0:T(8,128)S(1)}, u32[]{:S(2)}, u32[]{:S(2)}) %collective-permute-start.8) | collective-permute-done | bytes 1572896 | tf_op jit(solution)/shard_map/ppermute | solution.py:18
  85.9 1.5 add.104.near_ref
  87.5 0.9 copy-done.8
  88.4 10.8 %shard_map.70 = (f32[4,192,512]{2,1,0:T(8,128)S(1)}, f32[4,192,512]{2,1,0:T(8,128)S(1)}) custom-call(s32[9]{0:T(128)S(1)} %pad_add_fusion.place_ref, f32[3072,1536]{1,0:T(8,128)} %a_ref.3, f32[192,512]{1,0:T(8,128)S(1)} %copy-done.8, f32[192,512]{1,0:T(8,128)S(1)} %collective-permute-done.1.refs_1_, f32[192,512]{1,0:T(8,128)S(1)} %collective-permute-done.2.refs_2_, ...), custom_call_target="tpu_custom_call" | custom-call | flops 7247757312 | bytes 15728640 | tf_op jit(solution)/shard_map/pallas_call | solution.py:141
  99.5 3.3 %collective-permute-done.9 = f32[4,192,512]{2,1,0:T(8,128)S(1)} collective-permute-done((f32[4,192,512]{2,1,0:T(8,128)S(1)}, f32[4,192,512]{2,1,0:T(8,128)S(1)}, u32[]{:S(2)}, u32[]{:S(2)}) %collective-permute-start.9) | collective-permute-done | bytes 1572896 | tf_op jit(solution)/shard_map/ppermute | solution.py:18
  102.8 1.5 add.105.far_ref
  104.5 1.2 copy-done
  105.7 1.4 copy-done.1
  107.1 1.9 %copy-done.3 = f32[1536,512]{1,0:T(8,128)S(1)} copy-done((f32[1536,512]{1,0:T(8,128)S(1)}, f32[1536,512]{1,0:T(8,128)}, u32[]{:S(2)}) %copy-start.3) | copy-done | bytes 3145752
  109.1 2.7 %shard_map.72 = (f32[256,256]{1,0:T(8,128)S(1)}, f32[256,256]{1,0:T(8,128)S(1)}) custom-call(f32[4,192,512]{2,1,0:T(8,128)S(1)} %copy-done, f32[4,192,512]{2,1,0:T(8,128)S(1)} %copy-done.1, f32[8,192,512]{2,1,0:T(8,128)S(1)} %bitcast.30), custom_call_target="tpu_custom_call" | custom-call | flops 1207959552 | bytes 6291456 | tf_op jit(solution)/shard_map/pallas_call | solution.py:176
  112.0 1.4 collective-permute-done.11
  113.5 2.1 %collective-permute-start.12 = (f32[64,256]{1,0:T(8,128)S(1)}, f32[64,256]{1,0:T(8,128)S(1)}, u32[]{:S(2)}, u32[]{:S(2)}) collective-permute-start(f32[64,256]{1,0:T(8,128)S(1)} %get-tuple-element.18), channel_id=1, source_target_pairs={{0,32},{32,64},{64,96},{96,0},{1,33},{33,65},{65,97},{97,1},{2,34}... | collective-permute-start | bytes 196616 | tf_op jit(solution)/shard_map/ppermute | solution.py:18
  115.6 2.4 %collective-permute-start.13 = (f32[64,256]{1,0:T(8,128)S(1)}, f32[64,256]{1,0:T(8,128)S(1)}, u32[]{:S(2)}, u32[]{:S(2)}) collective-permute-start(f32[64,256]{1,0:T(8,128)S(1)} %get-tuple-element.20), channel_id=1, source_target_pairs={{0,64},{32,96},{64,0},{96,32},{1,65},{33,97},{65,1},{97,33},{2,66}... | collective-permute-start | bytes 196616 | tf_op jit(solution)/shard_map/ppermute | solution.py:18
  118.0 2.0 %collective-permute-start.14 = (f32[64,256]{1,0:T(8,128)S(1)}, f32[64,256]{1,0:T(8,128)S(1)}, u32[]{:S(2)}, u32[]{:S(2)}) collective-permute-start(f32[64,256]{1,0:T(8,128)S(1)} %get-tuple-element.19), channel_id=1, source_target_pairs={{0,96},{32,0},{64,32},{96,64},{1,97},{33,1},{65,33},{97,65},{2,98}... | collective-permute-start | bytes 196616 | tf_op jit(solution)/shard_map/ppermute | solution.py:18
  120.0 1.7 collective-permute-done.13
  122.3 3.2 %collective-permute-start.15 = (f32[64,256]{1,0:T(8,128)S(1)}, f32[64,256]{1,0:T(8,128)S(1)}, u32[]{:S(2)}, u32[]{:S(2)}) collective-permute-start(f32[64,256]{1,0:T(8,128)S(1)} %add_add_fusion.1), channel_id=1, source_target_pairs={{0,4},{4,8},{8,12},{12,0},{1,5},{5,9},{9,13},{13,1},{2,6},{6,10},{... | collective-permute-start | bytes 196616 | tf_op jit(solution)/shard_map/ppermute | solution.py:18
  125.5 2.8 %collective-permute-start.17 = (f32[64,256]{1,0:T(8,128)S(1)}, f32[64,256]{1,0:T(8,128)S(1)}, u32[]{:S(2)}, u32[]{:S(2)}) collective-permute-start(f32[64,256]{1,0:T(8,128)S(1)} %add_add_fusion.1), channel_id=1, source_target_pairs={{0,12},{4,0},{8,4},{12,8},{1,13},{5,1},{9,5},{13,9},{2,14},{6,2},{... | collective-permute-start | bytes 196616 | tf_op jit(solution)/shard_map/ppermute | solution.py:18
  128.3 4.0 %collective-permute-done.16 = f32[64,256]{1,0:T(8,128)S(1)} collective-permute-done((f32[64,256]{1,0:T(8,128)S(1)}, f32[64,256]{1,0:T(8,128)S(1)}, u32[]{:S(2)}, u32[]{:S(2)}) %collective-permute-start.16) | collective-permute-done | bytes 65568 | tf_op jit(solution)/shard_map/ppermute | solution.py:18
  132.3 2.5 %collective-permute-start.18 = (f32[64,256]{1,0:T(8,128)S(1)}, f32[64,256]{1,0:T(8,128)S(1)}, u32[]{:S(2)}, u32[]{:S(2)}) collective-permute-start(f32[64,256]{1,0:T(8,128)S(1)} %add_add_fusion), channel_id=1, source_target_pairs={{0,2},{2,0},{1,3},{3,1},{4,6},{6,4},{5,7},{7,5},{8,10},{10,8},{9,1... | collective-permute-start | bytes 196616 | tf_op jit(solution)/shard_map/ppermute | solution.py:18
  134.7 2.2 %collective-permute-done.18 = f32[64,256]{1,0:T(8,128)S(1)} collective-permute-done((f32[64,256]{1,0:T(8,128)S(1)}, f32[64,256]{1,0:T(8,128)S(1)}, u32[]{:S(2)}, u32[]{:S(2)}) %collective-permute-start.18) | collective-permute-done | bytes 65568 | tf_op jit(solution)/shard_map/ppermute | solution.py:18
  137.0 4.5 %collective-permute-start.19 = (f32[64,256]{1,0:T(8,128)S(1)}, f32[64,256]{1,0:T(8,128)S(1)}, u32[]{:S(2)}, u32[]{:S(2)}) collective-permute-start(f32[64,256]{1,0:T(8,128)S(1)} %add.121), channel_id=1, source_target_pairs={{0,16},{16,0},{1,17},{17,1},{2,18},{18,2},{3,19},{19,3},{4,20},{20... | collective-permute-start | bytes 196616 | tf_op jit(solution)/shard_map/ppermute | solution.py:18
  141.9 1.9 %collective-permute-done.19 = f32[64,256]{1,0:T(8,128)S(1)} collective-permute-done((f32[64,256]{1,0:T(8,128)S(1)}, f32[64,256]{1,0:T(8,128)S(1)}, u32[]{:S(2)}, u32[]{:S(2)}) %collective-permute-start.19) | collective-permute-done | bytes 65568 | tf_op jit(solution)/shard_map/ppermute | solution.py:18
  143.8 2.3 %collective-permute-start.20 = (f32[64,256]{1,0:T(8,128)S(1)}, f32[64,256]{1,0:T(8,128)S(1)}, u32[]{:S(2)}, u32[]{:S(2)}) collective-permute-start(f32[64,256]{1,0:T(8,128)S(1)} %add.122), channel_id=1, source_target_pairs={{0,96},{32,0},{64,32},{96,64},{1,97},{33,1},{65,33},{97,65},{2,98}... | collective-permute-start | bytes 196616 | tf_op jit(solution)/shard_map/ppermute | solution.py:18
  146.1 1.1 select_bitcast_fusion
  147.2 1.8 %collective-permute-start.10 = (f32[192,512]{1,0:T(8,128)S(1)}, f32[192,512]{1,0:T(8,128)S(1)}, u32[]{:S(2)}, u32[]{:S(2)}) collective-permute-start(f32[192,512]{1,0:T(8,128)S(1)} %select_bitcast_fusion), channel_id=1, source_target_pairs={{0,2},{2,0},{1,3},{3,1},{4,6},{6,4},{5,7},{7,5},{8,10},{10,8},{9,1... | collective-permute-start | bytes 1179656 | tf_op jit(solution)/shard_map/ppermute | solution.py:18
  149.0 1.1 collective-permute-start.21
  150.1 0.9 collective-permute-start.22
  151.1 3.7 %collective-permute-done.21 = f32[64,256]{1,0:T(8,128)S(1)} collective-permute-done((f32[64,256]{1,0:T(8,128)S(1)}, f32[64,256]{1,0:T(8,128)S(1)}, u32[]{:S(2)}, u32[]{:S(2)}) %collective-permute-start.21) | collective-permute-done | bytes 65568 | tf_op jit(solution)/shard_map/ppermute | solution.py:18
  154.8 0.8 collective-permute-done.22
  156.8 0.7 copy-done.10
  157.6 1.2 bitcast_add_fusion
  158.9 0.8 pad_maximum_fusion.1
  159.8 0.8 pad_maximum_fusion
  (80 shorter events, 6.2 us)
Async XLA Ops:
  8.0 96.5 %all-gather.3.cloned.1.call-start = ((), (), s32[]{:S(2)}) async-start(), calls=%async_computation.4 | async-start | bytes 3538944 | tf_op jit(solution)/shard_map/all_gather | solution.py:213
  9.4 1.0 copy-start.4
  10.4 1.0 copy-start.5
  12.0 0.7 copy-start.2
  12.0 0.7 collective-permute-start
  12.7 0.7 copy-start.6
  13.5 132.6 %reduce-scatter.3.cloned.1.call-start = ((), (), s32[]{:S(2)}) async-start(), calls=%async_computation.2 | async-start | bytes 1966080 | tf_op jit(solution)/shard_map/reduce_scatter | solution.py:221
  13.5 24.4 %collective-permute-start.1 = (f32[192,512]{1,0:T(8,128)}, f32[192,512]{1,0:T(8,128)S(1)}, u32[]{:S(2)}, u32[]{:S(2)}) collective-permute-start(f32[192,512]{1,0:T(8,128)} %copy-done.6), channel_id=1, source_target_pairs={{0,16},{16,0},{1,17},{17,1},{2,18},{18,2},{3,19},{19,3},{4,20},{20... | collective-permute-start | bytes 1179656 | tf_op jit(solution)/shard_map/ppermute | solution.py:18
  27.9 21.0 %collective-permute-start.2 = (f32[192,512]{1,0:T(8,128)}, f32[192,512]{1,0:T(8,128)S(1)}, u32[]{:S(2)}, u32[]{:S(2)}) collective-permute-start(f32[192,512]{1,0:T(8,128)} %copy-done.6), channel_id=1, source_target_pairs={{0,32},{32,0},{64,96},{96,64},{1,33},{33,1},{65,97},{97,65},{2,34}... | collective-permute-start | bytes 1179656 | tf_op jit(solution)/shard_map/ppermute | solution.py:18
  38.0 17.9 %collective-permute-start.5 = (f32[192,512]{1,0:T(8,128)S(1)}, f32[192,512]{1,0:T(8,128)S(1)}, u32[]{:S(2)}, u32[]{:S(2)}) collective-permute-start(f32[192,512]{1,0:T(8,128)S(1)} %collective-permute-done.1.refs_1_), channel_id=1, source_target_pairs={{0,96},{32,64},{64,32},{96,0},{1,97},{33,65},{65,33},{97,1},{2,98}... | collective-permute-start | bytes 1179656 | tf_op jit(solution)/shard_map/ppermute | solution.py:18
  45.9 18.5 %collective-permute-start.7 = (f32[192,512]{1,0:T(8,128)}, f32[192,512]{1,0:T(8,128)S(1)}, u32[]{:S(2)}, u32[]{:S(2)}) collective-permute-start(f32[192,512]{1,0:T(8,128)} %copy-done.6), channel_id=1, source_target_pairs={{0,96},{32,64},{64,32},{96,0},{1,97},{33,65},{65,33},{97,1},{2,98}... | collective-permute-start | bytes 1179656 | tf_op jit(solution)/shard_map/ppermute | solution.py:18
  45.9 18.4 %collective-permute-start.3 = (f32[192,512]{1,0:T(8,128)S(1)}, f32[192,512]{1,0:T(8,128)S(1)}, u32[]{:S(2)}, u32[]{:S(2)}) collective-permute-start(f32[192,512]{1,0:T(8,128)S(1)} %collective-permute-done.1.refs_1_), channel_id=1, source_target_pairs={{0,32},{32,0},{64,96},{96,64},{1,33},{33,1},{65,97},{97,65},{2,34}... | collective-permute-start | bytes 1179656 | tf_op jit(solution)/shard_map/ppermute | solution.py:18
  48.9 21.6 %collective-permute-start.4 = (f32[192,512]{1,0:T(8,128)S(1)}, f32[192,512]{1,0:T(8,128)S(1)}, u32[]{:S(2)}, u32[]{:S(2)}) collective-permute-start(f32[192,512]{1,0:T(8,128)S(1)} %collective-permute-done.2.refs_2_), channel_id=1, source_target_pairs={{0,96},{32,64},{64,32},{96,0},{1,97},{33,65},{65,33},{97,1},{2,98}... | collective-permute-start | bytes 1179656 | tf_op jit(solution)/shard_map/ppermute | solution.py:18
  55.9 14.7 %collective-permute-start.6 = (f32[192,512]{1,0:T(8,128)S(1)}, f32[192,512]{1,0:T(8,128)S(1)}, u32[]{:S(2)}, u32[]{:S(2)}) collective-permute-start(f32[192,512]{1,0:T(8,128)S(1)} %collective-permute-done.5.refs_7_), channel_id=1, source_target_pairs={{0,32},{32,0},{64,96},{96,64},{1,33},{33,1},{65,97},{97,65},{2,34}... | collective-permute-start | bytes 1179656 | tf_op jit(solution)/shard_map/ppermute | solution.py:18
  70.6 1.0 copy-start.7
  82.4 3.5 %collective-permute-start.8 = (f32[4,192,512]{2,1,0:T(8,128)S(1)}, f32[4,192,512]{2,1,0:T(8,128)S(1)}, u32[]{:S(2)}, u32[]{:S(2)}) collective-permute-start(f32[4,192,512]{2,1,0:T(8,128)S(1)} %get-tuple-element.9), channel_id=1, source_target_pairs={{0,1},{1,0},{2,3},{3,2},{4,5},{5,4},{6,7},{7,6},{8,9},{9,8},{10,11... | collective-permute-start | bytes 4718600 | tf_op jit(solution)/shard_map/ppermute | solution.py:18
  87.4 1.0 copy-start.8
  87.5 58.6 %reduce-scatter.5.cloned.1.call-start = ((), (), s32[]{:S(2)}) async-start(), calls=%async_computation.3 | async-start | bytes 1966080 | tf_op jit(solution)/shard_map/reduce_scatter | solution.py:221
  99.3 3.5 %collective-permute-start.9 = (f32[4,192,512]{2,1,0:T(8,128)S(1)}, f32[4,192,512]{2,1,0:T(8,128)S(1)}, u32[]{:S(2)}, u32[]{:S(2)}) collective-permute-start(f32[4,192,512]{2,1,0:T(8,128)S(1)} %get-tuple-element.11), channel_id=1, source_target_pairs={{0,1},{1,0},{2,3},{3,2},{4,5},{5,4},{6,7},{7,6},{8,9},{9,8},{10,11... | collective-permute-start | bytes 4718600 | tf_op jit(solution)/shard_map/ppermute | solution.py:18
  104.3 1.4 copy-start
  105.7 1.4 copy-start.1
  107.1 1.9 %copy-start.3 = (f32[1536,512]{1,0:T(8,128)S(1)}, f32[1536,512]{1,0:T(8,128)}, u32[]{:S(2)}) copy-start(f32[1536,512]{1,0:T(8,128)} %all-gather.3.cloned.1.call-done) | copy-start | bytes 9437188
  111.8 1.6 collective-permute-start.11
  113.5 6.5 %collective-permute-start.12 = (f32[64,256]{1,0:T(8,128)S(1)}, f32[64,256]{1,0:T(8,128)S(1)}, u32[]{:S(2)}, u32[]{:S(2)}) collective-permute-start(f32[64,256]{1,0:T(8,128)S(1)} %get-tuple-element.18), channel_id=1, source_target_pairs={{0,32},{32,64},{64,96},{96,0},{1,33},{33,65},{65,97},{97,1},{2,34}... | collective-permute-start | bytes 196616 | tf_op jit(solution)/shard_map/ppermute | solution.py:18
  115.6 6.0 %collective-permute-start.13 = (f32[64,256]{1,0:T(8,128)S(1)}, f32[64,256]{1,0:T(8,128)S(1)}, u32[]{:S(2)}, u32[]{:S(2)}) collective-permute-start(f32[64,256]{1,0:T(8,128)S(1)} %get-tuple-element.20), channel_id=1, source_target_pairs={{0,64},{32,96},{64,0},{96,32},{1,65},{33,97},{65,1},{97,33},{2,66}... | collective-permute-start | bytes 196616 | tf_op jit(solution)/shard_map/ppermute | solution.py:18
  118.0 4.3 %collective-permute-start.14 = (f32[64,256]{1,0:T(8,128)S(1)}, f32[64,256]{1,0:T(8,128)S(1)}, u32[]{:S(2)}, u32[]{:S(2)}) collective-permute-start(f32[64,256]{1,0:T(8,128)S(1)} %get-tuple-element.19), channel_id=1, source_target_pairs={{0,96},{32,0},{64,32},{96,64},{1,97},{33,1},{65,33},{97,65},{2,98}... | collective-permute-start | bytes 196616 | tf_op jit(solution)/shard_map/ppermute | solution.py:18
  122.3 5.9 %collective-permute-start.15 = (f32[64,256]{1,0:T(8,128)S(1)}, f32[64,256]{1,0:T(8,128)S(1)}, u32[]{:S(2)}, u32[]{:S(2)}) collective-permute-start(f32[64,256]{1,0:T(8,128)S(1)} %add_add_fusion.1), channel_id=1, source_target_pairs={{0,4},{4,8},{8,12},{12,0},{1,5},{5,9},{9,13},{13,1},{2,6},{6,10},{... | collective-permute-start | bytes 196616 | tf_op jit(solution)/shard_map/ppermute | solution.py:18
  125.5 6.7 %collective-permute-start.16 = (f32[64,256]{1,0:T(8,128)S(1)}, f32[64,256]{1,0:T(8,128)S(1)}, u32[]{:S(2)}, u32[]{:S(2)}) collective-permute-start(f32[64,256]{1,0:T(8,128)S(1)} %add_add_fusion.1), channel_id=1, source_target_pairs={{0,8},{4,12},{8,0},{12,4},{1,9},{5,13},{9,1},{13,5},{2,10},{6,14},... | collective-permute-start | bytes 196616 | tf_op jit(solution)/shard_map/ppermute | solution.py:18
  125.5 6.7 %collective-permute-start.17 = (f32[64,256]{1,0:T(8,128)S(1)}, f32[64,256]{1,0:T(8,128)S(1)}, u32[]{:S(2)}, u32[]{:S(2)}) collective-permute-start(f32[64,256]{1,0:T(8,128)S(1)} %add_add_fusion.1), channel_id=1, source_target_pairs={{0,12},{4,0},{8,4},{12,8},{1,13},{5,1},{9,5},{13,9},{2,14},{6,2},{... | collective-permute-start | bytes 196616 | tf_op jit(solution)/shard_map/ppermute | solution.py:18
  132.3 4.7 %collective-permute-start.18 = (f32[64,256]{1,0:T(8,128)S(1)}, f32[64,256]{1,0:T(8,128)S(1)}, u32[]{:S(2)}, u32[]{:S(2)}) collective-permute-start(f32[64,256]{1,0:T(8,128)S(1)} %add_add_fusion), channel_id=1, source_target_pairs={{0,2},{2,0},{1,3},{3,1},{4,6},{6,4},{5,7},{7,5},{8,10},{10,8},{9,1... | collective-permute-start | bytes 196616 | tf_op jit(solution)/shard_map/ppermute | solution.py:18
  137.0 6.8 %collective-permute-start.19 = (f32[64,256]{1,0:T(8,128)S(1)}, f32[64,256]{1,0:T(8,128)S(1)}, u32[]{:S(2)}, u32[]{:S(2)}) collective-permute-start(f32[64,256]{1,0:T(8,128)S(1)} %add.121), channel_id=1, source_target_pairs={{0,16},{16,0},{1,17},{17,1},{2,18},{18,2},{3,19},{19,3},{4,20},{20... | collective-permute-start | bytes 196616 | tf_op jit(solution)/shard_map/ppermute | solution.py:18
  143.8 7.3 %collective-permute-start.20 = (f32[64,256]{1,0:T(8,128)S(1)}, f32[64,256]{1,0:T(8,128)S(1)}, u32[]{:S(2)}, u32[]{:S(2)}) collective-permute-start(f32[64,256]{1,0:T(8,128)S(1)} %add.122), channel_id=1, source_target_pairs={{0,96},{32,0},{64,32},{96,64},{1,97},{33,1},{65,33},{97,65},{2,98}... | collective-permute-start | bytes 196616 | tf_op jit(solution)/shard_map/ppermute | solution.py:18
  146.1 11.5 %copy-start.11 = (f32[1,192,512]{2,1,0:T(8,128)S(1)}, f32[1,192,512]{2,1,0:T(8,128)}, u32[]{:S(2)}) copy-start(f32[1,192,512]{2,1,0:T(8,128)} %reduce-scatter.3.cloned.1.call-done) | copy-start | bytes 1179652
  146.1 11.5 %copy-start.12 = (f32[1,192,512]{2,1,0:T(8,128)S(1)}, f32[1,192,512]{2,1,0:T(8,128)}, u32[]{:S(2)}) copy-start(f32[1,192,512]{2,1,0:T(8,128)} %reduce-scatter.5.cloned.1.call-done) | copy-start | bytes 1179652
  147.2 9.6 %collective-permute-start.10 = (f32[192,512]{1,0:T(8,128)S(1)}, f32[192,512]{1,0:T(8,128)S(1)}, u32[]{:S(2)}, u32[]{:S(2)}) collective-permute-start(f32[192,512]{1,0:T(8,128)S(1)} %select_bitcast_fusion), channel_id=1, source_target_pairs={{0,2},{2,0},{1,3},{3,1},{4,6},{6,4},{5,7},{7,5},{8,10},{10,8},{9,1... | collective-permute-start | bytes 1179656 | tf_op jit(solution)/shard_map/ppermute | solution.py:18
  149.0 5.8 %collective-permute-start.21 = (f32[64,256]{1,0:T(8,128)S(1)}, f32[64,256]{1,0:T(8,128)S(1)}, u32[]{:S(2)}, u32[]{:S(2)}) collective-permute-start(f32[64,256]{1,0:T(8,128)S(1)} %add.122), channel_id=1, source_target_pairs={{0,64},{32,96},{64,0},{96,32},{1,65},{33,97},{65,1},{97,33},{2,66}... | collective-permute-start | bytes 196616 | tf_op jit(solution)/shard_map/ppermute | solution.py:18
  150.1 5.5 %collective-permute-start.22 = (f32[64,256]{1,0:T(8,128)S(1)}, f32[64,256]{1,0:T(8,128)S(1)}, u32[]{:S(2)}, u32[]{:S(2)}) collective-permute-start(f32[64,256]{1,0:T(8,128)S(1)} %add.122), channel_id=1, source_target_pairs={{0,32},{32,64},{64,96},{96,0},{1,33},{33,65},{65,97},{97,1},{2,34}... | collective-permute-start | bytes 196616 | tf_op jit(solution)/shard_map/ppermute | solution.py:18
  156.8 0.7 copy-start.10
  157.6 2.1 %copy-start.9 = (f32[256,256]{1,0:T(8,128)S(1)}, f32[256,256]{1,0:T(8,128)}, u32[]{:S(2)}) copy-start(f32[256,256]{1,0:T(8,128)} %shard_map.73) | copy-start | bytes 786436
  157.6 2.1 %copy-start.13 = (f32[2,256,256]{2,1,0:T(8,128)S(1)}, f32[2,256,256]{2,1,0:T(8,128)}, u32[]{:S(2)}) copy-start(f32[2,256,256]{2,1,0:T(8,128)} %param.8) | copy-start | bytes 1572868
  157.6 2.1 %collective-permute-start.23 = (f32[256,256]{1,0:T(8,128)}, f32[256,256]{1,0:T(8,128)S(1)}, u32[]{:S(2)}, u32[]{:S(2)}) collective-permute-start(f32[256,256]{1,0:T(8,128)} %shard_map.73), channel_id=1, source_target_pairs={{0,1},{1,0},{2,3},{3,2},{4,5},{5,4},{6,7},{7,6},{8,9},{9,8},{10,11... | collective-permute-start | bytes 786440 | tf_op jit(solution)/shard_map/ppermute | solution.py:18
Sparse Core Ops, SparseCore 0:
  13.6 90.8 all-gather.2
Sparse Core Ops, SparseCore 1:
  87.5 29.1 reduce-scatter.2
  119.0 25.8 reduce-scatter.4

commit v12 on v11

--- a/solution.py
+++ b/solution.py
@@ -104,7 +104,7 @@
     return pl.pallas_call(
         normed_kernel,
         out_shape=jax.ShapeDtypeStruct((piece, count * wide), F32),
-        compiler_params=pltpu.CompilerParams(vmem_limit_bytes=16 << 20),
+        compiler_params=pltpu.CompilerParams(vmem_limit_bytes=56 << 20),
         cost_estimate=pl.CostEstimate(
             flops=12 * count * piece * wide * wide, bytes_accessed=8 * count * piece * wide, transcendentals=0
         ),

time: 170 us -> 171 us (level)
  Pallas kernels: 24.9 us -> 26.9 us
  local copies, waits for them, and re-layouts: 12.3 us -> 10.3 us
    unnamed x34 -> x28, local copies, waits for them, and re-layouts: 10.1 us -> 8.05 us
    pallas_call x1, Pallas kernels: 0.55 us -> 2.5 us  [normed_rows(): pl.pallas_call(normed_kernel, out_shape=jax.ShapeDtypeStruct((piece, coun...]
  transfers between devices with their start and end apart: 27 -> 27, of which waited for: 16 -> 16; matrix products, arithmetic and copies ran while one was open for 5% -> 5% of each run, Pallas kernels for 15% -> 14%
where the time goes in v12:
time: 171 us; the launch traced here: 169 us
  starting transfers between devices  62.2 us (36%)
  waiting for transfers between devices  45.6 us (27%)
  Pallas kernels  26.9 us (16%)
  between operations  15.7 us (9%)
  local copies, waits for them, and re-layouts  10.3 us (6%)
  other arithmetic  8.17 us (5%)
    ppermute x23, starting transfers between devices, send(): return lax.ppermute(x, axis, [(i, to(i)) for i in range(size)])  60.4 us
    ppermute x23, waiting for transfers between devices, send(): return lax.ppermute(x, axis, [(i, to(i)) for i in range(size)])  45.4 us
    pallas_call x2, Pallas kernels, product(): pl.pallas_call(product_kernel, grid_spec=pltpu.PrefetchScalarGridSpec(num...  21.7 us
    unnamed x28, local copies, waits for them, and re-layouts  8.05 us
  transfers between devices with their start and end apart: 27, of which 16 were waited for; matrix products, arithmetic and copies ran while one was open for 5% of the time, Pallas kernels for 14%

profile of v12, /device:TPU:0, one launch (start us, length us, event | category | flops | bytes accessed | tf_op | source)
XLA Modules:
  0.0 168.8 jit_solution(9605082269456325312)
XLA Ops:
  8.1 0.8 fusion.12
  10.0 2.5 %shard_map.68.refs_0_ = f32[192,512]{1,0:T(8,128)} custom-call(f32[2,192,256]{2,1,0:T(8,128)} %panel_ref.1, f32[2,256,256]{2,1,0:T(8,128)} %factor_ref.1, f32[2,192,1]{2,1,0:T(8,128)} %pad_maximum_fusion.2.mask_ref), custom_call_target="tpu_custom_call" | custom-call | flops 301989888 | bytes 786432 | tf_op jit(solution)/shard_map/pallas_call | solution.py:104
  12.5 1.6 collective-permute-start
  14.2 0.7 copy-done.3
  15.0 13.8 %collective-permute-start.1 = (f32[192,512]{1,0:T(8,128)}, f32[192,512]{1,0:T(8,128)S(1)}, u32[]{:S(2)}, u32[]{:S(2)}) collective-permute-start(f32[192,512]{1,0:T(8,128)} %copy-done.3), channel_id=1, source_target_pairs={{0,16},{16,0},{1,17},{17,1},{2,18},{18,2},{3,19},{19,3},{4,20},{20... | collective-permute-start | bytes 1179656 | tf_op jit(solution)/shard_map/ppermute | solution.py:18
  28.8 3.7 %collective-permute-start.2 = (f32[192,512]{1,0:T(8,128)}, f32[192,512]{1,0:T(8,128)S(1)}, u32[]{:S(2)}, u32[]{:S(2)}) collective-permute-start(f32[192,512]{1,0:T(8,128)} %copy-done.3), channel_id=1, source_target_pairs={{0,32},{32,0},{64,96},{96,64},{1,33},{33,1},{65,97},{97,65},{2,34}... | collective-permute-start | bytes 1179656 | tf_op jit(solution)/shard_map/ppermute | solution.py:18
  32.5 6.2 %collective-permute-done.1.refs_1_ = f32[192,512]{1,0:T(8,128)S(1)} collective-permute-done((f32[192,512]{1,0:T(8,128)}, f32[192,512]{1,0:T(8,128)S(1)}, u32[]{:S(2)}, u32[]{:S(2)}) %collective-permute-start.1) | collective-permute-done | bytes 393248 | tf_op jit(solution)/shard_map/ppermute | solution.py:18
  38.7 7.9 %collective-permute-start.5 = (f32[192,512]{1,0:T(8,128)S(1)}, f32[192,512]{1,0:T(8,128)S(1)}, u32[]{:S(2)}, u32[]{:S(2)}) collective-permute-start(f32[192,512]{1,0:T(8,128)S(1)} %collective-permute-done.1.refs_1_), channel_id=1, source_target_pairs={{0,96},{32,64},{64,32},{96,0},{1,97},{33,65},{65,33},{97,1},{2,98}... | collective-permute-start | bytes 1179656 | tf_op jit(solution)/shard_map/ppermute | solution.py:18
  46.7 3.0 %collective-permute-start.3 = (f32[192,512]{1,0:T(8,128)S(1)}, f32[192,512]{1,0:T(8,128)S(1)}, u32[]{:S(2)}, u32[]{:S(2)}) collective-permute-start(f32[192,512]{1,0:T(8,128)S(1)} %collective-permute-done.1.refs_1_), channel_id=1, source_target_pairs={{0,32},{32,0},{64,96},{96,64},{1,33},{33,1},{65,97},{97,65},{2,34}... | collective-permute-start | bytes 1179656 | tf_op jit(solution)/shard_map/ppermute | solution.py:18
  49.7 2.6 %collective-permute-start.4 = (f32[192,512]{1,0:T(8,128)S(1)}, f32[192,512]{1,0:T(8,128)S(1)}, u32[]{:S(2)}, u32[]{:S(2)}) collective-permute-start(f32[192,512]{1,0:T(8,128)S(1)} %collective-permute-done.2.refs_2_), channel_id=1, source_target_pairs={{0,96},{32,64},{64,32},{96,0},{1,97},{33,65},{65,33},{97,1},{2,98}... | collective-permute-start | bytes 1179656 | tf_op jit(solution)/shard_map/ppermute | solution.py:18
  52.3 4.4 %collective-permute-done.5.refs_7_ = f32[192,512]{1,0:T(8,128)S(1)} collective-permute-done((f32[192,512]{1,0:T(8,128)S(1)}, f32[192,512]{1,0:T(8,128)S(1)}, u32[]{:S(2)}, u32[]{:S(2)}) %collective-permute-start.5) | collective-permute-done | bytes 393248 | tf_op jit(solution)/shard_map/ppermute | solution.py:18
  56.6 3.0 %collective-permute-start.6 = (f32[192,512]{1,0:T(8,128)S(1)}, f32[192,512]{1,0:T(8,128)S(1)}, u32[]{:S(2)}, u32[]{:S(2)}) collective-permute-start(f32[192,512]{1,0:T(8,128)S(1)} %collective-permute-done.5.refs_7_), channel_id=1, source_target_pairs={{0,32},{32,0},{64,96},{96,64},{1,33},{33,1},{65,97},{97,65},{2,34}... | collective-permute-start | bytes 1179656 | tf_op jit(solution)/shard_map/ppermute | solution.py:18
  59.8 5.3 %collective-permute-done.7.refs_6_ = f32[192,512]{1,0:T(8,128)S(1)} collective-permute-done((f32[192,512]{1,0:T(8,128)}, f32[192,512]{1,0:T(8,128)S(1)}, u32[]{:S(2)}, u32[]{:S(2)}) %collective-permute-start.7) | collective-permute-done | bytes 393248 | tf_op jit(solution)/shard_map/ppermute | solution.py:18
  65.1 6.3 %collective-permute-done.4.refs_4_ = f32[192,512]{1,0:T(8,128)S(1)} collective-permute-done((f32[192,512]{1,0:T(8,128)S(1)}, f32[192,512]{1,0:T(8,128)S(1)}, u32[]{:S(2)}, u32[]{:S(2)}) %collective-permute-start.4) | collective-permute-done | bytes 393248 | tf_op jit(solution)/shard_map/ppermute | solution.py:18
  71.3 1.0 copy-done.4
  72.3 10.8 %shard_map.69 = (f32[4,192,512]{2,1,0:T(8,128)S(1)}, f32[4,192,512]{2,1,0:T(8,128)S(1)}) custom-call(s32[9]{0:T(128)S(1)} %pad_add_fusion.place_ref, f32[3072,1536]{1,0:T(8,128)} %a_ref.3, f32[192,512]{1,0:T(8,128)S(1)} %copy-done.4, f32[192,512]{1,0:T(8,128)S(1)} %collective-permute-done.1.refs_1_, f32[192,512]{1,0:T(8,128)S(1)} %collective-permute-done.2.refs_2_, ...), custom_call_target="tpu_custom_call" | custom-call | flops 7247757312 | bytes 15728640 | tf_op jit(solution)/shard_map/pallas_call | solution.py:141
  83.3 3.4 %collective-permute-done.8 = f32[4,192,512]{2,1,0:T(8,128)S(1)} collective-permute-done((f32[4,192,512]{2,1,0:T(8,128)S(1)}, f32[4,192,512]{2,1,0:T(8,128)S(1)}, u32[]{:S(2)}, u32[]{:S(2)}) %collective-permute-start.8) | collective-permute-done | bytes 1572896 | tf_op jit(solution)/shard_map/ppermute | solution.py:18
  86.7 1.5 add.104.near_ref
  88.3 0.9 copy-done.5
  89.2 10.9 %shard_map.70 = (f32[4,192,512]{2,1,0:T(8,128)S(1)}, f32[4,192,512]{2,1,0:T(8,128)S(1)}) custom-call(s32[9]{0:T(128)S(1)} %pad_add_fusion.place_ref, f32[3072,1536]{1,0:T(8,128)} %a_ref.3, f32[192,512]{1,0:T(8,128)S(1)} %copy-done.5, f32[192,512]{1,0:T(8,128)S(1)} %collective-permute-done.1.refs_1_, f32[192,512]{1,0:T(8,128)S(1)} %collective-permute-done.2.refs_2_, ...), custom_call_target="tpu_custom_call" | custom-call | flops 7247757312 | bytes 15728640 | tf_op jit(solution)/shard_map/pallas_call | solution.py:141
  100.3 3.3 %collective-permute-done.9 = f32[4,192,512]{2,1,0:T(8,128)S(1)} collective-permute-done((f32[4,192,512]{2,1,0:T(8,128)S(1)}, f32[4,192,512]{2,1,0:T(8,128)S(1)}, u32[]{:S(2)}, u32[]{:S(2)}) %collective-permute-start.9) | collective-permute-done | bytes 1572896 | tf_op jit(solution)/shard_map/ppermute | solution.py:18
  103.5 1.5 add.105.far_ref
  105.2 1.2 copy-done
  106.5 1.4 copy-done.1
  107.9 1.9 %copy-done.2 = f32[1536,512]{1,0:T(8,128)S(1)} copy-done((f32[1536,512]{1,0:T(8,128)S(1)}, f32[1536,512]{1,0:T(8,128)}, u32[]{:S(2)}) %copy-start.2) | copy-done | bytes 3145752
  109.8 2.7 %shard_map.72 = (f32[256,256]{1,0:T(8,128)S(1)}, f32[256,256]{1,0:T(8,128)S(1)}) custom-call(f32[4,192,512]{2,1,0:T(8,128)S(1)} %copy-done, f32[4,192,512]{2,1,0:T(8,128)S(1)} %copy-done.1, f32[8,192,512]{2,1,0:T(8,128)S(1)} %bitcast.30), custom_call_target="tpu_custom_call" | custom-call | flops 1207959552 | bytes 6291456 | tf_op jit(solution)/shard_map/pallas_call | solution.py:176
  112.8 1.4 collective-permute-done.11
  114.3 2.1 %collective-permute-start.12 = (f32[64,256]{1,0:T(8,128)S(1)}, f32[64,256]{1,0:T(8,128)S(1)}, u32[]{:S(2)}, u32[]{:S(2)}) collective-permute-start(f32[64,256]{1,0:T(8,128)S(1)} %get-tuple-element.18), channel_id=1, source_target_pairs={{0,32},{32,64},{64,96},{96,0},{1,33},{33,65},{65,97},{97,1},{2,34}... | collective-permute-start | bytes 196616 | tf_op jit(solution)/shard_map/ppermute | solution.py:18
  116.4 2.4 %collective-permute-start.13 = (f32[64,256]{1,0:T(8,128)S(1)}, f32[64,256]{1,0:T(8,128)S(1)}, u32[]{:S(2)}, u32[]{:S(2)}) collective-permute-start(f32[64,256]{1,0:T(8,128)S(1)} %get-tuple-element.20), channel_id=1, source_target_pairs={{0,64},{32,96},{64,0},{96,32},{1,65},{33,97},{65,1},{97,33},{2,66}... | collective-permute-start | bytes 196616 | tf_op jit(solution)/shard_map/ppermute | solution.py:18
  118.8 2.0 %collective-permute-start.14 = (f32[64,256]{1,0:T(8,128)S(1)}, f32[64,256]{1,0:T(8,128)S(1)}, u32[]{:S(2)}, u32[]{:S(2)}) collective-permute-start(f32[64,256]{1,0:T(8,128)S(1)} %get-tuple-element.19), channel_id=1, source_target_pairs={{0,96},{32,0},{64,32},{96,64},{1,97},{33,1},{65,33},{97,65},{2,98}... | collective-permute-start | bytes 196616 | tf_op jit(solution)/shard_map/ppermute | solution.py:18
  120.8 1.7 collective-permute-done.13
  123.1 3.1 %collective-permute-start.15 = (f32[64,256]{1,0:T(8,128)S(1)}, f32[64,256]{1,0:T(8,128)S(1)}, u32[]{:S(2)}, u32[]{:S(2)}) collective-permute-start(f32[64,256]{1,0:T(8,128)S(1)} %add_add_fusion.1), channel_id=1, source_target_pairs={{0,4},{4,8},{8,12},{12,0},{1,5},{5,9},{9,13},{13,1},{2,6},{6,10},{... | collective-permute-start | bytes 196616 | tf_op jit(solution)/shard_map/ppermute | solution.py:18
  126.2 2.8 %collective-permute-start.17 = (f32[64,256]{1,0:T(8,128)S(1)}, f32[64,256]{1,0:T(8,128)S(1)}, u32[]{:S(2)}, u32[]{:S(2)}) collective-permute-start(f32[64,256]{1,0:T(8,128)S(1)} %add_add_fusion.1), channel_id=1, source_target_pairs={{0,12},{4,0},{8,4},{12,8},{1,13},{5,1},{9,5},{13,9},{2,14},{6,2},{... | collective-permute-start | bytes 196616 | tf_op jit(solution)/shard_map/ppermute | solution.py:18
  129.0 3.8 %collective-permute-done.16 = f32[64,256]{1,0:T(8,128)S(1)} collective-permute-done((f32[64,256]{1,0:T(8,128)S(1)}, f32[64,256]{1,0:T(8,128)S(1)}, u32[]{:S(2)}, u32[]{:S(2)}) %collective-permute-start.16) | collective-permute-done | bytes 65568 | tf_op jit(solution)/shard_map/ppermute | solution.py:18
  132.9 2.7 %collective-permute-start.18 = (f32[64,256]{1,0:T(8,128)S(1)}, f32[64,256]{1,0:T(8,128)S(1)}, u32[]{:S(2)}, u32[]{:S(2)}) collective-permute-start(f32[64,256]{1,0:T(8,128)S(1)} %add_add_fusion), channel_id=1, source_target_pairs={{0,2},{2,0},{1,3},{3,1},{4,6},{6,4},{5,7},{7,5},{8,10},{10,8},{9,1... | collective-permute-start | bytes 196616 | tf_op jit(solution)/shard_map/ppermute | solution.py:18
  135.5 2.2 %collective-permute-done.18 = f32[64,256]{1,0:T(8,128)S(1)} collective-permute-done((f32[64,256]{1,0:T(8,128)S(1)}, f32[64,256]{1,0:T(8,128)S(1)}, u32[]{:S(2)}, u32[]{:S(2)}) %collective-permute-start.18) | collective-permute-done | bytes 65568 | tf_op jit(solution)/shard_map/ppermute | solution.py:18
  137.8 4.5 %collective-permute-start.19 = (f32[64,256]{1,0:T(8,128)S(1)}, f32[64,256]{1,0:T(8,128)S(1)}, u32[]{:S(2)}, u32[]{:S(2)}) collective-permute-start(f32[64,256]{1,0:T(8,128)S(1)} %add.121), channel_id=1, source_target_pairs={{0,16},{16,0},{1,17},{17,1},{2,18},{18,2},{3,19},{19,3},{4,20},{20... | collective-permute-start | bytes 196616 | tf_op jit(solution)/shard_map/ppermute | solution.py:18
  142.7 1.9 %collective-permute-done.19 = f32[64,256]{1,0:T(8,128)S(1)} collective-permute-done((f32[64,256]{1,0:T(8,128)S(1)}, f32[64,256]{1,0:T(8,128)S(1)}, u32[]{:S(2)}, u32[]{:S(2)}) %collective-permute-start.19) | collective-permute-done | bytes 65568 | tf_op jit(solution)/shard_map/ppermute | solution.py:18
  144.5 2.2 %collective-permute-start.20 = (f32[64,256]{1,0:T(8,128)S(1)}, f32[64,256]{1,0:T(8,128)S(1)}, u32[]{:S(2)}, u32[]{:S(2)}) collective-permute-start(f32[64,256]{1,0:T(8,128)S(1)} %add.122), channel_id=1, source_target_pairs={{0,96},{32,0},{64,32},{96,64},{1,97},{33,1},{65,33},{97,65},{2,98}... | collective-permute-start | bytes 196616 | tf_op jit(solution)/shard_map/ppermute | solution.py:18
  146.8 1.1 select_bitcast_fusion
  147.9 1.8 %collective-permute-start.10 = (f32[192,512]{1,0:T(8,128)S(1)}, f32[192,512]{1,0:T(8,128)S(1)}, u32[]{:S(2)}, u32[]{:S(2)}) collective-permute-start(f32[192,512]{1,0:T(8,128)S(1)} %select_bitcast_fusion), channel_id=1, source_target_pairs={{0,2},{2,0},{1,3},{3,1},{4,6},{6,4},{5,7},{7,5},{8,10},{10,8},{9,1... | collective-permute-start | bytes 1179656 | tf_op jit(solution)/shard_map/ppermute | solution.py:18
  149.7 1.1 collective-permute-start.21
  150.8 1.0 collective-permute-start.22
  151.9 3.6 %collective-permute-done.21 = f32[64,256]{1,0:T(8,128)S(1)} collective-permute-done((f32[64,256]{1,0:T(8,128)S(1)}, f32[64,256]{1,0:T(8,128)S(1)}, u32[]{:S(2)}, u32[]{:S(2)}) %collective-permute-start.21) | collective-permute-done | bytes 65568 | tf_op jit(solution)/shard_map/ppermute | solution.py:18
  155.5 0.8 collective-permute-done.22
  158.4 1.2 bitcast_add_fusion
  159.7 0.8 pad_maximum_fusion.1
  160.6 0.8 pad_maximum_fusion
  (74 shorter events, 5.6 us)
Async XLA Ops:
  8.0 97.3 %all-gather.3.cloned.1.call-start = ((), (), s32[]{:S(2)}) async-start(), calls=%async_computation.4 | async-start | bytes 3538944 | tf_op jit(solution)/shard_map/all_gather | solution.py:213
  12.5 1.6 collective-permute-start
  14.2 0.7 copy-start.3
  15.0 131.8 %reduce-scatter.3.cloned.1.call-start = ((), (), s32[]{:S(2)}) async-start(), calls=%async_computation.2 | async-start | bytes 1966080 | tf_op jit(solution)/shard_map/reduce_scatter | solution.py:221
  15.0 23.7 %collective-permute-start.1 = (f32[192,512]{1,0:T(8,128)}, f32[192,512]{1,0:T(8,128)S(1)}, u32[]{:S(2)}, u32[]{:S(2)}) collective-permute-start(f32[192,512]{1,0:T(8,128)} %copy-done.3), channel_id=1, source_target_pairs={{0,16},{16,0},{1,17},{17,1},{2,18},{18,2},{3,19},{19,3},{4,20},{20... | collective-permute-start | bytes 1179656 | tf_op jit(solution)/shard_map/ppermute | solution.py:18
  28.8 20.9 %collective-permute-start.2 = (f32[192,512]{1,0:T(8,128)}, f32[192,512]{1,0:T(8,128)S(1)}, u32[]{:S(2)}, u32[]{:S(2)}) collective-permute-start(f32[192,512]{1,0:T(8,128)} %copy-done.3), channel_id=1, source_target_pairs={{0,32},{32,0},{64,96},{96,64},{1,33},{33,1},{65,97},{97,65},{2,34}... | collective-permute-start | bytes 1179656 | tf_op jit(solution)/shard_map/ppermute | solution.py:18
  38.7 17.9 %collective-permute-start.5 = (f32[192,512]{1,0:T(8,128)S(1)}, f32[192,512]{1,0:T(8,128)S(1)}, u32[]{:S(2)}, u32[]{:S(2)}) collective-permute-start(f32[192,512]{1,0:T(8,128)S(1)} %collective-permute-done.1.refs_1_), channel_id=1, source_target_pairs={{0,96},{32,64},{64,32},{96,0},{1,97},{33,65},{65,33},{97,1},{2,98}... | collective-permute-start | bytes 1179656 | tf_op jit(solution)/shard_map/ppermute | solution.py:18
  46.6 18.5 %collective-permute-start.7 = (f32[192,512]{1,0:T(8,128)}, f32[192,512]{1,0:T(8,128)S(1)}, u32[]{:S(2)}, u32[]{:S(2)}) collective-permute-start(f32[192,512]{1,0:T(8,128)} %copy-done.3), channel_id=1, source_target_pairs={{0,96},{32,64},{64,32},{96,0},{1,97},{33,65},{65,33},{97,1},{2,98}... | collective-permute-start | bytes 1179656 | tf_op jit(solution)/shard_map/ppermute | solution.py:18
  46.7 18.4 %collective-permute-start.3 = (f32[192,512]{1,0:T(8,128)S(1)}, f32[192,512]{1,0:T(8,128)S(1)}, u32[]{:S(2)}, u32[]{:S(2)}) collective-permute-start(f32[192,512]{1,0:T(8,128)S(1)} %collective-permute-done.1.refs_1_), channel_id=1, source_target_pairs={{0,32},{32,0},{64,96},{96,64},{1,33},{33,1},{65,97},{97,65},{2,34}... | collective-permute-start | bytes 1179656 | tf_op jit(solution)/shard_map/ppermute | solution.py:18
  49.7 21.6 %collective-permute-start.4 = (f32[192,512]{1,0:T(8,128)S(1)}, f32[192,512]{1,0:T(8,128)S(1)}, u32[]{:S(2)}, u32[]{:S(2)}) collective-permute-start(f32[192,512]{1,0:T(8,128)S(1)} %collective-permute-done.2.refs_2_), channel_id=1, source_target_pairs={{0,96},{32,64},{64,32},{96,0},{1,97},{33,65},{65,33},{97,1},{2,98}... | collective-permute-start | bytes 1179656 | tf_op jit(solution)/shard_map/ppermute | solution.py:18
  56.6 14.7 %collective-permute-start.6 = (f32[192,512]{1,0:T(8,128)S(1)}, f32[192,512]{1,0:T(8,128)S(1)}, u32[]{:S(2)}, u32[]{:S(2)}) collective-permute-start(f32[192,512]{1,0:T(8,128)S(1)} %collective-permute-done.5.refs_7_), channel_id=1, source_target_pairs={{0,32},{32,0},{64,96},{96,64},{1,33},{33,1},{65,97},{97,65},{2,34}... | collective-permute-start | bytes 1179656 | tf_op jit(solution)/shard_map/ppermute | solution.py:18
  71.3 1.0 copy-start.4
  83.2 3.5 %collective-permute-start.8 = (f32[4,192,512]{2,1,0:T(8,128)S(1)}, f32[4,192,512]{2,1,0:T(8,128)S(1)}, u32[]{:S(2)}, u32[]{:S(2)}) collective-permute-start(f32[4,192,512]{2,1,0:T(8,128)S(1)} %get-tuple-element.9), channel_id=1, source_target_pairs={{0,1},{1,0},{2,3},{3,2},{4,5},{5,4},{6,7},{7,6},{8,9},{9,8},{10,11... | collective-permute-start | bytes 4718600 | tf_op jit(solution)/shard_map/ppermute | solution.py:18
  88.2 1.0 copy-start.5
  88.2 58.5 %reduce-scatter.5.cloned.1.call-start = ((), (), s32[]{:S(2)}) async-start(), calls=%async_computation.3 | async-start | bytes 1966080 | tf_op jit(solution)/shard_map/reduce_scatter | solution.py:221
  100.1 3.5 %collective-permute-start.9 = (f32[4,192,512]{2,1,0:T(8,128)S(1)}, f32[4,192,512]{2,1,0:T(8,128)S(1)}, u32[]{:S(2)}, u32[]{:S(2)}) collective-permute-start(f32[4,192,512]{2,1,0:T(8,128)S(1)} %get-tuple-element.11), channel_id=1, source_target_pairs={{0,1},{1,0},{2,3},{3,2},{4,5},{5,4},{6,7},{7,6},{8,9},{9,8},{10,11... | collective-permute-start | bytes 4718600 | tf_op jit(solution)/shard_map/ppermute | solution.py:18
  105.1 1.4 copy-start
  106.5 1.4 copy-start.1
  107.9 1.9 %copy-start.2 = (f32[1536,512]{1,0:T(8,128)S(1)}, f32[1536,512]{1,0:T(8,128)}, u32[]{:S(2)}) copy-start(f32[1536,512]{1,0:T(8,128)} %all-gather.3.cloned.1.call-done) | copy-start | bytes 9437188
  112.6 1.6 collective-permute-start.11
  114.3 6.5 %collective-permute-start.12 = (f32[64,256]{1,0:T(8,128)S(1)}, f32[64,256]{1,0:T(8,128)S(1)}, u32[]{:S(2)}, u32[]{:S(2)}) collective-permute-start(f32[64,256]{1,0:T(8,128)S(1)} %get-tuple-element.18), channel_id=1, source_target_pairs={{0,32},{32,64},{64,96},{96,0},{1,33},{33,65},{65,97},{97,1},{2,34}... | collective-permute-start | bytes 196616 | tf_op jit(solution)/shard_map/ppermute | solution.py:18
  116.4 6.0 %collective-permute-start.13 = (f32[64,256]{1,0:T(8,128)S(1)}, f32[64,256]{1,0:T(8,128)S(1)}, u32[]{:S(2)}, u32[]{:S(2)}) collective-permute-start(f32[64,256]{1,0:T(8,128)S(1)} %get-tuple-element.20), channel_id=1, source_target_pairs={{0,64},{32,96},{64,0},{96,32},{1,65},{33,97},{65,1},{97,33},{2,66}... | collective-permute-start | bytes 196616 | tf_op jit(solution)/shard_map/ppermute | solution.py:18
  118.8 4.3 %collective-permute-start.14 = (f32[64,256]{1,0:T(8,128)S(1)}, f32[64,256]{1,0:T(8,128)S(1)}, u32[]{:S(2)}, u32[]{:S(2)}) collective-permute-start(f32[64,256]{1,0:T(8,128)S(1)} %get-tuple-element.19), channel_id=1, source_target_pairs={{0,96},{32,0},{64,32},{96,64},{1,97},{33,1},{65,33},{97,65},{2,98}... | collective-permute-start | bytes 196616 | tf_op jit(solution)/shard_map/ppermute | solution.py:18
  123.1 5.9 %collective-permute-start.15 = (f32[64,256]{1,0:T(8,128)S(1)}, f32[64,256]{1,0:T(8,128)S(1)}, u32[]{:S(2)}, u32[]{:S(2)}) collective-permute-start(f32[64,256]{1,0:T(8,128)S(1)} %add_add_fusion.1), channel_id=1, source_target_pairs={{0,4},{4,8},{8,12},{12,0},{1,5},{5,9},{9,13},{13,1},{2,6},{6,10},{... | collective-permute-start | bytes 196616 | tf_op jit(solution)/shard_map/ppermute | solution.py:18
  126.2 6.6 %collective-permute-start.16 = (f32[64,256]{1,0:T(8,128)S(1)}, f32[64,256]{1,0:T(8,128)S(1)}, u32[]{:S(2)}, u32[]{:S(2)}) collective-permute-start(f32[64,256]{1,0:T(8,128)S(1)} %add_add_fusion.1), channel_id=1, source_target_pairs={{0,8},{4,12},{8,0},{12,4},{1,9},{5,13},{9,1},{13,5},{2,10},{6,14},... | collective-permute-start | bytes 196616 | tf_op jit(solution)/shard_map/ppermute | solution.py:18
  126.2 6.6 %collective-permute-start.17 = (f32[64,256]{1,0:T(8,128)S(1)}, f32[64,256]{1,0:T(8,128)S(1)}, u32[]{:S(2)}, u32[]{:S(2)}) collective-permute-start(f32[64,256]{1,0:T(8,128)S(1)} %add_add_fusion.1), channel_id=1, source_target_pairs={{0,12},{4,0},{8,4},{12,8},{1,13},{5,1},{9,5},{13,9},{2,14},{6,2},{... | collective-permute-start | bytes 196616 | tf_op jit(solution)/shard_map/ppermute | solution.py:18
  132.9 4.9 %collective-permute-start.18 = (f32[64,256]{1,0:T(8,128)S(1)}, f32[64,256]{1,0:T(8,128)S(1)}, u32[]{:S(2)}, u32[]{:S(2)}) collective-permute-start(f32[64,256]{1,0:T(8,128)S(1)} %add_add_fusion), channel_id=1, source_target_pairs={{0,2},{2,0},{1,3},{3,1},{4,6},{6,4},{5,7},{7,5},{8,10},{10,8},{9,1... | collective-permute-start | bytes 196616 | tf_op jit(solution)/shard_map/ppermute | solution.py:18
  137.8 6.7 %collective-permute-start.19 = (f32[64,256]{1,0:T(8,128)S(1)}, f32[64,256]{1,0:T(8,128)S(1)}, u32[]{:S(2)}, u32[]{:S(2)}) collective-permute-start(f32[64,256]{1,0:T(8,128)S(1)} %add.121), channel_id=1, source_target_pairs={{0,16},{16,0},{1,17},{17,1},{2,18},{18,2},{3,19},{19,3},{4,20},{20... | collective-permute-start | bytes 196616 | tf_op jit(solution)/shard_map/ppermute | solution.py:18
  144.5 7.3 %collective-permute-start.20 = (f32[64,256]{1,0:T(8,128)S(1)}, f32[64,256]{1,0:T(8,128)S(1)}, u32[]{:S(2)}, u32[]{:S(2)}) collective-permute-start(f32[64,256]{1,0:T(8,128)S(1)} %add.122), channel_id=1, source_target_pairs={{0,96},{32,0},{64,32},{96,64},{1,97},{33,1},{65,33},{97,65},{2,98}... | collective-permute-start | bytes 196616 | tf_op jit(solution)/shard_map/ppermute | solution.py:18
  146.8 11.6 %copy-start.8 = (f32[1,192,512]{2,1,0:T(8,128)S(1)}, f32[1,192,512]{2,1,0:T(8,128)}, u32[]{:S(2)}) copy-start(f32[1,192,512]{2,1,0:T(8,128)} %reduce-scatter.3.cloned.1.call-done) | copy-start | bytes 1179652
  146.8 11.6 %copy-start.9 = (f32[1,192,512]{2,1,0:T(8,128)S(1)}, f32[1,192,512]{2,1,0:T(8,128)}, u32[]{:S(2)}) copy-start(f32[1,192,512]{2,1,0:T(8,128)} %reduce-scatter.5.cloned.1.call-done) | copy-start | bytes 1179652
  147.9 9.7 %collective-permute-start.10 = (f32[192,512]{1,0:T(8,128)S(1)}, f32[192,512]{1,0:T(8,128)S(1)}, u32[]{:S(2)}, u32[]{:S(2)}) collective-permute-start(f32[192,512]{1,0:T(8,128)S(1)} %select_bitcast_fusion), channel_id=1, source_target_pairs={{0,2},{2,0},{1,3},{3,1},{4,6},{6,4},{5,7},{7,5},{8,10},{10,8},{9,1... | collective-permute-start | bytes 1179656 | tf_op jit(solution)/shard_map/ppermute | solution.py:18
  149.7 5.8 %collective-permute-start.21 = (f32[64,256]{1,0:T(8,128)S(1)}, f32[64,256]{1,0:T(8,128)S(1)}, u32[]{:S(2)}, u32[]{:S(2)}) collective-permute-start(f32[64,256]{1,0:T(8,128)S(1)} %add.122), channel_id=1, source_target_pairs={{0,64},{32,96},{64,0},{96,32},{1,65},{33,97},{65,1},{97,33},{2,66}... | collective-permute-start | bytes 196616 | tf_op jit(solution)/shard_map/ppermute | solution.py:18
  150.8 5.5 %collective-permute-start.22 = (f32[64,256]{1,0:T(8,128)S(1)}, f32[64,256]{1,0:T(8,128)S(1)}, u32[]{:S(2)}, u32[]{:S(2)}) collective-permute-start(f32[64,256]{1,0:T(8,128)S(1)} %add.122), channel_id=1, source_target_pairs={{0,32},{32,64},{64,96},{96,0},{1,33},{33,65},{65,97},{97,1},{2,34}... | collective-permute-start | bytes 196616 | tf_op jit(solution)/shard_map/ppermute | solution.py:18
  157.6 0.7 copy-start.7
  158.4 2.1 %copy-start.6 = (f32[256,256]{1,0:T(8,128)S(1)}, f32[256,256]{1,0:T(8,128)}, u32[]{:S(2)}) copy-start(f32[256,256]{1,0:T(8,128)} %shard_map.73) | copy-start | bytes 786436
  158.4 2.1 %copy-start.10 = (f32[2,256,256]{2,1,0:T(8,128)S(1)}, f32[2,256,256]{2,1,0:T(8,128)}, u32[]{:S(2)}) copy-start(f32[2,256,256]{2,1,0:T(8,128)} %param.8) | copy-start | bytes 1572868
  158.4 2.1 %collective-permute-start.23 = (f32[256,256]{1,0:T(8,128)}, f32[256,256]{1,0:T(8,128)S(1)}, u32[]{:S(2)}, u32[]{:S(2)}) collective-permute-start(f32[256,256]{1,0:T(8,128)} %shard_map.73), channel_id=1, source_target_pairs={{0,1},{1,0},{2,3},{3,2},{4,5},{5,4},{6,7},{7,6},{8,9},{9,8},{10,11... | collective-permute-start | bytes 786440 | tf_op jit(solution)/shard_map/ppermute | solution.py:18
Sparse Core Ops, SparseCore 0:
  15.1 90.1 all-gather.2
Sparse Core Ops, SparseCore 1:
  88.3 29.2 reduce-scatter.2
  119.9 25.7 reduce-scatter.4
